TPU v7x, 128 devices: a whole 4x4x4 slice. The times are simulated.
128 devices in a mesh: blk: 32 (over z, x, y_hi), sub: 4 (over y_lo, core).
Axes of the slice: x: 4, y: 4 (y_hi: 2, y_lo: 2; y = y_hi * 2 + y_lo), z: 4, core: 2. Of those that a mesh axis runs over, the one named last changes fastest.
Arguments:
- features: bfloat16 [49152, 768], P(('blk', 'sub')), may hold values from -6 to 6
- scales: bfloat16 [49152], P('blk'), may hold values from 0.5 to 4
- neighbor_lists: int32 [9, 16, 49152], P(None, None, 'blk'), may hold values from 0 to 1535, as said below
- eigen_block: float32 [64, 49152], P(None, ('blk', 'sub')), may hold values from -6 to 6
Outputs:
- embedding: float32 [64, 49152], P(None, ('blk', 'sub'))
Inputs may be any that keep to these rules, and one draw needn't show every extreme that they name: For each j and point p, the 16 entries neighbor_lists[j, :, p] are distinct positions within the row block that lies j - 4 blocks before p's block, counted cyclically.
All inputs are finite; a program needn't handle non-finite values.
Results may differ from a plain program's by a relative error of at most 0.0039.
Values may be sent and summed in bfloat16 or wider, within the bound.
No kernel may reach another device: no remote copies, remote signals or barrier semaphores. Data moves between devices by JAX's collectives and lax.ppermute only.
A program may use at most 128 MiB of HBM per device.

v0:
```python
import functools
import math

import jax
import jax.numpy as jnp
from jax import lax
from jax.experimental import pallas as pl
from jax.experimental.pallas import tpu as pltpu
from jax.sharding import PartitionSpec as P

F = 768
ROWS = 384
SLOTS = 4
EIG = 64
NNB = 16
BAND = ((1, 2), (-2, 0), (-3, 2), (4, 0))
FOLDED = 2.0 * math.log2(math.e) / F
NT = (((1,), (1,)), ((), ()))
LIMIT = 48 * 1024 * 1024


def moved(value, blocks, flip):
    n_blk, n_sub = lax.axis_size("blk"), lax.axis_size("sub")
    pairs = [
        (b * n_sub + s, ((b + blocks) % n_blk) * n_sub + (s ^ flip))
        for b in range(n_blk)
        for s in range(n_sub)
    ]
    return lax.ppermute(value, ("blk", "sub"), pairs)


def call(body, outs, scratch=(), flops=10**9, smem=0):
    vmem = pl.BlockSpec(memory_space=pltpu.VMEM)

    def run(*args):
        specs = [pl.BlockSpec(memory_space=pltpu.SMEM)] * smem + [vmem] * (len(args) - smem)
        return pl.pallas_call(
            body,
            out_shape=outs,
            in_specs=specs,
            out_specs=jax.tree.map(lambda _: vmem, outs),
            scratch_shapes=list(scratch),
            compiler_params=pltpu.CompilerParams(vmem_limit_bytes=LIMIT),
            cost_estimate=pl.CostEstimate(flops=flops, bytes_accessed=4 * 10**6, transcendentals=0),
        )(*args)

    return run


def f32(*shape):
    return jax.ShapeDtypeStruct(shape, jnp.float32)


def bf16(*shape):
    return jax.ShapeDtypeStruct(shape, jnp.bfloat16)


def norms_kernel(f0, f1, f2, f3, out):
    ones = jnp.ones((8, F), jnp.bfloat16)
    for slot, ref in enumerate((f0, f1, f2, f3)):
        value = ref[...].astype(jnp.float32)
        square = value * value
        high = square.astype(jnp.bfloat16)
        low = (square - high.astype(jnp.float32)).astype(jnp.bfloat16)
        total = lax.dot_general(ones, high, NT, preferred_element_type=jnp.float32)
        total = total + lax.dot_general(ones, low, NT, preferred_element_type=jnp.float32)
        out[slot : slot + 1, :] = total[0:1, :]


def tile_kernel(flip, reverse, sub, f0, f1, f2, f3, moving, norms, scales, lists, aux, tile, row, col, inner, words, cols):
    me = sub[0]
    feats = moving[...].astype(jnp.float32)
    half_norm = 0.5 * jnp.sum(feats * feats, axis=1, keepdims=True)

    block_scale = aux[16:17, :]
    pieces = []
    if reverse:
        position = aux[0:16, :].astype(jnp.int32)
        group = position >> 7
        slice_at = (group * 11) >> 5
        group = (slice_at ^ me) * 3 + group - 3 * slice_at
        pieces = [(position & 127).astype(jnp.float32), jnp.left_shift(1, group).astype(jnp.float32)]
    else:
        pieces = [jnp.zeros((32, ROWS), jnp.float32)]
    stacked = jnp.concatenate(
        pieces + [FOLDED / block_scale, jnp.zeros((95, ROWS), jnp.float32)], axis=0
    )
    turned = stacked.T
    move_scale = turned[:, 32:33]
    if reverse:
        lane = lax.broadcasted_iota(jnp.int32, (64, 128), 1).astype(jnp.float32)
        for at in range(0, ROWS, 64):
            part = turned[at : at + 64]
            word = jnp.zeros((64, 128), jnp.float32)
            for m in range(NNB):
                word = word + jnp.where(part[:, m : m + 1] == lane, part[:, 16 + m : 17 + m], 0.0)
            words[at : at + 64, :] = word.astype(jnp.int32)

    row_at = lax.broadcasted_iota(jnp.int32, (8, ROWS), 0)
    for slot, ref in enumerate((f0, f1, f2, f3)):
        inner[...] = lax.dot_general(moving[...], ref[...], NT, preferred_element_type=jnp.float32)
        start = pl.multiple_of((me ^ slot) * ROWS, 128)
        listed = lists[:, pl.ds(start, ROWS)] - (me ^ flip) * ROWS
        inside = (listed >= 0) & (listed < ROWS)
        sublane = listed & 7
        bit = jnp.where(inside, listed >> 3, 0)
        first = jnp.where(inside & (bit < 24), jnp.left_shift(1, bit), 0)
        second = jnp.where(inside & (bit >= 24), jnp.left_shift(1, jnp.maximum(bit - 24, 0)), 0)
        low = jnp.zeros((8, ROWS), jnp.int32)
        high = jnp.zeros((8, ROWS), jnp.int32)
        for m in range(NNB):
            same = sublane[m : m + 1, :] == row_at
            low = low | jnp.where(same, first[m : m + 1, :], 0)
            high = high | jnp.where(same, second[m : m + 1, :], 0)
        norm = 0.5 * norms[slot : slot + 1, :]
        scale = 1.0 / scales[:, pl.ds(start, ROWS)]
        row_sum = jnp.zeros((8, ROWS), jnp.float32)
        step = 32
        for at in range(0, ROWS, step):
            source = low if at < 192 else high
            counts = [
                (source >> ((at // 8 + c) % 24)) & 1 for c in range(step // 8)
            ]
            count = jnp.concatenate(counts, axis=0)
            if reverse:
                word = words[at : at + step, :]
                count = count + jnp.concatenate(
                    [(word >> (3 * slot + g)) & 1 for g in range(3)], axis=1
                )
            power = inner[at : at + step, :] - half_norm[at : at + step] - norm
            power = power * move_scale[at : at + step] * scale
            weight = jnp.exp2(power) * count.astype(jnp.float32)
            tile[at : at + step, slot * ROWS : (slot + 1) * ROWS] = weight.astype(jnp.bfloat16)
            for c in range(step // 8):
                row_sum = row_sum + weight[8 * c : 8 * c + 8, :]
            lanes = weight[:, 0:128] + weight[:, 128:256] + weight[:, 256:384]
            if slot == 0:
                cols[at : at + step, :] = lanes
            else:
                cols[at : at + step, :] = cols[at : at + step, :] + lanes
        row[slot : slot + 1, :] = jnp.sum(row_sum, axis=0, keepdims=True)
    col[...] = jnp.sum(cols[...].T, axis=0, keepdims=True)


def col_kernel(e0, e1, e2, e3, root, t0, t1, t2, t3, t4, z0, z1, z2, z3, z4):
    block = jnp.concatenate(
        [(ref[...] * root[slot : slot + 1, :]).astype(jnp.bfloat16) for slot, ref in enumerate((e0, e1, e2, e3))],
        axis=1,
    )
    for tile, out in ((t1, z1), (t2, z2), (t3, z3), (t4, z4), (t0, z0)):
        out[...] = lax.dot_general(block, tile[...], NT, preferred_element_type=jnp.float32).astype(out.dtype)


def row_kernel(x0, x1, x2, x3, x4, t0, t1, t2, t3, t4, kept, sent):
    for half, out in ((1, sent), (0, kept)):
        at = half * 2 * ROWS
        total = jnp.zeros((EIG, 2 * ROWS), jnp.float32)
        for vectors, tile in ((x0, t0), (x1, t1), (x2, t2), (x3, t3), (x4, t4)):
            total = total + jnp.dot(
                vectors[...], tile[:, at : at + 2 * ROWS], preferred_element_type=jnp.float32
            )
        out[...] = total.astype(out.dtype)


def mix_kernel(own, root, y0, y1, y2, z0, z1, z2, z3, z4, mixed, gram):
    sides = y0[...] + y1[...].astype(jnp.float32) + y2[...] + z0[...]
    for part in (z1, z2, z3, z4):
        sides = sides + part[...].astype(jnp.float32)
    inv = root[0:1, :]
    value = inv * (own[...] * inv + 0.5 * sides)
    mixed[...] = value
    gram[...] = lax.dot_general(
        value, value, NT, precision=lax.Precision.HIGHEST, preferred_element_type=jnp.float32
    )


def solve_kernel(factor, gram, mixed, out):
    rows = lax.broadcasted_iota(jnp.int32, (EIG, 2 * EIG), 0)
    lanes = lax.broadcasted_iota(jnp.int32, (EIG, 2 * EIG), 1)
    unit = (rows + EIG == lanes).astype(jnp.float32)
    work = jnp.concatenate([gram[...], jnp.zeros((EIG, EIG), jnp.float32)], axis=1) + unit
    done = []
    for j in range(EIG):
        pivot = work[j : j + 1, :]
        root = lax.rsqrt(jnp.broadcast_to(pivot[:, j : j + 1], (1, 2 * EIG)))
        pivot = pivot * root
        done.append(pivot)
        if j + 1 < EIG:
            lower = jnp.broadcast_to(work[:, j : j + 1], (EIG, 2 * EIG)) * root
            work = work - lower * pivot
    inverse = jnp.concatenate(done, axis=0)[:, EIG:]
    out[...] = factor * jnp.dot(
        inverse, mixed[...], precision=lax.Precision.HIGHEST, preferred_element_type=jnp.float32
    )


def local(features, scales, neighbor_lists, eigen_block):
    sub = lax.axis_index("sub").astype(jnp.int32)
    half = (neighbor_lists.shape[0] - 1) // 2
    total_rows = ROWS * lax.axis_size("blk") * lax.axis_size("sub")
    sub_arg = sub.reshape(1)

    own_lists = lax.dynamic_slice_in_dim(neighbor_lists, sub * ROWS, ROWS, axis=2)
    own_scale = lax.dynamic_slice_in_dim(scales, sub * ROWS, ROWS).astype(jnp.float32)
    aux = jnp.concatenate(
        [
            own_lists.astype(jnp.float32),
            jnp.broadcast_to(own_scale[None, None, :], (2 * half + 1, 8, ROWS)),
        ],
        axis=1,
    )
    block_scales = scales.astype(jnp.float32)[None, :]

    slot2 = moved(features, 0, 2)
    slices = [moved(features, d, u) for d, u in BAND]
    side = [moved(aux[half - d], d, u) for d, u in BAND]
    slot1 = moved(features, 0, 1)
    slot3 = moved(slot2, 0, 1)
    block = (features, slot1, slot2, slot3)
    norms = call(norms_kernel, f32(SLOTS, ROWS))(*block)

    tile_outs = (bf16(ROWS, SLOTS * ROWS), f32(SLOTS, ROWS), f32(1, ROWS))
    scratch = (
        pltpu.VMEM((ROWS, ROWS), jnp.float32),
        pltpu.VMEM((ROWS, 128), jnp.int32),
        pltpu.VMEM((ROWS, 128), jnp.float32),
    )
    tiles, rows, cols = [], [], []
    work = [((0, 0), features, aux[half])] + list(zip(BAND, slices, side))
    for index, ((d, u), moving, extra) in enumerate(work):
        body = functools.partial(tile_kernel, u, index > 0)
        tile, row, col = call(body, tile_outs, scratch, 3 * 10**9, 1)(
            sub_arg, *block, moving, norms, block_scales, neighbor_lists[half + d], extra
        )
        tiles.append(tile)
        rows.append(row)
        cols.append(col if index == 0 else moved(col, -d, u))

    e1 = moved(eigen_block, 0, 1)
    e2 = moved(eigen_block, 0, 2)
    e3 = moved(e2, 0, 1)

    own_cols = functools.reduce(jnp.add, cols)
    sums = functools.reduce(jnp.add, rows)
    sums = jnp.concatenate([sums[0:1] + own_cols, sums[1:]], axis=0)
    other = moved(sums, 0, 1)
    sums = sums + jnp.concatenate([other[1:2], other[0:1], other[3:4], other[2:3]], axis=0)
    other = moved(sums, 0, 2)
    sums = sums + jnp.concatenate([other[2:4], other[0:2]], axis=0)
    root = lax.rsqrt(1.0 + 0.5 * sums)
    scaled_low = (eigen_block * root[0:1]).astype(jnp.bfloat16)
    vectors = [moved(scaled_low, d, u) for d, u in BAND]

    z_outs = (f32(EIG, ROWS),) + (bf16(EIG, ROWS),) * 4
    z = call(col_kernel, z_outs, (), 10**9)(eigen_block, e1, e2, e3, root, *tiles)
    back = [moved(part, -d, u) for (d, u), part in zip(BAND, z[1:])]
    kept, sent = call(row_kernel, (f32(EIG, 2 * ROWS), bf16(EIG, 2 * ROWS)), (), 10**9)(
        scaled_low, *vectors, *tiles
    )
    got = moved(sent, 0, 2)
    pair = moved(kept[:, ROWS:] + got[:, ROWS:].astype(jnp.float32), 0, 1)
    mixed, gram = call(mix_kernel, (f32(EIG, ROWS), f32(EIG, EIG)))(
        eigen_block, root, kept[:, :ROWS], got[:, :ROWS], pair, z[0], *back
    )
    flip = 1
    while flip < lax.axis_size("sub"):
        gram = gram + moved(gram, 0, flip)
        flip *= 2
    flip = 1
    n_blk, n_sub = lax.axis_size("blk"), lax.axis_size("sub")
    while flip < n_blk:
        gram = gram + lax.ppermute(gram, "blk", [(b, b ^ flip) for b in range(n_blk)])
        flip *= 2
    body = functools.partial(solve_kernel, math.sqrt(total_rows))
    return call(body, f32(EIG, ROWS))(gram, mixed)


def solution(mesh):
    placed = (P(("blk", "sub"), None), P("blk"), P(None, None, "blk"), P(None, ("blk", "sub")))
    return jax.shard_map(
        local, mesh=mesh, in_specs=placed, out_specs=P(None, ("blk", "sub")), check_vma=False
    )
```

profile of v0, /device:TPU:0, one launch (start us, length us, event | category | flops | bytes accessed | tf_op | source)
XLA Modules:
  0.0 169.0 jit_solution(9647877782420982170)
XLA Ops:
  0.0 1.7 collective-permute-start.1
  1.7 8.1 %collective-permute-start.7 = (bf16[384,768]{1,0:T(8,128)(2,1)}, bf16[384,768]{1,0:T(8,128)(2,1)}, u32[]{:S(2)}, u32[]{:S(2)}) collective-permute-start(bf16[384,768]{1,0:T(8,128)(2,1)} %f0.11), channel_id=1, source_target_pairs={{0,118},{1,119},{2,116},{3,117},{4,122},{5,123},{6,120},{7,121},{8... | collective-permute-start | bytes 1769480 | tf_op jit(solution)/shard_map/ppermute | solution.py:29
  9.8 1.1 collective-permute-start.5
  10.9 0.5 collective-permute-start.3
  11.4 3.9 %collective-permute-done.1.f2 = bf16[384,768]{1,0:T(8,128)(2,1)S(1)} collective-permute-done((bf16[384,768]{1,0:T(8,128)(2,1)}, bf16[384,768]{1,0:T(8,128)(2,1)S(1)}, u32[]{:S(2)}, u32[]{:S(2)}) %collective-permute-start.1) | collective-permute-done | bytes 589856 | tf_op jit(solution)/shard_map/ppermute | solution.py:29
  15.3 0.0 collective-permute-start.2
  15.3 1.1 slice_bitcast_fusion.3
  16.4 0.7 reshape.5.scales
  17.1 1.0 dynamic-slice_convert_fusion
  18.0 0.8 dynamic-slice_convert_fusion.1
  18.8 0.0 collective-permute-done.f1
  18.9 3.2 %collective-permute-start.9 = (bf16[384,768]{1,0:T(8,128)(2,1)S(1)}, bf16[384,768]{1,0:T(8,128)(2,1)S(1)}, u32[]{:S(2)}, u32[]{:S(2)}) collective-permute-start(bf16[384,768]{1,0:T(8,128)(2,1)S(1)} %copy-done.2), channel_id=1, source_target_pairs={{0,16},{1,17},{2,18},{3,19},{4,20},{5,21},{6,22},{7,23},{8,24},{9,... | collective-permute-start | bytes 1769480 | tf_op jit(solution)/shard_map/ppermute | solution.py:29
  22.1 6.0 %collective-permute-start.8 = (f32[24,384]{1,0:T(8,128)S(1)}, f32[24,384]{1,0:T(8,128)S(1)}, u32[]{:S(2)}, u32[]{:S(2)}) collective-permute-start(f32[24,384]{1,0:T(8,128)S(1)} %get-tuple-element.59), channel_id=1, source_target_pairs={{0,118},{1,119},{2,116},{3,117},{4,122},{5,123},{6,120},{7,121},{8... | collective-permute-start | bytes 110600 | tf_op jit(solution)/shard_map/ppermute | solution.py:29
  28.1 1.4 shard_map.46.norms
  29.4 20.1 %collective-permute-done.8.aux = f32[24,384]{1,0:T(8,128)S(1)} collective-permute-done((f32[24,384]{1,0:T(8,128)S(1)}, f32[24,384]{1,0:T(8,128)S(1)}, u32[]{:S(2)}, u32[]{:S(2)}) %collective-permute-start.8) | collective-permute-done | bytes 36896 | tf_op jit(solution)/shard_map/ppermute | solution.py:29
  49.6 6.2 %collective-permute-start.4 = (f32[24,384]{1,0:T(8,128)S(1)}, f32[24,384]{1,0:T(8,128)S(1)}, u32[]{:S(2)}, u32[]{:S(2)}) collective-permute-start(f32[24,384]{1,0:T(8,128)S(1)} %get-tuple-element.58), channel_id=1, source_target_pairs={{0,6},{1,7},{2,4},{3,5},{4,10},{5,11},{6,8},{7,9},{8,14},{9,15},{1... | collective-permute-start | bytes 110600 | tf_op jit(solution)/shard_map/ppermute | solution.py:29
  55.8 5.2 %collective-permute-start.6 = (f32[24,384]{1,0:T(8,128)S(1)}, f32[24,384]{1,0:T(8,128)S(1)}, u32[]{:S(2)}, u32[]{:S(2)}) collective-permute-start(f32[24,384]{1,0:T(8,128)S(1)} %get-tuple-element.60), channel_id=1, source_target_pairs={{0,120},{1,121},{2,122},{3,123},{4,124},{5,125},{6,126},{7,127},{8... | collective-permute-start | bytes 110600 | tf_op jit(solution)/shard_map/ppermute | solution.py:29
  61.1 4.3 %shard_map.50 = (bf16[384,1536]{1,0:T(8,128)(2,1)S(1)}, f32[4,384]{1,0:T(4,128)S(1)}, f32[1,384]{1,0:T(1,128)S(1)}) custom-call(s32[1]{0:T(128)} %bitcast.sub, bf16[384,768]{1,0:T(8,128)(2,1)S(1)} %copy-done.2, bf16[384,768]{1,0:T(8,128)(2,1)S(1)} %collective-permute-done.f1, bf16[384,768]{1,0:T(8,128)(2,1)S(1)} %collective-permute-done.1.f2, ...), custom_call_target="tpu_custom_call" | custom-call | flops 3000000000 | bytes 4000000 | tf_op jit(solution)/shard_map/pallas_call | solution.py:37
  65.4 0.1 collective-permute-start.10
  65.5 0.3 collective-permute-start.13
  65.7 4.3 %shard_map.49 = (bf16[384,1536]{1,0:T(8,128)(2,1)S(1)}, f32[4,384]{1,0:T(4,128)S(1)}, f32[1,384]{1,0:T(1,128)S(1)}) custom-call(s32[1]{0:T(128)} %bitcast.sub, bf16[384,768]{1,0:T(8,128)(2,1)S(1)} %copy-done.2, bf16[384,768]{1,0:T(8,128)(2,1)S(1)} %collective-permute-done.f1, bf16[384,768]{1,0:T(8,128)(2,1)S(1)} %collective-permute-done.1.f2, ...), custom_call_target="tpu_custom_call" | custom-call | flops 3000000000 | bytes 4000000 | tf_op jit(solution)/shard_map/pallas_call | solution.py:37
  70.0 0.1 collective-permute-start.12
  70.1 3.4 %shard_map.48 = (bf16[384,1536]{1,0:T(8,128)(2,1)S(1)}, f32[4,384]{1,0:T(4,128)S(1)}, f32[1,384]{1,0:T(1,128)S(1)}) custom-call(s32[1]{0:T(128)} %bitcast.sub, bf16[384,768]{1,0:T(8,128)(2,1)S(1)} %copy-done.2, bf16[384,768]{1,0:T(8,128)(2,1)S(1)} %collective-permute-done.f1, bf16[384,768]{1,0:T(8,128)(2,1)S(1)} %collective-permute-done.1.f2, ...), custom_call_target="tpu_custom_call" | custom-call | flops 3000000000 | bytes 4000000 | tf_op jit(solution)/shard_map/pallas_call | solution.py:37
  73.5 5.1 %collective-permute-start.11 = (f32[1,384]{1,0:T(1,128)S(1)}, f32[1,384]{1,0:T(1,128)S(1)}, u32[]{:S(2)}, u32[]{:S(2)}) collective-permute-start(f32[1,384]{1,0:T(1,128)S(1)} %get-tuple-element.35), channel_id=1, source_target_pairs={{0,126},{1,127},{2,124},{3,125},{4,2},{5,3},{6,0},{7,1},{8,6},{9,7... | collective-permute-start | bytes 4616 | tf_op jit(solution)/shard_map/ppermute | solution.py:29
  78.6 0.0 collective-permute-done.10.aux
  78.6 0.0 collective-permute-done.9.moving
  78.6 3.4 %shard_map.51 = (bf16[384,1536]{1,0:T(8,128)(2,1)S(1)}, f32[4,384]{1,0:T(4,128)S(1)}, f32[1,384]{1,0:T(1,128)S(1)}) custom-call(s32[1]{0:T(128)} %bitcast.sub, bf16[384,768]{1,0:T(8,128)(2,1)S(1)} %copy-done.2, bf16[384,768]{1,0:T(8,128)(2,1)S(1)} %collective-permute-done.f1, bf16[384,768]{1,0:T(8,128)(2,1)S(1)} %collective-permute-done.1.f2, ...), custom_call_target="tpu_custom_call" | custom-call | flops 3000000000 | bytes 4000000 | tf_op jit(solution)/shard_map/pallas_call | solution.py:37
  82.0 1.1 copy-done
  83.1 4.7 %collective-permute-start.14 = (f32[1,384]{1,0:T(1,128)S(1)}, f32[1,384]{1,0:T(1,128)S(1)}, u32[]{:S(2)}, u32[]{:S(2)}) collective-permute-start(f32[1,384]{1,0:T(1,128)S(1)} %get-tuple-element.38), channel_id=1, source_target_pairs={{0,112},{1,113},{2,114},{3,115},{4,116},{5,117},{6,118},{7,119},{8... | collective-permute-start | bytes 4616 | tf_op jit(solution)/shard_map/ppermute | solution.py:29
  87.8 1.9 %shard_map.47 = (bf16[384,1536]{1,0:T(8,128)(2,1)S(1)}, f32[4,384]{1,0:T(4,128)S(1)}, f32[1,384]{1,0:T(1,128)S(1)}) custom-call(s32[1]{0:T(128)} %bitcast.sub, bf16[384,768]{1,0:T(8,128)(2,1)S(1)} %copy-done.2, bf16[384,768]{1,0:T(8,128)(2,1)S(1)} %collective-permute-done.f1, bf16[384,768]{1,0:T(8,128)(2,1)S(1)} %collective-permute-done.1.f2, ...), custom_call_target="tpu_custom_call" | custom-call | flops 3000000000 | bytes 4000000 | tf_op jit(solution)/shard_map/pallas_call | solution.py:37
  89.7 0.1 collective-permute-start.15
  89.8 1.2 collective-permute-done.15
  91.0 0.1 collective-permute-start.16
  91.1 3.6 %collective-permute-done.16 = f32[4,384]{1,0:T(4,128)S(1)} collective-permute-done((f32[4,384]{1,0:T(4,128)S(1)}, f32[4,384]{1,0:T(4,128)S(1)}, u32[]{:S(2)}, u32[]{:S(2)}) %collective-permute-start.16) | collective-permute-done | bytes 6176 | tf_op jit(solution)/shard_map/ppermute | solution.py:29
  94.8 0.1 collective-permute-start.20
  94.9 4.1 %collective-permute-start.19 = (bf16[64,384]{1,0:T(8,128)(2,1)S(1)}, bf16[64,384]{1,0:T(8,128)(2,1)S(1)}, u32[]{:S(2)}, u32[]{:S(2)}) collective-permute-start(bf16[64,384]{1,0:T(8,128)(2,1)S(1)} %multiply_convert_fusion.x0), channel_id=1, source_target_pairs={{0,118},{1,119},{2,116},{3,117},{4,122},{5,123},{6,120},{7,121},{8... | collective-permute-start | bytes 147464 | tf_op jit(solution)/shard_map/ppermute | solution.py:29
  99.0 2.9 %collective-permute-start.18 = (bf16[64,384]{1,0:T(8,128)(2,1)S(1)}, bf16[64,384]{1,0:T(8,128)(2,1)S(1)}, u32[]{:S(2)}, u32[]{:S(2)}) collective-permute-start(bf16[64,384]{1,0:T(8,128)(2,1)S(1)} %multiply_convert_fusion.x0), channel_id=1, source_target_pairs={{0,120},{1,121},{2,122},{3,123},{4,124},{5,125},{6,126},{7,127},{8... | collective-permute-start | bytes 147464 | tf_op jit(solution)/shard_map/ppermute | solution.py:29
  101.9 1.8 %collective-permute-start.17 = (bf16[64,384]{1,0:T(8,128)(2,1)S(1)}, bf16[64,384]{1,0:T(8,128)(2,1)S(1)}, u32[]{:S(2)}, u32[]{:S(2)}) collective-permute-start(bf16[64,384]{1,0:T(8,128)(2,1)S(1)} %multiply_convert_fusion.x0), channel_id=1, source_target_pairs={{0,6},{1,7},{2,4},{3,5},{4,10},{5,11},{6,8},{7,9},{8,14},{9,15},{1... | collective-permute-start | bytes 147464 | tf_op jit(solution)/shard_map/ppermute | solution.py:29
  103.8 7.7 %collective-permute-done.17.x1 = bf16[64,384]{1,0:T(8,128)(2,1)S(1)} collective-permute-done((bf16[64,384]{1,0:T(8,128)(2,1)S(1)}, bf16[64,384]{1,0:T(8,128)(2,1)S(1)}, u32[]{:S(2)}, u32[]{:S(2)}) %collective-permute-start.17) | collective-permute-done | bytes 49184 | tf_op jit(solution)/shard_map/ppermute | solution.py:29
  111.4 2.3 %shard_map.52 = (f32[64,768]{1,0:T(8,128)S(1)}, bf16[64,768]{1,0:T(8,128)(2,1)S(1)}) custom-call(bf16[64,384]{1,0:T(8,128)(2,1)S(1)} %multiply_convert_fusion.x0, bf16[64,384]{1,0:T(8,128)(2,1)S(1)} %collective-permute-done.17.x1, bf16[64,384]{1,0:T(8,128)(2,1)S(1)} %collective-permute-done.18.x2, bf16[64,384]{1,0:T(8,128)(2,1)S(1)} %collective-permute-done.19.x3, ...), custom_call_target="tpu_custom_call" | custom-call | flops 1000000000 | bytes 4000000 | tf_op jit(solution)/shard_map/pallas_call | solution.py:37
  113.7 0.1 collective-permute-start.21
  113.8 0.1 collective-permute-start.23
  113.9 0.5 collective-permute-start.25
  114.4 4.0 %collective-permute-done.21 = bf16[64,768]{1,0:T(8,128)(2,1)S(1)} collective-permute-done((bf16[64,768]{1,0:T(8,128)(2,1)S(1)}, bf16[64,768]{1,0:T(8,128)(2,1)S(1)}, u32[]{:S(2)}, u32[]{:S(2)}) %collective-permute-start.21) | collective-permute-done | bytes 98336 | tf_op jit(solution)/shard_map/ppermute | solution.py:29
  118.4 0.1 collective-permute-start.22
  118.5 3.1 %shard_map.53 = (f32[64,384]{1,0:T(8,128)S(1)}, bf16[64,384]{1,0:T(8,128)(2,1)S(1)}, bf16[64,384]{1,0:T(8,128)(2,1)S(1)}, bf16[64,384]{1,0:T(8,128)(2,1)S(1)}, bf16[64,384]{1,0:T(8,128)(2,1)S(1)}) custom-call(f32[64,384]{1,0:T(8,128)S(1)} %copy-done.1, f32[64,384]{1,0:T(8,128)S(1)} %collective-permute-done.23.e1, f32[64,384]{1,0:T(8,128)S(1)} %collective-permute-done.24.e2, ...), custom_call_target="tpu_custom_call" | custom-call | flops 1000000000 | bytes 4000000 | tf_op jit(solution)/shard_map/pallas_call | solution.py:37
  121.7 0.1 collective-permute-start.26
  121.7 0.1 collective-permute-start.27
  121.8 0.1 collective-permute-start.28
  121.9 9.3 %collective-permute-start.29 = (bf16[64,384]{1,0:T(8,128)(2,1)S(1)}, bf16[64,384]{1,0:T(8,128)(2,1)S(1)}, u32[]{:S(2)}, u32[]{:S(2)}) collective-permute-start(bf16[64,384]{1,0:T(8,128)(2,1)S(1)} %get-tuple-element.50), channel_id=1, source_target_pairs={{0,112},{1,113},{2,114},{3,115},{4,116},{5,117},{6,118},{7,119},{8... | collective-permute-start | bytes 147464 | tf_op jit(solution)/shard_map/ppermute | solution.py:29
  131.2 1.0 collective-permute-done.28.z3
  132.3 0.7 collective-permute-done.29.z4
  133.0 0.3 shard_map.54
  133.3 0.1 collective-permute-start.30
  133.4 1.2 collective-permute-done.30
  134.6 3.9 %collective-permute-done.31 = f32[64,64]{1,0:T(8,128)S(1)} collective-permute-done((f32[64,64]{1,0:T(8,128)S(1)}, f32[64,64]{1,0:T(8,128)S(1)}, u32[]{:S(2)}, u32[]{:S(2)}) %collective-permute-start.31) | collective-permute-done | bytes 16416 | tf_op jit(solution)/shard_map/ppermute | solution.py:29
  138.5 1.5 collective-permute-start.32
  140.0 3.9 %collective-permute-done.32 = f32[64,64]{1,0:T(8,128)S(1)} collective-permute-done((f32[64,64]{1,0:T(8,128)S(1)}, f32[64,64]{1,0:T(8,128)S(1)}, u32[]{:S(2)}, u32[]{:S(2)}) %collective-permute-start.32) | collective-permute-done | bytes 16416 | tf_op jit(solution)/shard_map/ppermute | solution.py:272
  143.9 3.9 %collective-permute-done.33 = f32[64,64]{1,0:T(8,128)S(1)} collective-permute-done((f32[64,64]{1,0:T(8,128)S(1)}, f32[64,64]{1,0:T(8,128)S(1)}, u32[]{:S(2)}, u32[]{:S(2)}) %collective-permute-start.33) | collective-permute-done | bytes 16416 | tf_op jit(solution)/shard_map/ppermute | solution.py:272
  147.8 5.4 %collective-permute-done.34 = f32[64,64]{1,0:T(8,128)S(1)} collective-permute-done((f32[64,64]{1,0:T(8,128)S(1)}, f32[64,64]{1,0:T(8,128)S(1)}, u32[]{:S(2)}, u32[]{:S(2)}) %collective-permute-start.34) | collective-permute-done | bytes 16416 | tf_op jit(solution)/shard_map/ppermute | solution.py:272
  153.3 4.2 %collective-permute-done.35 = f32[64,64]{1,0:T(8,128)S(1)} collective-permute-done((f32[64,64]{1,0:T(8,128)S(1)}, f32[64,64]{1,0:T(8,128)S(1)}, u32[]{:S(2)}, u32[]{:S(2)}) %collective-permute-start.35) | collective-permute-done | bytes 16416 | tf_op jit(solution)/shard_map/ppermute | solution.py:272
  157.5 2.1 %collective-permute-start.36 = (f32[64,64]{1,0:T(8,128)S(1)}, f32[64,64]{1,0:T(8,128)S(1)}, u32[]{:S(2)}, u32[]{:S(2)}) collective-permute-start(f32[64,64]{1,0:T(8,128)S(1)} %add.87), channel_id=1, source_target_pairs={{0,64},{4,68},{8,72},{12,76},{16,80},{20,84},{24,88},{28,92},{32,9... | collective-permute-start | bytes 49160 | tf_op jit(solution)/shard_map/ppermute | solution.py:272
  159.6 3.3 %collective-permute-done.36 = f32[64,64]{1,0:T(8,128)S(1)} collective-permute-done((f32[64,64]{1,0:T(8,128)S(1)}, f32[64,64]{1,0:T(8,128)S(1)}, u32[]{:S(2)}, u32[]{:S(2)}) %collective-permute-start.36) | collective-permute-done | bytes 16416 | tf_op jit(solution)/shard_map/ppermute | solution.py:272
  162.9 6.2 %shard_map.55 = f32[64,384]{1,0:T(8,128)} custom-call(f32[64,64]{1,0:T(8,128)S(1)} %add.88.gram, f32[64,384]{1,0:T(8,128)S(1)} %get-tuple-element.52.mixed), custom_call_target="tpu_custom_call" | custom-call | flops 1000000000 | bytes 4000000 | tf_op jit(solution)/shard_map/pallas_call | solution.py:37
  (51 shorter events, 0.3 us)
Async XLA Ops:
  0.0 18.9 %copy-start.2 = (bf16[384,768]{1,0:T(8,128)(2,1)S(1)}, bf16[384,768]{1,0:T(8,128)(2,1)}, u32[]{:S(2)}) copy-start(bf16[384,768]{1,0:T(8,128)(2,1)} %f0.11) | copy-start | bytes 1769476
  0.0 15.3 %collective-permute-start.1 = (bf16[384,768]{1,0:T(8,128)(2,1)}, bf16[384,768]{1,0:T(8,128)(2,1)S(1)}, u32[]{:S(2)}, u32[]{:S(2)}) collective-permute-start(bf16[384,768]{1,0:T(8,128)(2,1)} %f0.11), channel_id=1, source_target_pairs={{0,2},{1,3},{2,0},{3,1},{4,6},{5,7},{6,4},{7,5},{8,10},{9,11},{10,... | collective-permute-start | bytes 1769480 | tf_op jit(solution)/shard_map/ppermute | solution.py:29
  1.7 54.2 %collective-permute-start.7 = (bf16[384,768]{1,0:T(8,128)(2,1)}, bf16[384,768]{1,0:T(8,128)(2,1)}, u32[]{:S(2)}, u32[]{:S(2)}) collective-permute-start(bf16[384,768]{1,0:T(8,128)(2,1)} %f0.11), channel_id=1, source_target_pairs={{0,118},{1,119},{2,116},{3,117},{4,122},{5,123},{6,120},{7,121},{8... | collective-permute-start | bytes 1769480 | tf_op jit(solution)/shard_map/ppermute | solution.py:29
  9.8 55.7 %collective-permute-start.5 = (bf16[384,768]{1,0:T(8,128)(2,1)}, bf16[384,768]{1,0:T(8,128)(2,1)}, u32[]{:S(2)}, u32[]{:S(2)}) collective-permute-start(bf16[384,768]{1,0:T(8,128)(2,1)} %f0.11), channel_id=1, source_target_pairs={{0,120},{1,121},{2,122},{3,123},{4,124},{5,125},{6,126},{7,127},{8... | collective-permute-start | bytes 1769480 | tf_op jit(solution)/shard_map/ppermute | solution.py:29
  10.9 59.2 %collective-permute-start.3 = (bf16[384,768]{1,0:T(8,128)(2,1)}, bf16[384,768]{1,0:T(8,128)(2,1)S(1)}, u32[]{:S(2)}, u32[]{:S(2)}) collective-permute-start(bf16[384,768]{1,0:T(8,128)(2,1)} %f0.11), channel_id=1, source_target_pairs={{0,6},{1,7},{2,4},{3,5},{4,10},{5,11},{6,8},{7,9},{8,14},{9,15},{1... | collective-permute-start | bytes 1769480 | tf_op jit(solution)/shard_map/ppermute | solution.py:29
  11.4 7.5 %collective-permute-start = (bf16[384,768]{1,0:T(8,128)(2,1)}, bf16[384,768]{1,0:T(8,128)(2,1)S(1)}, u32[]{:S(2)}, u32[]{:S(2)}) collective-permute-start(bf16[384,768]{1,0:T(8,128)(2,1)} %f0.11), channel_id=1, source_target_pairs={{0,1},{1,0},{2,3},{3,2},{4,5},{5,4},{6,7},{7,6},{8,9},{9,8},{10,11... | collective-permute-start | bytes 1769480 | tf_op jit(solution)/shard_map/ppermute | solution.py:29
  15.3 6.8 %collective-permute-start.2 = (bf16[384,768]{1,0:T(8,128)(2,1)S(1)}, bf16[384,768]{1,0:T(8,128)(2,1)S(1)}, u32[]{:S(2)}, u32[]{:S(2)}) collective-permute-start(bf16[384,768]{1,0:T(8,128)(2,1)S(1)} %collective-permute-done.1.f2), channel_id=1, source_target_pairs={{0,1},{1,0},{2,3},{3,2},{4,5},{5,4},{6,7},{7,6},{8,9},{9,8},{10,11... | collective-permute-start | bytes 1769480 | tf_op jit(solution)/shard_map/ppermute | solution.py:29
  18.9 59.8 %collective-permute-start.9 = (bf16[384,768]{1,0:T(8,128)(2,1)S(1)}, bf16[384,768]{1,0:T(8,128)(2,1)S(1)}, u32[]{:S(2)}, u32[]{:S(2)}) collective-permute-start(bf16[384,768]{1,0:T(8,128)(2,1)S(1)} %copy-done.2), channel_id=1, source_target_pairs={{0,16},{1,17},{2,18},{3,19},{4,20},{5,21},{6,22},{7,23},{8,24},{9,... | collective-permute-start | bytes 1769480 | tf_op jit(solution)/shard_map/ppermute | solution.py:29
  22.1 27.5 %collective-permute-start.8 = (f32[24,384]{1,0:T(8,128)S(1)}, f32[24,384]{1,0:T(8,128)S(1)}, u32[]{:S(2)}, u32[]{:S(2)}) collective-permute-start(f32[24,384]{1,0:T(8,128)S(1)} %get-tuple-element.59), channel_id=1, source_target_pairs={{0,118},{1,119},{2,116},{3,117},{4,122},{5,123},{6,120},{7,121},{8... | collective-permute-start | bytes 110600 | tf_op jit(solution)/shard_map/ppermute | solution.py:29
  49.6 20.5 %collective-permute-start.4 = (f32[24,384]{1,0:T(8,128)S(1)}, f32[24,384]{1,0:T(8,128)S(1)}, u32[]{:S(2)}, u32[]{:S(2)}) collective-permute-start(f32[24,384]{1,0:T(8,128)S(1)} %get-tuple-element.58), channel_id=1, source_target_pairs={{0,6},{1,7},{2,4},{3,5},{4,10},{5,11},{6,8},{7,9},{8,14},{9,15},{1... | collective-permute-start | bytes 110600 | tf_op jit(solution)/shard_map/ppermute | solution.py:29
  55.8 9.5 %collective-permute-start.6 = (f32[24,384]{1,0:T(8,128)S(1)}, f32[24,384]{1,0:T(8,128)S(1)}, u32[]{:S(2)}, u32[]{:S(2)}) collective-permute-start(f32[24,384]{1,0:T(8,128)S(1)} %get-tuple-element.60), channel_id=1, source_target_pairs={{0,120},{1,121},{2,122},{3,123},{4,124},{5,125},{6,126},{7,127},{8... | collective-permute-start | bytes 110600 | tf_op jit(solution)/shard_map/ppermute | solution.py:29
  65.4 13.3 %collective-permute-start.10 = (f32[24,384]{1,0:T(8,128)S(1)}, f32[24,384]{1,0:T(8,128)S(1)}, u32[]{:S(2)}, u32[]{:S(2)}) collective-permute-start(f32[24,384]{1,0:T(8,128)S(1)} %get-tuple-element.62), channel_id=1, source_target_pairs={{0,16},{1,17},{2,18},{3,19},{4,20},{5,21},{6,22},{7,23},{8,24},{9,... | collective-permute-start | bytes 110600 | tf_op jit(solution)/shard_map/ppermute | solution.py:29
  65.5 24.2 %collective-permute-start.13 = (f32[1,384]{1,0:T(1,128)S(1)}, f32[1,384]{1,0:T(1,128)S(1)}, u32[]{:S(2)}, u32[]{:S(2)}) collective-permute-start(f32[1,384]{1,0:T(1,128)S(1)} %get-tuple-element.37), channel_id=1, source_target_pairs={{0,14},{1,15},{2,12},{3,13},{4,18},{5,19},{6,16},{7,17},{8,22},{9,... | collective-permute-start | bytes 4616 | tf_op jit(solution)/shard_map/ppermute | solution.py:29
  70.0 19.6 %collective-permute-start.12 = (f32[1,384]{1,0:T(1,128)S(1)}, f32[1,384]{1,0:T(1,128)S(1)}, u32[]{:S(2)}, u32[]{:S(2)}) collective-permute-start(f32[1,384]{1,0:T(1,128)S(1)} %get-tuple-element.36), channel_id=1, source_target_pairs={{0,8},{1,9},{2,10},{3,11},{4,12},{5,13},{6,14},{7,15},{8,16},{9,17... | collective-permute-start | bytes 4616 | tf_op jit(solution)/shard_map/ppermute | solution.py:29
  73.5 16.2 %collective-permute-start.11 = (f32[1,384]{1,0:T(1,128)S(1)}, f32[1,384]{1,0:T(1,128)S(1)}, u32[]{:S(2)}, u32[]{:S(2)}) collective-permute-start(f32[1,384]{1,0:T(1,128)S(1)} %get-tuple-element.35), channel_id=1, source_target_pairs={{0,126},{1,127},{2,124},{3,125},{4,2},{5,3},{6,0},{7,1},{8,6},{9,7... | collective-permute-start | bytes 4616 | tf_op jit(solution)/shard_map/ppermute | solution.py:29
  82.0 1.1 copy-start
  83.1 6.6 %collective-permute-start.14 = (f32[1,384]{1,0:T(1,128)S(1)}, f32[1,384]{1,0:T(1,128)S(1)}, u32[]{:S(2)}, u32[]{:S(2)}) collective-permute-start(f32[1,384]{1,0:T(1,128)S(1)} %get-tuple-element.38), channel_id=1, source_target_pairs={{0,112},{1,113},{2,114},{3,115},{4,116},{5,117},{6,118},{7,119},{8... | collective-permute-start | bytes 4616 | tf_op jit(solution)/shard_map/ppermute | solution.py:29
  87.8 7.0 %copy-start.1 = (f32[64,384]{1,0:T(8,128)S(1)}, f32[64,384]{1,0:T(8,128)}, u32[]{:S(2)}) copy-start(f32[64,384]{1,0:T(8,128)} %own.1) | copy-start | bytes 294916
  89.7 1.2 collective-permute-start.15
  91.0 3.7 %collective-permute-start.16 = (f32[4,384]{1,0:T(4,128)S(1)}, f32[4,384]{1,0:T(4,128)S(1)}, u32[]{:S(2)}, u32[]{:S(2)}) collective-permute-start(f32[4,384]{1,0:T(4,128)S(1)} %maximum_add_fusion), channel_id=1, source_target_pairs={{0,2},{1,3},{2,0},{3,1},{4,6},{5,7},{6,4},{7,5},{8,10},{9,11},{10,... | collective-permute-start | bytes 18440 | tf_op jit(solution)/shard_map/ppermute | solution.py:29
  94.8 9.0 %collective-permute-start.20 = (bf16[64,384]{1,0:T(8,128)(2,1)S(1)}, bf16[64,384]{1,0:T(8,128)(2,1)S(1)}, u32[]{:S(2)}, u32[]{:S(2)}) collective-permute-start(bf16[64,384]{1,0:T(8,128)(2,1)S(1)} %multiply_convert_fusion.x0), channel_id=1, source_target_pairs={{0,16},{1,17},{2,18},{3,19},{4,20},{5,21},{6,22},{7,23},{8,24},{9,... | collective-permute-start | bytes 147464 | tf_op jit(solution)/shard_map/ppermute | solution.py:29
  94.9 8.9 %collective-permute-start.19 = (bf16[64,384]{1,0:T(8,128)(2,1)S(1)}, bf16[64,384]{1,0:T(8,128)(2,1)S(1)}, u32[]{:S(2)}, u32[]{:S(2)}) collective-permute-start(bf16[64,384]{1,0:T(8,128)(2,1)S(1)} %multiply_convert_fusion.x0), channel_id=1, source_target_pairs={{0,118},{1,119},{2,116},{3,117},{4,122},{5,123},{6,120},{7,121},{8... | collective-permute-start | bytes 147464 | tf_op jit(solution)/shard_map/ppermute | solution.py:29
  99.0 4.7 %collective-permute-start.18 = (bf16[64,384]{1,0:T(8,128)(2,1)S(1)}, bf16[64,384]{1,0:T(8,128)(2,1)S(1)}, u32[]{:S(2)}, u32[]{:S(2)}) collective-permute-start(bf16[64,384]{1,0:T(8,128)(2,1)S(1)} %multiply_convert_fusion.x0), channel_id=1, source_target_pairs={{0,120},{1,121},{2,122},{3,123},{4,124},{5,125},{6,126},{7,127},{8... | collective-permute-start | bytes 147464 | tf_op jit(solution)/shard_map/ppermute | solution.py:29
  101.9 9.5 %collective-permute-start.17 = (bf16[64,384]{1,0:T(8,128)(2,1)S(1)}, bf16[64,384]{1,0:T(8,128)(2,1)S(1)}, u32[]{:S(2)}, u32[]{:S(2)}) collective-permute-start(bf16[64,384]{1,0:T(8,128)(2,1)S(1)} %multiply_convert_fusion.x0), channel_id=1, source_target_pairs={{0,6},{1,7},{2,4},{3,5},{4,10},{5,11},{6,8},{7,9},{8,14},{9,15},{1... | collective-permute-start | bytes 147464 | tf_op jit(solution)/shard_map/ppermute | solution.py:29
  103.7 10.2 %collective-permute-start.24 = (f32[64,384]{1,0:T(8,128)S(1)}, f32[64,384]{1,0:T(8,128)S(1)}, u32[]{:S(2)}, u32[]{:S(2)}) collective-permute-start(f32[64,384]{1,0:T(8,128)S(1)} %copy-done.1), channel_id=1, source_target_pairs={{0,2},{1,3},{2,0},{3,1},{4,6},{5,7},{6,4},{7,5},{8,10},{9,11},{10,... | collective-permute-start | bytes 294920 | tf_op jit(solution)/shard_map/ppermute | solution.py:29
  113.7 4.7 %collective-permute-start.21 = (bf16[64,768]{1,0:T(8,128)(2,1)S(1)}, bf16[64,768]{1,0:T(8,128)(2,1)S(1)}, u32[]{:S(2)}, u32[]{:S(2)}) collective-permute-start(bf16[64,768]{1,0:T(8,128)(2,1)S(1)} %get-tuple-element.45), channel_id=1, source_target_pairs={{0,2},{1,3},{2,0},{3,1},{4,6},{5,7},{6,4},{7,5},{8,10},{9,11},{10,... | collective-permute-start | bytes 294920 | tf_op jit(solution)/shard_map/ppermute | solution.py:29
  113.8 4.7 %collective-permute-start.23 = (f32[64,384]{1,0:T(8,128)S(1)}, f32[64,384]{1,0:T(8,128)S(1)}, u32[]{:S(2)}, u32[]{:S(2)}) collective-permute-start(f32[64,384]{1,0:T(8,128)S(1)} %copy-done.1), channel_id=1, source_target_pairs={{0,1},{1,0},{2,3},{3,2},{4,5},{5,4},{6,7},{7,6},{8,9},{9,8},{10,11... | collective-permute-start | bytes 294920 | tf_op jit(solution)/shard_map/ppermute | solution.py:29
  113.9 4.6 %collective-permute-start.25 = (f32[64,384]{1,0:T(8,128)S(1)}, f32[64,384]{1,0:T(8,128)S(1)}, u32[]{:S(2)}, u32[]{:S(2)}) collective-permute-start(f32[64,384]{1,0:T(8,128)S(1)} %collective-permute-done.24.e2), channel_id=1, source_target_pairs={{0,1},{1,0},{2,3},{3,2},{4,5},{5,4},{6,7},{7,6},{8,9},{9,8},{10,11... | collective-permute-start | bytes 294920 | tf_op jit(solution)/shard_map/ppermute | solution.py:29
  118.4 14.5 %collective-permute-start.22 = (f32[64,384]{1,0:T(8,128)S(1)}, f32[64,384]{1,0:T(8,128)S(1)}, u32[]{:S(2)}, u32[]{:S(2)}) collective-permute-start(f32[64,384]{1,0:T(8,128)S(1)} %get-tuple-element.63), channel_id=1, source_target_pairs={{0,1},{1,0},{2,3},{3,2},{4,5},{5,4},{6,7},{7,6},{8,9},{9,8},{10,11... | collective-permute-start | bytes 294920 | tf_op jit(solution)/shard_map/ppermute | solution.py:29
  121.7 9.6 %collective-permute-start.26 = (bf16[64,384]{1,0:T(8,128)(2,1)S(1)}, bf16[64,384]{1,0:T(8,128)(2,1)S(1)}, u32[]{:S(2)}, u32[]{:S(2)}) collective-permute-start(bf16[64,384]{1,0:T(8,128)(2,1)S(1)} %get-tuple-element.47), channel_id=1, source_target_pairs={{0,126},{1,127},{2,124},{3,125},{4,2},{5,3},{6,0},{7,1},{8,6},{9,7... | collective-permute-start | bytes 147464 | tf_op jit(solution)/shard_map/ppermute | solution.py:29
  121.7 9.5 %collective-permute-start.27 = (bf16[64,384]{1,0:T(8,128)(2,1)S(1)}, bf16[64,384]{1,0:T(8,128)(2,1)S(1)}, u32[]{:S(2)}, u32[]{:S(2)}) collective-permute-start(bf16[64,384]{1,0:T(8,128)(2,1)S(1)} %get-tuple-element.48), channel_id=1, source_target_pairs={{0,8},{1,9},{2,10},{3,11},{4,12},{5,13},{6,14},{7,15},{8,16},{9,17... | collective-permute-start | bytes 147464 | tf_op jit(solution)/shard_map/ppermute | solution.py:29
  121.8 10.4 %collective-permute-start.28 = (bf16[64,384]{1,0:T(8,128)(2,1)S(1)}, bf16[64,384]{1,0:T(8,128)(2,1)S(1)}, u32[]{:S(2)}, u32[]{:S(2)}) collective-permute-start(bf16[64,384]{1,0:T(8,128)(2,1)S(1)} %get-tuple-element.49), channel_id=1, source_target_pairs={{0,14},{1,15},{2,12},{3,13},{4,18},{5,19},{6,16},{7,17},{8,22},{9,... | collective-permute-start | bytes 147464 | tf_op jit(solution)/shard_map/ppermute | solution.py:29
  121.9 11.1 %collective-permute-start.29 = (bf16[64,384]{1,0:T(8,128)(2,1)S(1)}, bf16[64,384]{1,0:T(8,128)(2,1)S(1)}, u32[]{:S(2)}, u32[]{:S(2)}) collective-permute-start(bf16[64,384]{1,0:T(8,128)(2,1)S(1)} %get-tuple-element.50), channel_id=1, source_target_pairs={{0,112},{1,113},{2,114},{3,115},{4,116},{5,117},{6,118},{7,119},{8... | collective-permute-start | bytes 147464 | tf_op jit(solution)/shard_map/ppermute | solution.py:29
  133.3 1.3 collective-permute-start.30
  134.6 3.9 %collective-permute-start.31 = (f32[64,64]{1,0:T(8,128)S(1)}, f32[64,64]{1,0:T(8,128)S(1)}, u32[]{:S(2)}, u32[]{:S(2)}) collective-permute-start(f32[64,64]{1,0:T(8,128)S(1)} %add.82), channel_id=1, source_target_pairs={{0,2},{1,3},{2,0},{3,1},{4,6},{5,7},{6,4},{7,5},{8,10},{9,11},{10,... | collective-permute-start | bytes 49160 | tf_op jit(solution)/shard_map/ppermute | solution.py:29
  138.5 5.4 %collective-permute-start.32 = (f32[64,64]{1,0:T(8,128)S(1)}, f32[64,64]{1,0:T(8,128)S(1)}, u32[]{:S(2)}, u32[]{:S(2)}) collective-permute-start(f32[64,64]{1,0:T(8,128)S(1)} %add.83), channel_id=1, source_target_pairs={{0,4},{4,0},{8,12},{12,8},{16,20},{20,16},{24,28},{28,24},{32,36},... | collective-permute-start | bytes 49160 | tf_op jit(solution)/shard_map/ppermute | solution.py:272
  143.9 3.9 %collective-permute-start.33 = (f32[64,64]{1,0:T(8,128)S(1)}, f32[64,64]{1,0:T(8,128)S(1)}, u32[]{:S(2)}, u32[]{:S(2)}) collective-permute-start(f32[64,64]{1,0:T(8,128)S(1)} %add.84), channel_id=1, source_target_pairs={{0,8},{4,12},{8,0},{12,4},{16,24},{20,28},{24,16},{28,20},{32,40},... | collective-permute-start | bytes 49160 | tf_op jit(solution)/shard_map/ppermute | solution.py:272
  147.8 5.4 %collective-permute-start.34 = (f32[64,64]{1,0:T(8,128)S(1)}, f32[64,64]{1,0:T(8,128)S(1)}, u32[]{:S(2)}, u32[]{:S(2)}) collective-permute-start(f32[64,64]{1,0:T(8,128)S(1)} %add.85), channel_id=1, source_target_pairs={{0,16},{4,20},{8,24},{12,28},{16,0},{20,4},{24,8},{28,12},{32,48},... | collective-permute-start | bytes 49160 | tf_op jit(solution)/shard_map/ppermute | solution.py:272
  153.3 4.2 %collective-permute-start.35 = (f32[64,64]{1,0:T(8,128)S(1)}, f32[64,64]{1,0:T(8,128)S(1)}, u32[]{:S(2)}, u32[]{:S(2)}) collective-permute-start(f32[64,64]{1,0:T(8,128)S(1)} %add.86), channel_id=1, source_target_pairs={{0,32},{4,36},{8,40},{12,44},{16,48},{20,52},{24,56},{28,60},{32,0... | collective-permute-start | bytes 49160 | tf_op jit(solution)/shard_map/ppermute | solution.py:272
  157.5 5.4 %collective-permute-start.36 = (f32[64,64]{1,0:T(8,128)S(1)}, f32[64,64]{1,0:T(8,128)S(1)}, u32[]{:S(2)}, u32[]{:S(2)}) collective-permute-start(f32[64,64]{1,0:T(8,128)S(1)} %add.87), channel_id=1, source_target_pairs={{0,64},{4,68},{8,72},{12,76},{16,80},{20,84},{24,88},{28,92},{32,9... | collective-permute-start | bytes 49160 | tf_op jit(solution)/shard_map/ppermute | solution.py:272
where the time goes:
time: 169 us
  waiting for transfers between devices  68 us (40%)
  starting transfers between devices  65.4 us (39%)
  Pallas kernels  30.4 us (18%)
  local copies, waits for them, and re-layouts  2.93 us (2%)
  other arithmetic  1.87 us (1%)
    ppermute x32, starting transfers between devices, moved(): return lax.ppermute(value, ('blk', 'sub'), pairs)  61.8 us
    ppermute x32, waiting for transfers between devices, moved(): return lax.ppermute(value, ('blk', 'sub'), pairs)  47.3 us
    pallas_call x10, Pallas kernels, run(): pl.pallas_call(body, out_shape=outs, in_specs=specs, out_specs=jax.tree.m...  30.4 us
    ppermute x5, waiting for transfers between devices, local(): lax.ppermute(gram, 'blk', [(b, b ^ flip) for b in range(n_blk)])  20.7 us
    ppermute x5, starting transfers between devices, local(): lax.ppermute(gram, 'blk', [(b, b ^ flip) for b in range(n_blk)])  3.65 us
  transfers between devices with their start and end apart: 37, of which 15 were waited for; matrix products, arithmetic and copies ran while one was open for 2% of the time, Pallas kernels for 14%

commit v1 on v0

--- a/solution.py
+++ b/solution.py
@@ -13,7 +13,9 @@
 SLOTS = 4
 EIG = 64
 NNB = 16
-BAND = ((1, 2), (-2, 0), (-3, 2), (4, 0))
+BAND = ((1, 2), (-2, 0), (3, 2), (-4, 0))
+ONWARD = ((2, 0), (-2, 0))
+EXTRA = 3 * NNB
 FOLDED = 2.0 * math.log2(math.e) / F
 NT = (((1,), (1,)), ((), ()))
 LIMIT = 48 * 1024 * 1024
@@ -29,16 +31,19 @@
     return lax.ppermute(value, ("blk", "sub"), pairs)
 
 
-def call(body, outs, scratch=(), flops=10**9, smem=0):
-    vmem = pl.BlockSpec(memory_space=pltpu.VMEM)
-
+VMEM = pl.BlockSpec(memory_space=pltpu.VMEM)
+SMEM = pl.BlockSpec(memory_space=pltpu.SMEM)
+HBM = pl.BlockSpec(memory_space=pltpu.HBM)
+
+
+def call(body, outs, scratch=(), flops=10**9, specs=None):
     def run(*args):
-        specs = [pl.BlockSpec(memory_space=pltpu.SMEM)] * smem + [vmem] * (len(args) - smem)
         return pl.pallas_call(
             body,
+            grid=(1,),
             out_shape=outs,
-            in_specs=specs,
-            out_specs=jax.tree.map(lambda _: vmem, outs),
+            in_specs=list(specs) if specs else [VMEM] * len(args),
+            out_specs=jax.tree.map(lambda _: VMEM, outs),
             scratch_shapes=list(scratch),
             compiler_params=pltpu.CompilerParams(vmem_limit_bytes=LIMIT),
             cost_estimate=pl.CostEstimate(flops=flops, bytes_accessed=4 * 10**6, transcendentals=0),
@@ -67,23 +72,51 @@
         out[slot : slot + 1, :] = total[0:1, :]
 
 
-def tile_kernel(flip, reverse, sub, f0, f1, f2, f3, moving, norms, scales, lists, aux, tile, row, col, inner, words, cols):
+def pack_kernel(half, sub, features, scales, lists, first, second, held, sems, wide):
+    at = pl.multiple_of(sub[0] * ROWS, 128)
+    copies = [
+        pltpu.make_async_copy(lists.at[half - d, :, pl.ds(at, ROWS)], held.at[index], sems.at[index])
+        for index, (d, _) in enumerate(BAND)
+    ]
+    bulk = [
+        pltpu.make_async_copy(features, out.at[:ROWS, :], wide.at[index])
+        for index, out in enumerate((first, second))
+    ]
+    for copy in bulk + copies:
+        copy.start()
+    scale = jnp.concatenate([scales[:, pl.ds(at, ROWS)], jnp.ones((1, ROWS), jnp.float32)], axis=1)
+    scale = jnp.broadcast_to(scale, (NNB, 2 * ROWS)).astype(jnp.bfloat16)
+    for out in (first, second):
+        out[ROWS + 2 * NNB :, :] = scale
+    for index in range(len(BAND)):
+        copies[index].wait()
+        position = held[index]
+        digits = jnp.concatenate([position >> 6, position & 63], axis=1)
+        out = (first, second)[index % 2]
+        start = ROWS + NNB * (index // 2)
+        out[start : start + NNB, :] = digits.astype(jnp.float32).astype(jnp.bfloat16)
+    for copy in bulk:
+        copy.wait()
+
+
+def tile_kernel(flip, reverse, sub, f0, f1, f2, f3, moving, norms, scales, before, lists, tile, row, col, inner, words, cols):
     me = sub[0]
-    feats = moving[...].astype(jnp.float32)
+    feats = moving[:ROWS, :].astype(jnp.float32)
     half_norm = 0.5 * jnp.sum(feats * feats, axis=1, keepdims=True)
 
-    block_scale = aux[16:17, :]
-    pieces = []
     if reverse:
-        position = aux[0:16, :].astype(jnp.int32)
+        digits = moving[ROWS + reverse - NNB : ROWS + reverse, :].astype(jnp.float32).astype(jnp.int32)
+        position = digits[:, :ROWS] * 64 + digits[:, ROWS:]
         group = position >> 7
         slice_at = (group * 11) >> 5
         group = (slice_at ^ me) * 3 + group - 3 * slice_at
         pieces = [(position & 127).astype(jnp.float32), jnp.left_shift(1, group).astype(jnp.float32)]
+        own_scale = moving[ROWS + 2 * NNB :, :ROWS].astype(jnp.float32)[0:1]
     else:
         pieces = [jnp.zeros((32, ROWS), jnp.float32)]
+        own_scale = scales[:, pl.ds(pl.multiple_of(me * ROWS, 128), ROWS)]
     stacked = jnp.concatenate(
-        pieces + [FOLDED / block_scale, jnp.zeros((95, ROWS), jnp.float32)], axis=0
+        pieces + [FOLDED / own_scale, jnp.zeros((95, ROWS), jnp.float32)], axis=0
     )
     turned = stacked.T
     move_scale = turned[:, 32:33]
@@ -98,9 +131,9 @@
 
     row_at = lax.broadcasted_iota(jnp.int32, (8, ROWS), 0)
     for slot, ref in enumerate((f0, f1, f2, f3)):
-        inner[...] = lax.dot_general(moving[...], ref[...], NT, preferred_element_type=jnp.float32)
+        inner[...] = lax.dot_general(moving[:ROWS, :], ref[...], NT, preferred_element_type=jnp.float32)
         start = pl.multiple_of((me ^ slot) * ROWS, 128)
-        listed = lists[:, pl.ds(start, ROWS)] - (me ^ flip) * ROWS
+        listed = lists[0, :, pl.ds(start, ROWS)] - (me ^ flip) * ROWS
         inside = (listed >= 0) & (listed < ROWS)
         sublane = listed & 7
         bit = jnp.where(inside, listed >> 3, 0)
@@ -138,7 +171,7 @@
                 cols[at : at + step, :] = lanes
             else:
                 cols[at : at + step, :] = cols[at : at + step, :] + lanes
-        row[slot : slot + 1, :] = jnp.sum(row_sum, axis=0, keepdims=True)
+        row[slot : slot + 1, :] = before[slot : slot + 1, :] + jnp.sum(row_sum, axis=0, keepdims=True)
     col[...] = jnp.sum(cols[...].T, axis=0, keepdims=True)
 
 
@@ -169,16 +202,18 @@
     inv = root[0:1, :]
     value = inv * (own[...] * inv + 0.5 * sides)
     mixed[...] = value
-    gram[...] = lax.dot_general(
+    total = lax.dot_general(
         value, value, NT, precision=lax.Precision.HIGHEST, preferred_element_type=jnp.float32
     )
+    gram[...] = jnp.concatenate([total[: EIG // 2], total[EIG // 2 :]], axis=1)
 
 
 def solve_kernel(factor, gram, mixed, out):
     rows = lax.broadcasted_iota(jnp.int32, (EIG, 2 * EIG), 0)
     lanes = lax.broadcasted_iota(jnp.int32, (EIG, 2 * EIG), 1)
     unit = (rows + EIG == lanes).astype(jnp.float32)
-    work = jnp.concatenate([gram[...], jnp.zeros((EIG, EIG), jnp.float32)], axis=1) + unit
+    square = jnp.concatenate([gram[:, :EIG], gram[:, EIG:]], axis=0)
+    work = jnp.concatenate([square, jnp.zeros((EIG, EIG), jnp.float32)], axis=1) + unit
     done = []
     for j in range(EIG):
         pivot = work[j : j + 1, :]
@@ -200,21 +235,26 @@
     total_rows = ROWS * lax.axis_size("blk") * lax.axis_size("sub")
     sub_arg = sub.reshape(1)
 
-    own_lists = lax.dynamic_slice_in_dim(neighbor_lists, sub * ROWS, ROWS, axis=2)
-    own_scale = lax.dynamic_slice_in_dim(scales, sub * ROWS, ROWS).astype(jnp.float32)
-    aux = jnp.concatenate(
-        [
-            own_lists.astype(jnp.float32),
-            jnp.broadcast_to(own_scale[None, None, :], (2 * half + 1, 8, ROWS)),
-        ],
-        axis=1,
-    )
     block_scales = scales.astype(jnp.float32)[None, :]
-
-    slot2 = moved(features, 0, 2)
-    slices = [moved(features, d, u) for d, u in BAND]
-    side = [moved(aux[half - d], d, u) for d, u in BAND]
-    slot1 = moved(features, 0, 1)
+    first, second = call(
+        functools.partial(pack_kernel, half),
+        (bf16(ROWS + EXTRA, F),) * 2,
+        (
+            pltpu.VMEM((len(BAND), NNB, ROWS), jnp.int32),
+            pltpu.SemaphoreType.DMA((len(BAND),)),
+            pltpu.SemaphoreType.DMA((2,)),
+        ),
+        10**7,
+        (SMEM, HBM, VMEM, HBM),
+    )(sub_arg, features, block_scales, neighbor_lists)
+
+    first, second, ready = lax.optimization_barrier((first, second, features))
+    first = moved(first, *BAND[0])
+    second = moved(second, *BAND[1])
+    slot2 = moved(ready, 0, 2)
+    slot1 = moved(ready, 0, 1)
+    third = moved(first, *ONWARD[0])
+    fourth = moved(second, *ONWARD[1])
     slot3 = moved(slot2, 0, 1)
     block = (features, slot1, slot2, slot3)
     norms = call(norms_kernel, f32(SLOTS, ROWS))(*block)
@@ -225,41 +265,40 @@
         pltpu.VMEM((ROWS, 128), jnp.int32),
         pltpu.VMEM((ROWS, 128), jnp.float32),
     )
-    tiles, rows, cols = [], [], []
-    work = [((0, 0), features, aux[half])] + list(zip(BAND, slices, side))
-    for index, ((d, u), moving, extra) in enumerate(work):
-        body = functools.partial(tile_kernel, u, index > 0)
-        tile, row, col = call(body, tile_outs, scratch, 3 * 10**9, 1)(
-            sub_arg, *block, moving, norms, block_scales, neighbor_lists[half + d], extra
-        )
+    row = jnp.zeros((SLOTS, ROWS), jnp.float32)
+    tiles, cols = [], []
+    work = [((0, 0), features)] + list(zip(BAND, (first, second, third, fourth)))
+    for index, ((d, u), moving) in enumerate(work):
+        body = functools.partial(tile_kernel, u, NNB * ((index + 1) // 2))
+        listed = pl.BlockSpec((1, NNB, SLOTS * ROWS), lambda i, at=half + d: (at, 0, 0))
+        tile, row, col = call(
+            body, tile_outs, scratch, 3 * 10**9, (SMEM,) + (VMEM,) * 8 + (listed,)
+        )(sub_arg, *block, moving, norms, block_scales, row, neighbor_lists)
         tiles.append(tile)
-        rows.append(row)
         cols.append(col if index == 0 else moved(col, -d, u))
 
     e1 = moved(eigen_block, 0, 1)
     e2 = moved(eigen_block, 0, 2)
     e3 = moved(e2, 0, 1)
 
-    own_cols = functools.reduce(jnp.add, cols)
-    sums = functools.reduce(jnp.add, rows)
-    sums = jnp.concatenate([sums[0:1] + own_cols, sums[1:]], axis=0)
-    other = moved(sums, 0, 1)
-    sums = sums + jnp.concatenate([other[1:2], other[0:1], other[3:4], other[2:3]], axis=0)
-    other = moved(sums, 0, 2)
-    sums = sums + jnp.concatenate([other[2:4], other[0:2]], axis=0)
-    root = lax.rsqrt(1.0 + 0.5 * sums)
-    scaled_low = (eigen_block * root[0:1]).astype(jnp.bfloat16)
+    pair = row[0:2] + moved(row[2:4], 0, 2)
+    own = pair[0:1] + moved(pair[1:2], 0, 1)
+    root = lax.rsqrt(1.0 + 0.5 * (own + functools.reduce(jnp.add, cols)))
+    scaled_low = (eigen_block * root).astype(jnp.bfloat16)
     vectors = [moved(scaled_low, d, u) for d, u in BAND]
+    root = jnp.concatenate([root, moved(root, 0, 1)], axis=0)
+    root = jnp.concatenate([root, moved(root, 0, 2)], axis=0)
 
     z_outs = (f32(EIG, ROWS),) + (bf16(EIG, ROWS),) * 4
-    z = call(col_kernel, z_outs, (), 10**9)(eigen_block, e1, e2, e3, root, *tiles)
+    z = call(col_kernel, z_outs, (), 10**8)(eigen_block, e1, e2, e3, root, *tiles)
     back = [moved(part, -d, u) for (d, u), part in zip(BAND, z[1:])]
+    vectors, _ = lax.optimization_barrier((vectors, z[0]))
     kept, sent = call(row_kernel, (f32(EIG, 2 * ROWS), bf16(EIG, 2 * ROWS)), (), 10**9)(
         scaled_low, *vectors, *tiles
     )
     got = moved(sent, 0, 2)
     pair = moved(kept[:, ROWS:] + got[:, ROWS:].astype(jnp.float32), 0, 1)
-    mixed, gram = call(mix_kernel, (f32(EIG, ROWS), f32(EIG, EIG)))(
+    mixed, gram = call(mix_kernel, (f32(EIG, ROWS), f32(EIG // 2, 2 * EIG)))(
         eigen_block, root, kept[:, :ROWS], got[:, :ROWS], pair, z[0], *back
     )
     flip = 1

time: 169 us -> 144 us (0.85)
  starting transfers between devices: 65.4 us -> 45 us
  waiting for transfers between devices: 68 us -> 65.2 us
  other arithmetic: 1.87 us -> 0.11 us
    ppermute x32 -> x30, starting transfers between devices: 61.8 us -> 45 us  [moved(): return lax.ppermute(value, ('blk', 'sub'), pairs)]
    ppermute x32 -> x30, waiting for transfers between devices: 47.3 us -> 42 us  [moved(): return lax.ppermute(value, ('blk', 'sub'), pairs)]
    ppermute x5, starting transfers between devices: 3.65 us -> 0.01 us  [local(): lax.ppermute(gram, 'blk', [(b, b ^ flip) for b in range(n_blk)])]
    ppermute x5, waiting for transfers between devices: 20.7 us -> 23.2 us  [local(): lax.ppermute(gram, 'blk', [(b, b ^ flip) for b in range(n_blk)])]
    unnamed x6 -> x12, local copies, waits for them, and re-layouts: 1.07 us -> 3.31 us
    convert_element_type x3 -> x1, other arithmetic: 1.73 us -> 0.01 us  [local(): scaled_low = (eigen_block * root).astype(jnp.bfloat16)]
    pallas_call x10 -> x11, Pallas kernels: 30.4 us -> 29.4 us  [run(): pl.pallas_call(body, grid=(1,), out_shape=outs, in_specs=list(specs) if s...]
  transfers between devices with their start and end apart: 37 -> 35, of which waited for: 15 -> 18; matrix products, arithmetic and copies ran while one was open for 2% -> 0% of each run, Pallas kernels for 14% -> 12%
where the time goes in v1:
time: 144 us
  waiting for transfers between devices  65.2 us (45%)
  starting transfers between devices  45 us (31%)
  Pallas kernels  29.4 us (20%)
  local copies, waits for them, and re-layouts  4.02 us (3%)
    ppermute x30, starting transfers between devices, moved(): return lax.ppermute(value, ('blk', 'sub'), pairs)  45 us
    ppermute x30, waiting for transfers between devices, moved(): return lax.ppermute(value, ('blk', 'sub'), pairs)  42 us
    pallas_call x11, Pallas kernels, run(): pl.pallas_call(body, grid=(1,), out_shape=outs, in_specs=list(specs) if s...  29.4 us
    ppermute x5, waiting for transfers between devices, local(): lax.ppermute(gram, 'blk', [(b, b ^ flip) for b in range(n_blk)])  23.2 us
    unnamed x12, local copies, waits for them, and re-layouts  3.31 us
  transfers between devices with their start and end apart: 35, of which 18 were waited for; matrix products, arithmetic and copies ran while one was open for 0% of the time, Pallas kernels for 12%

profile of v1, /device:TPU:0, one launch (start us, length us, event | category | flops | bytes accessed | tf_op | source)
XLA Modules:
  0.0 144.0 jit_solution(16625047596530947666)
XLA Ops:
  0.0 0.7 reshape.4.scales
  0.7 1.2 copy-done.1
  1.9 1.1 copy-done.3
  2.9 0.4 shard_map.46
  3.3 0.0 copy-start.2
  3.3 1.7 %collective-permute-start.1 = (bf16[384,768]{1,0:T(8,128)(2,1)S(1)}, bf16[384,768]{1,0:T(8,128)(2,1)S(1)}, u32[]{:S(2)}, u32[]{:S(2)}) collective-permute-start(bf16[384,768]{1,0:T(8,128)(2,1)S(1)} %copy-done.3), channel_id=1, source_target_pairs={{0,2},{1,3},{2,0},{3,1},{4,6},{5,7},{6,4},{7,5},{8,10},{9,11},{10,... | collective-permute-start | bytes 1769480 | tf_op jit(solution)/shard_map/ppermute | solution.py:31
  5.1 2.2 %collective-permute-start.5 = (bf16[432,768]{1,0:T(8,128)(2,1)S(1)}, bf16[432,768]{1,0:T(8,128)(2,1)S(1)}, u32[]{:S(2)}, u32[]{:S(2)}) collective-permute-start(bf16[432,768]{1,0:T(8,128)(2,1)S(1)} %get-tuple-element.42), channel_id=1, source_target_pairs={{0,6},{1,7},{2,4},{3,5},{4,10},{5,11},{6,8},{7,9},{8,14},{9,15},{1... | collective-permute-start | bytes 1990664 | tf_op jit(solution)/shard_map/ppermute | solution.py:31
  7.3 6.2 %collective-permute-start.3 = (bf16[432,768]{1,0:T(8,128)(2,1)S(1)}, bf16[432,768]{1,0:T(8,128)(2,1)S(1)}, u32[]{:S(2)}, u32[]{:S(2)}) collective-permute-start(bf16[432,768]{1,0:T(8,128)(2,1)S(1)} %get-tuple-element.41), channel_id=1, source_target_pairs={{0,120},{1,121},{2,122},{3,123},{4,124},{5,125},{6,126},{7,127},{8... | collective-permute-start | bytes 1990664 | tf_op jit(solution)/shard_map/ppermute | solution.py:31
  13.5 4.9 %collective-permute-done.1.f2 = bf16[384,768]{1,0:T(8,128)(2,1)S(1)} collective-permute-done((bf16[384,768]{1,0:T(8,128)(2,1)S(1)}, bf16[384,768]{1,0:T(8,128)(2,1)S(1)}, u32[]{:S(2)}, u32[]{:S(2)}) %collective-permute-start.1) | collective-permute-done | bytes 589856 | tf_op jit(solution)/shard_map/ppermute | solution.py:31
  18.4 9.1 %collective-permute-done.5.moving = bf16[432,768]{1,0:T(8,128)(2,1)S(1)} collective-permute-done((bf16[432,768]{1,0:T(8,128)(2,1)S(1)}, bf16[432,768]{1,0:T(8,128)(2,1)S(1)}, u32[]{:S(2)}, u32[]{:S(2)}) %collective-permute-start.5) | collective-permute-done | bytes 663584 | tf_op jit(solution)/shard_map/ppermute | solution.py:31
  27.6 0.0 collective-permute-start.6
  27.6 5.3 %collective-permute-start.4 = (bf16[432,768]{1,0:T(8,128)(2,1)S(1)}, bf16[432,768]{1,0:T(8,128)(2,1)S(1)}, u32[]{:S(2)}, u32[]{:S(2)}) collective-permute-start(bf16[432,768]{1,0:T(8,128)(2,1)S(1)} %collective-permute-done.3.moving), channel_id=1, source_target_pairs={{0,120},{1,121},{2,122},{3,123},{4,124},{5,125},{6,126},{7,127},{8... | collective-permute-start | bytes 1990664 | tf_op jit(solution)/shard_map/ppermute | solution.py:31
  32.9 0.0 collective-permute-done.2.f3
  32.9 1.4 shard_map.47.norms
  34.3 0.0 copy-done.2
  34.3 2.0 %shard_map.48 = (bf16[384,1536]{1,0:T(8,128)(2,1)S(1)}, f32[4,384]{1,0:T(4,128)S(1)}, f32[1,384]{1,0:T(1,128)S(1)}) custom-call(s32[1]{0:T(128)} %bitcast.sub, bf16[384,768]{1,0:T(8,128)(2,1)S(1)} %copy-done.4, bf16[384,768]{1,0:T(8,128)(2,1)S(1)} %collective-permute-done.f1, bf16[384,768]{1,0:T(8,128)(2,1)S(1)} %collective-permute-done.1.f2, ...), custom_call_target="tpu_custom_call" | custom-call | flops 3000000000 | bytes 4000000 | tf_op jit(solution)/shard_map/pallas_call | solution.py:41
  36.3 3.4 %shard_map.49 = (bf16[384,1536]{1,0:T(8,128)(2,1)S(1)}, f32[4,384]{1,0:T(4,128)S(1)}, f32[1,384]{1,0:T(1,128)S(1)}) custom-call(s32[1]{0:T(128)} %bitcast.sub, bf16[384,768]{1,0:T(8,128)(2,1)S(1)} %copy-done.4, bf16[384,768]{1,0:T(8,128)(2,1)S(1)} %collective-permute-done.f1, bf16[384,768]{1,0:T(8,128)(2,1)S(1)} %collective-permute-done.1.f2, ...), custom_call_target="tpu_custom_call" | custom-call | flops 3000000000 | bytes 4000000 | tf_op jit(solution)/shard_map/pallas_call | solution.py:41
  39.7 3.4 %shard_map.50 = (bf16[384,1536]{1,0:T(8,128)(2,1)S(1)}, f32[4,384]{1,0:T(4,128)S(1)}, f32[1,384]{1,0:T(1,128)S(1)}) custom-call(s32[1]{0:T(128)} %bitcast.sub, bf16[384,768]{1,0:T(8,128)(2,1)S(1)} %copy-done.4, bf16[384,768]{1,0:T(8,128)(2,1)S(1)} %collective-permute-done.f1, bf16[384,768]{1,0:T(8,128)(2,1)S(1)} %collective-permute-done.1.f2, ...), custom_call_target="tpu_custom_call" | custom-call | flops 3000000000 | bytes 4000000 | tf_op jit(solution)/shard_map/pallas_call | solution.py:41
  43.1 3.6 %collective-permute-done.6.moving = bf16[432,768]{1,0:T(8,128)(2,1)S(1)} collective-permute-done((bf16[432,768]{1,0:T(8,128)(2,1)S(1)}, bf16[432,768]{1,0:T(8,128)(2,1)S(1)}, u32[]{:S(2)}, u32[]{:S(2)}) %collective-permute-start.6) | collective-permute-done | bytes 663584 | tf_op jit(solution)/shard_map/ppermute | solution.py:31
  46.7 3.6 %shard_map.51 = (bf16[384,1536]{1,0:T(8,128)(2,1)S(1)}, f32[4,384]{1,0:T(4,128)S(1)}, f32[1,384]{1,0:T(1,128)S(1)}) custom-call(s32[1]{0:T(128)} %bitcast.sub, bf16[384,768]{1,0:T(8,128)(2,1)S(1)} %copy-done.4, bf16[384,768]{1,0:T(8,128)(2,1)S(1)} %collective-permute-done.f1, bf16[384,768]{1,0:T(8,128)(2,1)S(1)} %collective-permute-done.1.f2, ...), custom_call_target="tpu_custom_call" | custom-call | flops 3000000000 | bytes 4000000 | tf_op jit(solution)/shard_map/pallas_call | solution.py:41
  50.2 0.0 collective-permute-done.4.moving
  50.3 0.0 copy-start.5
  50.3 3.4 %shard_map.52 = (bf16[384,1536]{1,0:T(8,128)(2,1)S(1)}, f32[4,384]{1,0:T(4,128)S(1)}, f32[1,384]{1,0:T(1,128)S(1)}) custom-call(s32[1]{0:T(128)} %bitcast.sub, bf16[384,768]{1,0:T(8,128)(2,1)S(1)} %copy-done.4, bf16[384,768]{1,0:T(8,128)(2,1)S(1)} %collective-permute-done.f1, bf16[384,768]{1,0:T(8,128)(2,1)S(1)} %collective-permute-done.1.f2, ...), custom_call_target="tpu_custom_call" | custom-call | flops 3000000000 | bytes 4000000 | tf_op jit(solution)/shard_map/pallas_call | solution.py:41
  53.6 1.0 copy-done
  54.7 0.7 collective-permute-start.7
  55.4 0.0 collective-permute-start.10
  55.4 2.3 %collective-permute-start.9 = (f32[1,384]{1,0:T(1,128)S(1)}, f32[1,384]{1,0:T(1,128)S(1)}, u32[]{:S(2)}, u32[]{:S(2)}) collective-permute-start(f32[1,384]{1,0:T(1,128)S(1)} %get-tuple-element.49), channel_id=1, source_target_pairs={{0,126},{1,127},{2,124},{3,125},{4,2},{5,3},{6,0},{7,1},{8,6},{9,7... | collective-permute-start | bytes 4616 | tf_op jit(solution)/shard_map/ppermute | solution.py:31
  57.7 0.0 collective-permute-start.12
  57.7 6.0 %collective-permute-start.11 = (f32[1,384]{1,0:T(1,128)S(1)}, f32[1,384]{1,0:T(1,128)S(1)}, u32[]{:S(2)}, u32[]{:S(2)}) collective-permute-start(f32[1,384]{1,0:T(1,128)S(1)} %get-tuple-element.51), channel_id=1, source_target_pairs={{0,118},{1,119},{2,116},{3,117},{4,122},{5,123},{6,120},{7,121},{8... | collective-permute-start | bytes 4616 | tf_op jit(solution)/shard_map/ppermute | solution.py:31
  63.7 0.0 collective-permute-done.7
  63.7 0.1 collective-permute-start.8
  63.8 0.2 collective-permute-start.20
  64.0 0.0 collective-permute-done.9
  64.0 0.8 collective-permute-done.12
  64.9 0.1 collective-permute-done.11
  65.0 0.2 collective-permute-start.13
  65.2 0.4 collective-permute-start.19
  65.6 3.4 %collective-permute-done.20.e2 = f32[64,384]{1,0:T(8,128)S(1)} collective-permute-done((f32[64,384]{1,0:T(8,128)S(1)}, f32[64,384]{1,0:T(8,128)S(1)}, u32[]{:S(2)}, u32[]{:S(2)}) %collective-permute-start.20) | collective-permute-done | bytes 98336 | tf_op jit(solution)/shard_map/ppermute | solution.py:31
  69.1 0.3 collective-permute-start.14
  69.4 0.3 collective-permute-start.15
  69.7 5.1 %collective-permute-start.16 = (bf16[64,384]{1,0:T(8,128)(2,1)S(1)}, bf16[64,384]{1,0:T(8,128)(2,1)S(1)}, u32[]{:S(2)}, u32[]{:S(2)}) collective-permute-start(bf16[64,384]{1,0:T(8,128)(2,1)S(1)} %multiply_convert_fusion.x0), channel_id=1, source_target_pairs={{0,120},{1,121},{2,122},{3,123},{4,124},{5,125},{6,126},{7,127},{8... | collective-permute-start | bytes 147464 | tf_op jit(solution)/shard_map/ppermute | solution.py:31
  74.7 3.7 %collective-permute-start.18 = (bf16[64,384]{1,0:T(8,128)(2,1)S(1)}, bf16[64,384]{1,0:T(8,128)(2,1)S(1)}, u32[]{:S(2)}, u32[]{:S(2)}) collective-permute-start(bf16[64,384]{1,0:T(8,128)(2,1)S(1)} %multiply_convert_fusion.x0), channel_id=1, source_target_pairs={{0,112},{1,113},{2,114},{3,115},{4,116},{5,117},{6,118},{7,119},{8... | collective-permute-start | bytes 147464 | tf_op jit(solution)/shard_map/ppermute | solution.py:31
  78.4 3.1 %shard_map.53 = (f32[64,384]{1,0:T(8,128)S(1)}, bf16[64,384]{1,0:T(8,128)(2,1)S(1)}, bf16[64,384]{1,0:T(8,128)(2,1)S(1)}, bf16[64,384]{1,0:T(8,128)(2,1)S(1)}, bf16[64,384]{1,0:T(8,128)(2,1)S(1)}) custom-call(f32[64,384]{1,0:T(8,128)S(1)} %copy-done.5, f32[64,384]{1,0:T(8,128)S(1)} %collective-permute-done.19.e1, f32[64,384]{1,0:T(8,128)S(1)} %collective-permute-done.20.e2, ...), custom_call_target="tpu_custom_call" | custom-call | flops 100000000 | bytes 4000000 | tf_op jit(solution)/shard_map/pallas_call | solution.py:41
  81.6 3.0 %collective-permute-done.17.x3 = bf16[64,384]{1,0:T(8,128)(2,1)S(1)} collective-permute-done((bf16[64,384]{1,0:T(8,128)(2,1)S(1)}, bf16[64,384]{1,0:T(8,128)(2,1)S(1)}, u32[]{:S(2)}, u32[]{:S(2)}) %collective-permute-start.17) | collective-permute-done | bytes 49184 | tf_op jit(solution)/shard_map/ppermute | solution.py:31
  84.6 2.3 %shard_map.54 = (f32[64,768]{1,0:T(8,128)S(1)}, bf16[64,768]{1,0:T(8,128)(2,1)S(1)}) custom-call(bf16[64,384]{1,0:T(8,128)(2,1)S(1)} %multiply_convert_fusion.x0, bf16[64,384]{1,0:T(8,128)(2,1)S(1)} %collective-permute-done.15.x1, bf16[64,384]{1,0:T(8,128)(2,1)S(1)} %collective-permute-done.16.x2, bf16[64,384]{1,0:T(8,128)(2,1)S(1)} %collective-permute-done.17.x3, ...), custom_call_target="tpu_custom_call" | custom-call | flops 1000000000 | bytes 4000000 | tf_op jit(solution)/shard_map/pallas_call | solution.py:41
  86.9 0.3 collective-permute-start.22
  87.1 4.4 %collective-permute-done.22 = bf16[64,768]{1,0:T(8,128)(2,1)S(1)} collective-permute-done((bf16[64,768]{1,0:T(8,128)(2,1)S(1)}, bf16[64,768]{1,0:T(8,128)(2,1)S(1)}, u32[]{:S(2)}, u32[]{:S(2)}) %collective-permute-start.22) | collective-permute-done | bytes 98336 | tf_op jit(solution)/shard_map/ppermute | solution.py:31
  91.6 0.1 collective-permute-start.23
  91.7 2.1 %collective-permute-start.24 = (bf16[64,384]{1,0:T(8,128)(2,1)S(1)}, bf16[64,384]{1,0:T(8,128)(2,1)S(1)}, u32[]{:S(2)}, u32[]{:S(2)}) collective-permute-start(bf16[64,384]{1,0:T(8,128)(2,1)S(1)} %get-tuple-element.65), channel_id=1, source_target_pairs={{0,126},{1,127},{2,124},{3,125},{4,2},{5,3},{6,0},{7,1},{8,6},{9,7... | collective-permute-start | bytes 147464 | tf_op jit(solution)/shard_map/ppermute | solution.py:31
  93.7 2.2 %collective-permute-start.25 = (bf16[64,384]{1,0:T(8,128)(2,1)S(1)}, bf16[64,384]{1,0:T(8,128)(2,1)S(1)}, u32[]{:S(2)}, u32[]{:S(2)}) collective-permute-start(bf16[64,384]{1,0:T(8,128)(2,1)S(1)} %get-tuple-element.66), channel_id=1, source_target_pairs={{0,8},{1,9},{2,10},{3,11},{4,12},{5,13},{6,14},{7,15},{8,16},{9,17... | collective-permute-start | bytes 147464 | tf_op jit(solution)/shard_map/ppermute | solution.py:31
  95.9 5.6 %collective-permute-start.26 = (bf16[64,384]{1,0:T(8,128)(2,1)S(1)}, bf16[64,384]{1,0:T(8,128)(2,1)S(1)}, u32[]{:S(2)}, u32[]{:S(2)}) collective-permute-start(bf16[64,384]{1,0:T(8,128)(2,1)S(1)} %get-tuple-element.67), channel_id=1, source_target_pairs={{0,118},{1,119},{2,116},{3,117},{4,122},{5,123},{6,120},{7,121},{8... | collective-permute-start | bytes 147464 | tf_op jit(solution)/shard_map/ppermute | solution.py:31
  101.6 0.1 collective-permute-done.25.z2
  101.7 1.6 %collective-permute-done.26.z3 = bf16[64,384]{1,0:T(8,128)(2,1)S(1)} collective-permute-done((bf16[64,384]{1,0:T(8,128)(2,1)S(1)}, bf16[64,384]{1,0:T(8,128)(2,1)S(1)}, u32[]{:S(2)}, u32[]{:S(2)}) %collective-permute-start.26) | collective-permute-done | bytes 49184 | tf_op jit(solution)/shard_map/ppermute | solution.py:31
  103.3 6.0 %collective-permute-done.27.z4 = bf16[64,384]{1,0:T(8,128)(2,1)S(1)} collective-permute-done((bf16[64,384]{1,0:T(8,128)(2,1)S(1)}, bf16[64,384]{1,0:T(8,128)(2,1)S(1)}, u32[]{:S(2)}, u32[]{:S(2)}) %collective-permute-start.27) | collective-permute-done | bytes 49184 | tf_op jit(solution)/shard_map/ppermute | solution.py:31
  109.3 0.4 shard_map.55
  109.6 0.0 collective-permute-start.28
  109.7 1.2 collective-permute-done.28
  110.9 3.7 %collective-permute-done.29 = f32[32,128]{1,0:T(8,128)S(1)} collective-permute-done((f32[32,128]{1,0:T(8,128)S(1)}, f32[32,128]{1,0:T(8,128)S(1)}, u32[]{:S(2)}, u32[]{:S(2)}) %collective-permute-start.29) | collective-permute-done | bytes 16416 | tf_op jit(solution)/shard_map/ppermute | solution.py:31
  114.6 5.2 %collective-permute-done.30 = f32[32,128]{1,0:T(8,128)S(1)} collective-permute-done((f32[32,128]{1,0:T(8,128)S(1)}, f32[32,128]{1,0:T(8,128)S(1)}, u32[]{:S(2)}, u32[]{:S(2)}) %collective-permute-start.30) | collective-permute-done | bytes 16416 | tf_op jit(solution)/shard_map/ppermute | solution.py:311
  119.8 3.7 %collective-permute-done.31 = f32[32,128]{1,0:T(8,128)S(1)} collective-permute-done((f32[32,128]{1,0:T(8,128)S(1)}, f32[32,128]{1,0:T(8,128)S(1)}, u32[]{:S(2)}, u32[]{:S(2)}) %collective-permute-start.31) | collective-permute-done | bytes 16416 | tf_op jit(solution)/shard_map/ppermute | solution.py:311
  123.6 5.2 %collective-permute-done.32 = f32[32,128]{1,0:T(8,128)S(1)} collective-permute-done((f32[32,128]{1,0:T(8,128)S(1)}, f32[32,128]{1,0:T(8,128)S(1)}, u32[]{:S(2)}, u32[]{:S(2)}) %collective-permute-start.32) | collective-permute-done | bytes 16416 | tf_op jit(solution)/shard_map/ppermute | solution.py:311
  128.8 3.7 %collective-permute-done.33 = f32[32,128]{1,0:T(8,128)S(1)} collective-permute-done((f32[32,128]{1,0:T(8,128)S(1)}, f32[32,128]{1,0:T(8,128)S(1)}, u32[]{:S(2)}, u32[]{:S(2)}) %collective-permute-start.33) | collective-permute-done | bytes 16416 | tf_op jit(solution)/shard_map/ppermute | solution.py:311
  132.6 5.2 %collective-permute-done.34 = f32[32,128]{1,0:T(8,128)S(1)} collective-permute-done((f32[32,128]{1,0:T(8,128)S(1)}, f32[32,128]{1,0:T(8,128)S(1)}, u32[]{:S(2)}, u32[]{:S(2)}) %collective-permute-start.34) | collective-permute-done | bytes 16416 | tf_op jit(solution)/shard_map/ppermute | solution.py:311
  137.8 6.2 %shard_map.56 = f32[64,384]{1,0:T(8,128)} custom-call(f32[32,128]{1,0:T(8,128)S(1)} %add.67.gram, f32[64,384]{1,0:T(8,128)S(1)} %get-tuple-element.70.mixed), custom_call_target="tpu_custom_call" | custom-call | flops 1000000000 | bytes 4000000 | tf_op jit(solution)/shard_map/pallas_call | solution.py:41
  (47 shorter events, 0.2 us)
Async XLA Ops:
  0.7 1.2 copy-start.1
  1.9 1.1 copy-start.3
  2.9 30.0 %copy-start.4 = (bf16[384,768]{1,0:T(8,128)(2,1)S(1)}, bf16[384,768]{1,0:T(8,128)(2,1)}, u32[]{:S(2)}) copy-start(bf16[384,768]{1,0:T(8,128)(2,1)} %f0.11) | copy-start | bytes 1769476
  3.3 31.0 %copy-start.2 = (s32[9,16,1536]{2,1,0:T(8,128)S(1)}, s32[9,16,1536]{2,1,0:T(8,128)}, u32[]{:S(2)}) copy-start(s32[9,16,1536]{2,1,0:T(8,128)} %lists.11) | copy-start | bytes 2654212
  3.3 15.1 %collective-permute-start.1 = (bf16[384,768]{1,0:T(8,128)(2,1)S(1)}, bf16[384,768]{1,0:T(8,128)(2,1)S(1)}, u32[]{:S(2)}, u32[]{:S(2)}) collective-permute-start(bf16[384,768]{1,0:T(8,128)(2,1)S(1)} %copy-done.3), channel_id=1, source_target_pairs={{0,2},{1,3},{2,0},{3,1},{4,6},{5,7},{6,4},{7,5},{8,10},{9,11},{10,... | collective-permute-start | bytes 1769480 | tf_op jit(solution)/shard_map/ppermute | solution.py:31
  5.1 22.5 %collective-permute-start.5 = (bf16[432,768]{1,0:T(8,128)(2,1)S(1)}, bf16[432,768]{1,0:T(8,128)(2,1)S(1)}, u32[]{:S(2)}, u32[]{:S(2)}) collective-permute-start(bf16[432,768]{1,0:T(8,128)(2,1)S(1)} %get-tuple-element.42), channel_id=1, source_target_pairs={{0,6},{1,7},{2,4},{3,5},{4,10},{5,11},{6,8},{7,9},{8,14},{9,15},{1... | collective-permute-start | bytes 1990664 | tf_op jit(solution)/shard_map/ppermute | solution.py:31
  7.3 20.3 %collective-permute-start.3 = (bf16[432,768]{1,0:T(8,128)(2,1)S(1)}, bf16[432,768]{1,0:T(8,128)(2,1)S(1)}, u32[]{:S(2)}, u32[]{:S(2)}) collective-permute-start(bf16[432,768]{1,0:T(8,128)(2,1)S(1)} %get-tuple-element.41), channel_id=1, source_target_pairs={{0,120},{1,121},{2,122},{3,123},{4,124},{5,125},{6,126},{7,127},{8... | collective-permute-start | bytes 1990664 | tf_op jit(solution)/shard_map/ppermute | solution.py:31
  13.5 19.4 %collective-permute-start = (bf16[384,768]{1,0:T(8,128)(2,1)S(1)}, bf16[384,768]{1,0:T(8,128)(2,1)S(1)}, u32[]{:S(2)}, u32[]{:S(2)}) collective-permute-start(bf16[384,768]{1,0:T(8,128)(2,1)S(1)} %copy-done.3), channel_id=1, source_target_pairs={{0,1},{1,0},{2,3},{3,2},{4,5},{5,4},{6,7},{7,6},{8,9},{9,8},{10,11... | collective-permute-start | bytes 1769480 | tf_op jit(solution)/shard_map/ppermute | solution.py:31
  18.4 14.5 %collective-permute-start.2 = (bf16[384,768]{1,0:T(8,128)(2,1)S(1)}, bf16[384,768]{1,0:T(8,128)(2,1)S(1)}, u32[]{:S(2)}, u32[]{:S(2)}) collective-permute-start(bf16[384,768]{1,0:T(8,128)(2,1)S(1)} %collective-permute-done.1.f2), channel_id=1, source_target_pairs={{0,1},{1,0},{2,3},{3,2},{4,5},{5,4},{6,7},{7,6},{8,9},{9,8},{10,11... | collective-permute-start | bytes 1769480 | tf_op jit(solution)/shard_map/ppermute | solution.py:31
  27.6 19.1 %collective-permute-start.6 = (bf16[432,768]{1,0:T(8,128)(2,1)S(1)}, bf16[432,768]{1,0:T(8,128)(2,1)S(1)}, u32[]{:S(2)}, u32[]{:S(2)}) collective-permute-start(bf16[432,768]{1,0:T(8,128)(2,1)S(1)} %collective-permute-done.5.moving), channel_id=1, source_target_pairs={{0,8},{1,9},{2,10},{3,11},{4,12},{5,13},{6,14},{7,15},{8,16},{9,17... | collective-permute-start | bytes 1990664 | tf_op jit(solution)/shard_map/ppermute | solution.py:31
  27.6 22.7 %collective-permute-start.4 = (bf16[432,768]{1,0:T(8,128)(2,1)S(1)}, bf16[432,768]{1,0:T(8,128)(2,1)S(1)}, u32[]{:S(2)}, u32[]{:S(2)}) collective-permute-start(bf16[432,768]{1,0:T(8,128)(2,1)S(1)} %collective-permute-done.3.moving), channel_id=1, source_target_pairs={{0,120},{1,121},{2,122},{3,123},{4,124},{5,125},{6,126},{7,127},{8... | collective-permute-start | bytes 1990664 | tf_op jit(solution)/shard_map/ppermute | solution.py:31
  50.3 13.6 %copy-start.5 = (f32[64,384]{1,0:T(8,128)S(1)}, f32[64,384]{1,0:T(8,128)}, u32[]{:S(2)}) copy-start(f32[64,384]{1,0:T(8,128)} %own.1) | copy-start | bytes 294916
  53.6 1.1 copy-start
  54.7 9.0 %collective-permute-start.7 = (f32[2,384]{1,0:T(2,128)S(1)}, f32[2,384]{1,0:T(2,128)S(1)}, u32[]{:S(2)}, u32[]{:S(2)}) collective-permute-start(f32[2,384]{1,0:T(2,128)S(1)} %slice.25), channel_id=1, source_target_pairs={{0,2},{1,3},{2,0},{3,1},{4,6},{5,7},{6,4},{7,5},{8,10},{9,11},{10,... | collective-permute-start | bytes 9224 | tf_op jit(solution)/shard_map/ppermute | solution.py:31
  55.4 8.4 %collective-permute-start.10 = (f32[1,384]{1,0:T(1,128)S(1)}, f32[1,384]{1,0:T(1,128)S(1)}, u32[]{:S(2)}, u32[]{:S(2)}) collective-permute-start(f32[1,384]{1,0:T(1,128)S(1)} %get-tuple-element.50), channel_id=1, source_target_pairs={{0,8},{1,9},{2,10},{3,11},{4,12},{5,13},{6,14},{7,15},{8,16},{9,17... | collective-permute-start | bytes 4616 | tf_op jit(solution)/shard_map/ppermute | solution.py:31
  55.4 8.7 %collective-permute-start.9 = (f32[1,384]{1,0:T(1,128)S(1)}, f32[1,384]{1,0:T(1,128)S(1)}, u32[]{:S(2)}, u32[]{:S(2)}) collective-permute-start(f32[1,384]{1,0:T(1,128)S(1)} %get-tuple-element.49), channel_id=1, source_target_pairs={{0,126},{1,127},{2,124},{3,125},{4,2},{5,3},{6,0},{7,1},{8,6},{9,7... | collective-permute-start | bytes 4616 | tf_op jit(solution)/shard_map/ppermute | solution.py:31
  57.7 7.2 %collective-permute-start.12 = (f32[1,384]{1,0:T(1,128)S(1)}, f32[1,384]{1,0:T(1,128)S(1)}, u32[]{:S(2)}, u32[]{:S(2)}) collective-permute-start(f32[1,384]{1,0:T(1,128)S(1)} %get-tuple-element.52), channel_id=1, source_target_pairs={{0,16},{1,17},{2,18},{3,19},{4,20},{5,21},{6,22},{7,23},{8,24},{9,... | collective-permute-start | bytes 4616 | tf_op jit(solution)/shard_map/ppermute | solution.py:31
  57.7 7.3 %collective-permute-start.11 = (f32[1,384]{1,0:T(1,128)S(1)}, f32[1,384]{1,0:T(1,128)S(1)}, u32[]{:S(2)}, u32[]{:S(2)}) collective-permute-start(f32[1,384]{1,0:T(1,128)S(1)} %get-tuple-element.51), channel_id=1, source_target_pairs={{0,118},{1,119},{2,116},{3,117},{4,122},{5,123},{6,120},{7,121},{8... | collective-permute-start | bytes 4616 | tf_op jit(solution)/shard_map/ppermute | solution.py:31
  63.7 1.3 collective-permute-start.8
  63.8 5.2 %collective-permute-start.20 = (f32[64,384]{1,0:T(8,128)S(1)}, f32[64,384]{1,0:T(8,128)S(1)}, u32[]{:S(2)}, u32[]{:S(2)}) collective-permute-start(f32[64,384]{1,0:T(8,128)S(1)} %copy-done.5), channel_id=1, source_target_pairs={{0,2},{1,3},{2,0},{3,1},{4,6},{5,7},{6,4},{7,5},{8,10},{9,11},{10,... | collective-permute-start | bytes 294920 | tf_op jit(solution)/shard_map/ppermute | solution.py:31
  65.0 4.0 %collective-permute-start.13 = (f32[1,384]{1,0:T(1,128)S(1)}, f32[1,384]{1,0:T(1,128)S(1)}, u32[]{:S(2)}, u32[]{:S(2)}) collective-permute-start(f32[1,384]{1,0:T(1,128)S(1)} %get-tuple-element.72), channel_id=1, source_target_pairs={{0,1},{1,0},{2,3},{3,2},{4,5},{5,4},{6,7},{7,6},{8,9},{9,8},{10,11... | collective-permute-start | bytes 4616 | tf_op jit(solution)/shard_map/ppermute | solution.py:31
  65.2 9.5 %collective-permute-start.19 = (f32[64,384]{1,0:T(8,128)S(1)}, f32[64,384]{1,0:T(8,128)S(1)}, u32[]{:S(2)}, u32[]{:S(2)}) collective-permute-start(f32[64,384]{1,0:T(8,128)S(1)} %copy-done.5), channel_id=1, source_target_pairs={{0,1},{1,0},{2,3},{3,2},{4,5},{5,4},{6,7},{7,6},{8,9},{9,8},{10,11... | collective-permute-start | bytes 294920 | tf_op jit(solution)/shard_map/ppermute | solution.py:31
  69.0 9.4 %collective-permute-start.21 = (f32[64,384]{1,0:T(8,128)S(1)}, f32[64,384]{1,0:T(8,128)S(1)}, u32[]{:S(2)}, u32[]{:S(2)}) collective-permute-start(f32[64,384]{1,0:T(8,128)S(1)} %collective-permute-done.20.e2), channel_id=1, source_target_pairs={{0,1},{1,0},{2,3},{3,2},{4,5},{5,4},{6,7},{7,6},{8,9},{9,8},{10,11... | collective-permute-start | bytes 294920 | tf_op jit(solution)/shard_map/ppermute | solution.py:31
  69.1 5.7 %collective-permute-start.14 = (f32[2,384]{1,0:T(2,128)S(1)}, f32[2,384]{1,0:T(2,128)S(1)}, u32[]{:S(2)}, u32[]{:S(2)}) collective-permute-start(f32[2,384]{1,0:T(2,128)S(1)} %pad_maximum_fusion.1), channel_id=1, source_target_pairs={{0,2},{1,3},{2,0},{3,1},{4,6},{5,7},{6,4},{7,5},{8,10},{9,11},{10,... | collective-permute-start | bytes 9224 | tf_op jit(solution)/shard_map/ppermute | solution.py:31
  69.4 12.2 %collective-permute-start.15 = (bf16[64,384]{1,0:T(8,128)(2,1)S(1)}, bf16[64,384]{1,0:T(8,128)(2,1)S(1)}, u32[]{:S(2)}, u32[]{:S(2)}) collective-permute-start(bf16[64,384]{1,0:T(8,128)(2,1)S(1)} %multiply_convert_fusion.x0), channel_id=1, source_target_pairs={{0,6},{1,7},{2,4},{3,5},{4,10},{5,11},{6,8},{7,9},{8,14},{9,15},{1... | collective-permute-start | bytes 147464 | tf_op jit(solution)/shard_map/ppermute | solution.py:31
  69.7 11.9 %collective-permute-start.16 = (bf16[64,384]{1,0:T(8,128)(2,1)S(1)}, bf16[64,384]{1,0:T(8,128)(2,1)S(1)}, u32[]{:S(2)}, u32[]{:S(2)}) collective-permute-start(bf16[64,384]{1,0:T(8,128)(2,1)S(1)} %multiply_convert_fusion.x0), channel_id=1, source_target_pairs={{0,120},{1,121},{2,122},{3,123},{4,124},{5,125},{6,126},{7,127},{8... | collective-permute-start | bytes 147464 | tf_op jit(solution)/shard_map/ppermute | solution.py:31
  74.7 9.8 %collective-permute-start.17 = (bf16[64,384]{1,0:T(8,128)(2,1)S(1)}, bf16[64,384]{1,0:T(8,128)(2,1)S(1)}, u32[]{:S(2)}, u32[]{:S(2)}) collective-permute-start(bf16[64,384]{1,0:T(8,128)(2,1)S(1)} %multiply_convert_fusion.x0), channel_id=1, source_target_pairs={{0,14},{1,15},{2,12},{3,13},{4,18},{5,19},{6,16},{7,17},{8,22},{9,... | collective-permute-start | bytes 147464 | tf_op jit(solution)/shard_map/ppermute | solution.py:31
  74.7 9.8 %collective-permute-start.18 = (bf16[64,384]{1,0:T(8,128)(2,1)S(1)}, bf16[64,384]{1,0:T(8,128)(2,1)S(1)}, u32[]{:S(2)}, u32[]{:S(2)}) collective-permute-start(bf16[64,384]{1,0:T(8,128)(2,1)S(1)} %multiply_convert_fusion.x0), channel_id=1, source_target_pairs={{0,112},{1,113},{2,114},{3,115},{4,116},{5,117},{6,118},{7,119},{8... | collective-permute-start | bytes 147464 | tf_op jit(solution)/shard_map/ppermute | solution.py:31
  86.9 4.7 %collective-permute-start.22 = (bf16[64,768]{1,0:T(8,128)(2,1)S(1)}, bf16[64,768]{1,0:T(8,128)(2,1)S(1)}, u32[]{:S(2)}, u32[]{:S(2)}) collective-permute-start(bf16[64,768]{1,0:T(8,128)(2,1)S(1)} %get-tuple-element.64), channel_id=1, source_target_pairs={{0,2},{1,3},{2,0},{3,1},{4,6},{5,7},{6,4},{7,5},{8,10},{9,11},{10,... | collective-permute-start | bytes 294920 | tf_op jit(solution)/shard_map/ppermute | solution.py:31
  91.6 17.7 %collective-permute-start.23 = (f32[64,384]{1,0:T(8,128)S(1)}, f32[64,384]{1,0:T(8,128)S(1)}, u32[]{:S(2)}, u32[]{:S(2)}) collective-permute-start(f32[64,384]{1,0:T(8,128)S(1)} %get-tuple-element.73), channel_id=1, source_target_pairs={{0,1},{1,0},{2,3},{3,2},{4,5},{5,4},{6,7},{7,6},{8,9},{9,8},{10,11... | collective-permute-start | bytes 294920 | tf_op jit(solution)/shard_map/ppermute | solution.py:31
  91.7 9.9 %collective-permute-start.24 = (bf16[64,384]{1,0:T(8,128)(2,1)S(1)}, bf16[64,384]{1,0:T(8,128)(2,1)S(1)}, u32[]{:S(2)}, u32[]{:S(2)}) collective-permute-start(bf16[64,384]{1,0:T(8,128)(2,1)S(1)} %get-tuple-element.65), channel_id=1, source_target_pairs={{0,126},{1,127},{2,124},{3,125},{4,2},{5,3},{6,0},{7,1},{8,6},{9,7... | collective-permute-start | bytes 147464 | tf_op jit(solution)/shard_map/ppermute | solution.py:31
  93.7 7.9 %collective-permute-start.25 = (bf16[64,384]{1,0:T(8,128)(2,1)S(1)}, bf16[64,384]{1,0:T(8,128)(2,1)S(1)}, u32[]{:S(2)}, u32[]{:S(2)}) collective-permute-start(bf16[64,384]{1,0:T(8,128)(2,1)S(1)} %get-tuple-element.66), channel_id=1, source_target_pairs={{0,8},{1,9},{2,10},{3,11},{4,12},{5,13},{6,14},{7,15},{8,16},{9,17... | collective-permute-start | bytes 147464 | tf_op jit(solution)/shard_map/ppermute | solution.py:31
  95.9 7.4 %collective-permute-start.26 = (bf16[64,384]{1,0:T(8,128)(2,1)S(1)}, bf16[64,384]{1,0:T(8,128)(2,1)S(1)}, u32[]{:S(2)}, u32[]{:S(2)}) collective-permute-start(bf16[64,384]{1,0:T(8,128)(2,1)S(1)} %get-tuple-element.67), channel_id=1, source_target_pairs={{0,118},{1,119},{2,116},{3,117},{4,122},{5,123},{6,120},{7,121},{8... | collective-permute-start | bytes 147464 | tf_op jit(solution)/shard_map/ppermute | solution.py:31
  101.6 7.7 %collective-permute-start.27 = (bf16[64,384]{1,0:T(8,128)(2,1)S(1)}, bf16[64,384]{1,0:T(8,128)(2,1)S(1)}, u32[]{:S(2)}, u32[]{:S(2)}) collective-permute-start(bf16[64,384]{1,0:T(8,128)(2,1)S(1)} %get-tuple-element.68), channel_id=1, source_target_pairs={{0,16},{1,17},{2,18},{3,19},{4,20},{5,21},{6,22},{7,23},{8,24},{9,... | collective-permute-start | bytes 147464 | tf_op jit(solution)/shard_map/ppermute | solution.py:31
  109.6 1.2 collective-permute-start.28
  110.8 3.7 %collective-permute-start.29 = (f32[32,128]{1,0:T(8,128)S(1)}, f32[32,128]{1,0:T(8,128)S(1)}, u32[]{:S(2)}, u32[]{:S(2)}) collective-permute-start(f32[32,128]{1,0:T(8,128)S(1)} %add.61), channel_id=1, source_target_pairs={{0,2},{1,3},{2,0},{3,1},{4,6},{5,7},{6,4},{7,5},{8,10},{9,11},{10,... | collective-permute-start | bytes 49160 | tf_op jit(solution)/shard_map/ppermute | solution.py:31
  114.6 5.2 %collective-permute-start.30 = (f32[32,128]{1,0:T(8,128)S(1)}, f32[32,128]{1,0:T(8,128)S(1)}, u32[]{:S(2)}, u32[]{:S(2)}) collective-permute-start(f32[32,128]{1,0:T(8,128)S(1)} %add.62), channel_id=1, source_target_pairs={{0,4},{4,0},{8,12},{12,8},{16,20},{20,16},{24,28},{28,24},{32,36},... | collective-permute-start | bytes 49160 | tf_op jit(solution)/shard_map/ppermute | solution.py:311
  119.8 3.7 %collective-permute-start.31 = (f32[32,128]{1,0:T(8,128)S(1)}, f32[32,128]{1,0:T(8,128)S(1)}, u32[]{:S(2)}, u32[]{:S(2)}) collective-permute-start(f32[32,128]{1,0:T(8,128)S(1)} %add.63), channel_id=1, source_target_pairs={{0,8},{4,12},{8,0},{12,4},{16,24},{20,28},{24,16},{28,20},{32,40},... | collective-permute-start | bytes 49160 | tf_op jit(solution)/shard_map/ppermute | solution.py:311
  123.6 5.2 %collective-permute-start.32 = (f32[32,128]{1,0:T(8,128)S(1)}, f32[32,128]{1,0:T(8,128)S(1)}, u32[]{:S(2)}, u32[]{:S(2)}) collective-permute-start(f32[32,128]{1,0:T(8,128)S(1)} %add.64), channel_id=1, source_target_pairs={{0,16},{4,20},{8,24},{12,28},{16,0},{20,4},{24,8},{28,12},{32,48},... | collective-permute-start | bytes 49160 | tf_op jit(solution)/shard_map/ppermute | solution.py:311
  128.8 3.7 %collective-permute-start.33 = (f32[32,128]{1,0:T(8,128)S(1)}, f32[32,128]{1,0:T(8,128)S(1)}, u32[]{:S(2)}, u32[]{:S(2)}) collective-permute-start(f32[32,128]{1,0:T(8,128)S(1)} %add.65), channel_id=1, source_target_pairs={{0,32},{4,36},{8,40},{12,44},{16,48},{20,52},{24,56},{28,60},{32,0... | collective-permute-start | bytes 49160 | tf_op jit(solution)/shard_map/ppermute | solution.py:311
  132.6 5.2 %collective-permute-start.34 = (f32[32,128]{1,0:T(8,128)S(1)}, f32[32,128]{1,0:T(8,128)S(1)}, u32[]{:S(2)}, u32[]{:S(2)}) collective-permute-start(f32[32,128]{1,0:T(8,128)S(1)} %add.66), channel_id=1, source_target_pairs={{0,64},{4,68},{8,72},{12,76},{16,80},{20,84},{24,88},{28,92},{32,9... | collective-permute-start | bytes 49160 | tf_op jit(solution)/shard_map/ppermute | solution.py:311

commit v2 on v1

v2 whole, which is shorter than its diff:
```python
import functools
import math

import jax
import jax.numpy as jnp
from jax import lax
from jax.experimental import pallas as pl
from jax.experimental.pallas import tpu as pltpu
from jax.sharding import PartitionSpec as P

F = 768
ROWS = 384
SLOTS = 4
EIG = 64
NNB = 16
BAND = ((1, 2), (-2, 0), (3, 2), (-4, 0))
ONWARD = ((2, 0), (-2, 0))
EXTRA = 3 * NNB
ROUNDS = ((0, 1), (0, 2), (1, 2), (2, 0), (6, 0), (8, 0), (24, 0))
FOLDED = 2.0 * math.log2(math.e) / F
NT = (((1,), (1,)), ((), ()))
LIMIT = 24 * 1024 * 1024


def moved(value, blocks, flip):
    n_blk, n_sub = lax.axis_size("blk"), lax.axis_size("sub")
    pairs = [
        (b * n_sub + s, ((b + blocks) % n_blk) * n_sub + (s ^ flip))
        for b in range(n_blk)
        for s in range(n_sub)
    ]
    return lax.ppermute(value, ("blk", "sub"), pairs)


VMEM = pl.BlockSpec(memory_space=pltpu.VMEM)
SMEM = pl.BlockSpec(memory_space=pltpu.SMEM)
HBM = pl.BlockSpec(memory_space=pltpu.HBM)


def call(body, outs, scratch=(), specs=None, flops=1000):
    def run(*args):
        return pl.pallas_call(
            body,
            grid=(1,),
            out_shape=outs,
            in_specs=list(specs) if specs else [VMEM] * len(args),
            out_specs=jax.tree.map(lambda _: VMEM, outs),
            scratch_shapes=list(scratch),
            compiler_params=pltpu.CompilerParams(vmem_limit_bytes=LIMIT),
            cost_estimate=pl.CostEstimate(flops=flops, bytes_accessed=1000, transcendentals=0),
        )(*args)

    return run


def f32(*shape):
    return jax.ShapeDtypeStruct(shape, jnp.float32)


def bf16(*shape):
    return jax.ShapeDtypeStruct(shape, jnp.bfloat16)


def own_tile_kernel(sub, f0, f1, f2, f3, scales, lists, tile, row, col, norms, inner, words, cols):
    ones = jnp.ones((8, F), jnp.bfloat16)
    for slot, ref in enumerate((f0, f1, f2, f3)):
        value = ref[...].astype(jnp.float32)
        square = value * value
        high = square.astype(jnp.bfloat16)
        low = (square - high.astype(jnp.float32)).astype(jnp.bfloat16)
        total = lax.dot_general(ones, high, NT, preferred_element_type=jnp.float32)
        total = total + lax.dot_general(ones, low, NT, preferred_element_type=jnp.float32)
        norms[slot : slot + 1, :] = total[0:1, :]
    tile_kernel(0, 0, sub, f0, f1, f2, f3, f0, norms, scales, None, lists, tile, row, col, inner, words, cols)


def band_tile_kernel(flip, reverse, sub, *refs):
    tile_kernel(flip, reverse, sub, *refs[:8], *refs[-7:])


def pack_kernel(half, sub, features, scales, lists, first, second):
    at = pl.multiple_of(sub[0] * ROWS, 128)
    scale = jnp.concatenate([scales[:, pl.ds(at, ROWS)], jnp.ones((1, ROWS), jnp.float32)], axis=1)
    scale = jnp.broadcast_to(scale, (NNB, 2 * ROWS)).astype(jnp.bfloat16)
    for out, chosen in ((first, BAND[0::2]), (second, BAND[1::2])):
        out[:ROWS, :] = features[...]
        for index, (d, _) in enumerate(chosen):
            position = lists[half - d]
            digits = jnp.concatenate([position >> 6, position & 63], axis=1)
            start = ROWS + NNB * index
            out[start : start + NNB, :] = digits.astype(jnp.float32).astype(jnp.bfloat16)
        out[ROWS + 2 * NNB :, :] = scale


def tile_kernel(flip, reverse, sub, f0, f1, f2, f3, moving, norms, scales, before, lists, tile, row, col, inner, words, cols):
    me = sub[0]
    feats = moving[:ROWS, :].astype(jnp.float32)
    half_norm = 0.5 * jnp.sum(feats * feats, axis=1, keepdims=True)

    if reverse:
        digits = moving[ROWS + reverse - NNB : ROWS + reverse, :].astype(jnp.float32).astype(jnp.int32)
        position = digits[:, :ROWS] * 64 + digits[:, ROWS:]
        group = position >> 7
        slice_at = (group * 11) >> 5
        group = (slice_at ^ me) * 3 + group - 3 * slice_at
        pieces = [(position & 127).astype(jnp.float32), jnp.left_shift(1, group).astype(jnp.float32)]
        own_scale = moving[ROWS + 2 * NNB :, :ROWS].astype(jnp.float32)[0:1]
    else:
        pieces = [jnp.zeros((32, ROWS), jnp.float32)]
        own_scale = scales[:, pl.ds(pl.multiple_of(me * ROWS, 128), ROWS)]
    stacked = jnp.concatenate(
        pieces + [FOLDED / own_scale, jnp.zeros((95, ROWS), jnp.float32)], axis=0
    )
    turned = stacked.T
    move_scale = turned[:, 32:33]
    if reverse:
        lane = lax.broadcasted_iota(jnp.int32, (64, 128), 1).astype(jnp.float32)
        for at in range(0, ROWS, 64):
            part = turned[at : at + 64]
            word = jnp.zeros((64, 128), jnp.float32)
            for m in range(NNB):
                word = word + jnp.where(part[:, m : m + 1] == lane, part[:, 16 + m : 17 + m], 0.0)
            words[at : at + 64, :] = word.astype(jnp.int32)

    row_at = lax.broadcasted_iota(jnp.int32, (8, ROWS), 0)
    for slot, ref in enumerate((f0, f1, f2, f3)):
        inner[slot] = lax.dot_general(moving[:ROWS, :], ref[...], NT, preferred_element_type=jnp.float32)
        start = pl.multiple_of((me ^ slot) * ROWS, 128)
        listed = lists[0, :, pl.ds(start, ROWS)] - (me ^ flip) * ROWS
        inside = (listed >= 0) & (listed < ROWS)
        sublane = listed & 7
        bit = jnp.where(inside, listed >> 3, 0)
        first = jnp.where(inside & (bit < 24), jnp.left_shift(1, bit), 0)
        second = jnp.where(inside & (bit >= 24), jnp.left_shift(1, jnp.maximum(bit - 24, 0)), 0)
        low = jnp.zeros((8, ROWS), jnp.int32)
        high = jnp.zeros((8, ROWS), jnp.int32)
        for m in range(NNB):
            same = sublane[m : m + 1, :] == row_at
            low = low | jnp.where(same, first[m : m + 1, :], 0)
            high = high | jnp.where(same, second[m : m + 1, :], 0)
        norm = 0.5 * norms[slot : slot + 1, :]
        scale = 1.0 / scales[:, pl.ds(start, ROWS)]
        row_sum = jnp.zeros((8, ROWS), jnp.float32)
        step = 32
        for at in range(0, ROWS, step):
            source = low if at < 192 else high
            counts = [
                (source >> ((at // 8 + c) % 24)) & 1 for c in range(step // 8)
            ]
            count = jnp.concatenate(counts, axis=0)
            if reverse:
                word = words[at : at + step, :]
                count = count + jnp.concatenate(
                    [(word >> (3 * slot + g)) & 1 for g in range(3)], axis=1
                )
            power = inner[slot, at : at + step, :] - half_norm[at : at + step] - norm
            power = power * move_scale[at : at + step] * scale
            weight = jnp.exp2(power) * count.astype(jnp.float32)
            tile[at : at + step, slot * ROWS : (slot + 1) * ROWS] = weight.astype(jnp.bfloat16)
            for c in range(step // 8):
                row_sum = row_sum + weight[8 * c : 8 * c + 8, :]
            lanes = weight[:, 0:128] + weight[:, 128:256] + weight[:, 256:384]
            if slot == 0:
                cols[at : at + step, :] = lanes
            else:
                cols[at : at + step, :] = cols[at : at + step, :] + lanes
        total = jnp.sum(row_sum, axis=0, keepdims=True)
        row[slot : slot + 1, :] = before[slot : slot + 1, :] + total if reverse else total
    col[...] = jnp.sum(cols[...].T, axis=0, keepdims=True)


def col_kernel(x0, x1, far, t0, t1, t2, t3, t4, z0, z1, z2, z3, z4):
    block = jnp.concatenate([x0[...], x1[...], far[:EIG, :], far[EIG:, :]], axis=1)
    for tile, out in ((t1, z1), (t2, z2), (t3, z3), (t4, z4), (t0, z0)):
        out[...] = lax.dot_general(block, tile[...], NT, preferred_element_type=jnp.float32).astype(out.dtype)


def row_kernel(x0, x1, x2, x3, x4, t0, t1, t2, t3, t4, y0, y2, sent):
    for slot, out, at_out in ((1, sent, 0), (3, sent, EIG), (0, y0, 0), (2, y2, 0)):
        at = slot * ROWS
        total = jnp.zeros((EIG, ROWS), jnp.float32)
        for vectors, tile in ((x0, t0), (x1, t1), (x2, t2), (x3, t3), (x4, t4)):
            total = total + jnp.dot(
                vectors[...], tile[:, at : at + ROWS], preferred_element_type=jnp.float32
            )
        out[at_out : at_out + EIG, :] = total


def mix_kernel(own, root, y0, y1, y2, z0, z1, z2, z3, z4, mixed, gram):
    sides = y0[...] + y1[:EIG, :] + y2[...].astype(jnp.float32) + z0[...]
    for part in (z1, z2, z3, z4):
        sides = sides + part[...].astype(jnp.float32)
    inv = root[0:1, :]
    value = inv * (own[...] * inv + 0.5 * sides)
    mixed[...] = value
    total = lax.dot_general(
        value, value, NT, precision=lax.Precision.HIGHEST, preferred_element_type=jnp.float32
    )
    gram[...] = jnp.concatenate([total[: EIG // 2], total[EIG // 2 :]], axis=1)


def solve_kernel(factor, gram, mixed, out):
    rows = lax.broadcasted_iota(jnp.int32, (EIG, 2 * EIG), 0)
    lanes = lax.broadcasted_iota(jnp.int32, (EIG, 2 * EIG), 1)
    unit = (rows + EIG == lanes).astype(jnp.float32)
    square = jnp.concatenate([gram[:, :EIG], gram[:, EIG:]], axis=0)
    work = jnp.concatenate([square, jnp.zeros((EIG, EIG), jnp.float32)], axis=1) + unit
    done = []
    for at in range(0, EIG, 8):
        wide = [jnp.broadcast_to(work[:, at + j : at + j + 1], (EIG - at, 2 * EIG)) for j in range(8)]
        for j in range(8):
            root = lax.rsqrt(wide[j][j : j + 1, :])
            pivot = work[j : j + 1, :] * root
            done.append(pivot)
            lower = wide[j] * root
            work = work - lower * pivot
            for other in range(j + 1, 8):
                wide[other] = wide[other] - lower * (wide[other][j : j + 1, :] * root)
        work = work[8:]
    inverse = jnp.concatenate(done, axis=0)[:, EIG:]
    out[...] = factor * jnp.dot(
        inverse, mixed[...], precision=lax.Precision.HIGHEST, preferred_element_type=jnp.float32
    )


def local(features, scales, neighbor_lists, eigen_block):
    sub = lax.axis_index("sub").astype(jnp.int32)
    half = (neighbor_lists.shape[0] - 1) // 2
    total_rows = ROWS * lax.axis_size("blk") * lax.axis_size("sub")
    sub_arg = sub.reshape(1)

    block_scales = scales.astype(jnp.float32)[None, :]
    own_lists = lax.dynamic_slice_in_dim(neighbor_lists, sub * ROWS, ROWS, axis=2)
    first, second = call(
        functools.partial(pack_kernel, half),
        (bf16(ROWS + EXTRA, F),) * 2,
        specs=(SMEM, VMEM, VMEM, VMEM),
    )(sub_arg, features, block_scales, own_lists)

    first, second, ready = lax.optimization_barrier((first, second, features))
    first = moved(first, *BAND[0])
    second = moved(second, *BAND[1])
    slot2 = moved(ready, 0, 2)
    slot1 = moved(ready, 0, 1)
    slot3 = moved(slot2, 0, 1)
    block = (features, slot1, slot2, slot3)

    tile_outs = (bf16(ROWS, SLOTS * ROWS), f32(SLOTS, ROWS), f32(1, ROWS))
    scratch = (
        pltpu.VMEM((SLOTS, ROWS, ROWS), jnp.float32),
        pltpu.VMEM((ROWS, 128), jnp.int32),
        pltpu.VMEM((ROWS, 128), jnp.float32),
    )

    def listed(d):
        return pl.BlockSpec((1, NNB, SLOTS * ROWS), lambda i: (half + d, 0, 0))

    def band_tile(index, moving, row, tokens=(), flops=1000):
        d, u = BAND[index]
        body = functools.partial(band_tile_kernel, u, NNB * (1 + index // 2))
        specs = (SMEM,) + (VMEM,) * 8 + (HBM,) * len(tokens) + (listed(d),)
        args = (sub_arg, *block, moving, norms, block_scales, row, *tokens, neighbor_lists)
        tile, row, col = call(body, tile_outs, scratch, specs, flops)(*args)
        return tile, row, moved(col, -d, u)

    tile0, row, col0, norms = call(
        own_tile_kernel,
        tile_outs + (f32(SLOTS, ROWS),),
        scratch,
        (SMEM,) + (VMEM,) * 5 + (listed(0),),
    )(sub_arg, *block, block_scales, neighbor_lists)
    first, second, row = lax.optimization_barrier((first, second, row))
    third = moved(first, *ONWARD[0])
    fourth = moved(second, *ONWARD[1])
    tile1, row, col1 = band_tile(0, first, row)
    tile2, row, col2 = band_tile(1, second, row)
    tile3, row, col3 = band_tile(2, third, row, (col1,))
    tile4, row, col4 = band_tile(3, fourth, row, (col2,), 4 * 10**9)
    tiles = (tile0, tile1, tile2, tile3, tile4)

    pair = row[0:2] + moved(row[2:4], 0, 2)
    own = pair[0:1] + moved(pair[1:2], 0, 1)
    root = lax.rsqrt(1.0 + 0.5 * (own + col0 + col1 + col2 + col3 + col4))
    scaled_low = (eigen_block * root).astype(jnp.bfloat16)
    vectors = [moved(scaled_low, d, u) for d, u in BAND]
    x1 = moved(scaled_low, 0, 1)
    far = moved(jnp.concatenate([scaled_low, x1], axis=0), 0, 2)

    z_outs = (f32(EIG, ROWS),) + (bf16(EIG, ROWS),) * 4
    z0, z1, z2, z3, z4 = call(col_kernel, z_outs)(scaled_low, x1, far, *tiles)
    back = [moved(part, -d, u) for (d, u), part in zip(BAND, (z1, z2, z3, z4))]
    vectors, _ = lax.optimization_barrier((vectors, z0))
    y_outs = (f32(EIG, ROWS), f32(EIG, ROWS), f32(2 * EIG, ROWS))
    y0, y2, sent = call(row_kernel, y_outs)(scaled_low, *vectors, *tiles)
    other = moved(sent, 0, 1)
    across = moved((y2 + other[EIG:]).astype(jnp.bfloat16), 0, 2)
    mixed, gram = call(mix_kernel, (f32(EIG, ROWS), f32(EIG // 2, 2 * EIG)))(
        eigen_block, root, y0, other, across, z0, *back
    )
    n_blk, n_sub = lax.axis_size("blk"), lax.axis_size("sub")
    for flip_blk, flip_sub in ROUNDS:
        pairs = [
            (b * n_sub + s, (b ^ flip_blk) * n_sub + (s ^ flip_sub))
            for b in range(n_blk)
            for s in range(n_sub)
        ]
        gram = gram + lax.ppermute(gram, ("blk", "sub"), pairs)
    body = functools.partial(solve_kernel, math.sqrt(total_rows))
    return call(body, f32(EIG, ROWS))(gram, mixed)


def solution(mesh):
    placed = (P(("blk", "sub"), None), P("blk"), P(None, None, "blk"), P(None, ("blk", "sub")))
    return jax.shard_map(
        local, mesh=mesh, in_specs=placed, out_specs=P(None, ("blk", "sub")), check_vma=False
    )
```

time: 144 us -> 133 us (0.924)
  waiting for transfers between devices: 65.2 us -> 51.1 us
  starting transfers between devices: 45 us -> 55.8 us
  Pallas kernels: 29.4 us -> 22.5 us
    ppermute x30 -> x25, waiting for transfers between devices: 42 us -> 29.7 us  [moved(): return lax.ppermute(value, ('blk', 'sub'), pairs)]
    ppermute x5 -> x7, starting transfers between devices: 0.01 us -> 10.1 us  [local(): gram = gram + lax.ppermute(gram, ('blk', 'sub'), pairs)]
    pallas_call x11 -> x10, Pallas kernels: 29.4 us -> 22.5 us  [run(): pl.pallas_call(body, grid=(1,), out_shape=outs, in_specs=list(specs) if s...]
    unnamed x12 -> x6, local copies, waits for them, and re-layouts: 3.31 us -> 1.07 us
    ppermute x5 -> x7, waiting for transfers between devices: 23.2 us -> 21.3 us  [local(): gram = gram + lax.ppermute(gram, ('blk', 'sub'), pairs)]
    ppermute x30 -> x25, starting transfers between devices: 45 us -> 45.7 us  [moved(): return lax.ppermute(value, ('blk', 'sub'), pairs)]
  transfers between devices with their start and end apart: 35 -> 32, of which waited for: 18 -> 19; matrix products, arithmetic and copies ran while one was open for 0% -> 0% of each run, Pallas kernels for 12% -> 11%
where the time goes in v2:
time: 133 us; the launch traced here: 132 us
  starting transfers between devices  55.8 us (42%)
  waiting for transfers between devices  51.1 us (38%)
  Pallas kernels  22.5 us (17%)
  local copies, waits for them, and re-layouts  2.8 us (2%)
    ppermute x25, starting transfers between devices, moved(): return lax.ppermute(value, ('blk', 'sub'), pairs)  45.7 us
    ppermute x25, waiting for transfers between devices, moved(): return lax.ppermute(value, ('blk', 'sub'), pairs)  29.7 us
    pallas_call x10, Pallas kernels, run(): pl.pallas_call(body, grid=(1,), out_shape=outs, in_specs=list(specs) if s...  22.5 us
    ppermute x7, waiting for transfers between devices, local(): gram = gram + lax.ppermute(gram, ('blk', 'sub'), pairs)  21.3 us
    ppermute x7, starting transfers between devices, local(): gram = gram + lax.ppermute(gram, ('blk', 'sub'), pairs)  10.1 us
  transfers between devices with their start and end apart: 32, of which 19 were waited for; matrix products, arithmetic and copies ran while one was open for 0% of the time, Pallas kernels for 11%

profile of v2, /device:TPU:0, one launch (start us, length us, event | category | flops | bytes accessed | tf_op | source)
XLA Modules:
  0.0 132.5 jit_solution(7613970004849283635)
XLA Ops:
  0.0 0.8 reshape.4.scales.refs_6_
  0.8 0.9 constant_dynamic-slice_fusion.lists
  1.7 0.0 copy-start.1
  1.7 1.1 copy-done.1
  2.8 0.1 shard_map.46
  2.9 1.7 %collective-permute-start.1 = (bf16[384,768]{1,0:T(8,128)(2,1)S(1)}, bf16[384,768]{1,0:T(8,128)(2,1)S(1)}, u32[]{:S(2)}, u32[]{:S(2)}) collective-permute-start(bf16[384,768]{1,0:T(8,128)(2,1)S(1)} %copy-done.1), channel_id=1, source_target_pairs={{0,2},{1,3},{2,0},{3,1},{4,6},{5,7},{6,4},{7,5},{8,10},{9,11},{10,... | collective-permute-start | bytes 1769480 | tf_op jit(solution)/shard_map/ppermute | solution.py:32
  4.6 2.2 %collective-permute-start.3 = (bf16[432,768]{1,0:T(8,128)(2,1)S(1)}, bf16[432,768]{1,0:T(8,128)(2,1)S(1)}, u32[]{:S(2)}, u32[]{:S(2)}) collective-permute-start(bf16[432,768]{1,0:T(8,128)(2,1)S(1)} %get-tuple-element.46), channel_id=1, source_target_pairs={{0,6},{1,7},{2,4},{3,5},{4,10},{5,11},{6,8},{7,9},{8,14},{9,15},{1... | collective-permute-start | bytes 1990664 | tf_op jit(solution)/shard_map/ppermute | solution.py:32
  6.8 6.2 %collective-permute-start.4 = (bf16[432,768]{1,0:T(8,128)(2,1)S(1)}, bf16[432,768]{1,0:T(8,128)(2,1)S(1)}, u32[]{:S(2)}, u32[]{:S(2)}) collective-permute-start(bf16[432,768]{1,0:T(8,128)(2,1)S(1)} %get-tuple-element.47), channel_id=1, source_target_pairs={{0,120},{1,121},{2,122},{3,123},{4,124},{5,125},{6,126},{7,127},{8... | collective-permute-start | bytes 1990664 | tf_op jit(solution)/shard_map/ppermute | solution.py:32
  13.0 0.0 collective-permute-start
  13.0 4.9 %collective-permute-done.1.f2.refs_2_ = bf16[384,768]{1,0:T(8,128)(2,1)S(1)} collective-permute-done((bf16[384,768]{1,0:T(8,128)(2,1)S(1)}, bf16[384,768]{1,0:T(8,128)(2,1)S(1)}, u32[]{:S(2)}, u32[]{:S(2)}) %collective-permute-start.1) | collective-permute-done | bytes 589856 | tf_op jit(solution)/shard_map/ppermute | solution.py:32
  18.0 0.0 collective-permute-start.2
  18.0 0.0 collective-permute-done.f1.refs_1_
  18.0 2.0 %collective-permute-done.2.f3.refs_3_ = bf16[384,768]{1,0:T(8,128)(2,1)S(1)} collective-permute-done((bf16[384,768]{1,0:T(8,128)(2,1)S(1)}, bf16[384,768]{1,0:T(8,128)(2,1)S(1)}, u32[]{:S(2)}, u32[]{:S(2)}) %collective-permute-start.2) | collective-permute-done | bytes 589856 | tf_op jit(solution)/shard_map/ppermute | solution.py:32
  20.0 3.2 %shard_map.47 = (bf16[384,1536]{1,0:T(8,128)(2,1)S(1)}, f32[4,384]{1,0:T(4,128)S(1)}, f32[1,384]{1,0:T(1,128)S(1)}, f32[4,384]{1,0:T(4,128)S(1)}) custom-call(s32[1]{0:T(128)} %bitcast.sub, bf16[384,768]{1,0:T(8,128)(2,1)S(1)} %copy-done.1, bf16[384,768]{1,0:T(8,128)(2,1)S(1)} %collective-permute-done.f1.refs_1_, ...), custom_call_target="tpu_custom_call" | custom-call | flops 1000 | bytes 1000 | tf_op jit(solution)/shard_map/pallas_call | solution.py:42
  23.2 3.9 %collective-permute-done.3.refs_4_ = bf16[432,768]{1,0:T(8,128)(2,1)S(1)} collective-permute-done((bf16[432,768]{1,0:T(8,128)(2,1)S(1)}, bf16[432,768]{1,0:T(8,128)(2,1)S(1)}, u32[]{:S(2)}, u32[]{:S(2)}) %collective-permute-start.3) | collective-permute-done | bytes 663584 | tf_op jit(solution)/shard_map/ppermute | solution.py:32
  27.1 0.0 collective-permute-done.4.refs_4_
  27.1 0.0 collective-permute-start.6
  27.1 5.3 %collective-permute-start.5 = (bf16[432,768]{1,0:T(8,128)(2,1)S(1)}, bf16[432,768]{1,0:T(8,128)(2,1)S(1)}, u32[]{:S(2)}, u32[]{:S(2)}) collective-permute-start(bf16[432,768]{1,0:T(8,128)(2,1)S(1)} %collective-permute-done.4.refs_4_), channel_id=1, source_target_pairs={{0,120},{1,121},{2,122},{3,123},{4,124},{5,125},{6,126},{7,127},{8... | collective-permute-start | bytes 1990664 | tf_op jit(solution)/shard_map/ppermute | solution.py:32
  32.5 3.4 %shard_map.48 = (bf16[384,1536]{1,0:T(8,128)(2,1)S(1)}, f32[4,384]{1,0:T(4,128)S(1)}, f32[1,384]{1,0:T(1,128)S(1)}) custom-call(s32[1]{0:T(128)} %bitcast.sub, bf16[384,768]{1,0:T(8,128)(2,1)S(1)} %copy-done.1, bf16[384,768]{1,0:T(8,128)(2,1)S(1)} %collective-permute-done.f1.refs_1_, bf16[384,768]{1,0:T(8,128)(2,1)S(1)} %collective-permute-done.1.f2.refs_2_, ...), custom_call_target="tpu_custom_call" | custom-call | flops 1000 | bytes 1000 | tf_op jit(solution)/shard_map/pallas_call | solution.py:42
  35.8 2.0 %collective-permute-start.7 = (f32[1,384]{1,0:T(1,128)S(1)}, f32[1,384]{1,0:T(1,128)S(1)}, u32[]{:S(2)}, u32[]{:S(2)}) collective-permute-start(f32[1,384]{1,0:T(1,128)S(1)} %get-tuple-element.55), channel_id=1, source_target_pairs={{0,126},{1,127},{2,124},{3,125},{4,2},{5,3},{6,0},{7,1},{8,6},{9,7... | collective-permute-start | bytes 4616 | tf_op jit(solution)/shard_map/ppermute | solution.py:32
  37.8 3.4 %shard_map.49 = (bf16[384,1536]{1,0:T(8,128)(2,1)S(1)}, f32[4,384]{1,0:T(4,128)S(1)}, f32[1,384]{1,0:T(1,128)S(1)}) custom-call(s32[1]{0:T(128)} %bitcast.sub, bf16[384,768]{1,0:T(8,128)(2,1)S(1)} %copy-done.1, bf16[384,768]{1,0:T(8,128)(2,1)S(1)} %collective-permute-done.f1.refs_1_, bf16[384,768]{1,0:T(8,128)(2,1)S(1)} %collective-permute-done.1.f2.refs_2_, ...), custom_call_target="tpu_custom_call" | custom-call | flops 1000 | bytes 1000 | tf_op jit(solution)/shard_map/pallas_call | solution.py:42
  41.2 0.1 collective-permute-start.8
  41.3 4.2 %collective-permute-done.7.refs_8_ = f32[1,384]{1,0:T(1,128)S(1)} collective-permute-done((f32[1,384]{1,0:T(1,128)S(1)}, f32[1,384]{1,0:T(1,128)S(1)}, u32[]{:S(2)}, u32[]{:S(2)}) %collective-permute-start.7) | collective-permute-done | bytes 1568 | tf_op jit(solution)/shard_map/ppermute | solution.py:32
  45.5 0.7 collective-permute-done.6.refs_4_
  46.2 3.4 %shard_map.50 = (bf16[384,1536]{1,0:T(8,128)(2,1)S(1)}, f32[4,384]{1,0:T(4,128)S(1)}, f32[1,384]{1,0:T(1,128)S(1)}) custom-call(s32[1]{0:T(128)} %bitcast.sub, bf16[384,768]{1,0:T(8,128)(2,1)S(1)} %copy-done.1, bf16[384,768]{1,0:T(8,128)(2,1)S(1)} %collective-permute-done.f1.refs_1_, bf16[384,768]{1,0:T(8,128)(2,1)S(1)} %collective-permute-done.1.f2.refs_2_, ...), custom_call_target="tpu_custom_call" | custom-call | flops 1000 | bytes 1000 | tf_op jit(solution)/shard_map/pallas_call | solution.py:42
  49.6 0.0 copy-start.2
  49.6 3.4 %shard_map.51 = (bf16[384,1536]{1,0:T(8,128)(2,1)S(1)}, f32[4,384]{1,0:T(4,128)S(1)}, f32[1,384]{1,0:T(1,128)S(1)}) custom-call(s32[1]{0:T(128)} %bitcast.sub, bf16[384,768]{1,0:T(8,128)(2,1)S(1)} %copy-done.1, bf16[384,768]{1,0:T(8,128)(2,1)S(1)} %collective-permute-done.f1.refs_1_, bf16[384,768]{1,0:T(8,128)(2,1)S(1)} %collective-permute-done.1.f2.refs_2_, ...), custom_call_target="tpu_custom_call" | custom-call | flops 4000000000 | bytes 1000 | tf_op jit(solution)/shard_map/pallas_call | solution.py:42
  53.0 0.8 collective-permute-start.9
  53.8 6.8 %collective-permute-start.11 = (f32[1,384]{1,0:T(1,128)S(1)}, f32[1,384]{1,0:T(1,128)S(1)}, u32[]{:S(2)}, u32[]{:S(2)}) collective-permute-start(f32[1,384]{1,0:T(1,128)S(1)} %get-tuple-element.60), channel_id=1, source_target_pairs={{0,118},{1,119},{2,116},{3,117},{4,122},{5,123},{6,120},{7,121},{8... | collective-permute-start | bytes 4616 | tf_op jit(solution)/shard_map/ppermute | solution.py:32
  60.6 0.1 collective-permute-start.10
  60.7 0.2 collective-permute-done.12
  61.0 1.0 collective-permute-done.11
  62.0 0.4 collective-permute-start.17
  62.4 1.1 collective-permute-done.17.x1
  63.5 0.8 collective-permute-start.18
  64.3 2.6 %collective-permute-start.16 = (bf16[64,384]{1,0:T(8,128)(2,1)S(1)}, bf16[64,384]{1,0:T(8,128)(2,1)S(1)}, u32[]{:S(2)}, u32[]{:S(2)}) collective-permute-start(bf16[64,384]{1,0:T(8,128)(2,1)S(1)} %multiply_convert_fusion.x0), channel_id=1, source_target_pairs={{0,112},{1,113},{2,114},{3,115},{4,116},{5,117},{6,118},{7,119},{8... | collective-permute-start | bytes 147464 | tf_op jit(solution)/shard_map/ppermute | solution.py:32
  66.9 6.0 %collective-permute-start.15 = (bf16[64,384]{1,0:T(8,128)(2,1)S(1)}, bf16[64,384]{1,0:T(8,128)(2,1)S(1)}, u32[]{:S(2)}, u32[]{:S(2)}) collective-permute-start(bf16[64,384]{1,0:T(8,128)(2,1)S(1)} %multiply_convert_fusion.x0), channel_id=1, source_target_pairs={{0,14},{1,15},{2,12},{3,13},{4,18},{5,19},{6,16},{7,17},{8,22},{9,... | collective-permute-start | bytes 147464 | tf_op jit(solution)/shard_map/ppermute | solution.py:32
  73.0 4.1 %collective-permute-start.14 = (bf16[64,384]{1,0:T(8,128)(2,1)S(1)}, bf16[64,384]{1,0:T(8,128)(2,1)S(1)}, u32[]{:S(2)}, u32[]{:S(2)}) collective-permute-start(bf16[64,384]{1,0:T(8,128)(2,1)S(1)} %multiply_convert_fusion.x0), channel_id=1, source_target_pairs={{0,120},{1,121},{2,122},{3,123},{4,124},{5,125},{6,126},{7,127},{8... | collective-permute-start | bytes 147464 | tf_op jit(solution)/shard_map/ppermute | solution.py:32
  77.1 1.8 %shard_map.52 = (f32[64,384]{1,0:T(8,128)S(1)}, bf16[64,384]{1,0:T(8,128)(2,1)S(1)}, bf16[64,384]{1,0:T(8,128)(2,1)S(1)}, bf16[64,384]{1,0:T(8,128)(2,1)S(1)}, bf16[64,384]{1,0:T(8,128)(2,1)S(1)}) custom-call(bf16[64,384]{1,0:T(8,128)(2,1)S(1)} %multiply_convert_fusion.x0, bf16[64,384]{1,0:T(8,128)(2,1)S(1)} %collective-permute-done.17.x1, ...), custom_call_target="tpu_custom_call" | custom-call | flops 1000 | bytes 1000 | tf_op jit(solution)/shard_map/pallas_call | solution.py:42
  78.9 7.6 %collective-permute-done.13.x1 = bf16[64,384]{1,0:T(8,128)(2,1)S(1)} collective-permute-done((bf16[64,384]{1,0:T(8,128)(2,1)S(1)}, bf16[64,384]{1,0:T(8,128)(2,1)S(1)}, u32[]{:S(2)}, u32[]{:S(2)}) %collective-permute-start.13) | collective-permute-done | bytes 49184 | tf_op jit(solution)/shard_map/ppermute | solution.py:32
  86.6 1.1 shard_map.53
  87.7 0.1 collective-permute-start.19
  87.8 0.1 collective-permute-start.21
  87.9 0.1 collective-permute-start.22
  87.9 1.9 %collective-permute-start.23 = (bf16[64,384]{1,0:T(8,128)(2,1)S(1)}, bf16[64,384]{1,0:T(8,128)(2,1)S(1)}, u32[]{:S(2)}, u32[]{:S(2)}) collective-permute-start(bf16[64,384]{1,0:T(8,128)(2,1)S(1)} %get-tuple-element.77), channel_id=1, source_target_pairs={{0,118},{1,119},{2,116},{3,117},{4,122},{5,123},{6,120},{7,121},{8... | collective-permute-start | bytes 147464 | tf_op jit(solution)/shard_map/ppermute | solution.py:32
  89.9 4.2 %collective-permute-start.24 = (bf16[64,384]{1,0:T(8,128)(2,1)S(1)}, bf16[64,384]{1,0:T(8,128)(2,1)S(1)}, u32[]{:S(2)}, u32[]{:S(2)}) collective-permute-start(bf16[64,384]{1,0:T(8,128)(2,1)S(1)} %get-tuple-element.78), channel_id=1, source_target_pairs={{0,16},{1,17},{2,18},{3,19},{4,20},{5,21},{6,22},{7,23},{8,24},{9,... | collective-permute-start | bytes 147464 | tf_op jit(solution)/shard_map/ppermute | solution.py:32
  94.1 0.1 collective-permute-start.20
  94.2 1.2 collective-permute-done.22.z2
  95.3 2.2 %collective-permute-done.24.z4 = bf16[64,384]{1,0:T(8,128)(2,1)S(1)} collective-permute-done((bf16[64,384]{1,0:T(8,128)(2,1)S(1)}, bf16[64,384]{1,0:T(8,128)(2,1)S(1)}, u32[]{:S(2)}, u32[]{:S(2)}) %collective-permute-start.24) | collective-permute-done | bytes 49184 | tf_op jit(solution)/shard_map/ppermute | solution.py:32
  97.6 0.7 collective-permute-done.20.y2
  98.2 0.4 shard_map.54
  98.6 0.0 collective-permute-start.25
  98.6 1.2 collective-permute-done.25
  99.8 0.0 collective-permute-start.26
  99.8 3.7 %collective-permute-done.26 = f32[32,128]{1,0:T(8,128)S(1)} collective-permute-done((f32[32,128]{1,0:T(8,128)S(1)}, f32[32,128]{1,0:T(8,128)S(1)}, u32[]{:S(2)}, u32[]{:S(2)}) %collective-permute-start.26) | collective-permute-done | bytes 16416 | tf_op jit(solution)/shard_map/ppermute | solution.py:307
  103.6 5.4 %collective-permute-start.27 = (f32[32,128]{1,0:T(8,128)S(1)}, f32[32,128]{1,0:T(8,128)S(1)}, u32[]{:S(2)}, u32[]{:S(2)}) collective-permute-start(f32[32,128]{1,0:T(8,128)S(1)} %add.66), channel_id=1, source_target_pairs={{0,6},{1,7},{2,4},{3,5},{4,2},{5,3},{6,0},{7,1},{8,14},{9,15},{10,... | collective-permute-start | bytes 49160 | tf_op jit(solution)/shard_map/ppermute | solution.py:307
  109.0 1.7 %collective-permute-done.27 = f32[32,128]{1,0:T(8,128)S(1)} collective-permute-done((f32[32,128]{1,0:T(8,128)S(1)}, f32[32,128]{1,0:T(8,128)S(1)}, u32[]{:S(2)}, u32[]{:S(2)}) %collective-permute-start.27) | collective-permute-done | bytes 16416 | tf_op jit(solution)/shard_map/ppermute | solution.py:307
  110.7 4.0 %collective-permute-start.28 = (f32[32,128]{1,0:T(8,128)S(1)}, f32[32,128]{1,0:T(8,128)S(1)}, u32[]{:S(2)}, u32[]{:S(2)}) collective-permute-start(f32[32,128]{1,0:T(8,128)S(1)} %add.67), channel_id=1, source_target_pairs={{0,8},{1,9},{2,10},{3,11},{4,12},{5,13},{6,14},{7,15},{8,0},{9,1},... | collective-permute-start | bytes 49160 | tf_op jit(solution)/shard_map/ppermute | solution.py:307
  114.7 1.7 %collective-permute-done.28 = f32[32,128]{1,0:T(8,128)S(1)} collective-permute-done((f32[32,128]{1,0:T(8,128)S(1)}, f32[32,128]{1,0:T(8,128)S(1)}, u32[]{:S(2)}, u32[]{:S(2)}) %collective-permute-start.28) | collective-permute-done | bytes 16416 | tf_op jit(solution)/shard_map/ppermute | solution.py:307
  116.4 4.9 %collective-permute-done.29 = f32[32,128]{1,0:T(8,128)S(1)} collective-permute-done((f32[32,128]{1,0:T(8,128)S(1)}, f32[32,128]{1,0:T(8,128)S(1)}, u32[]{:S(2)}, u32[]{:S(2)}) %collective-permute-start.29) | collective-permute-done | bytes 16416 | tf_op jit(solution)/shard_map/ppermute | solution.py:307
  121.4 3.7 %collective-permute-done.30 = f32[32,128]{1,0:T(8,128)S(1)} collective-permute-done((f32[32,128]{1,0:T(8,128)S(1)}, f32[32,128]{1,0:T(8,128)S(1)}, u32[]{:S(2)}, u32[]{:S(2)}) %collective-permute-start.30) | collective-permute-done | bytes 16416 | tf_op jit(solution)/shard_map/ppermute | solution.py:307
  125.1 0.6 collective-permute-start.31
  125.7 4.3 %collective-permute-done.31 = f32[32,128]{1,0:T(8,128)S(1)} collective-permute-done((f32[32,128]{1,0:T(8,128)S(1)}, f32[32,128]{1,0:T(8,128)S(1)}, u32[]{:S(2)}, u32[]{:S(2)}) %collective-permute-start.31) | collective-permute-done | bytes 16416 | tf_op jit(solution)/shard_map/ppermute | solution.py:307
  130.1 2.4 %shard_map.55 = f32[64,384]{1,0:T(8,128)} custom-call(f32[32,128]{1,0:T(8,128)S(1)} %add.71.gram, f32[64,384]{1,0:T(8,128)S(1)} %get-tuple-element.80.mixed), custom_call_target="tpu_custom_call" | custom-call | flops 1000 | bytes 1000 | tf_op jit(solution)/shard_map/pallas_call | solution.py:42
  (32 shorter events, 0.2 us)
Async XLA Ops:
  0.0 20.0 %copy-start = (s32[9,16,1536]{2,1,0:T(8,128)S(1)}, s32[9,16,1536]{2,1,0:T(8,128)}, u32[]{:S(2)}) copy-start(s32[9,16,1536]{2,1,0:T(8,128)} %refs_9_.3) | copy-start | bytes 2654212
  1.7 1.1 copy-start.1
  2.9 15.1 %collective-permute-start.1 = (bf16[384,768]{1,0:T(8,128)(2,1)S(1)}, bf16[384,768]{1,0:T(8,128)(2,1)S(1)}, u32[]{:S(2)}, u32[]{:S(2)}) collective-permute-start(bf16[384,768]{1,0:T(8,128)(2,1)S(1)} %copy-done.1), channel_id=1, source_target_pairs={{0,2},{1,3},{2,0},{3,1},{4,6},{5,7},{6,4},{7,5},{8,10},{9,11},{10,... | collective-permute-start | bytes 1769480 | tf_op jit(solution)/shard_map/ppermute | solution.py:32
  4.6 22.5 %collective-permute-start.3 = (bf16[432,768]{1,0:T(8,128)(2,1)S(1)}, bf16[432,768]{1,0:T(8,128)(2,1)S(1)}, u32[]{:S(2)}, u32[]{:S(2)}) collective-permute-start(bf16[432,768]{1,0:T(8,128)(2,1)S(1)} %get-tuple-element.46), channel_id=1, source_target_pairs={{0,6},{1,7},{2,4},{3,5},{4,10},{5,11},{6,8},{7,9},{8,14},{9,15},{1... | collective-permute-start | bytes 1990664 | tf_op jit(solution)/shard_map/ppermute | solution.py:32
  6.8 20.3 %collective-permute-start.4 = (bf16[432,768]{1,0:T(8,128)(2,1)S(1)}, bf16[432,768]{1,0:T(8,128)(2,1)S(1)}, u32[]{:S(2)}, u32[]{:S(2)}) collective-permute-start(bf16[432,768]{1,0:T(8,128)(2,1)S(1)} %get-tuple-element.47), channel_id=1, source_target_pairs={{0,120},{1,121},{2,122},{3,123},{4,124},{5,125},{6,126},{7,127},{8... | collective-permute-start | bytes 1990664 | tf_op jit(solution)/shard_map/ppermute | solution.py:32
  13.0 4.9 %collective-permute-start = (bf16[384,768]{1,0:T(8,128)(2,1)S(1)}, bf16[384,768]{1,0:T(8,128)(2,1)S(1)}, u32[]{:S(2)}, u32[]{:S(2)}) collective-permute-start(bf16[384,768]{1,0:T(8,128)(2,1)S(1)} %copy-done.1), channel_id=1, source_target_pairs={{0,1},{1,0},{2,3},{3,2},{4,5},{5,4},{6,7},{7,6},{8,9},{9,8},{10,11... | collective-permute-start | bytes 1769480 | tf_op jit(solution)/shard_map/ppermute | solution.py:32
  18.0 2.0 %collective-permute-start.2 = (bf16[384,768]{1,0:T(8,128)(2,1)S(1)}, bf16[384,768]{1,0:T(8,128)(2,1)S(1)}, u32[]{:S(2)}, u32[]{:S(2)}) collective-permute-start(bf16[384,768]{1,0:T(8,128)(2,1)S(1)} %collective-permute-done.1.f2.refs_2_), channel_id=1, source_target_pairs={{0,1},{1,0},{2,3},{3,2},{4,5},{5,4},{6,7},{7,6},{8,9},{9,8},{10,11... | collective-permute-start | bytes 1769480 | tf_op jit(solution)/shard_map/ppermute | solution.py:32
  27.1 19.1 %collective-permute-start.6 = (bf16[432,768]{1,0:T(8,128)(2,1)S(1)}, bf16[432,768]{1,0:T(8,128)(2,1)S(1)}, u32[]{:S(2)}, u32[]{:S(2)}) collective-permute-start(bf16[432,768]{1,0:T(8,128)(2,1)S(1)} %collective-permute-done.3.refs_4_), channel_id=1, source_target_pairs={{0,8},{1,9},{2,10},{3,11},{4,12},{5,13},{6,14},{7,15},{8,16},{9,17... | collective-permute-start | bytes 1990664 | tf_op jit(solution)/shard_map/ppermute | solution.py:32
  27.1 22.5 %collective-permute-start.5 = (bf16[432,768]{1,0:T(8,128)(2,1)S(1)}, bf16[432,768]{1,0:T(8,128)(2,1)S(1)}, u32[]{:S(2)}, u32[]{:S(2)}) collective-permute-start(bf16[432,768]{1,0:T(8,128)(2,1)S(1)} %collective-permute-done.4.refs_4_), channel_id=1, source_target_pairs={{0,120},{1,121},{2,122},{3,123},{4,124},{5,125},{6,126},{7,127},{8... | collective-permute-start | bytes 1990664 | tf_op jit(solution)/shard_map/ppermute | solution.py:32
  35.8 9.7 %collective-permute-start.7 = (f32[1,384]{1,0:T(1,128)S(1)}, f32[1,384]{1,0:T(1,128)S(1)}, u32[]{:S(2)}, u32[]{:S(2)}) collective-permute-start(f32[1,384]{1,0:T(1,128)S(1)} %get-tuple-element.55), channel_id=1, source_target_pairs={{0,126},{1,127},{2,124},{3,125},{4,2},{5,3},{6,0},{7,1},{8,6},{9,7... | collective-permute-start | bytes 4616 | tf_op jit(solution)/shard_map/ppermute | solution.py:32
  41.2 8.4 %collective-permute-start.8 = (f32[1,384]{1,0:T(1,128)S(1)}, f32[1,384]{1,0:T(1,128)S(1)}, u32[]{:S(2)}, u32[]{:S(2)}) collective-permute-start(f32[1,384]{1,0:T(1,128)S(1)} %get-tuple-element.57), channel_id=1, source_target_pairs={{0,8},{1,9},{2,10},{3,11},{4,12},{5,13},{6,14},{7,15},{8,16},{9,17... | collective-permute-start | bytes 4616 | tf_op jit(solution)/shard_map/ppermute | solution.py:32
  49.6 12.4 %copy-start.2 = (f32[64,384]{1,0:T(8,128)S(1)}, f32[64,384]{1,0:T(8,128)}, u32[]{:S(2)}) copy-start(f32[64,384]{1,0:T(8,128)} %own.1) | copy-start | bytes 294916
  53.0 7.6 %collective-permute-start.9 = (f32[2,384]{1,0:T(2,128)S(1)}, f32[2,384]{1,0:T(2,128)S(1)}, u32[]{:S(2)}, u32[]{:S(2)}) collective-permute-start(f32[2,384]{1,0:T(2,128)S(1)} %slice.16), channel_id=1, source_target_pairs={{0,2},{1,3},{2,0},{3,1},{4,6},{5,7},{6,4},{7,5},{8,10},{9,11},{10,... | collective-permute-start | bytes 9224 | tf_op jit(solution)/shard_map/ppermute | solution.py:32
  53.8 7.2 %collective-permute-start.12 = (f32[1,384]{1,0:T(1,128)S(1)}, f32[1,384]{1,0:T(1,128)S(1)}, u32[]{:S(2)}, u32[]{:S(2)}) collective-permute-start(f32[1,384]{1,0:T(1,128)S(1)} %get-tuple-element.61), channel_id=1, source_target_pairs={{0,16},{1,17},{2,18},{3,19},{4,20},{5,21},{6,22},{7,23},{8,24},{9,... | collective-permute-start | bytes 4616 | tf_op jit(solution)/shard_map/ppermute | solution.py:32
  53.8 8.1 %collective-permute-start.11 = (f32[1,384]{1,0:T(1,128)S(1)}, f32[1,384]{1,0:T(1,128)S(1)}, u32[]{:S(2)}, u32[]{:S(2)}) collective-permute-start(f32[1,384]{1,0:T(1,128)S(1)} %get-tuple-element.60), channel_id=1, source_target_pairs={{0,118},{1,119},{2,116},{3,117},{4,122},{5,123},{6,120},{7,121},{8... | collective-permute-start | bytes 4616 | tf_op jit(solution)/shard_map/ppermute | solution.py:32
  60.6 1.3 collective-permute-start.10
  62.0 1.5 %collective-permute-start.17 = (bf16[64,384]{1,0:T(8,128)(2,1)S(1)}, bf16[64,384]{1,0:T(8,128)(2,1)S(1)}, u32[]{:S(2)}, u32[]{:S(2)}) collective-permute-start(bf16[64,384]{1,0:T(8,128)(2,1)S(1)} %multiply_convert_fusion.x0), channel_id=1, source_target_pairs={{0,1},{1,0},{2,3},{3,2},{4,5},{5,4},{6,7},{7,6},{8,9},{9,8},{10,11... | collective-permute-start | bytes 147464 | tf_op jit(solution)/shard_map/ppermute | solution.py:32
  63.5 13.5 %collective-permute-start.18 = (bf16[128,384]{1,0:T(8,128)(2,1)S(1)}, bf16[128,384]{1,0:T(8,128)(2,1)S(1)}, u32[]{:S(2)}, u32[]{:S(2)}) collective-permute-start(bf16[128,384]{1,0:T(8,128)(2,1)S(1)} %pad_maximum_fusion), channel_id=1, source_target_pairs={{0,2},{1,3},{2,0},{3,1},{4,6},{5,7},{6,4},{7,5},{8,10},{9,11},{10,... | collective-permute-start | bytes 294920 | tf_op jit(solution)/shard_map/ppermute | solution.py:32
  64.3 14.6 %collective-permute-start.16 = (bf16[64,384]{1,0:T(8,128)(2,1)S(1)}, bf16[64,384]{1,0:T(8,128)(2,1)S(1)}, u32[]{:S(2)}, u32[]{:S(2)}) collective-permute-start(bf16[64,384]{1,0:T(8,128)(2,1)S(1)} %multiply_convert_fusion.x0), channel_id=1, source_target_pairs={{0,112},{1,113},{2,114},{3,115},{4,116},{5,117},{6,118},{7,119},{8... | collective-permute-start | bytes 147464 | tf_op jit(solution)/shard_map/ppermute | solution.py:32
  66.9 12.0 %collective-permute-start.15 = (bf16[64,384]{1,0:T(8,128)(2,1)S(1)}, bf16[64,384]{1,0:T(8,128)(2,1)S(1)}, u32[]{:S(2)}, u32[]{:S(2)}) collective-permute-start(bf16[64,384]{1,0:T(8,128)(2,1)S(1)} %multiply_convert_fusion.x0), channel_id=1, source_target_pairs={{0,14},{1,15},{2,12},{3,13},{4,18},{5,19},{6,16},{7,17},{8,22},{9,... | collective-permute-start | bytes 147464 | tf_op jit(solution)/shard_map/ppermute | solution.py:32
  73.0 6.0 %collective-permute-start.14 = (bf16[64,384]{1,0:T(8,128)(2,1)S(1)}, bf16[64,384]{1,0:T(8,128)(2,1)S(1)}, u32[]{:S(2)}, u32[]{:S(2)}) collective-permute-start(bf16[64,384]{1,0:T(8,128)(2,1)S(1)} %multiply_convert_fusion.x0), channel_id=1, source_target_pairs={{0,120},{1,121},{2,122},{3,123},{4,124},{5,125},{6,126},{7,127},{8... | collective-permute-start | bytes 147464 | tf_op jit(solution)/shard_map/ppermute | solution.py:32
  77.0 9.5 %collective-permute-start.13 = (bf16[64,384]{1,0:T(8,128)(2,1)S(1)}, bf16[64,384]{1,0:T(8,128)(2,1)S(1)}, u32[]{:S(2)}, u32[]{:S(2)}) collective-permute-start(bf16[64,384]{1,0:T(8,128)(2,1)S(1)} %multiply_convert_fusion.x0), channel_id=1, source_target_pairs={{0,6},{1,7},{2,4},{3,5},{4,10},{5,11},{6,8},{7,9},{8,14},{9,15},{1... | collective-permute-start | bytes 147464 | tf_op jit(solution)/shard_map/ppermute | solution.py:32
  87.7 6.4 %collective-permute-start.19 = (f32[128,384]{1,0:T(8,128)S(1)}, f32[128,384]{1,0:T(8,128)S(1)}, u32[]{:S(2)}, u32[]{:S(2)}) collective-permute-start(f32[128,384]{1,0:T(8,128)S(1)} %get-tuple-element.73), channel_id=1, source_target_pairs={{0,1},{1,0},{2,3},{3,2},{4,5},{5,4},{6,7},{7,6},{8,9},{9,8},{10,11... | collective-permute-start | bytes 589832 | tf_op jit(solution)/shard_map/ppermute | solution.py:32
  87.8 6.4 %collective-permute-start.21 = (bf16[64,384]{1,0:T(8,128)(2,1)S(1)}, bf16[64,384]{1,0:T(8,128)(2,1)S(1)}, u32[]{:S(2)}, u32[]{:S(2)}) collective-permute-start(bf16[64,384]{1,0:T(8,128)(2,1)S(1)} %get-tuple-element.75), channel_id=1, source_target_pairs={{0,126},{1,127},{2,124},{3,125},{4,2},{5,3},{6,0},{7,1},{8,6},{9,7... | collective-permute-start | bytes 147464 | tf_op jit(solution)/shard_map/ppermute | solution.py:32
  87.9 7.5 %collective-permute-start.22 = (bf16[64,384]{1,0:T(8,128)(2,1)S(1)}, bf16[64,384]{1,0:T(8,128)(2,1)S(1)}, u32[]{:S(2)}, u32[]{:S(2)}) collective-permute-start(bf16[64,384]{1,0:T(8,128)(2,1)S(1)} %get-tuple-element.76), channel_id=1, source_target_pairs={{0,8},{1,9},{2,10},{3,11},{4,12},{5,13},{6,14},{7,15},{8,16},{9,17... | collective-permute-start | bytes 147464 | tf_op jit(solution)/shard_map/ppermute | solution.py:32
  87.9 7.4 %collective-permute-start.23 = (bf16[64,384]{1,0:T(8,128)(2,1)S(1)}, bf16[64,384]{1,0:T(8,128)(2,1)S(1)}, u32[]{:S(2)}, u32[]{:S(2)}) collective-permute-start(bf16[64,384]{1,0:T(8,128)(2,1)S(1)} %get-tuple-element.77), channel_id=1, source_target_pairs={{0,118},{1,119},{2,116},{3,117},{4,122},{5,123},{6,120},{7,121},{8... | collective-permute-start | bytes 147464 | tf_op jit(solution)/shard_map/ppermute | solution.py:32
  89.9 7.7 %collective-permute-start.24 = (bf16[64,384]{1,0:T(8,128)(2,1)S(1)}, bf16[64,384]{1,0:T(8,128)(2,1)S(1)}, u32[]{:S(2)}, u32[]{:S(2)}) collective-permute-start(bf16[64,384]{1,0:T(8,128)(2,1)S(1)} %get-tuple-element.78), channel_id=1, source_target_pairs={{0,16},{1,17},{2,18},{3,19},{4,20},{5,21},{6,22},{7,23},{8,24},{9,... | collective-permute-start | bytes 147464 | tf_op jit(solution)/shard_map/ppermute | solution.py:32
  94.1 4.2 %collective-permute-start.20 = (bf16[64,384]{1,0:T(8,128)(2,1)S(1)}, bf16[64,384]{1,0:T(8,128)(2,1)S(1)}, u32[]{:S(2)}, u32[]{:S(2)}) collective-permute-start(bf16[64,384]{1,0:T(8,128)(2,1)S(1)} %fusion), channel_id=1, source_target_pairs={{0,2},{1,3},{2,0},{3,1},{4,6},{5,7},{6,4},{7,5},{8,10},{9,11},{10,... | collective-permute-start | bytes 147464 | tf_op jit(solution)/shard_map/ppermute | solution.py:32
  98.6 1.2 collective-permute-start.25
  99.8 3.7 %collective-permute-start.26 = (f32[32,128]{1,0:T(8,128)S(1)}, f32[32,128]{1,0:T(8,128)S(1)}, u32[]{:S(2)}, u32[]{:S(2)}) collective-permute-start(f32[32,128]{1,0:T(8,128)S(1)} %add.65), channel_id=1, source_target_pairs={{0,2},{1,3},{2,0},{3,1},{4,6},{5,7},{6,4},{7,5},{8,10},{9,11},{10,... | collective-permute-start | bytes 49160 | tf_op jit(solution)/shard_map/ppermute | solution.py:307
  103.6 7.1 %collective-permute-start.27 = (f32[32,128]{1,0:T(8,128)S(1)}, f32[32,128]{1,0:T(8,128)S(1)}, u32[]{:S(2)}, u32[]{:S(2)}) collective-permute-start(f32[32,128]{1,0:T(8,128)S(1)} %add.66), channel_id=1, source_target_pairs={{0,6},{1,7},{2,4},{3,5},{4,2},{5,3},{6,0},{7,1},{8,14},{9,15},{10,... | collective-permute-start | bytes 49160 | tf_op jit(solution)/shard_map/ppermute | solution.py:307
  110.7 5.7 %collective-permute-start.28 = (f32[32,128]{1,0:T(8,128)S(1)}, f32[32,128]{1,0:T(8,128)S(1)}, u32[]{:S(2)}, u32[]{:S(2)}) collective-permute-start(f32[32,128]{1,0:T(8,128)S(1)} %add.67), channel_id=1, source_target_pairs={{0,8},{1,9},{2,10},{3,11},{4,12},{5,13},{6,14},{7,15},{8,0},{9,1},... | collective-permute-start | bytes 49160 | tf_op jit(solution)/shard_map/ppermute | solution.py:307
  116.4 4.9 %collective-permute-start.29 = (f32[32,128]{1,0:T(8,128)S(1)}, f32[32,128]{1,0:T(8,128)S(1)}, u32[]{:S(2)}, u32[]{:S(2)}) collective-permute-start(f32[32,128]{1,0:T(8,128)S(1)} %add.68), channel_id=1, source_target_pairs={{0,24},{1,25},{2,26},{3,27},{4,28},{5,29},{6,30},{7,31},{8,16},{9,... | collective-permute-start | bytes 49160 | tf_op jit(solution)/shard_map/ppermute | solution.py:307
  121.4 3.7 %collective-permute-start.30 = (f32[32,128]{1,0:T(8,128)S(1)}, f32[32,128]{1,0:T(8,128)S(1)}, u32[]{:S(2)}, u32[]{:S(2)}) collective-permute-start(f32[32,128]{1,0:T(8,128)S(1)} %add.69), channel_id=1, source_target_pairs={{0,32},{1,33},{2,34},{3,35},{4,36},{5,37},{6,38},{7,39},{8,40},{9,... | collective-permute-start | bytes 49160 | tf_op jit(solution)/shard_map/ppermute | solution.py:307
  125.1 4.9 %collective-permute-start.31 = (f32[32,128]{1,0:T(8,128)S(1)}, f32[32,128]{1,0:T(8,128)S(1)}, u32[]{:S(2)}, u32[]{:S(2)}) collective-permute-start(f32[32,128]{1,0:T(8,128)S(1)} %add.70), channel_id=1, source_target_pairs={{0,96},{1,97},{2,98},{3,99},{4,100},{5,101},{6,102},{7,103},{8,104... | collective-permute-start | bytes 49160 | tf_op jit(solution)/shard_map/ppermute | solution.py:307

commit v3 on v2

--- a/solution.py
+++ b/solution.py
@@ -16,7 +16,7 @@
 BAND = ((1, 2), (-2, 0), (3, 2), (-4, 0))
 ONWARD = ((2, 0), (-2, 0))
 EXTRA = 3 * NNB
-ROUNDS = ((0, 1), (0, 2), (1, 2), (2, 0), (6, 0), (8, 0), (24, 0))
+ROUNDS = (((0, 1),), ((0, 2), (1, 0), (1, 2)), ((2, 0), (4, 0), (6, 0)), ((8, 0), (16, 0), (24, 0)))
 FOLDED = 2.0 * math.log2(math.e) / F
 NT = (((1,), (1,)), ((), ()))
 LIMIT = 24 * 1024 * 1024
@@ -114,13 +114,11 @@
     turned = stacked.T
     move_scale = turned[:, 32:33]
     if reverse:
-        lane = lax.broadcasted_iota(jnp.int32, (64, 128), 1).astype(jnp.float32)
-        for at in range(0, ROWS, 64):
-            part = turned[at : at + 64]
-            word = jnp.zeros((64, 128), jnp.float32)
-            for m in range(NNB):
-                word = word + jnp.where(part[:, m : m + 1] == lane, part[:, 16 + m : 17 + m], 0.0)
-            words[at : at + 64, :] = word.astype(jnp.int32)
+        sublane = lax.broadcasted_iota(jnp.int32, (128, ROWS), 0).astype(jnp.float32)
+        word = jnp.zeros((128, ROWS), jnp.float32)
+        for m in range(NNB):
+            word = word + jnp.where(pieces[0][m : m + 1, :] == sublane, pieces[1][m : m + 1, :], 0.0)
+        words[...] = word.T.astype(jnp.int32)
 
     row_at = lax.broadcasted_iota(jnp.int32, (8, ROWS), 0)
     for slot, ref in enumerate((f0, f1, f2, f3)):
@@ -237,7 +235,9 @@
         specs=(SMEM, VMEM, VMEM, VMEM),
     )(sub_arg, features, block_scales, own_lists)
 
-    first, second, ready = lax.optimization_barrier((first, second, features))
+    first, second, ready, all_lists = lax.optimization_barrier(
+        (first, second, features, neighbor_lists)
+    )
     first = moved(first, *BAND[0])
     second = moved(second, *BAND[1])
     slot2 = moved(ready, 0, 2)
@@ -259,7 +259,7 @@
         d, u = BAND[index]
         body = functools.partial(band_tile_kernel, u, NNB * (1 + index // 2))
         specs = (SMEM,) + (VMEM,) * 8 + (HBM,) * len(tokens) + (listed(d),)
-        args = (sub_arg, *block, moving, norms, block_scales, row, *tokens, neighbor_lists)
+        args = (sub_arg, *block, moving, norms, block_scales, row, *tokens, all_lists)
         tile, row, col = call(body, tile_outs, scratch, specs, flops)(*args)
         return tile, row, moved(col, -d, u)
 
@@ -268,14 +268,14 @@
         tile_outs + (f32(SLOTS, ROWS),),
         scratch,
         (SMEM,) + (VMEM,) * 5 + (listed(0),),
-    )(sub_arg, *block, block_scales, neighbor_lists)
+    )(sub_arg, *block, block_scales, all_lists)
     first, second, row = lax.optimization_barrier((first, second, row))
     third = moved(first, *ONWARD[0])
     fourth = moved(second, *ONWARD[1])
     tile1, row, col1 = band_tile(0, first, row)
     tile2, row, col2 = band_tile(1, second, row)
-    tile3, row, col3 = band_tile(2, third, row, (col1,))
-    tile4, row, col4 = band_tile(3, fourth, row, (col2,), 4 * 10**9)
+    tile3, row, col3 = band_tile(2, third, row)
+    tile4, row, col4 = band_tile(3, fourth, row, (col1, col2), 4 * 10**9)
     tiles = (tile0, tile1, tile2, tile3, tile4)
 
     pair = row[0:2] + moved(row[2:4], 0, 2)
@@ -298,13 +298,16 @@
         eigen_block, root, y0, other, across, z0, *back
     )
     n_blk, n_sub = lax.axis_size("blk"), lax.axis_size("sub")
-    for flip_blk, flip_sub in ROUNDS:
-        pairs = [
-            (b * n_sub + s, (b ^ flip_blk) * n_sub + (s ^ flip_sub))
-            for b in range(n_blk)
-            for s in range(n_sub)
-        ]
-        gram = gram + lax.ppermute(gram, ("blk", "sub"), pairs)
+    for partners in ROUNDS:
+        parts = [gram]
+        for flip_blk, flip_sub in partners:
+            pairs = [
+                (b * n_sub + s, (b ^ flip_blk) * n_sub + (s ^ flip_sub))
+                for b in range(n_blk)
+                for s in range(n_sub)
+            ]
+            parts.append(lax.ppermute(gram, ("blk", "sub"), pairs))
+        gram = functools.reduce(jnp.add, parts)
     body = functools.partial(solve_kernel, math.sqrt(total_rows))
     return call(body, f32(EIG, ROWS))(gram, mixed)
 

time: 133 us -> 125 us (0.940)
  waiting for transfers between devices: 51.1 us -> 42.9 us
  starting transfers between devices: 55.8 us -> 60.3 us
  Pallas kernels: 22.5 us -> 18.4 us
    ppermute x7 -> x10, waiting for transfers between devices: 21.3 us -> 11.1 us  [local(): parts.append(lax.ppermute(gram, ('blk', 'sub'), pairs))]
    ppermute x7 -> x10, starting transfers between devices: 10.1 us -> 14.9 us  [local(): parts.append(lax.ppermute(gram, ('blk', 'sub'), pairs))]
    pallas_call x10, Pallas kernels: 22.5 us -> 18.4 us  [run(): pl.pallas_call(body, grid=(1,), out_shape=outs, in_specs=list(specs) if s...]
    ppermute x25, waiting for transfers between devices: 29.7 us -> 31.8 us  [moved(): return lax.ppermute(value, ('blk', 'sub'), pairs)]
  transfers between devices with their start and end apart: 32 -> 35, of which waited for: 19 -> 19; matrix products, arithmetic and copies ran while one was open for 0% -> 0% of each run, Pallas kernels for 11% -> 10%
where the time goes in v3:
time: 125 us
  starting transfers between devices  60.3 us (48%)
  waiting for transfers between devices  42.9 us (34%)
  Pallas kernels  18.4 us (15%)
  local copies, waits for them, and re-layouts  2.8 us (2%)
    ppermute x25, starting transfers between devices, moved(): return lax.ppermute(value, ('blk', 'sub'), pairs)  45.4 us
    ppermute x25, waiting for transfers between devices, moved(): return lax.ppermute(value, ('blk', 'sub'), pairs)  31.8 us
    pallas_call x10, Pallas kernels, run(): pl.pallas_call(body, grid=(1,), out_shape=outs, in_specs=list(specs) if s...  18.4 us
    ppermute x10, starting transfers between devices, local(): parts.append(lax.ppermute(gram, ('blk', 'sub'), pairs))  14.9 us
    ppermute x10, waiting for transfers between devices, local(): parts.append(lax.ppermute(gram, ('blk', 'sub'), pairs))  11.1 us
  transfers between devices with their start and end apart: 35, of which 19 were waited for; matrix products, arithmetic and copies ran while one was open for 0% of the time, Pallas kernels for 10%

profile of v3, /device:TPU:0, one launch (start us, length us, event | category | flops | bytes accessed | tf_op | source)
XLA Modules:
  0.0 124.8 jit_solution(1162116272903813036)
XLA Ops:
  0.0 0.8 reshape.4.scales.refs_6_
  0.8 0.9 constant_dynamic-slice_fusion.lists
  1.7 0.0 copy-start.1
  1.7 1.1 copy-done.1
  2.8 0.1 shard_map.46
  2.9 1.7 %collective-permute-start.1 = (bf16[384,768]{1,0:T(8,128)(2,1)S(1)}, bf16[384,768]{1,0:T(8,128)(2,1)S(1)}, u32[]{:S(2)}, u32[]{:S(2)}) collective-permute-start(bf16[384,768]{1,0:T(8,128)(2,1)S(1)} %copy-done.1), channel_id=1, source_target_pairs={{0,2},{1,3},{2,0},{3,1},{4,6},{5,7},{6,4},{7,5},{8,10},{9,11},{10,... | collective-permute-start | bytes 1769480 | tf_op jit(solution)/shard_map/ppermute | solution.py:32
  4.6 2.2 %collective-permute-start.3 = (bf16[432,768]{1,0:T(8,128)(2,1)S(1)}, bf16[432,768]{1,0:T(8,128)(2,1)S(1)}, u32[]{:S(2)}, u32[]{:S(2)}) collective-permute-start(bf16[432,768]{1,0:T(8,128)(2,1)S(1)} %get-tuple-element.47), channel_id=1, source_target_pairs={{0,6},{1,7},{2,4},{3,5},{4,10},{5,11},{6,8},{7,9},{8,14},{9,15},{1... | collective-permute-start | bytes 1990664 | tf_op jit(solution)/shard_map/ppermute | solution.py:32
  6.8 6.2 %collective-permute-start.4 = (bf16[432,768]{1,0:T(8,128)(2,1)S(1)}, bf16[432,768]{1,0:T(8,128)(2,1)S(1)}, u32[]{:S(2)}, u32[]{:S(2)}) collective-permute-start(bf16[432,768]{1,0:T(8,128)(2,1)S(1)} %get-tuple-element.48), channel_id=1, source_target_pairs={{0,120},{1,121},{2,122},{3,123},{4,124},{5,125},{6,126},{7,127},{8... | collective-permute-start | bytes 1990664 | tf_op jit(solution)/shard_map/ppermute | solution.py:32
  13.0 0.0 collective-permute-start
  13.0 4.9 %collective-permute-done.1.f2.refs_2_ = bf16[384,768]{1,0:T(8,128)(2,1)S(1)} collective-permute-done((bf16[384,768]{1,0:T(8,128)(2,1)S(1)}, bf16[384,768]{1,0:T(8,128)(2,1)S(1)}, u32[]{:S(2)}, u32[]{:S(2)}) %collective-permute-start.1) | collective-permute-done | bytes 589856 | tf_op jit(solution)/shard_map/ppermute | solution.py:32
  18.0 0.0 collective-permute-done.f1.refs_1_
  18.0 2.0 %collective-permute-done.2.f3.refs_3_ = bf16[384,768]{1,0:T(8,128)(2,1)S(1)} collective-permute-done((bf16[384,768]{1,0:T(8,128)(2,1)S(1)}, bf16[384,768]{1,0:T(8,128)(2,1)S(1)}, u32[]{:S(2)}, u32[]{:S(2)}) %collective-permute-start.2) | collective-permute-done | bytes 589856 | tf_op jit(solution)/shard_map/ppermute | solution.py:32
  20.0 3.2 %shard_map.47 = (bf16[384,1536]{1,0:T(8,128)(2,1)S(1)}, f32[4,384]{1,0:T(4,128)S(1)}, f32[1,384]{1,0:T(1,128)S(1)}, f32[4,384]{1,0:T(4,128)S(1)}) custom-call(s32[1]{0:T(128)} %bitcast.sub, bf16[384,768]{1,0:T(8,128)(2,1)S(1)} %copy-done.1, bf16[384,768]{1,0:T(8,128)(2,1)S(1)} %collective-permute-done.f1.refs_1_, ...), custom_call_target="tpu_custom_call" | custom-call | flops 1000 | bytes 1000 | tf_op jit(solution)/shard_map/pallas_call | solution.py:42
  23.2 3.9 %collective-permute-done.3.refs_4_ = bf16[432,768]{1,0:T(8,128)(2,1)S(1)} collective-permute-done((bf16[432,768]{1,0:T(8,128)(2,1)S(1)}, bf16[432,768]{1,0:T(8,128)(2,1)S(1)}, u32[]{:S(2)}, u32[]{:S(2)}) %collective-permute-start.3) | collective-permute-done | bytes 663584 | tf_op jit(solution)/shard_map/ppermute | solution.py:32
  27.1 5.3 %collective-permute-start.5 = (bf16[432,768]{1,0:T(8,128)(2,1)S(1)}, bf16[432,768]{1,0:T(8,128)(2,1)S(1)}, u32[]{:S(2)}, u32[]{:S(2)}) collective-permute-start(bf16[432,768]{1,0:T(8,128)(2,1)S(1)} %collective-permute-done.4.refs_4_), channel_id=1, source_target_pairs={{0,120},{1,121},{2,122},{3,123},{4,124},{5,125},{6,126},{7,127},{8... | collective-permute-start | bytes 1990664 | tf_op jit(solution)/shard_map/ppermute | solution.py:32
  32.5 2.4 %shard_map.48 = (bf16[384,1536]{1,0:T(8,128)(2,1)S(1)}, f32[4,384]{1,0:T(4,128)S(1)}, f32[1,384]{1,0:T(1,128)S(1)}) custom-call(s32[1]{0:T(128)} %bitcast.sub, bf16[384,768]{1,0:T(8,128)(2,1)S(1)} %copy-done.1, bf16[384,768]{1,0:T(8,128)(2,1)S(1)} %collective-permute-done.f1.refs_1_, bf16[384,768]{1,0:T(8,128)(2,1)S(1)} %collective-permute-done.1.f2.refs_2_, ...), custom_call_target="tpu_custom_call" | custom-call | flops 1000 | bytes 1000 | tf_op jit(solution)/shard_map/pallas_call | solution.py:42
  34.9 1.8 %collective-permute-start.7 = (f32[1,384]{1,0:T(1,128)S(1)}, f32[1,384]{1,0:T(1,128)S(1)}, u32[]{:S(2)}, u32[]{:S(2)}) collective-permute-start(f32[1,384]{1,0:T(1,128)S(1)} %get-tuple-element.58), channel_id=1, source_target_pairs={{0,126},{1,127},{2,124},{3,125},{4,2},{5,3},{6,0},{7,1},{8,6},{9,7... | collective-permute-start | bytes 4616 | tf_op jit(solution)/shard_map/ppermute | solution.py:32
  36.7 2.3 %shard_map.49 = (bf16[384,1536]{1,0:T(8,128)(2,1)S(1)}, f32[4,384]{1,0:T(4,128)S(1)}, f32[1,384]{1,0:T(1,128)S(1)}) custom-call(s32[1]{0:T(128)} %bitcast.sub, bf16[384,768]{1,0:T(8,128)(2,1)S(1)} %copy-done.1, bf16[384,768]{1,0:T(8,128)(2,1)S(1)} %collective-permute-done.f1.refs_1_, bf16[384,768]{1,0:T(8,128)(2,1)S(1)} %collective-permute-done.1.f2.refs_2_, ...), custom_call_target="tpu_custom_call" | custom-call | flops 1000 | bytes 1000 | tf_op jit(solution)/shard_map/pallas_call | solution.py:42
  39.0 0.3 collective-permute-start.8
  39.3 6.9 %collective-permute-done.6.refs_4_ = bf16[432,768]{1,0:T(8,128)(2,1)S(1)} collective-permute-done((bf16[432,768]{1,0:T(8,128)(2,1)S(1)}, bf16[432,768]{1,0:T(8,128)(2,1)S(1)}, u32[]{:S(2)}, u32[]{:S(2)}) %collective-permute-start.6) | collective-permute-done | bytes 663584 | tf_op jit(solution)/shard_map/ppermute | solution.py:32
  46.2 2.3 %shard_map.50 = (bf16[384,1536]{1,0:T(8,128)(2,1)S(1)}, f32[4,384]{1,0:T(4,128)S(1)}, f32[1,384]{1,0:T(1,128)S(1)}) custom-call(s32[1]{0:T(128)} %bitcast.sub, bf16[384,768]{1,0:T(8,128)(2,1)S(1)} %copy-done.1, bf16[384,768]{1,0:T(8,128)(2,1)S(1)} %collective-permute-done.f1.refs_1_, bf16[384,768]{1,0:T(8,128)(2,1)S(1)} %collective-permute-done.1.f2.refs_2_, ...), custom_call_target="tpu_custom_call" | custom-call | flops 1000 | bytes 1000 | tf_op jit(solution)/shard_map/pallas_call | solution.py:42
  48.6 0.0 copy-start.2
  48.6 2.3 %shard_map.51 = (bf16[384,1536]{1,0:T(8,128)(2,1)S(1)}, f32[4,384]{1,0:T(4,128)S(1)}, f32[1,384]{1,0:T(1,128)S(1)}) custom-call(s32[1]{0:T(128)} %bitcast.sub, bf16[384,768]{1,0:T(8,128)(2,1)S(1)} %copy-done.1, bf16[384,768]{1,0:T(8,128)(2,1)S(1)} %collective-permute-done.f1.refs_1_, bf16[384,768]{1,0:T(8,128)(2,1)S(1)} %collective-permute-done.1.f2.refs_2_, ...), custom_call_target="tpu_custom_call" | custom-call | flops 4000000000 | bytes 1000 | tf_op jit(solution)/shard_map/pallas_call | solution.py:42
  51.0 0.8 collective-permute-start.9
  51.7 6.8 %collective-permute-start.11 = (f32[1,384]{1,0:T(1,128)S(1)}, f32[1,384]{1,0:T(1,128)S(1)}, u32[]{:S(2)}, u32[]{:S(2)}) collective-permute-start(f32[1,384]{1,0:T(1,128)S(1)} %get-tuple-element.62), channel_id=1, source_target_pairs={{0,118},{1,119},{2,116},{3,117},{4,122},{5,123},{6,120},{7,121},{8... | collective-permute-start | bytes 4616 | tf_op jit(solution)/shard_map/ppermute | solution.py:32
  58.6 0.1 collective-permute-start.10
  58.7 0.2 collective-permute-done.12
  58.9 1.0 collective-permute-done.11
  59.9 0.2 collective-permute-start.17
  60.1 1.1 collective-permute-done.17.x1
  61.2 0.8 collective-permute-start.18
  62.0 2.6 %collective-permute-start.16 = (bf16[64,384]{1,0:T(8,128)(2,1)S(1)}, bf16[64,384]{1,0:T(8,128)(2,1)S(1)}, u32[]{:S(2)}, u32[]{:S(2)}) collective-permute-start(bf16[64,384]{1,0:T(8,128)(2,1)S(1)} %multiply_convert_fusion.x0), channel_id=1, source_target_pairs={{0,112},{1,113},{2,114},{3,115},{4,116},{5,117},{6,118},{7,119},{8... | collective-permute-start | bytes 147464 | tf_op jit(solution)/shard_map/ppermute | solution.py:32
  64.6 3.6 %collective-permute-start.15 = (bf16[64,384]{1,0:T(8,128)(2,1)S(1)}, bf16[64,384]{1,0:T(8,128)(2,1)S(1)}, u32[]{:S(2)}, u32[]{:S(2)}) collective-permute-start(bf16[64,384]{1,0:T(8,128)(2,1)S(1)} %multiply_convert_fusion.x0), channel_id=1, source_target_pairs={{0,14},{1,15},{2,12},{3,13},{4,18},{5,19},{6,16},{7,17},{8,22},{9,... | collective-permute-start | bytes 147464 | tf_op jit(solution)/shard_map/ppermute | solution.py:32
  68.3 6.5 %collective-permute-start.14 = (bf16[64,384]{1,0:T(8,128)(2,1)S(1)}, bf16[64,384]{1,0:T(8,128)(2,1)S(1)}, u32[]{:S(2)}, u32[]{:S(2)}) collective-permute-start(bf16[64,384]{1,0:T(8,128)(2,1)S(1)} %multiply_convert_fusion.x0), channel_id=1, source_target_pairs={{0,120},{1,121},{2,122},{3,123},{4,124},{5,125},{6,126},{7,127},{8... | collective-permute-start | bytes 147464 | tf_op jit(solution)/shard_map/ppermute | solution.py:32
  74.8 1.8 %shard_map.52 = (f32[64,384]{1,0:T(8,128)S(1)}, bf16[64,384]{1,0:T(8,128)(2,1)S(1)}, bf16[64,384]{1,0:T(8,128)(2,1)S(1)}, bf16[64,384]{1,0:T(8,128)(2,1)S(1)}, bf16[64,384]{1,0:T(8,128)(2,1)S(1)}) custom-call(bf16[64,384]{1,0:T(8,128)(2,1)S(1)} %multiply_convert_fusion.x0, bf16[64,384]{1,0:T(8,128)(2,1)S(1)} %collective-permute-done.17.x1, ...), custom_call_target="tpu_custom_call" | custom-call | flops 1000 | bytes 1000 | tf_op jit(solution)/shard_map/pallas_call | solution.py:42
  76.6 7.6 %collective-permute-done.13.x1 = bf16[64,384]{1,0:T(8,128)(2,1)S(1)} collective-permute-done((bf16[64,384]{1,0:T(8,128)(2,1)S(1)}, bf16[64,384]{1,0:T(8,128)(2,1)S(1)}, u32[]{:S(2)}, u32[]{:S(2)}) %collective-permute-start.13) | collective-permute-done | bytes 49184 | tf_op jit(solution)/shard_map/ppermute | solution.py:32
  84.3 1.1 shard_map.53
  85.4 0.1 collective-permute-start.19
  85.5 0.1 collective-permute-start.21
  85.6 0.1 collective-permute-start.22
  85.6 1.9 %collective-permute-start.23 = (bf16[64,384]{1,0:T(8,128)(2,1)S(1)}, bf16[64,384]{1,0:T(8,128)(2,1)S(1)}, u32[]{:S(2)}, u32[]{:S(2)}) collective-permute-start(bf16[64,384]{1,0:T(8,128)(2,1)S(1)} %get-tuple-element.79), channel_id=1, source_target_pairs={{0,118},{1,119},{2,116},{3,117},{4,122},{5,123},{6,120},{7,121},{8... | collective-permute-start | bytes 147464 | tf_op jit(solution)/shard_map/ppermute | solution.py:32
  87.6 4.2 %collective-permute-start.24 = (bf16[64,384]{1,0:T(8,128)(2,1)S(1)}, bf16[64,384]{1,0:T(8,128)(2,1)S(1)}, u32[]{:S(2)}, u32[]{:S(2)}) collective-permute-start(bf16[64,384]{1,0:T(8,128)(2,1)S(1)} %get-tuple-element.80), channel_id=1, source_target_pairs={{0,16},{1,17},{2,18},{3,19},{4,20},{5,21},{6,22},{7,23},{8,24},{9,... | collective-permute-start | bytes 147464 | tf_op jit(solution)/shard_map/ppermute | solution.py:32
  91.8 0.1 collective-permute-start.20
  91.9 1.2 collective-permute-done.22.z2
  93.0 2.2 %collective-permute-done.24.z4 = bf16[64,384]{1,0:T(8,128)(2,1)S(1)} collective-permute-done((bf16[64,384]{1,0:T(8,128)(2,1)S(1)}, bf16[64,384]{1,0:T(8,128)(2,1)S(1)}, u32[]{:S(2)}, u32[]{:S(2)}) %collective-permute-start.24) | collective-permute-done | bytes 49184 | tf_op jit(solution)/shard_map/ppermute | solution.py:32
  95.3 0.7 collective-permute-done.20.y2
  95.9 0.4 shard_map.54
  96.3 0.2 collective-permute-start.25
  96.6 1.2 collective-permute-done.25
  97.7 5.4 %collective-permute-start.28 = (f32[32,128]{1,0:T(8,128)S(1)}, f32[32,128]{1,0:T(8,128)S(1)}, u32[]{:S(2)}, u32[]{:S(2)}) collective-permute-start(f32[32,128]{1,0:T(8,128)S(1)} %add.74), channel_id=1, source_target_pairs={{0,6},{1,7},{2,4},{3,5},{4,2},{5,3},{6,0},{7,1},{8,14},{9,15},{10,... | collective-permute-start | bytes 49160 | tf_op jit(solution)/shard_map/ppermute | solution.py:309
  103.2 0.9 collective-permute-start.26
  104.1 0.8 collective-permute-done.28
  104.9 3.5 %collective-permute-done.27 = f32[32,128]{1,0:T(8,128)S(1)} collective-permute-done((f32[32,128]{1,0:T(8,128)S(1)}, f32[32,128]{1,0:T(8,128)S(1)}, u32[]{:S(2)}, u32[]{:S(2)}) %collective-permute-start.27) | collective-permute-done | bytes 16416 | tf_op jit(solution)/shard_map/ppermute | solution.py:309
  108.4 0.1 collective-permute-start.31
  108.5 3.5 %collective-permute-start.30 = (f32[32,128]{1,0:T(8,128)S(1)}, f32[32,128]{1,0:T(8,128)S(1)}, u32[]{:S(2)}, u32[]{:S(2)}) collective-permute-start(f32[32,128]{1,0:T(8,128)S(1)} %add_add_fusion.2), channel_id=1, source_target_pairs={{0,16},{1,17},{2,18},{3,19},{4,20},{5,21},{6,22},{7,23},{8,24},{9,... | collective-permute-start | bytes 49160 | tf_op jit(solution)/shard_map/ppermute | solution.py:309
  112.0 0.6 collective-permute-start.29
  112.6 0.9 collective-permute-done.31
  113.4 0.4 collective-permute-done.30
  113.8 1.9 %collective-permute-done.29 = f32[32,128]{1,0:T(8,128)S(1)} collective-permute-done((f32[32,128]{1,0:T(8,128)S(1)}, f32[32,128]{1,0:T(8,128)S(1)}, u32[]{:S(2)}, u32[]{:S(2)}) %collective-permute-start.29) | collective-permute-done | bytes 16416 | tf_op jit(solution)/shard_map/ppermute | solution.py:309
  115.7 1.4 %collective-permute-start.34 = (f32[32,128]{1,0:T(8,128)S(1)}, f32[32,128]{1,0:T(8,128)S(1)}, u32[]{:S(2)}, u32[]{:S(2)}) collective-permute-start(f32[32,128]{1,0:T(8,128)S(1)} %add_add_fusion.1), channel_id=1, source_target_pairs={{0,96},{1,97},{2,98},{3,99},{4,100},{5,101},{6,102},{7,103},{8,104... | collective-permute-start | bytes 49160 | tf_op jit(solution)/shard_map/ppermute | solution.py:309
  117.1 2.7 %collective-permute-start.32 = (f32[32,128]{1,0:T(8,128)S(1)}, f32[32,128]{1,0:T(8,128)S(1)}, u32[]{:S(2)}, u32[]{:S(2)}) collective-permute-start(f32[32,128]{1,0:T(8,128)S(1)} %add_add_fusion.1), channel_id=1, source_target_pairs={{0,32},{1,33},{2,34},{3,35},{4,36},{5,37},{6,38},{7,39},{8,40},{9,... | collective-permute-start | bytes 49160 | tf_op jit(solution)/shard_map/ppermute | solution.py:309
  119.8 0.9 collective-permute-done.34
  120.7 1.7 %collective-permute-done.33 = f32[32,128]{1,0:T(8,128)S(1)} collective-permute-done((f32[32,128]{1,0:T(8,128)S(1)}, f32[32,128]{1,0:T(8,128)S(1)}, u32[]{:S(2)}, u32[]{:S(2)}) %collective-permute-start.33) | collective-permute-done | bytes 16416 | tf_op jit(solution)/shard_map/ppermute | solution.py:309
  122.4 2.4 %shard_map.55 = f32[64,384]{1,0:T(8,128)} custom-call(f32[32,128]{1,0:T(8,128)S(1)} %add_add_fusion.gram, f32[64,384]{1,0:T(8,128)S(1)} %get-tuple-element.82.mixed), custom_call_target="tpu_custom_call" | custom-call | flops 1000 | bytes 1000 | tf_op jit(solution)/shard_map/pallas_call | solution.py:42
  (35 shorter events, 0.2 us)
Async XLA Ops:
  0.0 20.0 %copy-start = (s32[9,16,1536]{2,1,0:T(8,128)S(1)}, s32[9,16,1536]{2,1,0:T(8,128)}, u32[]{:S(2)}) copy-start(s32[9,16,1536]{2,1,0:T(8,128)} %refs_10_) | copy-start | bytes 2654212
  1.7 1.1 copy-start.1
  2.9 15.1 %collective-permute-start.1 = (bf16[384,768]{1,0:T(8,128)(2,1)S(1)}, bf16[384,768]{1,0:T(8,128)(2,1)S(1)}, u32[]{:S(2)}, u32[]{:S(2)}) collective-permute-start(bf16[384,768]{1,0:T(8,128)(2,1)S(1)} %copy-done.1), channel_id=1, source_target_pairs={{0,2},{1,3},{2,0},{3,1},{4,6},{5,7},{6,4},{7,5},{8,10},{9,11},{10,... | collective-permute-start | bytes 1769480 | tf_op jit(solution)/shard_map/ppermute | solution.py:32
  4.6 22.5 %collective-permute-start.3 = (bf16[432,768]{1,0:T(8,128)(2,1)S(1)}, bf16[432,768]{1,0:T(8,128)(2,1)S(1)}, u32[]{:S(2)}, u32[]{:S(2)}) collective-permute-start(bf16[432,768]{1,0:T(8,128)(2,1)S(1)} %get-tuple-element.47), channel_id=1, source_target_pairs={{0,6},{1,7},{2,4},{3,5},{4,10},{5,11},{6,8},{7,9},{8,14},{9,15},{1... | collective-permute-start | bytes 1990664 | tf_op jit(solution)/shard_map/ppermute | solution.py:32
  6.8 20.3 %collective-permute-start.4 = (bf16[432,768]{1,0:T(8,128)(2,1)S(1)}, bf16[432,768]{1,0:T(8,128)(2,1)S(1)}, u32[]{:S(2)}, u32[]{:S(2)}) collective-permute-start(bf16[432,768]{1,0:T(8,128)(2,1)S(1)} %get-tuple-element.48), channel_id=1, source_target_pairs={{0,120},{1,121},{2,122},{3,123},{4,124},{5,125},{6,126},{7,127},{8... | collective-permute-start | bytes 1990664 | tf_op jit(solution)/shard_map/ppermute | solution.py:32
  13.0 4.9 %collective-permute-start = (bf16[384,768]{1,0:T(8,128)(2,1)S(1)}, bf16[384,768]{1,0:T(8,128)(2,1)S(1)}, u32[]{:S(2)}, u32[]{:S(2)}) collective-permute-start(bf16[384,768]{1,0:T(8,128)(2,1)S(1)} %copy-done.1), channel_id=1, source_target_pairs={{0,1},{1,0},{2,3},{3,2},{4,5},{5,4},{6,7},{7,6},{8,9},{9,8},{10,11... | collective-permute-start | bytes 1769480 | tf_op jit(solution)/shard_map/ppermute | solution.py:32
  18.0 2.0 %collective-permute-start.2 = (bf16[384,768]{1,0:T(8,128)(2,1)S(1)}, bf16[384,768]{1,0:T(8,128)(2,1)S(1)}, u32[]{:S(2)}, u32[]{:S(2)}) collective-permute-start(bf16[384,768]{1,0:T(8,128)(2,1)S(1)} %collective-permute-done.1.f2.refs_2_), channel_id=1, source_target_pairs={{0,1},{1,0},{2,3},{3,2},{4,5},{5,4},{6,7},{7,6},{8,9},{9,8},{10,11... | collective-permute-start | bytes 1769480 | tf_op jit(solution)/shard_map/ppermute | solution.py:32
  27.1 19.1 %collective-permute-start.6 = (bf16[432,768]{1,0:T(8,128)(2,1)S(1)}, bf16[432,768]{1,0:T(8,128)(2,1)S(1)}, u32[]{:S(2)}, u32[]{:S(2)}) collective-permute-start(bf16[432,768]{1,0:T(8,128)(2,1)S(1)} %collective-permute-done.3.refs_4_), channel_id=1, source_target_pairs={{0,8},{1,9},{2,10},{3,11},{4,12},{5,13},{6,14},{7,15},{8,16},{9,17... | collective-permute-start | bytes 1990664 | tf_op jit(solution)/shard_map/ppermute | solution.py:32
  27.1 21.5 %collective-permute-start.5 = (bf16[432,768]{1,0:T(8,128)(2,1)S(1)}, bf16[432,768]{1,0:T(8,128)(2,1)S(1)}, u32[]{:S(2)}, u32[]{:S(2)}) collective-permute-start(bf16[432,768]{1,0:T(8,128)(2,1)S(1)} %collective-permute-done.4.refs_4_), channel_id=1, source_target_pairs={{0,120},{1,121},{2,122},{3,123},{4,124},{5,125},{6,126},{7,127},{8... | collective-permute-start | bytes 1990664 | tf_op jit(solution)/shard_map/ppermute | solution.py:32
  34.9 13.7 %collective-permute-start.7 = (f32[1,384]{1,0:T(1,128)S(1)}, f32[1,384]{1,0:T(1,128)S(1)}, u32[]{:S(2)}, u32[]{:S(2)}) collective-permute-start(f32[1,384]{1,0:T(1,128)S(1)} %get-tuple-element.58), channel_id=1, source_target_pairs={{0,126},{1,127},{2,124},{3,125},{4,2},{5,3},{6,0},{7,1},{8,6},{9,7... | collective-permute-start | bytes 4616 | tf_op jit(solution)/shard_map/ppermute | solution.py:32
  39.0 9.6 %collective-permute-start.8 = (f32[1,384]{1,0:T(1,128)S(1)}, f32[1,384]{1,0:T(1,128)S(1)}, u32[]{:S(2)}, u32[]{:S(2)}) collective-permute-start(f32[1,384]{1,0:T(1,128)S(1)} %get-tuple-element.59), channel_id=1, source_target_pairs={{0,8},{1,9},{2,10},{3,11},{4,12},{5,13},{6,14},{7,15},{8,16},{9,17... | collective-permute-start | bytes 4616 | tf_op jit(solution)/shard_map/ppermute | solution.py:32
  48.6 11.3 %copy-start.2 = (f32[64,384]{1,0:T(8,128)S(1)}, f32[64,384]{1,0:T(8,128)}, u32[]{:S(2)}) copy-start(f32[64,384]{1,0:T(8,128)} %own.1) | copy-start | bytes 294916
  51.0 7.6 %collective-permute-start.9 = (f32[2,384]{1,0:T(2,128)S(1)}, f32[2,384]{1,0:T(2,128)S(1)}, u32[]{:S(2)}, u32[]{:S(2)}) collective-permute-start(f32[2,384]{1,0:T(2,128)S(1)} %slice.16), channel_id=1, source_target_pairs={{0,2},{1,3},{2,0},{3,1},{4,6},{5,7},{6,4},{7,5},{8,10},{9,11},{10,... | collective-permute-start | bytes 9224 | tf_op jit(solution)/shard_map/ppermute | solution.py:32
  51.7 7.2 %collective-permute-start.12 = (f32[1,384]{1,0:T(1,128)S(1)}, f32[1,384]{1,0:T(1,128)S(1)}, u32[]{:S(2)}, u32[]{:S(2)}) collective-permute-start(f32[1,384]{1,0:T(1,128)S(1)} %get-tuple-element.63), channel_id=1, source_target_pairs={{0,16},{1,17},{2,18},{3,19},{4,20},{5,21},{6,22},{7,23},{8,24},{9,... | collective-permute-start | bytes 4616 | tf_op jit(solution)/shard_map/ppermute | solution.py:32
  51.7 8.1 %collective-permute-start.11 = (f32[1,384]{1,0:T(1,128)S(1)}, f32[1,384]{1,0:T(1,128)S(1)}, u32[]{:S(2)}, u32[]{:S(2)}) collective-permute-start(f32[1,384]{1,0:T(1,128)S(1)} %get-tuple-element.62), channel_id=1, source_target_pairs={{0,118},{1,119},{2,116},{3,117},{4,122},{5,123},{6,120},{7,121},{8... | collective-permute-start | bytes 4616 | tf_op jit(solution)/shard_map/ppermute | solution.py:32
  58.6 1.3 %collective-permute-start.10 = (f32[1,384]{1,0:T(1,128)S(1)}, f32[1,384]{1,0:T(1,128)S(1)}, u32[]{:S(2)}, u32[]{:S(2)}) collective-permute-start(f32[1,384]{1,0:T(1,128)S(1)} %slice.21), channel_id=1, source_target_pairs={{0,1},{1,0},{2,3},{3,2},{4,5},{5,4},{6,7},{7,6},{8,9},{9,8},{10,11... | collective-permute-start | bytes 4616 | tf_op jit(solution)/shard_map/ppermute | solution.py:32
  59.9 1.3 %collective-permute-start.17 = (bf16[64,384]{1,0:T(8,128)(2,1)S(1)}, bf16[64,384]{1,0:T(8,128)(2,1)S(1)}, u32[]{:S(2)}, u32[]{:S(2)}) collective-permute-start(bf16[64,384]{1,0:T(8,128)(2,1)S(1)} %multiply_convert_fusion.x0), channel_id=1, source_target_pairs={{0,1},{1,0},{2,3},{3,2},{4,5},{5,4},{6,7},{7,6},{8,9},{9,8},{10,11... | collective-permute-start | bytes 147464 | tf_op jit(solution)/shard_map/ppermute | solution.py:32
  61.2 13.5 %collective-permute-start.18 = (bf16[128,384]{1,0:T(8,128)(2,1)S(1)}, bf16[128,384]{1,0:T(8,128)(2,1)S(1)}, u32[]{:S(2)}, u32[]{:S(2)}) collective-permute-start(bf16[128,384]{1,0:T(8,128)(2,1)S(1)} %pad_maximum_fusion), channel_id=1, source_target_pairs={{0,2},{1,3},{2,0},{3,1},{4,6},{5,7},{6,4},{7,5},{8,10},{9,11},{10,... | collective-permute-start | bytes 294920 | tf_op jit(solution)/shard_map/ppermute | solution.py:32
  62.0 14.6 %collective-permute-start.16 = (bf16[64,384]{1,0:T(8,128)(2,1)S(1)}, bf16[64,384]{1,0:T(8,128)(2,1)S(1)}, u32[]{:S(2)}, u32[]{:S(2)}) collective-permute-start(bf16[64,384]{1,0:T(8,128)(2,1)S(1)} %multiply_convert_fusion.x0), channel_id=1, source_target_pairs={{0,112},{1,113},{2,114},{3,115},{4,116},{5,117},{6,118},{7,119},{8... | collective-permute-start | bytes 147464 | tf_op jit(solution)/shard_map/ppermute | solution.py:32
  64.6 12.0 %collective-permute-start.15 = (bf16[64,384]{1,0:T(8,128)(2,1)S(1)}, bf16[64,384]{1,0:T(8,128)(2,1)S(1)}, u32[]{:S(2)}, u32[]{:S(2)}) collective-permute-start(bf16[64,384]{1,0:T(8,128)(2,1)S(1)} %multiply_convert_fusion.x0), channel_id=1, source_target_pairs={{0,14},{1,15},{2,12},{3,13},{4,18},{5,19},{6,16},{7,17},{8,22},{9,... | collective-permute-start | bytes 147464 | tf_op jit(solution)/shard_map/ppermute | solution.py:32
  68.3 8.3 %collective-permute-start.14 = (bf16[64,384]{1,0:T(8,128)(2,1)S(1)}, bf16[64,384]{1,0:T(8,128)(2,1)S(1)}, u32[]{:S(2)}, u32[]{:S(2)}) collective-permute-start(bf16[64,384]{1,0:T(8,128)(2,1)S(1)} %multiply_convert_fusion.x0), channel_id=1, source_target_pairs={{0,120},{1,121},{2,122},{3,123},{4,124},{5,125},{6,126},{7,127},{8... | collective-permute-start | bytes 147464 | tf_op jit(solution)/shard_map/ppermute | solution.py:32
  74.8 9.5 %collective-permute-start.13 = (bf16[64,384]{1,0:T(8,128)(2,1)S(1)}, bf16[64,384]{1,0:T(8,128)(2,1)S(1)}, u32[]{:S(2)}, u32[]{:S(2)}) collective-permute-start(bf16[64,384]{1,0:T(8,128)(2,1)S(1)} %multiply_convert_fusion.x0), channel_id=1, source_target_pairs={{0,6},{1,7},{2,4},{3,5},{4,10},{5,11},{6,8},{7,9},{8,14},{9,15},{1... | collective-permute-start | bytes 147464 | tf_op jit(solution)/shard_map/ppermute | solution.py:32
  85.4 6.4 %collective-permute-start.19 = (f32[128,384]{1,0:T(8,128)S(1)}, f32[128,384]{1,0:T(8,128)S(1)}, u32[]{:S(2)}, u32[]{:S(2)}) collective-permute-start(f32[128,384]{1,0:T(8,128)S(1)} %get-tuple-element.75), channel_id=1, source_target_pairs={{0,1},{1,0},{2,3},{3,2},{4,5},{5,4},{6,7},{7,6},{8,9},{9,8},{10,11... | collective-permute-start | bytes 589832 | tf_op jit(solution)/shard_map/ppermute | solution.py:32
  85.5 6.4 %collective-permute-start.21 = (bf16[64,384]{1,0:T(8,128)(2,1)S(1)}, bf16[64,384]{1,0:T(8,128)(2,1)S(1)}, u32[]{:S(2)}, u32[]{:S(2)}) collective-permute-start(bf16[64,384]{1,0:T(8,128)(2,1)S(1)} %get-tuple-element.77), channel_id=1, source_target_pairs={{0,126},{1,127},{2,124},{3,125},{4,2},{5,3},{6,0},{7,1},{8,6},{9,7... | collective-permute-start | bytes 147464 | tf_op jit(solution)/shard_map/ppermute | solution.py:32
  85.6 7.5 %collective-permute-start.22 = (bf16[64,384]{1,0:T(8,128)(2,1)S(1)}, bf16[64,384]{1,0:T(8,128)(2,1)S(1)}, u32[]{:S(2)}, u32[]{:S(2)}) collective-permute-start(bf16[64,384]{1,0:T(8,128)(2,1)S(1)} %get-tuple-element.78), channel_id=1, source_target_pairs={{0,8},{1,9},{2,10},{3,11},{4,12},{5,13},{6,14},{7,15},{8,16},{9,17... | collective-permute-start | bytes 147464 | tf_op jit(solution)/shard_map/ppermute | solution.py:32
  85.6 7.4 %collective-permute-start.23 = (bf16[64,384]{1,0:T(8,128)(2,1)S(1)}, bf16[64,384]{1,0:T(8,128)(2,1)S(1)}, u32[]{:S(2)}, u32[]{:S(2)}) collective-permute-start(bf16[64,384]{1,0:T(8,128)(2,1)S(1)} %get-tuple-element.79), channel_id=1, source_target_pairs={{0,118},{1,119},{2,116},{3,117},{4,122},{5,123},{6,120},{7,121},{8... | collective-permute-start | bytes 147464 | tf_op jit(solution)/shard_map/ppermute | solution.py:32
  87.6 7.7 %collective-permute-start.24 = (bf16[64,384]{1,0:T(8,128)(2,1)S(1)}, bf16[64,384]{1,0:T(8,128)(2,1)S(1)}, u32[]{:S(2)}, u32[]{:S(2)}) collective-permute-start(bf16[64,384]{1,0:T(8,128)(2,1)S(1)} %get-tuple-element.80), channel_id=1, source_target_pairs={{0,16},{1,17},{2,18},{3,19},{4,20},{5,21},{6,22},{7,23},{8,24},{9,... | collective-permute-start | bytes 147464 | tf_op jit(solution)/shard_map/ppermute | solution.py:32
  91.8 4.2 %collective-permute-start.20 = (bf16[64,384]{1,0:T(8,128)(2,1)S(1)}, bf16[64,384]{1,0:T(8,128)(2,1)S(1)}, u32[]{:S(2)}, u32[]{:S(2)}) collective-permute-start(bf16[64,384]{1,0:T(8,128)(2,1)S(1)} %fusion), channel_id=1, source_target_pairs={{0,2},{1,3},{2,0},{3,1},{4,6},{5,7},{6,4},{7,5},{8,10},{9,11},{10,... | collective-permute-start | bytes 147464 | tf_op jit(solution)/shard_map/ppermute | solution.py:32
  96.3 1.4 %collective-permute-start.25 = (f32[32,128]{1,0:T(8,128)S(1)}, f32[32,128]{1,0:T(8,128)S(1)}, u32[]{:S(2)}, u32[]{:S(2)}) collective-permute-start(f32[32,128]{1,0:T(8,128)S(1)} %get-tuple-element.81), channel_id=1, source_target_pairs={{0,1},{1,0},{2,3},{3,2},{4,5},{5,4},{6,7},{7,6},{8,9},{9,8},{10,11... | collective-permute-start | bytes 49160 | tf_op jit(solution)/shard_map/ppermute | solution.py:309
  97.7 7.1 %collective-permute-start.28 = (f32[32,128]{1,0:T(8,128)S(1)}, f32[32,128]{1,0:T(8,128)S(1)}, u32[]{:S(2)}, u32[]{:S(2)}) collective-permute-start(f32[32,128]{1,0:T(8,128)S(1)} %add.74), channel_id=1, source_target_pairs={{0,6},{1,7},{2,4},{3,5},{4,2},{5,3},{6,0},{7,1},{8,14},{9,15},{10,... | collective-permute-start | bytes 49160 | tf_op jit(solution)/shard_map/ppermute | solution.py:309
  103.2 5.2 %collective-permute-start.27 = (f32[32,128]{1,0:T(8,128)S(1)}, f32[32,128]{1,0:T(8,128)S(1)}, u32[]{:S(2)}, u32[]{:S(2)}) collective-permute-start(f32[32,128]{1,0:T(8,128)S(1)} %add.74), channel_id=1, source_target_pairs={{0,4},{1,5},{2,6},{3,7},{4,0},{5,1},{6,2},{7,3},{8,12},{9,13},{10,... | collective-permute-start | bytes 49160 | tf_op jit(solution)/shard_map/ppermute | solution.py:309
  103.2 5.2 %collective-permute-start.26 = (f32[32,128]{1,0:T(8,128)S(1)}, f32[32,128]{1,0:T(8,128)S(1)}, u32[]{:S(2)}, u32[]{:S(2)}) collective-permute-start(f32[32,128]{1,0:T(8,128)S(1)} %add.74), channel_id=1, source_target_pairs={{0,2},{1,3},{2,0},{3,1},{4,6},{5,7},{6,4},{7,5},{8,10},{9,11},{10,... | collective-permute-start | bytes 49160 | tf_op jit(solution)/shard_map/ppermute | solution.py:309
  108.4 5.0 %collective-permute-start.31 = (f32[32,128]{1,0:T(8,128)S(1)}, f32[32,128]{1,0:T(8,128)S(1)}, u32[]{:S(2)}, u32[]{:S(2)}) collective-permute-start(f32[32,128]{1,0:T(8,128)S(1)} %add_add_fusion.2), channel_id=1, source_target_pairs={{0,24},{1,25},{2,26},{3,27},{4,28},{5,29},{6,30},{7,31},{8,16},{9,... | collective-permute-start | bytes 49160 | tf_op jit(solution)/shard_map/ppermute | solution.py:309
  108.5 5.3 %collective-permute-start.30 = (f32[32,128]{1,0:T(8,128)S(1)}, f32[32,128]{1,0:T(8,128)S(1)}, u32[]{:S(2)}, u32[]{:S(2)}) collective-permute-start(f32[32,128]{1,0:T(8,128)S(1)} %add_add_fusion.2), channel_id=1, source_target_pairs={{0,16},{1,17},{2,18},{3,19},{4,20},{5,21},{6,22},{7,23},{8,24},{9,... | collective-permute-start | bytes 49160 | tf_op jit(solution)/shard_map/ppermute | solution.py:309
  112.0 3.7 %collective-permute-start.29 = (f32[32,128]{1,0:T(8,128)S(1)}, f32[32,128]{1,0:T(8,128)S(1)}, u32[]{:S(2)}, u32[]{:S(2)}) collective-permute-start(f32[32,128]{1,0:T(8,128)S(1)} %add_add_fusion.2), channel_id=1, source_target_pairs={{0,8},{1,9},{2,10},{3,11},{4,12},{5,13},{6,14},{7,15},{8,0},{9,1},... | collective-permute-start | bytes 49160 | tf_op jit(solution)/shard_map/ppermute | solution.py:309
  115.7 4.9 %collective-permute-start.34 = (f32[32,128]{1,0:T(8,128)S(1)}, f32[32,128]{1,0:T(8,128)S(1)}, u32[]{:S(2)}, u32[]{:S(2)}) collective-permute-start(f32[32,128]{1,0:T(8,128)S(1)} %add_add_fusion.1), channel_id=1, source_target_pairs={{0,96},{1,97},{2,98},{3,99},{4,100},{5,101},{6,102},{7,103},{8,104... | collective-permute-start | bytes 49160 | tf_op jit(solution)/shard_map/ppermute | solution.py:309
  117.1 5.2 %collective-permute-start.33 = (f32[32,128]{1,0:T(8,128)S(1)}, f32[32,128]{1,0:T(8,128)S(1)}, u32[]{:S(2)}, u32[]{:S(2)}) collective-permute-start(f32[32,128]{1,0:T(8,128)S(1)} %add_add_fusion.1), channel_id=1, source_target_pairs={{0,64},{1,65},{2,66},{3,67},{4,68},{5,69},{6,70},{7,71},{8,72},{9,... | collective-permute-start | bytes 49160 | tf_op jit(solution)/shard_map/ppermute | solution.py:309
  117.1 5.2 %collective-permute-start.32 = (f32[32,128]{1,0:T(8,128)S(1)}, f32[32,128]{1,0:T(8,128)S(1)}, u32[]{:S(2)}, u32[]{:S(2)}) collective-permute-start(f32[32,128]{1,0:T(8,128)S(1)} %add_add_fusion.1), channel_id=1, source_target_pairs={{0,32},{1,33},{2,34},{3,35},{4,36},{5,37},{6,38},{7,39},{8,40},{9,... | collective-permute-start | bytes 49160 | tf_op jit(solution)/shard_map/ppermute | solution.py:309

commit v4 on v3

--- a/solution.py
+++ b/solution.py
@@ -14,6 +14,7 @@
 EIG = 64
 NNB = 16
 BAND = ((1, 2), (-2, 0), (3, 2), (-4, 0))
+ROUTES = ((BAND[2], BAND[3]), (BAND[0], BAND[1]))
 ONWARD = ((2, 0), (-2, 0))
 EXTRA = 3 * NNB
 ROUNDS = (((0, 1),), ((0, 2), (1, 0), (1, 2)), ((2, 0), (4, 0), (6, 0)), ((8, 0), (16, 0), (24, 0)))
@@ -30,6 +31,19 @@
         for s in range(n_sub)
     ]
     return lax.ppermute(value, ("blk", "sub"), pairs)
+
+
+def routed(value, back=False):
+    n_blk, n_sub = lax.axis_size("blk"), lax.axis_size("sub")
+    outs = []
+    for part, routes in zip(value, ROUTES):
+        pairs = []
+        for b in range(n_blk):
+            for s in range(n_sub):
+                d, flip = routes[s % 2]
+                pairs.append((b * n_sub + s, ((b - d if back else b + d) % n_blk) * n_sub + (s ^ flip)))
+        outs.append(lax.ppermute(part, ("blk", "sub"), pairs))
+    return outs
 
 
 VMEM = pl.BlockSpec(memory_space=pltpu.VMEM)
@@ -167,27 +181,41 @@
     col[...] = jnp.sum(cols[...].T, axis=0, keepdims=True)
 
 
-def col_kernel(x0, x1, far, t0, t1, t2, t3, t4, z0, z1, z2, z3, z4):
+def col_kernel(sub, x0, x1, far, t0, t1, t2, t3, t4, z0, keep, give):
     block = jnp.concatenate([x0[...], x1[...], far[:EIG, :], far[EIG:, :]], axis=1)
-    for tile, out in ((t1, z1), (t2, z2), (t3, z3), (t4, z4), (t0, z0)):
-        out[...] = lax.dot_general(block, tile[...], NT, preferred_element_type=jnp.float32).astype(out.dtype)
-
-
-def row_kernel(x0, x1, x2, x3, x4, t0, t1, t2, t3, t4, y0, y2, sent):
-    for slot, out, at_out in ((1, sent, 0), (3, sent, EIG), (0, y0, 0), (2, y2, 0)):
-        at = slot * ROWS
-        total = jnp.zeros((EIG, ROWS), jnp.float32)
-        for vectors, tile in ((x0, t0), (x1, t1), (x2, t2), (x3, t3), (x4, t4)):
+    z1, z2, z3, z4 = [
+        lax.dot_general(block, tile[...], NT, preferred_element_type=jnp.float32)
+        for tile in (t1, t2, t3, t4)
+    ]
+    odd = sub[0] % 2 == 1
+    for at, (even_one, odd_one) in ((0, (z3, z4)), (EIG, (z1, z2))):
+        keep[at : at + EIG, :] = jnp.where(odd, odd_one, even_one).astype(jnp.bfloat16)
+        give[at : at + EIG, :] = jnp.where(odd, even_one, odd_one).astype(jnp.bfloat16)
+    z0[...] = lax.dot_general(block, t0[...], NT, preferred_element_type=jnp.float32)
+
+
+def row_kernel(sub, x0, one, two, got, t0, t1, t2, t3, t4, kept, sent):
+    odd = sub[0] % 2 == 1
+    one_x, two_x = one[:EIG, :].astype(jnp.float32), two[:EIG, :].astype(jnp.float32)
+    got_one, got_two = got[:EIG, :].astype(jnp.float32), got[EIG:, :].astype(jnp.float32)
+    x1 = jnp.where(odd, got_two, two_x).astype(jnp.bfloat16)
+    x2 = jnp.where(odd, two_x, got_two).astype(jnp.bfloat16)
+    x3 = jnp.where(odd, got_one, one_x).astype(jnp.bfloat16)
+    x4 = jnp.where(odd, one_x, got_one).astype(jnp.bfloat16)
+    for half, out in ((1, sent), (0, kept)):
+        at = half * 2 * ROWS
+        total = jnp.zeros((EIG, 2 * ROWS), jnp.float32)
+        for vectors, tile in ((x0[...], t0), (x1, t1), (x2, t2), (x3, t3), (x4, t4)):
             total = total + jnp.dot(
-                vectors[...], tile[:, at : at + ROWS], preferred_element_type=jnp.float32
+                vectors, tile[:, at : at + 2 * ROWS], preferred_element_type=jnp.float32
             )
-        out[at_out : at_out + EIG, :] = total
-
-
-def mix_kernel(own, root, y0, y1, y2, z0, z1, z2, z3, z4, mixed, gram):
-    sides = y0[...] + y1[:EIG, :] + y2[...].astype(jnp.float32) + z0[...]
-    for part in (z1, z2, z3, z4):
-        sides = sides + part[...].astype(jnp.float32)
+        out[...] = total.astype(out.dtype)
+
+
+def mix_kernel(own, root, kept, got, one, two, z0, swapped, mixed, gram):
+    sides = kept[:, :ROWS] + got[:, :ROWS].astype(jnp.float32) + z0[...] + swapped[...]
+    for part in (one, two):
+        sides = sides + part[:EIG, :].astype(jnp.float32)
     inv = root[0:1, :]
     value = inv * (own[...] * inv + 0.5 * sides)
     mixed[...] = value
@@ -282,20 +310,34 @@
     own = pair[0:1] + moved(pair[1:2], 0, 1)
     root = lax.rsqrt(1.0 + 0.5 * (own + col0 + col1 + col2 + col3 + col4))
     scaled_low = (eigen_block * root).astype(jnp.bfloat16)
-    vectors = [moved(scaled_low, d, u) for d, u in BAND]
-    x1 = moved(scaled_low, 0, 1)
-    far = moved(jnp.concatenate([scaled_low, x1], axis=0), 0, 2)
-
-    z_outs = (f32(EIG, ROWS),) + (bf16(EIG, ROWS),) * 4
-    z0, z1, z2, z3, z4 = call(col_kernel, z_outs)(scaled_low, x1, far, *tiles)
-    back = [moved(part, -d, u) for (d, u), part in zip(BAND, (z1, z2, z3, z4))]
-    vectors, _ = lax.optimization_barrier((vectors, z0))
-    y_outs = (f32(EIG, ROWS), f32(EIG, ROWS), f32(2 * EIG, ROWS))
-    y0, y2, sent = call(row_kernel, y_outs)(scaled_low, *vectors, *tiles)
-    other = moved(sent, 0, 1)
-    across = moved((y2 + other[EIG:]).astype(jnp.bfloat16), 0, 2)
+    pair = jnp.concatenate([scaled_low, moved(scaled_low, 0, 1)], axis=0)
+    one, two = routed((pair, pair))
+    far = moved(pair, 0, 2)
+    swapped = moved(jnp.concatenate([one[EIG:], two[EIG:]], axis=0), 0, 1)
+
+    with_sub = (SMEM,) + (VMEM,) * 8
+    z_outs = (f32(EIG, ROWS), bf16(2 * EIG, ROWS), bf16(2 * EIG, ROWS))
+    z0, keep, give = call(col_kernel, z_outs, specs=with_sub)(
+        sub_arg, scaled_low, pair[EIG:], far, *tiles
+    )
+    taken = moved(give, 0, 1)
+    one_back, two_back = routed(
+        (
+            jnp.concatenate([keep[:EIG], taken[:EIG]], axis=0),
+            jnp.concatenate([keep[EIG:], taken[EIG:]], axis=0),
+        ),
+        back=True,
+    )
+    swapped, _ = lax.optimization_barrier((swapped, z0))
+    y_outs = (f32(EIG, 2 * ROWS), bf16(EIG, 2 * ROWS))
+    kept, sent = call(row_kernel, y_outs, specs=with_sub + (VMEM,))(
+        sub_arg, scaled_low, one, two, swapped, *tiles
+    )
+    got = moved(sent, 0, 2)
+    owed = kept[:, ROWS:] + got[:, ROWS:].astype(jnp.float32)
+    owed = owed + one_back[EIG:].astype(jnp.float32) + two_back[EIG:].astype(jnp.float32)
     mixed, gram = call(mix_kernel, (f32(EIG, ROWS), f32(EIG // 2, 2 * EIG)))(
-        eigen_block, root, y0, other, across, z0, *back
+        eigen_block, root, kept, got, one_back, two_back, z0, moved(owed, 0, 1)
     )
     n_blk, n_sub = lax.axis_size("blk"), lax.axis_size("sub")
     for partners in ROUNDS:

time: 125 us -> 118 us (0.944)
  starting transfers between devices: 60.3 us -> 51.1 us
  waiting for transfers between devices: 42.9 us -> 44.8 us
    ppermute x25 -> x19, starting transfers between devices: 45.4 us -> 26.3 us  [moved(): return lax.ppermute(value, ('blk', 'sub'), pairs)]
    ppermute x0 -> x4, waiting for transfers between devices: none -> 12.8 us  [routed(): outs.append(lax.ppermute(part, ('blk', 'sub'), pairs))]
    ppermute x25 -> x19, waiting for transfers between devices: 31.8 us -> 21.4 us  [moved(): return lax.ppermute(value, ('blk', 'sub'), pairs)]
    ppermute x0 -> x4, starting transfers between devices: none -> 9.05 us  [routed(): outs.append(lax.ppermute(part, ('blk', 'sub'), pairs))]
  transfers between devices with their start and end apart: 35 -> 33, of which waited for: 19 -> 18; matrix products, arithmetic and copies ran while one was open for 0% -> 0% of each run, Pallas kernels for 10% -> 11%
where the time goes in v4:
time: 118 us; the launch traced here: 117 us
  starting transfers between devices  51.1 us (43%)
  waiting for transfers between devices  44.8 us (38%)
  Pallas kernels  18.4 us (16%)
  local copies, waits for them, and re-layouts  2.84 us (2%)
    ppermute x19, starting transfers between devices, moved(): return lax.ppermute(value, ('blk', 'sub'), pairs)  26.3 us
    ppermute x19, waiting for transfers between devices, moved(): return lax.ppermute(value, ('blk', 'sub'), pairs)  21.4 us
    pallas_call x10, Pallas kernels, run(): pl.pallas_call(body, grid=(1,), out_shape=outs, in_specs=list(specs) if s...  18.4 us
    ppermute x10, starting transfers between devices, local(): parts.append(lax.ppermute(gram, ('blk', 'sub'), pairs))  15.7 us
    ppermute x4, waiting for transfers between devices, routed(): outs.append(lax.ppermute(part, ('blk', 'sub'), pairs))  12.8 us
    ppermute x10, waiting for transfers between devices, local(): parts.append(lax.ppermute(gram, ('blk', 'sub'), pairs))  10.6 us
    ppermute x4, starting transfers between devices, routed(): outs.append(lax.ppermute(part, ('blk', 'sub'), pairs))  9.05 us
  transfers between devices with their start and end apart: 33, of which 18 were waited for; matrix products, arithmetic and copies ran while one was open for 0% of the time, Pallas kernels for 11%

profile of v4, /device:TPU:0, one launch (start us, length us, event | category | flops | bytes accessed | tf_op | source)
XLA Modules:
  0.0 117.4 jit_solution(3917012235322250053)
XLA Ops:
  0.0 0.8 reshape.4.scales.refs_6_
  0.8 0.9 constant_dynamic-slice_fusion.lists
  1.7 0.0 copy-start.1
  1.7 1.1 copy-done.1
  2.8 0.1 shard_map.46
  2.9 1.7 %collective-permute-start.1 = (bf16[384,768]{1,0:T(8,128)(2,1)S(1)}, bf16[384,768]{1,0:T(8,128)(2,1)S(1)}, u32[]{:S(2)}, u32[]{:S(2)}) collective-permute-start(bf16[384,768]{1,0:T(8,128)(2,1)S(1)} %copy-done.1), channel_id=1, source_target_pairs={{0,2},{1,3},{2,0},{3,1},{4,6},{5,7},{6,4},{7,5},{8,10},{9,11},{10,... | collective-permute-start | bytes 1769480 | tf_op jit(solution)/shard_map/ppermute | solution.py:33
  4.6 2.2 %collective-permute-start.3 = (bf16[432,768]{1,0:T(8,128)(2,1)S(1)}, bf16[432,768]{1,0:T(8,128)(2,1)S(1)}, u32[]{:S(2)}, u32[]{:S(2)}) collective-permute-start(bf16[432,768]{1,0:T(8,128)(2,1)S(1)} %get-tuple-element.41), channel_id=1, source_target_pairs={{0,6},{1,7},{2,4},{3,5},{4,10},{5,11},{6,8},{7,9},{8,14},{9,15},{1... | collective-permute-start | bytes 1990664 | tf_op jit(solution)/shard_map/ppermute | solution.py:33
  6.8 6.2 %collective-permute-start.4 = (bf16[432,768]{1,0:T(8,128)(2,1)S(1)}, bf16[432,768]{1,0:T(8,128)(2,1)S(1)}, u32[]{:S(2)}, u32[]{:S(2)}) collective-permute-start(bf16[432,768]{1,0:T(8,128)(2,1)S(1)} %get-tuple-element.42), channel_id=1, source_target_pairs={{0,120},{1,121},{2,122},{3,123},{4,124},{5,125},{6,126},{7,127},{8... | collective-permute-start | bytes 1990664 | tf_op jit(solution)/shard_map/ppermute | solution.py:33
  13.0 4.9 %collective-permute-done.1.f2.refs_2_ = bf16[384,768]{1,0:T(8,128)(2,1)S(1)} collective-permute-done((bf16[384,768]{1,0:T(8,128)(2,1)S(1)}, bf16[384,768]{1,0:T(8,128)(2,1)S(1)}, u32[]{:S(2)}, u32[]{:S(2)}) %collective-permute-start.1) | collective-permute-done | bytes 589856 | tf_op jit(solution)/shard_map/ppermute | solution.py:33
  18.0 0.0 collective-permute-start.2
  18.0 0.0 collective-permute-done.f1.refs_1_
  18.0 2.0 %collective-permute-done.2.f3.refs_3_ = bf16[384,768]{1,0:T(8,128)(2,1)S(1)} collective-permute-done((bf16[384,768]{1,0:T(8,128)(2,1)S(1)}, bf16[384,768]{1,0:T(8,128)(2,1)S(1)}, u32[]{:S(2)}, u32[]{:S(2)}) %collective-permute-start.2) | collective-permute-done | bytes 589856 | tf_op jit(solution)/shard_map/ppermute | solution.py:33
  20.0 3.2 %shard_map.47 = (bf16[384,1536]{1,0:T(8,128)(2,1)S(1)}, f32[4,384]{1,0:T(4,128)S(1)}, f32[1,384]{1,0:T(1,128)S(1)}, f32[4,384]{1,0:T(4,128)S(1)}) custom-call(s32[1]{0:T(128)} %bitcast.sub, bf16[384,768]{1,0:T(8,128)(2,1)S(1)} %copy-done.1, bf16[384,768]{1,0:T(8,128)(2,1)S(1)} %collective-permute-done.f1.refs_1_, ...), custom_call_target="tpu_custom_call" | custom-call | flops 1000 | bytes 1000 | tf_op jit(solution)/shard_map/pallas_call | solution.py:56
  23.2 3.9 %collective-permute-done.3.refs_4_ = bf16[432,768]{1,0:T(8,128)(2,1)S(1)} collective-permute-done((bf16[432,768]{1,0:T(8,128)(2,1)S(1)}, bf16[432,768]{1,0:T(8,128)(2,1)S(1)}, u32[]{:S(2)}, u32[]{:S(2)}) %collective-permute-start.3) | collective-permute-done | bytes 663584 | tf_op jit(solution)/shard_map/ppermute | solution.py:33
  27.1 0.0 collective-permute-done.4.refs_4_
  27.1 0.0 collective-permute-start.6
  27.1 5.3 %collective-permute-start.5 = (bf16[432,768]{1,0:T(8,128)(2,1)S(1)}, bf16[432,768]{1,0:T(8,128)(2,1)S(1)}, u32[]{:S(2)}, u32[]{:S(2)}) collective-permute-start(bf16[432,768]{1,0:T(8,128)(2,1)S(1)} %collective-permute-done.4.refs_4_), channel_id=1, source_target_pairs={{0,120},{1,121},{2,122},{3,123},{4,124},{5,125},{6,126},{7,127},{8... | collective-permute-start | bytes 1990664 | tf_op jit(solution)/shard_map/ppermute | solution.py:33
  32.5 2.4 %shard_map.48 = (bf16[384,1536]{1,0:T(8,128)(2,1)S(1)}, f32[4,384]{1,0:T(4,128)S(1)}, f32[1,384]{1,0:T(1,128)S(1)}) custom-call(s32[1]{0:T(128)} %bitcast.sub, bf16[384,768]{1,0:T(8,128)(2,1)S(1)} %copy-done.1, bf16[384,768]{1,0:T(8,128)(2,1)S(1)} %collective-permute-done.f1.refs_1_, bf16[384,768]{1,0:T(8,128)(2,1)S(1)} %collective-permute-done.1.f2.refs_2_, ...), custom_call_target="tpu_custom_call" | custom-call | flops 1000 | bytes 1000 | tf_op jit(solution)/shard_map/pallas_call | solution.py:56
  34.9 1.8 %collective-permute-start.7 = (f32[1,384]{1,0:T(1,128)S(1)}, f32[1,384]{1,0:T(1,128)S(1)}, u32[]{:S(2)}, u32[]{:S(2)}) collective-permute-start(f32[1,384]{1,0:T(1,128)S(1)} %get-tuple-element.52), channel_id=1, source_target_pairs={{0,126},{1,127},{2,124},{3,125},{4,2},{5,3},{6,0},{7,1},{8,6},{9,7... | collective-permute-start | bytes 4616 | tf_op jit(solution)/shard_map/ppermute | solution.py:33
  36.7 2.3 %shard_map.49 = (bf16[384,1536]{1,0:T(8,128)(2,1)S(1)}, f32[4,384]{1,0:T(4,128)S(1)}, f32[1,384]{1,0:T(1,128)S(1)}) custom-call(s32[1]{0:T(128)} %bitcast.sub, bf16[384,768]{1,0:T(8,128)(2,1)S(1)} %copy-done.1, bf16[384,768]{1,0:T(8,128)(2,1)S(1)} %collective-permute-done.f1.refs_1_, bf16[384,768]{1,0:T(8,128)(2,1)S(1)} %collective-permute-done.1.f2.refs_2_, ...), custom_call_target="tpu_custom_call" | custom-call | flops 1000 | bytes 1000 | tf_op jit(solution)/shard_map/pallas_call | solution.py:56
  39.0 0.3 collective-permute-start.8
  39.3 6.9 %collective-permute-done.6.refs_4_ = bf16[432,768]{1,0:T(8,128)(2,1)S(1)} collective-permute-done((bf16[432,768]{1,0:T(8,128)(2,1)S(1)}, bf16[432,768]{1,0:T(8,128)(2,1)S(1)}, u32[]{:S(2)}, u32[]{:S(2)}) %collective-permute-start.6) | collective-permute-done | bytes 663584 | tf_op jit(solution)/shard_map/ppermute | solution.py:33
  46.2 2.3 %shard_map.50 = (bf16[384,1536]{1,0:T(8,128)(2,1)S(1)}, f32[4,384]{1,0:T(4,128)S(1)}, f32[1,384]{1,0:T(1,128)S(1)}) custom-call(s32[1]{0:T(128)} %bitcast.sub, bf16[384,768]{1,0:T(8,128)(2,1)S(1)} %copy-done.1, bf16[384,768]{1,0:T(8,128)(2,1)S(1)} %collective-permute-done.f1.refs_1_, bf16[384,768]{1,0:T(8,128)(2,1)S(1)} %collective-permute-done.1.f2.refs_2_, ...), custom_call_target="tpu_custom_call" | custom-call | flops 1000 | bytes 1000 | tf_op jit(solution)/shard_map/pallas_call | solution.py:56
  48.6 0.0 copy-start.2
  48.6 2.4 %shard_map.51 = (bf16[384,1536]{1,0:T(8,128)(2,1)S(1)}, f32[4,384]{1,0:T(4,128)S(1)}, f32[1,384]{1,0:T(1,128)S(1)}) custom-call(s32[1]{0:T(128)} %bitcast.sub, bf16[384,768]{1,0:T(8,128)(2,1)S(1)} %copy-done.1, bf16[384,768]{1,0:T(8,128)(2,1)S(1)} %collective-permute-done.f1.refs_1_, bf16[384,768]{1,0:T(8,128)(2,1)S(1)} %collective-permute-done.1.f2.refs_2_, ...), custom_call_target="tpu_custom_call" | custom-call | flops 4000000000 | bytes 1000 | tf_op jit(solution)/shard_map/pallas_call | solution.py:56
  51.0 0.8 collective-permute-start.9
  51.7 6.8 %collective-permute-start.11 = (f32[1,384]{1,0:T(1,128)S(1)}, f32[1,384]{1,0:T(1,128)S(1)}, u32[]{:S(2)}, u32[]{:S(2)}) collective-permute-start(f32[1,384]{1,0:T(1,128)S(1)} %get-tuple-element.56), channel_id=1, source_target_pairs={{0,118},{1,119},{2,116},{3,117},{4,122},{5,123},{6,120},{7,121},{8... | collective-permute-start | bytes 4616 | tf_op jit(solution)/shard_map/ppermute | solution.py:33
  58.6 0.1 collective-permute-start.10
  58.7 0.2 collective-permute-done.12
  58.9 1.0 collective-permute-done.11
  59.9 0.2 collective-permute-start.13
  60.1 1.1 collective-permute-done.13.x1
  61.3 0.9 collective-permute-start.15
  62.2 0.9 collective-permute-start.14
  63.1 9.4 %collective-permute-done.15.two = bf16[128,384]{1,0:T(8,128)(2,1)S(1)} collective-permute-done((bf16[128,384]{1,0:T(8,128)(2,1)S(1)}, bf16[128,384]{1,0:T(8,128)(2,1)S(1)}, u32[]{:S(2)}, u32[]{:S(2)}) %collective-permute-start.15) | collective-permute-done | bytes 98336 | tf_op jit(solution)/shard_map/ppermute | solution.py:45
  72.4 1.2 %collective-permute-done.14.one = bf16[128,384]{1,0:T(8,128)(2,1)S(1)} collective-permute-done((bf16[128,384]{1,0:T(8,128)(2,1)S(1)}, bf16[128,384]{1,0:T(8,128)(2,1)S(1)}, u32[]{:S(2)}, u32[]{:S(2)}) %collective-permute-start.14) | collective-permute-done | bytes 98336 | tf_op jit(solution)/shard_map/ppermute | solution.py:45
  73.7 0.1 collective-permute-start.16
  73.8 1.8 %shard_map.52 = (f32[64,384]{1,0:T(8,128)S(1)}, bf16[128,384]{1,0:T(8,128)(2,1)S(1)}, bf16[128,384]{1,0:T(8,128)(2,1)S(1)}) custom-call(s32[1]{0:T(128)} %bitcast.sub, bf16[64,384]{1,0:T(8,128)(2,1)S(1)} %multiply_convert_fusion.x0, bf16[64,384]{1,0:T(8,128)(2,1)S(1)} %collective-permute-done.13.x1, bf16[128,384]{1,0:T(8,128)(2,1)S(1)} %collective-permute-done.17.far, ...), custom_call_target="tpu_custom_call" | custom-call | flops 1000 | bytes 1000 | tf_op jit(solution)/shard_map/pallas_call | solution.py:56
  75.6 0.6 collective-permute-start.19
  76.2 1.0 shard_map.53
  77.3 0.1 collective-permute-start.18
  77.4 2.8 %collective-permute-start.20 = (bf16[128,384]{1,0:T(8,128)(2,1)S(1)}, bf16[128,384]{1,0:T(8,128)(2,1)S(1)}, u32[]{:S(2)}, u32[]{:S(2)}) collective-permute-start(bf16[128,384]{1,0:T(8,128)(2,1)S(1)} %pad_maximum_fusion.2), channel_id=1, source_target_pairs={{0,118},{1,17},{2,116},{3,19},{4,122},{5,21},{6,120},{7,23},{8,126... | collective-permute-start | bytes 294920 | tf_op jit(solution)/shard_map/ppermute | solution.py:45
  80.2 4.5 %collective-permute-start.21 = (bf16[128,384]{1,0:T(8,128)(2,1)S(1)}, bf16[128,384]{1,0:T(8,128)(2,1)S(1)}, u32[]{:S(2)}, u32[]{:S(2)}) collective-permute-start(bf16[128,384]{1,0:T(8,128)(2,1)S(1)} %pad_maximum_fusion.3), channel_id=1, source_target_pairs={{0,126},{1,9},{2,124},{3,11},{4,2},{5,13},{6,0},{7,15},{8,6},{9,17... | collective-permute-start | bytes 294920 | tf_op jit(solution)/shard_map/ppermute | solution.py:45
  84.7 2.2 %collective-permute-done.21.two = bf16[128,384]{1,0:T(8,128)(2,1)S(1)} collective-permute-done((bf16[128,384]{1,0:T(8,128)(2,1)S(1)}, bf16[128,384]{1,0:T(8,128)(2,1)S(1)}, u32[]{:S(2)}, u32[]{:S(2)}) %collective-permute-start.21) | collective-permute-done | bytes 98336 | tf_op jit(solution)/shard_map/ppermute | solution.py:45
  86.9 0.1 collective-permute-start.22
  87.0 1.3 %collective-permute-done.22.swapped = f32[64,384]{1,0:T(8,128)S(1)} collective-permute-done((f32[64,384]{1,0:T(8,128)S(1)}, f32[64,384]{1,0:T(8,128)S(1)}, u32[]{:S(2)}, u32[]{:S(2)}) %collective-permute-start.22) | collective-permute-done | bytes 98336 | tf_op jit(solution)/shard_map/ppermute | solution.py:33
  88.3 0.3 shard_map.54
  88.7 0.2 collective-permute-start.23
  88.8 1.0 collective-permute-done.23
  89.9 2.0 %collective-permute-start.26 = (f32[32,128]{1,0:T(8,128)S(1)}, f32[32,128]{1,0:T(8,128)S(1)}, u32[]{:S(2)}, u32[]{:S(2)}) collective-permute-start(f32[32,128]{1,0:T(8,128)S(1)} %add.82), channel_id=1, source_target_pairs={{0,6},{1,7},{2,4},{3,5},{4,2},{5,3},{6,0},{7,1},{8,14},{9,15},{10,... | collective-permute-start | bytes 49160 | tf_op jit(solution)/shard_map/ppermute | solution.py:351
  91.9 1.0 collective-permute-start.25
  92.9 1.1 collective-permute-start.24
  94.0 0.9 collective-permute-done.26
  94.8 2.3 %collective-permute-done.25 = f32[32,128]{1,0:T(8,128)S(1)} collective-permute-done((f32[32,128]{1,0:T(8,128)S(1)}, f32[32,128]{1,0:T(8,128)S(1)}, u32[]{:S(2)}, u32[]{:S(2)}) %collective-permute-start.25) | collective-permute-done | bytes 16416 | tf_op jit(solution)/shard_map/ppermute | solution.py:351
  97.1 1.3 %collective-permute-start.29 = (f32[32,128]{1,0:T(8,128)S(1)}, f32[32,128]{1,0:T(8,128)S(1)}, u32[]{:S(2)}, u32[]{:S(2)}) collective-permute-start(f32[32,128]{1,0:T(8,128)S(1)} %add_add_fusion.2), channel_id=1, source_target_pairs={{0,24},{1,25},{2,26},{3,27},{4,28},{5,29},{6,30},{7,31},{8,16},{9,... | collective-permute-start | bytes 49160 | tf_op jit(solution)/shard_map/ppermute | solution.py:351
  98.4 1.2 %collective-permute-start.28 = (f32[32,128]{1,0:T(8,128)S(1)}, f32[32,128]{1,0:T(8,128)S(1)}, u32[]{:S(2)}, u32[]{:S(2)}) collective-permute-start(f32[32,128]{1,0:T(8,128)S(1)} %add_add_fusion.2), channel_id=1, source_target_pairs={{0,16},{1,17},{2,18},{3,19},{4,20},{5,21},{6,22},{7,23},{8,24},{9,... | collective-permute-start | bytes 49160 | tf_op jit(solution)/shard_map/ppermute | solution.py:351
  99.6 1.9 %collective-permute-start.27 = (f32[32,128]{1,0:T(8,128)S(1)}, f32[32,128]{1,0:T(8,128)S(1)}, u32[]{:S(2)}, u32[]{:S(2)}) collective-permute-start(f32[32,128]{1,0:T(8,128)S(1)} %add_add_fusion.2), channel_id=1, source_target_pairs={{0,8},{1,9},{2,10},{3,11},{4,12},{5,13},{6,14},{7,15},{8,0},{9,1},... | collective-permute-start | bytes 49160 | tf_op jit(solution)/shard_map/ppermute | solution.py:351
  101.5 0.9 collective-permute-done.29
  102.4 1.3 %collective-permute-done.28 = f32[32,128]{1,0:T(8,128)S(1)} collective-permute-done((f32[32,128]{1,0:T(8,128)S(1)}, f32[32,128]{1,0:T(8,128)S(1)}, u32[]{:S(2)}, u32[]{:S(2)}) %collective-permute-start.28) | collective-permute-done | bytes 16416 | tf_op jit(solution)/shard_map/ppermute | solution.py:351
  103.7 6.1 %collective-permute-start.32 = (f32[32,128]{1,0:T(8,128)S(1)}, f32[32,128]{1,0:T(8,128)S(1)}, u32[]{:S(2)}, u32[]{:S(2)}) collective-permute-start(f32[32,128]{1,0:T(8,128)S(1)} %add_add_fusion.1), channel_id=1, source_target_pairs={{0,96},{1,97},{2,98},{3,99},{4,100},{5,101},{6,102},{7,103},{8,104... | collective-permute-start | bytes 49160 | tf_op jit(solution)/shard_map/ppermute | solution.py:351
  109.7 0.9 collective-permute-start.30
  110.7 0.8 collective-permute-done.32
  111.5 3.5 %collective-permute-done.31 = f32[32,128]{1,0:T(8,128)S(1)} collective-permute-done((f32[32,128]{1,0:T(8,128)S(1)}, f32[32,128]{1,0:T(8,128)S(1)}, u32[]{:S(2)}, u32[]{:S(2)}) %collective-permute-start.31) | collective-permute-done | bytes 16416 | tf_op jit(solution)/shard_map/ppermute | solution.py:351
  115.0 2.4 %shard_map.55 = f32[64,384]{1,0:T(8,128)} custom-call(f32[32,128]{1,0:T(8,128)S(1)} %add_add_fusion.gram, f32[64,384]{1,0:T(8,128)S(1)} %get-tuple-element.70.mixed), custom_call_target="tpu_custom_call" | custom-call | flops 1000 | bytes 1000 | tf_op jit(solution)/shard_map/pallas_call | solution.py:56
  (38 shorter events, 0.2 us)
Async XLA Ops:
  0.0 20.0 %copy-start = (s32[9,16,1536]{2,1,0:T(8,128)S(1)}, s32[9,16,1536]{2,1,0:T(8,128)}, u32[]{:S(2)}) copy-start(s32[9,16,1536]{2,1,0:T(8,128)} %refs_10_) | copy-start | bytes 2654212
  1.7 1.1 copy-start.1
  2.9 15.1 %collective-permute-start.1 = (bf16[384,768]{1,0:T(8,128)(2,1)S(1)}, bf16[384,768]{1,0:T(8,128)(2,1)S(1)}, u32[]{:S(2)}, u32[]{:S(2)}) collective-permute-start(bf16[384,768]{1,0:T(8,128)(2,1)S(1)} %copy-done.1), channel_id=1, source_target_pairs={{0,2},{1,3},{2,0},{3,1},{4,6},{5,7},{6,4},{7,5},{8,10},{9,11},{10,... | collective-permute-start | bytes 1769480 | tf_op jit(solution)/shard_map/ppermute | solution.py:33
  4.6 22.5 %collective-permute-start.3 = (bf16[432,768]{1,0:T(8,128)(2,1)S(1)}, bf16[432,768]{1,0:T(8,128)(2,1)S(1)}, u32[]{:S(2)}, u32[]{:S(2)}) collective-permute-start(bf16[432,768]{1,0:T(8,128)(2,1)S(1)} %get-tuple-element.41), channel_id=1, source_target_pairs={{0,6},{1,7},{2,4},{3,5},{4,10},{5,11},{6,8},{7,9},{8,14},{9,15},{1... | collective-permute-start | bytes 1990664 | tf_op jit(solution)/shard_map/ppermute | solution.py:33
  6.8 20.3 %collective-permute-start.4 = (bf16[432,768]{1,0:T(8,128)(2,1)S(1)}, bf16[432,768]{1,0:T(8,128)(2,1)S(1)}, u32[]{:S(2)}, u32[]{:S(2)}) collective-permute-start(bf16[432,768]{1,0:T(8,128)(2,1)S(1)} %get-tuple-element.42), channel_id=1, source_target_pairs={{0,120},{1,121},{2,122},{3,123},{4,124},{5,125},{6,126},{7,127},{8... | collective-permute-start | bytes 1990664 | tf_op jit(solution)/shard_map/ppermute | solution.py:33
  13.0 4.9 %collective-permute-start = (bf16[384,768]{1,0:T(8,128)(2,1)S(1)}, bf16[384,768]{1,0:T(8,128)(2,1)S(1)}, u32[]{:S(2)}, u32[]{:S(2)}) collective-permute-start(bf16[384,768]{1,0:T(8,128)(2,1)S(1)} %copy-done.1), channel_id=1, source_target_pairs={{0,1},{1,0},{2,3},{3,2},{4,5},{5,4},{6,7},{7,6},{8,9},{9,8},{10,11... | collective-permute-start | bytes 1769480 | tf_op jit(solution)/shard_map/ppermute | solution.py:33
  18.0 2.0 %collective-permute-start.2 = (bf16[384,768]{1,0:T(8,128)(2,1)S(1)}, bf16[384,768]{1,0:T(8,128)(2,1)S(1)}, u32[]{:S(2)}, u32[]{:S(2)}) collective-permute-start(bf16[384,768]{1,0:T(8,128)(2,1)S(1)} %collective-permute-done.1.f2.refs_2_), channel_id=1, source_target_pairs={{0,1},{1,0},{2,3},{3,2},{4,5},{5,4},{6,7},{7,6},{8,9},{9,8},{10,11... | collective-permute-start | bytes 1769480 | tf_op jit(solution)/shard_map/ppermute | solution.py:33
  27.1 19.1 %collective-permute-start.6 = (bf16[432,768]{1,0:T(8,128)(2,1)S(1)}, bf16[432,768]{1,0:T(8,128)(2,1)S(1)}, u32[]{:S(2)}, u32[]{:S(2)}) collective-permute-start(bf16[432,768]{1,0:T(8,128)(2,1)S(1)} %collective-permute-done.3.refs_4_), channel_id=1, source_target_pairs={{0,8},{1,9},{2,10},{3,11},{4,12},{5,13},{6,14},{7,15},{8,16},{9,17... | collective-permute-start | bytes 1990664 | tf_op jit(solution)/shard_map/ppermute | solution.py:33
  27.1 21.5 %collective-permute-start.5 = (bf16[432,768]{1,0:T(8,128)(2,1)S(1)}, bf16[432,768]{1,0:T(8,128)(2,1)S(1)}, u32[]{:S(2)}, u32[]{:S(2)}) collective-permute-start(bf16[432,768]{1,0:T(8,128)(2,1)S(1)} %collective-permute-done.4.refs_4_), channel_id=1, source_target_pairs={{0,120},{1,121},{2,122},{3,123},{4,124},{5,125},{6,126},{7,127},{8... | collective-permute-start | bytes 1990664 | tf_op jit(solution)/shard_map/ppermute | solution.py:33
  34.9 13.7 %collective-permute-start.7 = (f32[1,384]{1,0:T(1,128)S(1)}, f32[1,384]{1,0:T(1,128)S(1)}, u32[]{:S(2)}, u32[]{:S(2)}) collective-permute-start(f32[1,384]{1,0:T(1,128)S(1)} %get-tuple-element.52), channel_id=1, source_target_pairs={{0,126},{1,127},{2,124},{3,125},{4,2},{5,3},{6,0},{7,1},{8,6},{9,7... | collective-permute-start | bytes 4616 | tf_op jit(solution)/shard_map/ppermute | solution.py:33
  39.0 9.6 %collective-permute-start.8 = (f32[1,384]{1,0:T(1,128)S(1)}, f32[1,384]{1,0:T(1,128)S(1)}, u32[]{:S(2)}, u32[]{:S(2)}) collective-permute-start(f32[1,384]{1,0:T(1,128)S(1)} %get-tuple-element.53), channel_id=1, source_target_pairs={{0,8},{1,9},{2,10},{3,11},{4,12},{5,13},{6,14},{7,15},{8,16},{9,17... | collective-permute-start | bytes 4616 | tf_op jit(solution)/shard_map/ppermute | solution.py:33
  48.6 11.3 %copy-start.2 = (f32[64,384]{1,0:T(8,128)S(1)}, f32[64,384]{1,0:T(8,128)}, u32[]{:S(2)}) copy-start(f32[64,384]{1,0:T(8,128)} %own.1) | copy-start | bytes 294916
  51.0 7.6 %collective-permute-start.9 = (f32[2,384]{1,0:T(2,128)S(1)}, f32[2,384]{1,0:T(2,128)S(1)}, u32[]{:S(2)}, u32[]{:S(2)}) collective-permute-start(f32[2,384]{1,0:T(2,128)S(1)} %slice.43), channel_id=1, source_target_pairs={{0,2},{1,3},{2,0},{3,1},{4,6},{5,7},{6,4},{7,5},{8,10},{9,11},{10,... | collective-permute-start | bytes 9224 | tf_op jit(solution)/shard_map/ppermute | solution.py:33
  51.7 7.2 %collective-permute-start.12 = (f32[1,384]{1,0:T(1,128)S(1)}, f32[1,384]{1,0:T(1,128)S(1)}, u32[]{:S(2)}, u32[]{:S(2)}) collective-permute-start(f32[1,384]{1,0:T(1,128)S(1)} %get-tuple-element.57), channel_id=1, source_target_pairs={{0,16},{1,17},{2,18},{3,19},{4,20},{5,21},{6,22},{7,23},{8,24},{9,... | collective-permute-start | bytes 4616 | tf_op jit(solution)/shard_map/ppermute | solution.py:33
  51.7 8.2 %collective-permute-start.11 = (f32[1,384]{1,0:T(1,128)S(1)}, f32[1,384]{1,0:T(1,128)S(1)}, u32[]{:S(2)}, u32[]{:S(2)}) collective-permute-start(f32[1,384]{1,0:T(1,128)S(1)} %get-tuple-element.56), channel_id=1, source_target_pairs={{0,118},{1,119},{2,116},{3,117},{4,122},{5,123},{6,120},{7,121},{8... | collective-permute-start | bytes 4616 | tf_op jit(solution)/shard_map/ppermute | solution.py:33
  58.6 1.3 %collective-permute-start.10 = (f32[1,384]{1,0:T(1,128)S(1)}, f32[1,384]{1,0:T(1,128)S(1)}, u32[]{:S(2)}, u32[]{:S(2)}) collective-permute-start(f32[1,384]{1,0:T(1,128)S(1)} %slice.57), channel_id=1, source_target_pairs={{0,1},{1,0},{2,3},{3,2},{4,5},{5,4},{6,7},{7,6},{8,9},{9,8},{10,11... | collective-permute-start | bytes 4616 | tf_op jit(solution)/shard_map/ppermute | solution.py:33
  59.9 1.3 %collective-permute-start.13 = (bf16[64,384]{1,0:T(8,128)(2,1)S(1)}, bf16[64,384]{1,0:T(8,128)(2,1)S(1)}, u32[]{:S(2)}, u32[]{:S(2)}) collective-permute-start(bf16[64,384]{1,0:T(8,128)(2,1)S(1)} %multiply_convert_fusion.x0), channel_id=1, source_target_pairs={{0,1},{1,0},{2,3},{3,2},{4,5},{5,4},{6,7},{7,6},{8,9},{9,8},{10,11... | collective-permute-start | bytes 147464 | tf_op jit(solution)/shard_map/ppermute | solution.py:33
  61.3 11.2 %collective-permute-start.15 = (bf16[128,384]{1,0:T(8,128)(2,1)S(1)}, bf16[128,384]{1,0:T(8,128)(2,1)S(1)}, u32[]{:S(2)}, u32[]{:S(2)}) collective-permute-start(bf16[128,384]{1,0:T(8,128)(2,1)S(1)} %pad_maximum_fusion), channel_id=1, source_target_pairs={{0,6},{1,121},{2,4},{3,123},{4,10},{5,125},{6,8},{7,127},{8,14},{9... | collective-permute-start | bytes 294920 | tf_op jit(solution)/shard_map/ppermute | solution.py:45
  62.2 11.5 %collective-permute-start.14 = (bf16[128,384]{1,0:T(8,128)(2,1)S(1)}, bf16[128,384]{1,0:T(8,128)(2,1)S(1)}, u32[]{:S(2)}, u32[]{:S(2)}) collective-permute-start(bf16[128,384]{1,0:T(8,128)(2,1)S(1)} %pad_maximum_fusion), channel_id=1, source_target_pairs={{0,14},{1,113},{2,12},{3,115},{4,18},{5,117},{6,16},{7,119},{8,22}... | collective-permute-start | bytes 294920 | tf_op jit(solution)/shard_map/ppermute | solution.py:45
  63.1 10.7 %collective-permute-start.17 = (bf16[128,384]{1,0:T(8,128)(2,1)S(1)}, bf16[128,384]{1,0:T(8,128)(2,1)S(1)}, u32[]{:S(2)}, u32[]{:S(2)}) collective-permute-start(bf16[128,384]{1,0:T(8,128)(2,1)S(1)} %pad_maximum_fusion), channel_id=1, source_target_pairs={{0,2},{1,3},{2,0},{3,1},{4,6},{5,7},{6,4},{7,5},{8,10},{9,11},{10,... | collective-permute-start | bytes 294920 | tf_op jit(solution)/shard_map/ppermute | solution.py:33
  73.7 2.5 %collective-permute-start.16 = (bf16[128,384]{1,0:T(8,128)(2,1)S(1)}, bf16[128,384]{1,0:T(8,128)(2,1)S(1)}, u32[]{:S(2)}, u32[]{:S(2)}) collective-permute-start(bf16[128,384]{1,0:T(8,128)(2,1)S(1)} %pad_maximum_fusion.1), channel_id=1, source_target_pairs={{0,1},{1,0},{2,3},{3,2},{4,5},{5,4},{6,7},{7,6},{8,9},{9,8},{10,11... | collective-permute-start | bytes 294920 | tf_op jit(solution)/shard_map/ppermute | solution.py:33
  75.6 1.7 %collective-permute-start.19 = (bf16[128,384]{1,0:T(8,128)(2,1)S(1)}, bf16[128,384]{1,0:T(8,128)(2,1)S(1)}, u32[]{:S(2)}, u32[]{:S(2)}) collective-permute-start(bf16[128,384]{1,0:T(8,128)(2,1)S(1)} %get-tuple-element.68), channel_id=1, source_target_pairs={{0,1},{1,0},{2,3},{3,2},{4,5},{5,4},{6,7},{7,6},{8,9},{9,8},{10,11... | collective-permute-start | bytes 294920 | tf_op jit(solution)/shard_map/ppermute | solution.py:33
  77.3 7.4 %collective-permute-start.18 = (bf16[64,768]{1,0:T(8,128)(2,1)S(1)}, bf16[64,768]{1,0:T(8,128)(2,1)S(1)}, u32[]{:S(2)}, u32[]{:S(2)}) collective-permute-start(bf16[64,768]{1,0:T(8,128)(2,1)S(1)} %get-tuple-element.66), channel_id=1, source_target_pairs={{0,2},{1,3},{2,0},{3,1},{4,6},{5,7},{6,4},{7,5},{8,10},{9,11},{10,... | collective-permute-start | bytes 294920 | tf_op jit(solution)/shard_map/ppermute | solution.py:33
  77.4 7.3 %collective-permute-start.20 = (bf16[128,384]{1,0:T(8,128)(2,1)S(1)}, bf16[128,384]{1,0:T(8,128)(2,1)S(1)}, u32[]{:S(2)}, u32[]{:S(2)}) collective-permute-start(bf16[128,384]{1,0:T(8,128)(2,1)S(1)} %pad_maximum_fusion.2), channel_id=1, source_target_pairs={{0,118},{1,17},{2,116},{3,19},{4,122},{5,21},{6,120},{7,23},{8,126... | collective-permute-start | bytes 294920 | tf_op jit(solution)/shard_map/ppermute | solution.py:45
  80.2 6.7 %collective-permute-start.21 = (bf16[128,384]{1,0:T(8,128)(2,1)S(1)}, bf16[128,384]{1,0:T(8,128)(2,1)S(1)}, u32[]{:S(2)}, u32[]{:S(2)}) collective-permute-start(bf16[128,384]{1,0:T(8,128)(2,1)S(1)} %pad_maximum_fusion.3), channel_id=1, source_target_pairs={{0,126},{1,9},{2,124},{3,11},{4,2},{5,13},{6,0},{7,15},{8,6},{9,17... | collective-permute-start | bytes 294920 | tf_op jit(solution)/shard_map/ppermute | solution.py:45
  86.9 1.4 %collective-permute-start.22 = (f32[64,384]{1,0:T(8,128)S(1)}, f32[64,384]{1,0:T(8,128)S(1)}, u32[]{:S(2)}, u32[]{:S(2)}) collective-permute-start(f32[64,384]{1,0:T(8,128)S(1)} %convert_add_fusion), channel_id=1, source_target_pairs={{0,1},{1,0},{2,3},{3,2},{4,5},{5,4},{6,7},{7,6},{8,9},{9,8},{10,11... | collective-permute-start | bytes 294920 | tf_op jit(solution)/shard_map/ppermute | solution.py:33
  88.7 1.2 %collective-permute-start.23 = (f32[32,128]{1,0:T(8,128)S(1)}, f32[32,128]{1,0:T(8,128)S(1)}, u32[]{:S(2)}, u32[]{:S(2)}) collective-permute-start(f32[32,128]{1,0:T(8,128)S(1)} %get-tuple-element.69), channel_id=1, source_target_pairs={{0,1},{1,0},{2,3},{3,2},{4,5},{5,4},{6,7},{7,6},{8,9},{9,8},{10,11... | collective-permute-start | bytes 49160 | tf_op jit(solution)/shard_map/ppermute | solution.py:351
  89.9 4.9 %collective-permute-start.26 = (f32[32,128]{1,0:T(8,128)S(1)}, f32[32,128]{1,0:T(8,128)S(1)}, u32[]{:S(2)}, u32[]{:S(2)}) collective-permute-start(f32[32,128]{1,0:T(8,128)S(1)} %add.82), channel_id=1, source_target_pairs={{0,6},{1,7},{2,4},{3,5},{4,2},{5,3},{6,0},{7,1},{8,14},{9,15},{10,... | collective-permute-start | bytes 49160 | tf_op jit(solution)/shard_map/ppermute | solution.py:351
  91.9 5.2 %collective-permute-start.25 = (f32[32,128]{1,0:T(8,128)S(1)}, f32[32,128]{1,0:T(8,128)S(1)}, u32[]{:S(2)}, u32[]{:S(2)}) collective-permute-start(f32[32,128]{1,0:T(8,128)S(1)} %add.82), channel_id=1, source_target_pairs={{0,4},{1,5},{2,6},{3,7},{4,0},{5,1},{6,2},{7,3},{8,12},{9,13},{10,... | collective-permute-start | bytes 49160 | tf_op jit(solution)/shard_map/ppermute | solution.py:351
  92.9 4.2 %collective-permute-start.24 = (f32[32,128]{1,0:T(8,128)S(1)}, f32[32,128]{1,0:T(8,128)S(1)}, u32[]{:S(2)}, u32[]{:S(2)}) collective-permute-start(f32[32,128]{1,0:T(8,128)S(1)} %add.82), channel_id=1, source_target_pairs={{0,2},{1,3},{2,0},{3,1},{4,6},{5,7},{6,4},{7,5},{8,10},{9,11},{10,... | collective-permute-start | bytes 49160 | tf_op jit(solution)/shard_map/ppermute | solution.py:351
  97.1 5.2 %collective-permute-start.29 = (f32[32,128]{1,0:T(8,128)S(1)}, f32[32,128]{1,0:T(8,128)S(1)}, u32[]{:S(2)}, u32[]{:S(2)}) collective-permute-start(f32[32,128]{1,0:T(8,128)S(1)} %add_add_fusion.2), channel_id=1, source_target_pairs={{0,24},{1,25},{2,26},{3,27},{4,28},{5,29},{6,30},{7,31},{8,16},{9,... | collective-permute-start | bytes 49160 | tf_op jit(solution)/shard_map/ppermute | solution.py:351
  98.4 5.2 %collective-permute-start.28 = (f32[32,128]{1,0:T(8,128)S(1)}, f32[32,128]{1,0:T(8,128)S(1)}, u32[]{:S(2)}, u32[]{:S(2)}) collective-permute-start(f32[32,128]{1,0:T(8,128)S(1)} %add_add_fusion.2), channel_id=1, source_target_pairs={{0,16},{1,17},{2,18},{3,19},{4,20},{5,21},{6,22},{7,23},{8,24},{9,... | collective-permute-start | bytes 49160 | tf_op jit(solution)/shard_map/ppermute | solution.py:351
  99.6 4.0 %collective-permute-start.27 = (f32[32,128]{1,0:T(8,128)S(1)}, f32[32,128]{1,0:T(8,128)S(1)}, u32[]{:S(2)}, u32[]{:S(2)}) collective-permute-start(f32[32,128]{1,0:T(8,128)S(1)} %add_add_fusion.2), channel_id=1, source_target_pairs={{0,8},{1,9},{2,10},{3,11},{4,12},{5,13},{6,14},{7,15},{8,0},{9,1},... | collective-permute-start | bytes 49160 | tf_op jit(solution)/shard_map/ppermute | solution.py:351
  103.7 7.8 %collective-permute-start.32 = (f32[32,128]{1,0:T(8,128)S(1)}, f32[32,128]{1,0:T(8,128)S(1)}, u32[]{:S(2)}, u32[]{:S(2)}) collective-permute-start(f32[32,128]{1,0:T(8,128)S(1)} %add_add_fusion.1), channel_id=1, source_target_pairs={{0,96},{1,97},{2,98},{3,99},{4,100},{5,101},{6,102},{7,103},{8,104... | collective-permute-start | bytes 49160 | tf_op jit(solution)/shard_map/ppermute | solution.py:351
  109.7 5.2 %collective-permute-start.31 = (f32[32,128]{1,0:T(8,128)S(1)}, f32[32,128]{1,0:T(8,128)S(1)}, u32[]{:S(2)}, u32[]{:S(2)}) collective-permute-start(f32[32,128]{1,0:T(8,128)S(1)} %add_add_fusion.1), channel_id=1, source_target_pairs={{0,64},{1,65},{2,66},{3,67},{4,68},{5,69},{6,70},{7,71},{8,72},{9,... | collective-permute-start | bytes 49160 | tf_op jit(solution)/shard_map/ppermute | solution.py:351
  109.7 5.2 %collective-permute-start.30 = (f32[32,128]{1,0:T(8,128)S(1)}, f32[32,128]{1,0:T(8,128)S(1)}, u32[]{:S(2)}, u32[]{:S(2)}) collective-permute-start(f32[32,128]{1,0:T(8,128)S(1)} %add_add_fusion.1), channel_id=1, source_target_pairs={{0,32},{1,33},{2,34},{3,35},{4,36},{5,37},{6,38},{7,39},{8,40},{9,... | collective-permute-start | bytes 49160 | tf_op jit(solution)/shard_map/ppermute | solution.py:351

commit v5 on v4

--- a/solution.py
+++ b/solution.py
@@ -13,10 +13,10 @@
 SLOTS = 4
 EIG = 64
 NNB = 16
-BAND = ((1, 2), (-2, 0), (3, 2), (-4, 0))
+BAND = ((-2, 0), (1, 2), (-4, 0), (3, 2))
 ROUTES = ((BAND[2], BAND[3]), (BAND[0], BAND[1]))
-ONWARD = ((2, 0), (-2, 0))
-EXTRA = 3 * NNB
+ONWARD = ((-2, 0), (2, 0))
+EXTRA = 2 * NNB
 ROUNDS = (((0, 1),), ((0, 2), (1, 0), (1, 2)), ((2, 0), (4, 0), (6, 0)), ((8, 0), (16, 0), (24, 0)))
 FOLDED = 2.0 * math.log2(math.e) / F
 NT = (((1,), (1,)), ((), ()))
@@ -98,12 +98,12 @@
     scale = jnp.broadcast_to(scale, (NNB, 2 * ROWS)).astype(jnp.bfloat16)
     for out, chosen in ((first, BAND[0::2]), (second, BAND[1::2])):
         out[:ROWS, :] = features[...]
-        for index, (d, _) in enumerate(chosen):
-            position = lists[half - d]
-            digits = jnp.concatenate([position >> 6, position & 63], axis=1)
-            start = ROWS + NNB * index
-            out[start : start + NNB, :] = digits.astype(jnp.float32).astype(jnp.bfloat16)
-        out[ROWS + 2 * NNB :, :] = scale
+        position = jnp.concatenate([lists[half - d] for d, _ in chosen], axis=1)
+        group = position >> 7
+        code = jnp.left_shift(128 + (position & 127), group & 7)
+        code = jnp.where(group >= 8, -code, code)
+        out[ROWS : ROWS + NNB, :] = code.astype(jnp.float32).astype(jnp.bfloat16)
+        out[ROWS + NNB :, :] = scale
 
 
 def tile_kernel(flip, reverse, sub, f0, f1, f2, f3, moving, norms, scales, before, lists, tile, row, col, inner, words, cols):
@@ -112,13 +112,18 @@
     half_norm = 0.5 * jnp.sum(feats * feats, axis=1, keepdims=True)
 
     if reverse:
-        digits = moving[ROWS + reverse - NNB : ROWS + reverse, :].astype(jnp.float32).astype(jnp.int32)
-        position = digits[:, :ROWS] * 64 + digits[:, ROWS:]
-        group = position >> 7
+        code = moving[ROWS : ROWS + NNB, (reverse - 1) * ROWS : reverse * ROWS].astype(jnp.float32)
+        code = code.astype(jnp.int32)
+        size = jnp.abs(code)
+        power = jnp.zeros_like(size)
+        for bit in range(1, 8):
+            power = power + (size >= (128 << bit)).astype(jnp.int32)
+        lane = (size >> power) - 128
+        group = power + jnp.where(code < 0, 8, 0)
         slice_at = (group * 11) >> 5
         group = (slice_at ^ me) * 3 + group - 3 * slice_at
-        pieces = [(position & 127).astype(jnp.float32), jnp.left_shift(1, group).astype(jnp.float32)]
-        own_scale = moving[ROWS + 2 * NNB :, :ROWS].astype(jnp.float32)[0:1]
+        pieces = [lane.astype(jnp.float32), jnp.left_shift(1, group).astype(jnp.float32)]
+        own_scale = moving[ROWS + NNB :, :ROWS].astype(jnp.float32)[0:1]
     else:
         pieces = [jnp.zeros((32, ROWS), jnp.float32)]
         own_scale = scales[:, pl.ds(pl.multiple_of(me * ROWS, 128), ROWS)]
@@ -285,7 +290,7 @@
 
     def band_tile(index, moving, row, tokens=(), flops=1000):
         d, u = BAND[index]
-        body = functools.partial(band_tile_kernel, u, NNB * (1 + index // 2))
+        body = functools.partial(band_tile_kernel, u, 1 + index // 2)
         specs = (SMEM,) + (VMEM,) * 8 + (HBM,) * len(tokens) + (listed(d),)
         args = (sub_arg, *block, moving, norms, block_scales, row, *tokens, all_lists)
         tile, row, col = call(body, tile_outs, scratch, specs, flops)(*args)

time: 118 us -> 114 us (0.966)
  starting transfers between devices: 51.1 us -> 44.2 us
  waiting for transfers between devices: 44.8 us -> 48.2 us
    ppermute x19, waiting for transfers between devices: 21.4 us -> 30.2 us  [moved(): return lax.ppermute(value, ('blk', 'sub'), pairs)]
    ppermute x4, starting transfers between devices: 9.05 us -> 4.49 us  [routed(): outs.append(lax.ppermute(part, ('blk', 'sub'), pairs))]
    ppermute x10, starting transfers between devices: 15.7 us -> 12.5 us  [local(): parts.append(lax.ppermute(gram, ('blk', 'sub'), pairs))]
    ppermute x4, waiting for transfers between devices: 12.8 us -> 9.6 us  [routed(): outs.append(lax.ppermute(part, ('blk', 'sub'), pairs))]
    ppermute x10, waiting for transfers between devices: 10.6 us -> 8.41 us  [local(): parts.append(lax.ppermute(gram, ('blk', 'sub'), pairs))]
  transfers between devices with their start and end apart: 33 -> 33, of which waited for: 18 -> 26; matrix products, arithmetic and copies ran while one was open for 0% -> 0% of each run, Pallas kernels for 11% -> 12%
where the time goes in v5:
time: 114 us
  waiting for transfers between devices  48.2 us (42%)
  starting transfers between devices  44.2 us (39%)
  Pallas kernels  18.4 us (16%)
  local copies, waits for them, and re-layouts  2.83 us (2%)
    ppermute x19, waiting for transfers between devices, moved(): return lax.ppermute(value, ('blk', 'sub'), pairs)  30.2 us
    ppermute x19, starting transfers between devices, moved(): return lax.ppermute(value, ('blk', 'sub'), pairs)  27.3 us
    pallas_call x10, Pallas kernels, run(): pl.pallas_call(body, grid=(1,), out_shape=outs, in_specs=list(specs) if s...  18.4 us
    ppermute x10, starting transfers between devices, local(): parts.append(lax.ppermute(gram, ('blk', 'sub'), pairs))  12.5 us
    ppermute x4, waiting for transfers between devices, routed(): outs.append(lax.ppermute(part, ('blk', 'sub'), pairs))  9.6 us
    ppermute x10, waiting for transfers between devices, local(): parts.append(lax.ppermute(gram, ('blk', 'sub'), pairs))  8.41 us
    ppermute x4, starting transfers between devices, routed(): outs.append(lax.ppermute(part, ('blk', 'sub'), pairs))  4.49 us
  transfers between devices with their start and end apart: 33, of which 26 were waited for; matrix products, arithmetic and copies ran while one was open for 0% of the time, Pallas kernels for 12%

profile of v5, /device:TPU:0, one launch (start us, length us, event | category | flops | bytes accessed | tf_op | source)
XLA Modules:
  0.0 114.0 jit_solution(12693567550106134180)
XLA Ops:
  0.0 0.8 reshape.4.scales.refs_6_
  0.8 0.9 constant_dynamic-slice_fusion.lists
  1.7 1.1 copy-done.1
  2.8 0.1 shard_map.46
  2.9 1.7 %collective-permute-start.1 = (bf16[384,768]{1,0:T(8,128)(2,1)S(1)}, bf16[384,768]{1,0:T(8,128)(2,1)S(1)}, u32[]{:S(2)}, u32[]{:S(2)}) collective-permute-start(bf16[384,768]{1,0:T(8,128)(2,1)S(1)} %copy-done.1), channel_id=1, source_target_pairs={{0,2},{1,3},{2,0},{3,1},{4,6},{5,7},{6,4},{7,5},{8,10},{9,11},{10,... | collective-permute-start | bytes 1769480 | tf_op jit(solution)/shard_map/ppermute | solution.py:33
  4.6 6.2 %collective-permute-start.3 = (bf16[416,768]{1,0:T(8,128)(2,1)S(1)}, bf16[416,768]{1,0:T(8,128)(2,1)S(1)}, u32[]{:S(2)}, u32[]{:S(2)}) collective-permute-start(bf16[416,768]{1,0:T(8,128)(2,1)S(1)} %get-tuple-element.41), channel_id=1, source_target_pairs={{0,120},{1,121},{2,122},{3,123},{4,124},{5,125},{6,126},{7,127},{8... | collective-permute-start | bytes 1916936 | tf_op jit(solution)/shard_map/ppermute | solution.py:33
  10.9 2.2 %collective-permute-start.4 = (bf16[416,768]{1,0:T(8,128)(2,1)S(1)}, bf16[416,768]{1,0:T(8,128)(2,1)S(1)}, u32[]{:S(2)}, u32[]{:S(2)}) collective-permute-start(bf16[416,768]{1,0:T(8,128)(2,1)S(1)} %get-tuple-element.42), channel_id=1, source_target_pairs={{0,6},{1,7},{2,4},{3,5},{4,10},{5,11},{6,8},{7,9},{8,14},{9,15},{1... | collective-permute-start | bytes 1916936 | tf_op jit(solution)/shard_map/ppermute | solution.py:33
  13.1 4.9 %collective-permute-done.1.f2.refs_2_ = bf16[384,768]{1,0:T(8,128)(2,1)S(1)} collective-permute-done((bf16[384,768]{1,0:T(8,128)(2,1)S(1)}, bf16[384,768]{1,0:T(8,128)(2,1)S(1)}, u32[]{:S(2)}, u32[]{:S(2)}) %collective-permute-start.1) | collective-permute-done | bytes 589856 | tf_op jit(solution)/shard_map/ppermute | solution.py:33
  18.0 2.0 %collective-permute-done.2.f3.refs_3_ = bf16[384,768]{1,0:T(8,128)(2,1)S(1)} collective-permute-done((bf16[384,768]{1,0:T(8,128)(2,1)S(1)}, bf16[384,768]{1,0:T(8,128)(2,1)S(1)}, u32[]{:S(2)}, u32[]{:S(2)}) %collective-permute-start.2) | collective-permute-done | bytes 589856 | tf_op jit(solution)/shard_map/ppermute | solution.py:33
  20.0 3.2 %shard_map.47 = (bf16[384,1536]{1,0:T(8,128)(2,1)S(1)}, f32[4,384]{1,0:T(4,128)S(1)}, f32[1,384]{1,0:T(1,128)S(1)}, f32[4,384]{1,0:T(4,128)S(1)}) custom-call(s32[1]{0:T(128)} %bitcast.sub, bf16[384,768]{1,0:T(8,128)(2,1)S(1)} %copy-done.1, bf16[384,768]{1,0:T(8,128)(2,1)S(1)} %collective-permute-done.f1.refs_1_, ...), custom_call_target="tpu_custom_call" | custom-call | flops 1000 | bytes 1000 | tf_op jit(solution)/shard_map/pallas_call | solution.py:56
  23.2 1.0 collective-permute-done.3.refs_4_
  24.2 7.6 %collective-permute-done.4.refs_4_ = bf16[416,768]{1,0:T(8,128)(2,1)S(1)} collective-permute-done((bf16[416,768]{1,0:T(8,128)(2,1)S(1)}, bf16[416,768]{1,0:T(8,128)(2,1)S(1)}, u32[]{:S(2)}, u32[]{:S(2)}) %collective-permute-start.4) | collective-permute-done | bytes 639008 | tf_op jit(solution)/shard_map/ppermute | solution.py:33
  31.9 2.0 %collective-permute-start.5 = (bf16[416,768]{1,0:T(8,128)(2,1)S(1)}, bf16[416,768]{1,0:T(8,128)(2,1)S(1)}, u32[]{:S(2)}, u32[]{:S(2)}) collective-permute-start(bf16[416,768]{1,0:T(8,128)(2,1)S(1)} %collective-permute-done.4.refs_4_), channel_id=1, source_target_pairs={{0,8},{1,9},{2,10},{3,11},{4,12},{5,13},{6,14},{7,15},{8,16},{9,17... | collective-permute-start | bytes 1916936 | tf_op jit(solution)/shard_map/ppermute | solution.py:33
  33.9 2.4 %shard_map.48 = (bf16[384,1536]{1,0:T(8,128)(2,1)S(1)}, f32[4,384]{1,0:T(4,128)S(1)}, f32[1,384]{1,0:T(1,128)S(1)}) custom-call(s32[1]{0:T(128)} %bitcast.sub, bf16[384,768]{1,0:T(8,128)(2,1)S(1)} %copy-done.1, bf16[384,768]{1,0:T(8,128)(2,1)S(1)} %collective-permute-done.f1.refs_1_, bf16[384,768]{1,0:T(8,128)(2,1)S(1)} %collective-permute-done.1.f2.refs_2_, ...), custom_call_target="tpu_custom_call" | custom-call | flops 1000 | bytes 1000 | tf_op jit(solution)/shard_map/pallas_call | solution.py:56
  36.4 2.4 %shard_map.49 = (bf16[384,1536]{1,0:T(8,128)(2,1)S(1)}, f32[4,384]{1,0:T(4,128)S(1)}, f32[1,384]{1,0:T(1,128)S(1)}) custom-call(s32[1]{0:T(128)} %bitcast.sub, bf16[384,768]{1,0:T(8,128)(2,1)S(1)} %copy-done.1, bf16[384,768]{1,0:T(8,128)(2,1)S(1)} %collective-permute-done.f1.refs_1_, bf16[384,768]{1,0:T(8,128)(2,1)S(1)} %collective-permute-done.1.f2.refs_2_, ...), custom_call_target="tpu_custom_call" | custom-call | flops 1000 | bytes 1000 | tf_op jit(solution)/shard_map/pallas_call | solution.py:56
  38.8 3.9 %collective-permute-start.8 = (f32[1,384]{1,0:T(1,128)S(1)}, f32[1,384]{1,0:T(1,128)S(1)}, u32[]{:S(2)}, u32[]{:S(2)}) collective-permute-start(f32[1,384]{1,0:T(1,128)S(1)} %get-tuple-element.53), channel_id=1, source_target_pairs={{0,126},{1,127},{2,124},{3,125},{4,2},{5,3},{6,0},{7,1},{8,6},{9,7... | collective-permute-start | bytes 4616 | tf_op jit(solution)/shard_map/ppermute | solution.py:33
  42.6 3.9 %collective-permute-done.6.refs_4_ = bf16[416,768]{1,0:T(8,128)(2,1)S(1)} collective-permute-done((bf16[416,768]{1,0:T(8,128)(2,1)S(1)}, bf16[416,768]{1,0:T(8,128)(2,1)S(1)}, u32[]{:S(2)}, u32[]{:S(2)}) %collective-permute-start.6) | collective-permute-done | bytes 639008 | tf_op jit(solution)/shard_map/ppermute | solution.py:33
  46.5 2.3 %shard_map.50 = (bf16[384,1536]{1,0:T(8,128)(2,1)S(1)}, f32[4,384]{1,0:T(4,128)S(1)}, f32[1,384]{1,0:T(1,128)S(1)}) custom-call(s32[1]{0:T(128)} %bitcast.sub, bf16[384,768]{1,0:T(8,128)(2,1)S(1)} %copy-done.1, bf16[384,768]{1,0:T(8,128)(2,1)S(1)} %collective-permute-done.f1.refs_1_, bf16[384,768]{1,0:T(8,128)(2,1)S(1)} %collective-permute-done.1.f2.refs_2_, ...), custom_call_target="tpu_custom_call" | custom-call | flops 1000 | bytes 1000 | tf_op jit(solution)/shard_map/pallas_call | solution.py:56
  48.9 1.0 collective-permute-done.7.refs_8_
  49.9 2.4 %shard_map.51 = (bf16[384,1536]{1,0:T(8,128)(2,1)S(1)}, f32[4,384]{1,0:T(4,128)S(1)}, f32[1,384]{1,0:T(1,128)S(1)}) custom-call(s32[1]{0:T(128)} %bitcast.sub, bf16[384,768]{1,0:T(8,128)(2,1)S(1)} %copy-done.1, bf16[384,768]{1,0:T(8,128)(2,1)S(1)} %collective-permute-done.f1.refs_1_, bf16[384,768]{1,0:T(8,128)(2,1)S(1)} %collective-permute-done.1.f2.refs_2_, ...), custom_call_target="tpu_custom_call" | custom-call | flops 4000000000 | bytes 1000 | tf_op jit(solution)/shard_map/pallas_call | solution.py:56
  52.3 1.0 collective-permute-start.9
  53.3 1.1 %collective-permute-start.12 = (f32[1,384]{1,0:T(1,128)S(1)}, f32[1,384]{1,0:T(1,128)S(1)}, u32[]{:S(2)}, u32[]{:S(2)}) collective-permute-start(f32[1,384]{1,0:T(1,128)S(1)} %get-tuple-element.57), channel_id=1, source_target_pairs={{0,118},{1,119},{2,116},{3,117},{4,122},{5,123},{6,120},{7,121},{8... | collective-permute-start | bytes 4616 | tf_op jit(solution)/shard_map/ppermute | solution.py:33
  54.4 4.0 %collective-permute-start.11 = (f32[1,384]{1,0:T(1,128)S(1)}, f32[1,384]{1,0:T(1,128)S(1)}, u32[]{:S(2)}, u32[]{:S(2)}) collective-permute-start(f32[1,384]{1,0:T(1,128)S(1)} %get-tuple-element.56), channel_id=1, source_target_pairs={{0,16},{1,17},{2,18},{3,19},{4,20},{5,21},{6,22},{7,23},{8,24},{9,... | collective-permute-start | bytes 4616 | tf_op jit(solution)/shard_map/ppermute | solution.py:33
  58.5 0.4 collective-permute-done.12
  59.0 2.7 %collective-permute-done.11 = f32[1,384]{1,0:T(1,128)S(1)} collective-permute-done((f32[1,384]{1,0:T(1,128)S(1)}, f32[1,384]{1,0:T(1,128)S(1)}, u32[]{:S(2)}, u32[]{:S(2)}) %collective-permute-start.11) | collective-permute-done | bytes 1568 | tf_op jit(solution)/shard_map/ppermute | solution.py:33
  61.7 0.1 collective-permute-start.13
  61.8 1.2 %collective-permute-done.13.x1 = bf16[64,384]{1,0:T(8,128)(2,1)S(1)} collective-permute-done((bf16[64,384]{1,0:T(8,128)(2,1)S(1)}, bf16[64,384]{1,0:T(8,128)(2,1)S(1)}, u32[]{:S(2)}, u32[]{:S(2)}) %collective-permute-start.13) | collective-permute-done | bytes 49184 | tf_op jit(solution)/shard_map/ppermute | solution.py:33
  63.0 3.3 %collective-permute-start.15 = (bf16[128,384]{1,0:T(8,128)(2,1)S(1)}, bf16[128,384]{1,0:T(8,128)(2,1)S(1)}, u32[]{:S(2)}, u32[]{:S(2)}) collective-permute-start(bf16[128,384]{1,0:T(8,128)(2,1)S(1)} %pad_maximum_fusion), channel_id=1, source_target_pairs={{0,120},{1,7},{2,122},{3,5},{4,124},{5,11},{6,126},{7,9},{8,0},{9,... | collective-permute-start | bytes 294920 | tf_op jit(solution)/shard_map/ppermute | solution.py:45
  66.3 0.2 collective-permute-start.14
  66.5 0.7 collective-permute-start.17
  67.2 2.4 %collective-permute-done.15.two = bf16[128,384]{1,0:T(8,128)(2,1)S(1)} collective-permute-done((bf16[128,384]{1,0:T(8,128)(2,1)S(1)}, bf16[128,384]{1,0:T(8,128)(2,1)S(1)}, u32[]{:S(2)}, u32[]{:S(2)}) %collective-permute-start.15) | collective-permute-done | bytes 98336 | tf_op jit(solution)/shard_map/ppermute | solution.py:45
  69.6 2.8 %collective-permute-done.14.one = bf16[128,384]{1,0:T(8,128)(2,1)S(1)} collective-permute-done((bf16[128,384]{1,0:T(8,128)(2,1)S(1)}, bf16[128,384]{1,0:T(8,128)(2,1)S(1)}, u32[]{:S(2)}, u32[]{:S(2)}) %collective-permute-start.14) | collective-permute-done | bytes 98336 | tf_op jit(solution)/shard_map/ppermute | solution.py:45
  72.5 3.9 %collective-permute-start.16 = (bf16[128,384]{1,0:T(8,128)(2,1)S(1)}, bf16[128,384]{1,0:T(8,128)(2,1)S(1)}, u32[]{:S(2)}, u32[]{:S(2)}) collective-permute-start(bf16[128,384]{1,0:T(8,128)(2,1)S(1)} %pad_maximum_fusion.1), channel_id=1, source_target_pairs={{0,1},{1,0},{2,3},{3,2},{4,5},{5,4},{6,7},{7,6},{8,9},{9,8},{10,11... | collective-permute-start | bytes 294920 | tf_op jit(solution)/shard_map/ppermute | solution.py:33
  76.4 1.8 %shard_map.52 = (f32[64,384]{1,0:T(8,128)S(1)}, bf16[128,384]{1,0:T(8,128)(2,1)S(1)}, bf16[128,384]{1,0:T(8,128)(2,1)S(1)}) custom-call(s32[1]{0:T(128)} %bitcast.sub, bf16[64,384]{1,0:T(8,128)(2,1)S(1)} %multiply_convert_fusion.x0, bf16[64,384]{1,0:T(8,128)(2,1)S(1)} %collective-permute-done.13.x1, bf16[128,384]{1,0:T(8,128)(2,1)S(1)} %collective-permute-done.17.far, ...), custom_call_target="tpu_custom_call" | custom-call | flops 1000 | bytes 1000 | tf_op jit(solution)/shard_map/pallas_call | solution.py:56
  78.2 0.1 collective-permute-start.19
  78.3 1.0 shard_map.53
  79.4 0.1 collective-permute-start.18
  79.5 0.1 collective-permute-done.19
  79.6 0.9 collective-permute-start.20
  80.7 4.0 %collective-permute-done.18.got = bf16[64,768]{1,0:T(8,128)(2,1)S(1)} collective-permute-done((bf16[64,768]{1,0:T(8,128)(2,1)S(1)}, bf16[64,768]{1,0:T(8,128)(2,1)S(1)}, u32[]{:S(2)}, u32[]{:S(2)}) %collective-permute-start.18) | collective-permute-done | bytes 98336 | tf_op jit(solution)/shard_map/ppermute | solution.py:33
  84.7 3.3 %collective-permute-done.20.one = bf16[128,384]{1,0:T(8,128)(2,1)S(1)} collective-permute-done((bf16[128,384]{1,0:T(8,128)(2,1)S(1)}, bf16[128,384]{1,0:T(8,128)(2,1)S(1)}, u32[]{:S(2)}, u32[]{:S(2)}) %collective-permute-start.20) | collective-permute-done | bytes 98336 | tf_op jit(solution)/shard_map/ppermute | solution.py:45
  88.0 1.0 collective-permute-done.21.two
  89.0 0.1 collective-permute-start.22
  89.1 1.3 %collective-permute-done.22.swapped = f32[64,384]{1,0:T(8,128)S(1)} collective-permute-done((f32[64,384]{1,0:T(8,128)S(1)}, f32[64,384]{1,0:T(8,128)S(1)}, u32[]{:S(2)}, u32[]{:S(2)}) %collective-permute-start.22) | collective-permute-done | bytes 98336 | tf_op jit(solution)/shard_map/ppermute | solution.py:33
  90.4 0.3 shard_map.54
  90.7 0.2 collective-permute-start.23
  90.9 1.0 collective-permute-done.23
  92.0 2.0 %collective-permute-start.26 = (f32[32,128]{1,0:T(8,128)S(1)}, f32[32,128]{1,0:T(8,128)S(1)}, u32[]{:S(2)}, u32[]{:S(2)}) collective-permute-start(f32[32,128]{1,0:T(8,128)S(1)} %add.82), channel_id=1, source_target_pairs={{0,6},{1,7},{2,4},{3,5},{4,2},{5,3},{6,0},{7,1},{8,14},{9,15},{10,... | collective-permute-start | bytes 49160 | tf_op jit(solution)/shard_map/ppermute | solution.py:356
  94.0 2.0 %collective-permute-start.25 = (f32[32,128]{1,0:T(8,128)S(1)}, f32[32,128]{1,0:T(8,128)S(1)}, u32[]{:S(2)}, u32[]{:S(2)}) collective-permute-start(f32[32,128]{1,0:T(8,128)S(1)} %add.82), channel_id=1, source_target_pairs={{0,4},{1,5},{2,6},{3,7},{4,0},{5,1},{6,2},{7,3},{8,12},{9,13},{10,... | collective-permute-start | bytes 49160 | tf_op jit(solution)/shard_map/ppermute | solution.py:356
  95.9 0.1 collective-permute-start.24
  96.1 0.9 collective-permute-done.26
  96.9 2.3 %collective-permute-done.25 = f32[32,128]{1,0:T(8,128)S(1)} collective-permute-done((f32[32,128]{1,0:T(8,128)S(1)}, f32[32,128]{1,0:T(8,128)S(1)}, u32[]{:S(2)}, u32[]{:S(2)}) %collective-permute-start.25) | collective-permute-done | bytes 16416 | tf_op jit(solution)/shard_map/ppermute | solution.py:356
  99.2 0.5 collective-permute-done.24
  99.7 1.2 %collective-permute-start.28 = (f32[32,128]{1,0:T(8,128)S(1)}, f32[32,128]{1,0:T(8,128)S(1)}, u32[]{:S(2)}, u32[]{:S(2)}) collective-permute-start(f32[32,128]{1,0:T(8,128)S(1)} %add_add_fusion.2), channel_id=1, source_target_pairs={{0,16},{1,17},{2,18},{3,19},{4,20},{5,21},{6,22},{7,23},{8,24},{9,... | collective-permute-start | bytes 49160 | tf_op jit(solution)/shard_map/ppermute | solution.py:356
  100.9 2.9 %collective-permute-start.27 = (f32[32,128]{1,0:T(8,128)S(1)}, f32[32,128]{1,0:T(8,128)S(1)}, u32[]{:S(2)}, u32[]{:S(2)}) collective-permute-start(f32[32,128]{1,0:T(8,128)S(1)} %add_add_fusion.2), channel_id=1, source_target_pairs={{0,8},{1,9},{2,10},{3,11},{4,12},{5,13},{6,14},{7,15},{8,0},{9,1},... | collective-permute-start | bytes 49160 | tf_op jit(solution)/shard_map/ppermute | solution.py:356
  103.8 0.9 collective-permute-done.29
  104.6 0.4 collective-permute-done.28
  105.0 0.7 collective-permute-done.27
  105.7 0.5 collective-permute-start.32
  106.2 3.6 %collective-permute-start.30 = (f32[32,128]{1,0:T(8,128)S(1)}, f32[32,128]{1,0:T(8,128)S(1)}, u32[]{:S(2)}, u32[]{:S(2)}) collective-permute-start(f32[32,128]{1,0:T(8,128)S(1)} %add_add_fusion.1), channel_id=1, source_target_pairs={{0,32},{1,33},{2,34},{3,35},{4,36},{5,37},{6,38},{7,39},{8,40},{9,... | collective-permute-start | bytes 49160 | tf_op jit(solution)/shard_map/ppermute | solution.py:356
  109.8 0.9 collective-permute-done.32
  110.6 0.8 collective-permute-done.31
  111.4 0.2 collective-permute-done.30
  111.7 2.4 %shard_map.55 = f32[64,384]{1,0:T(8,128)} custom-call(f32[32,128]{1,0:T(8,128)S(1)} %add_add_fusion.gram, f32[64,384]{1,0:T(8,128)S(1)} %get-tuple-element.70.mixed), custom_call_target="tpu_custom_call" | custom-call | flops 1000 | bytes 1000 | tf_op jit(solution)/shard_map/pallas_call | solution.py:56
  (38 shorter events, 0.5 us)
Async XLA Ops:
  0.0 20.0 %copy-start = (s32[9,16,1536]{2,1,0:T(8,128)S(1)}, s32[9,16,1536]{2,1,0:T(8,128)}, u32[]{:S(2)}) copy-start(s32[9,16,1536]{2,1,0:T(8,128)} %refs_10_) | copy-start | bytes 2654212
  1.7 1.1 copy-start.1
  2.9 15.1 %collective-permute-start.1 = (bf16[384,768]{1,0:T(8,128)(2,1)S(1)}, bf16[384,768]{1,0:T(8,128)(2,1)S(1)}, u32[]{:S(2)}, u32[]{:S(2)}) collective-permute-start(bf16[384,768]{1,0:T(8,128)(2,1)S(1)} %copy-done.1), channel_id=1, source_target_pairs={{0,2},{1,3},{2,0},{3,1},{4,6},{5,7},{6,4},{7,5},{8,10},{9,11},{10,... | collective-permute-start | bytes 1769480 | tf_op jit(solution)/shard_map/ppermute | solution.py:33
  4.6 19.6 %collective-permute-start.3 = (bf16[416,768]{1,0:T(8,128)(2,1)S(1)}, bf16[416,768]{1,0:T(8,128)(2,1)S(1)}, u32[]{:S(2)}, u32[]{:S(2)}) collective-permute-start(bf16[416,768]{1,0:T(8,128)(2,1)S(1)} %get-tuple-element.41), channel_id=1, source_target_pairs={{0,120},{1,121},{2,122},{3,123},{4,124},{5,125},{6,126},{7,127},{8... | collective-permute-start | bytes 1916936 | tf_op jit(solution)/shard_map/ppermute | solution.py:33
  10.9 21.0 %collective-permute-start.4 = (bf16[416,768]{1,0:T(8,128)(2,1)S(1)}, bf16[416,768]{1,0:T(8,128)(2,1)S(1)}, u32[]{:S(2)}, u32[]{:S(2)}) collective-permute-start(bf16[416,768]{1,0:T(8,128)(2,1)S(1)} %get-tuple-element.42), channel_id=1, source_target_pairs={{0,6},{1,7},{2,4},{3,5},{4,10},{5,11},{6,8},{7,9},{8,14},{9,15},{1... | collective-permute-start | bytes 1916936 | tf_op jit(solution)/shard_map/ppermute | solution.py:33
  13.1 4.9 %collective-permute-start = (bf16[384,768]{1,0:T(8,128)(2,1)S(1)}, bf16[384,768]{1,0:T(8,128)(2,1)S(1)}, u32[]{:S(2)}, u32[]{:S(2)}) collective-permute-start(bf16[384,768]{1,0:T(8,128)(2,1)S(1)} %copy-done.1), channel_id=1, source_target_pairs={{0,1},{1,0},{2,3},{3,2},{4,5},{5,4},{6,7},{7,6},{8,9},{9,8},{10,11... | collective-permute-start | bytes 1769480 | tf_op jit(solution)/shard_map/ppermute | solution.py:33
  18.0 2.0 %collective-permute-start.2 = (bf16[384,768]{1,0:T(8,128)(2,1)S(1)}, bf16[384,768]{1,0:T(8,128)(2,1)S(1)}, u32[]{:S(2)}, u32[]{:S(2)}) collective-permute-start(bf16[384,768]{1,0:T(8,128)(2,1)S(1)} %collective-permute-done.1.f2.refs_2_), channel_id=1, source_target_pairs={{0,1},{1,0},{2,3},{3,2},{4,5},{5,4},{6,7},{7,6},{8,9},{9,8},{10,11... | collective-permute-start | bytes 1769480 | tf_op jit(solution)/shard_map/ppermute | solution.py:33
  31.9 14.7 %collective-permute-start.6 = (bf16[416,768]{1,0:T(8,128)(2,1)S(1)}, bf16[416,768]{1,0:T(8,128)(2,1)S(1)}, u32[]{:S(2)}, u32[]{:S(2)}) collective-permute-start(bf16[416,768]{1,0:T(8,128)(2,1)S(1)} %collective-permute-done.3.refs_4_), channel_id=1, source_target_pairs={{0,120},{1,121},{2,122},{3,123},{4,124},{5,125},{6,126},{7,127},{8... | collective-permute-start | bytes 1916936 | tf_op jit(solution)/shard_map/ppermute | solution.py:33
  31.9 18.0 %collective-permute-start.5 = (bf16[416,768]{1,0:T(8,128)(2,1)S(1)}, bf16[416,768]{1,0:T(8,128)(2,1)S(1)}, u32[]{:S(2)}, u32[]{:S(2)}) collective-permute-start(bf16[416,768]{1,0:T(8,128)(2,1)S(1)} %collective-permute-done.4.refs_4_), channel_id=1, source_target_pairs={{0,8},{1,9},{2,10},{3,11},{4,12},{5,13},{6,14},{7,15},{8,16},{9,17... | collective-permute-start | bytes 1916936 | tf_op jit(solution)/shard_map/ppermute | solution.py:33
  36.3 13.6 %collective-permute-start.7 = (f32[1,384]{1,0:T(1,128)S(1)}, f32[1,384]{1,0:T(1,128)S(1)}, u32[]{:S(2)}, u32[]{:S(2)}) collective-permute-start(f32[1,384]{1,0:T(1,128)S(1)} %get-tuple-element.52), channel_id=1, source_target_pairs={{0,8},{1,9},{2,10},{3,11},{4,12},{5,13},{6,14},{7,15},{8,16},{9,17... | collective-permute-start | bytes 4616 | tf_op jit(solution)/shard_map/ppermute | solution.py:33
  38.8 11.1 %collective-permute-start.8 = (f32[1,384]{1,0:T(1,128)S(1)}, f32[1,384]{1,0:T(1,128)S(1)}, u32[]{:S(2)}, u32[]{:S(2)}) collective-permute-start(f32[1,384]{1,0:T(1,128)S(1)} %get-tuple-element.53), channel_id=1, source_target_pairs={{0,126},{1,127},{2,124},{3,125},{4,2},{5,3},{6,0},{7,1},{8,6},{9,7... | collective-permute-start | bytes 4616 | tf_op jit(solution)/shard_map/ppermute | solution.py:33
  49.9 11.8 %copy-start.2 = (f32[64,384]{1,0:T(8,128)S(1)}, f32[64,384]{1,0:T(8,128)}, u32[]{:S(2)}) copy-start(f32[64,384]{1,0:T(8,128)} %own.1) | copy-start | bytes 294916
  52.3 6.1 %collective-permute-start.9 = (f32[2,384]{1,0:T(2,128)S(1)}, f32[2,384]{1,0:T(2,128)S(1)}, u32[]{:S(2)}, u32[]{:S(2)}) collective-permute-start(f32[2,384]{1,0:T(2,128)S(1)} %slice.43), channel_id=1, source_target_pairs={{0,2},{1,3},{2,0},{3,1},{4,6},{5,7},{6,4},{7,5},{8,10},{9,11},{10,... | collective-permute-start | bytes 9224 | tf_op jit(solution)/shard_map/ppermute | solution.py:33
  53.3 5.7 %collective-permute-start.12 = (f32[1,384]{1,0:T(1,128)S(1)}, f32[1,384]{1,0:T(1,128)S(1)}, u32[]{:S(2)}, u32[]{:S(2)}) collective-permute-start(f32[1,384]{1,0:T(1,128)S(1)} %get-tuple-element.57), channel_id=1, source_target_pairs={{0,118},{1,119},{2,116},{3,117},{4,122},{5,123},{6,120},{7,121},{8... | collective-permute-start | bytes 4616 | tf_op jit(solution)/shard_map/ppermute | solution.py:33
  54.4 7.2 %collective-permute-start.11 = (f32[1,384]{1,0:T(1,128)S(1)}, f32[1,384]{1,0:T(1,128)S(1)}, u32[]{:S(2)}, u32[]{:S(2)}) collective-permute-start(f32[1,384]{1,0:T(1,128)S(1)} %get-tuple-element.56), channel_id=1, source_target_pairs={{0,16},{1,17},{2,18},{3,19},{4,20},{5,21},{6,22},{7,23},{8,24},{9,... | collective-permute-start | bytes 4616 | tf_op jit(solution)/shard_map/ppermute | solution.py:33
  58.4 3.2 %collective-permute-start.10 = (f32[1,384]{1,0:T(1,128)S(1)}, f32[1,384]{1,0:T(1,128)S(1)}, u32[]{:S(2)}, u32[]{:S(2)}) collective-permute-start(f32[1,384]{1,0:T(1,128)S(1)} %slice.57), channel_id=1, source_target_pairs={{0,1},{1,0},{2,3},{3,2},{4,5},{5,4},{6,7},{7,6},{8,9},{9,8},{10,11... | collective-permute-start | bytes 4616 | tf_op jit(solution)/shard_map/ppermute | solution.py:33
  61.7 1.3 %collective-permute-start.13 = (bf16[64,384]{1,0:T(8,128)(2,1)S(1)}, bf16[64,384]{1,0:T(8,128)(2,1)S(1)}, u32[]{:S(2)}, u32[]{:S(2)}) collective-permute-start(bf16[64,384]{1,0:T(8,128)(2,1)S(1)} %multiply_convert_fusion.x0), channel_id=1, source_target_pairs={{0,1},{1,0},{2,3},{3,2},{4,5},{5,4},{6,7},{7,6},{8,9},{9,8},{10,11... | collective-permute-start | bytes 147464 | tf_op jit(solution)/shard_map/ppermute | solution.py:33
  63.0 6.6 %collective-permute-start.15 = (bf16[128,384]{1,0:T(8,128)(2,1)S(1)}, bf16[128,384]{1,0:T(8,128)(2,1)S(1)}, u32[]{:S(2)}, u32[]{:S(2)}) collective-permute-start(bf16[128,384]{1,0:T(8,128)(2,1)S(1)} %pad_maximum_fusion), channel_id=1, source_target_pairs={{0,120},{1,7},{2,122},{3,5},{4,124},{5,11},{6,126},{7,9},{8,0},{9,... | collective-permute-start | bytes 294920 | tf_op jit(solution)/shard_map/ppermute | solution.py:45
  66.3 6.1 %collective-permute-start.14 = (bf16[128,384]{1,0:T(8,128)(2,1)S(1)}, bf16[128,384]{1,0:T(8,128)(2,1)S(1)}, u32[]{:S(2)}, u32[]{:S(2)}) collective-permute-start(bf16[128,384]{1,0:T(8,128)(2,1)S(1)} %pad_maximum_fusion), channel_id=1, source_target_pairs={{0,112},{1,15},{2,114},{3,13},{4,116},{5,19},{6,118},{7,17},{8,120... | collective-permute-start | bytes 294920 | tf_op jit(solution)/shard_map/ppermute | solution.py:45
  66.5 9.9 %collective-permute-start.17 = (bf16[128,384]{1,0:T(8,128)(2,1)S(1)}, bf16[128,384]{1,0:T(8,128)(2,1)S(1)}, u32[]{:S(2)}, u32[]{:S(2)}) collective-permute-start(bf16[128,384]{1,0:T(8,128)(2,1)S(1)} %pad_maximum_fusion), channel_id=1, source_target_pairs={{0,2},{1,3},{2,0},{3,1},{4,6},{5,7},{6,4},{7,5},{8,10},{9,11},{10,... | collective-permute-start | bytes 294920 | tf_op jit(solution)/shard_map/ppermute | solution.py:33
  72.5 5.9 %collective-permute-start.16 = (bf16[128,384]{1,0:T(8,128)(2,1)S(1)}, bf16[128,384]{1,0:T(8,128)(2,1)S(1)}, u32[]{:S(2)}, u32[]{:S(2)}) collective-permute-start(bf16[128,384]{1,0:T(8,128)(2,1)S(1)} %pad_maximum_fusion.1), channel_id=1, source_target_pairs={{0,1},{1,0},{2,3},{3,2},{4,5},{5,4},{6,7},{7,6},{8,9},{9,8},{10,11... | collective-permute-start | bytes 294920 | tf_op jit(solution)/shard_map/ppermute | solution.py:33
  78.2 1.4 %collective-permute-start.19 = (bf16[128,384]{1,0:T(8,128)(2,1)S(1)}, bf16[128,384]{1,0:T(8,128)(2,1)S(1)}, u32[]{:S(2)}, u32[]{:S(2)}) collective-permute-start(bf16[128,384]{1,0:T(8,128)(2,1)S(1)} %get-tuple-element.68), channel_id=1, source_target_pairs={{0,1},{1,0},{2,3},{3,2},{4,5},{5,4},{6,7},{7,6},{8,9},{9,8},{10,11... | collective-permute-start | bytes 294920 | tf_op jit(solution)/shard_map/ppermute | solution.py:33
  79.4 5.3 %collective-permute-start.18 = (bf16[64,768]{1,0:T(8,128)(2,1)S(1)}, bf16[64,768]{1,0:T(8,128)(2,1)S(1)}, u32[]{:S(2)}, u32[]{:S(2)}) collective-permute-start(bf16[64,768]{1,0:T(8,128)(2,1)S(1)} %get-tuple-element.66), channel_id=1, source_target_pairs={{0,2},{1,3},{2,0},{3,1},{4,6},{5,7},{6,4},{7,5},{8,10},{9,11},{10,... | collective-permute-start | bytes 294920 | tf_op jit(solution)/shard_map/ppermute | solution.py:33
  79.6 8.3 %collective-permute-start.20 = (bf16[128,384]{1,0:T(8,128)(2,1)S(1)}, bf16[128,384]{1,0:T(8,128)(2,1)S(1)}, u32[]{:S(2)}, u32[]{:S(2)}) collective-permute-start(bf16[128,384]{1,0:T(8,128)(2,1)S(1)} %pad_maximum_fusion.2), channel_id=1, source_target_pairs={{0,16},{1,119},{2,18},{3,117},{4,20},{5,123},{6,22},{7,121},{8,24}... | collective-permute-start | bytes 294920 | tf_op jit(solution)/shard_map/ppermute | solution.py:45
  80.6 8.4 %collective-permute-start.21 = (bf16[128,384]{1,0:T(8,128)(2,1)S(1)}, bf16[128,384]{1,0:T(8,128)(2,1)S(1)}, u32[]{:S(2)}, u32[]{:S(2)}) collective-permute-start(bf16[128,384]{1,0:T(8,128)(2,1)S(1)} %pad_maximum_fusion.3), channel_id=1, source_target_pairs={{0,8},{1,127},{2,10},{3,125},{4,12},{5,3},{6,14},{7,1},{8,16},{9,7... | collective-permute-start | bytes 294920 | tf_op jit(solution)/shard_map/ppermute | solution.py:45
  89.0 1.4 %collective-permute-start.22 = (f32[64,384]{1,0:T(8,128)S(1)}, f32[64,384]{1,0:T(8,128)S(1)}, u32[]{:S(2)}, u32[]{:S(2)}) collective-permute-start(f32[64,384]{1,0:T(8,128)S(1)} %convert_add_fusion), channel_id=1, source_target_pairs={{0,1},{1,0},{2,3},{3,2},{4,5},{5,4},{6,7},{7,6},{8,9},{9,8},{10,11... | collective-permute-start | bytes 294920 | tf_op jit(solution)/shard_map/ppermute | solution.py:33
  90.7 1.2 %collective-permute-start.23 = (f32[32,128]{1,0:T(8,128)S(1)}, f32[32,128]{1,0:T(8,128)S(1)}, u32[]{:S(2)}, u32[]{:S(2)}) collective-permute-start(f32[32,128]{1,0:T(8,128)S(1)} %get-tuple-element.69), channel_id=1, source_target_pairs={{0,1},{1,0},{2,3},{3,2},{4,5},{5,4},{6,7},{7,6},{8,9},{9,8},{10,11... | collective-permute-start | bytes 49160 | tf_op jit(solution)/shard_map/ppermute | solution.py:356
  92.0 4.9 %collective-permute-start.26 = (f32[32,128]{1,0:T(8,128)S(1)}, f32[32,128]{1,0:T(8,128)S(1)}, u32[]{:S(2)}, u32[]{:S(2)}) collective-permute-start(f32[32,128]{1,0:T(8,128)S(1)} %add.82), channel_id=1, source_target_pairs={{0,6},{1,7},{2,4},{3,5},{4,2},{5,3},{6,0},{7,1},{8,14},{9,15},{10,... | collective-permute-start | bytes 49160 | tf_op jit(solution)/shard_map/ppermute | solution.py:356
  94.0 5.2 %collective-permute-start.25 = (f32[32,128]{1,0:T(8,128)S(1)}, f32[32,128]{1,0:T(8,128)S(1)}, u32[]{:S(2)}, u32[]{:S(2)}) collective-permute-start(f32[32,128]{1,0:T(8,128)S(1)} %add.82), channel_id=1, source_target_pairs={{0,4},{1,5},{2,6},{3,7},{4,0},{5,1},{6,2},{7,3},{8,12},{9,13},{10,... | collective-permute-start | bytes 49160 | tf_op jit(solution)/shard_map/ppermute | solution.py:356
  95.9 3.7 %collective-permute-start.24 = (f32[32,128]{1,0:T(8,128)S(1)}, f32[32,128]{1,0:T(8,128)S(1)}, u32[]{:S(2)}, u32[]{:S(2)}) collective-permute-start(f32[32,128]{1,0:T(8,128)S(1)} %add.82), channel_id=1, source_target_pairs={{0,2},{1,3},{2,0},{3,1},{4,6},{5,7},{6,4},{7,5},{8,10},{9,11},{10,... | collective-permute-start | bytes 49160 | tf_op jit(solution)/shard_map/ppermute | solution.py:356
  99.7 4.9 %collective-permute-start.29 = (f32[32,128]{1,0:T(8,128)S(1)}, f32[32,128]{1,0:T(8,128)S(1)}, u32[]{:S(2)}, u32[]{:S(2)}) collective-permute-start(f32[32,128]{1,0:T(8,128)S(1)} %add_add_fusion.2), channel_id=1, source_target_pairs={{0,24},{1,25},{2,26},{3,27},{4,28},{5,29},{6,30},{7,31},{8,16},{9,... | collective-permute-start | bytes 49160 | tf_op jit(solution)/shard_map/ppermute | solution.py:356
  99.7 5.3 %collective-permute-start.28 = (f32[32,128]{1,0:T(8,128)S(1)}, f32[32,128]{1,0:T(8,128)S(1)}, u32[]{:S(2)}, u32[]{:S(2)}) collective-permute-start(f32[32,128]{1,0:T(8,128)S(1)} %add_add_fusion.2), channel_id=1, source_target_pairs={{0,16},{1,17},{2,18},{3,19},{4,20},{5,21},{6,22},{7,23},{8,24},{9,... | collective-permute-start | bytes 49160 | tf_op jit(solution)/shard_map/ppermute | solution.py:356
  100.9 4.8 %collective-permute-start.27 = (f32[32,128]{1,0:T(8,128)S(1)}, f32[32,128]{1,0:T(8,128)S(1)}, u32[]{:S(2)}, u32[]{:S(2)}) collective-permute-start(f32[32,128]{1,0:T(8,128)S(1)} %add_add_fusion.2), channel_id=1, source_target_pairs={{0,8},{1,9},{2,10},{3,11},{4,12},{5,13},{6,14},{7,15},{8,0},{9,1},... | collective-permute-start | bytes 49160 | tf_op jit(solution)/shard_map/ppermute | solution.py:356
  105.7 4.9 %collective-permute-start.32 = (f32[32,128]{1,0:T(8,128)S(1)}, f32[32,128]{1,0:T(8,128)S(1)}, u32[]{:S(2)}, u32[]{:S(2)}) collective-permute-start(f32[32,128]{1,0:T(8,128)S(1)} %add_add_fusion.1), channel_id=1, source_target_pairs={{0,96},{1,97},{2,98},{3,99},{4,100},{5,101},{6,102},{7,103},{8,104... | collective-permute-start | bytes 49160 | tf_op jit(solution)/shard_map/ppermute | solution.py:356
  106.2 5.2 %collective-permute-start.31 = (f32[32,128]{1,0:T(8,128)S(1)}, f32[32,128]{1,0:T(8,128)S(1)}, u32[]{:S(2)}, u32[]{:S(2)}) collective-permute-start(f32[32,128]{1,0:T(8,128)S(1)} %add_add_fusion.1), channel_id=1, source_target_pairs={{0,64},{1,65},{2,66},{3,67},{4,68},{5,69},{6,70},{7,71},{8,72},{9,... | collective-permute-start | bytes 49160 | tf_op jit(solution)/shard_map/ppermute | solution.py:356
  106.2 5.5 %collective-permute-start.30 = (f32[32,128]{1,0:T(8,128)S(1)}, f32[32,128]{1,0:T(8,128)S(1)}, u32[]{:S(2)}, u32[]{:S(2)}) collective-permute-start(f32[32,128]{1,0:T(8,128)S(1)} %add_add_fusion.1), channel_id=1, source_target_pairs={{0,32},{1,33},{2,34},{3,35},{4,36},{5,37},{6,38},{7,39},{8,40},{9,... | collective-permute-start | bytes 49160 | tf_op jit(solution)/shard_map/ppermute | solution.py:356

commit v6 on v5

--- a/solution.py
+++ b/solution.py
@@ -13,9 +13,9 @@
 SLOTS = 4
 EIG = 64
 NNB = 16
-BAND = ((-2, 0), (1, 2), (-4, 0), (3, 2))
+BAND = ((2, 0), (-1, 2), (4, 0), (-3, 2))
 ROUTES = ((BAND[2], BAND[3]), (BAND[0], BAND[1]))
-ONWARD = ((-2, 0), (2, 0))
+ONWARD = ((2, 0), (-2, 0))
 EXTRA = 2 * NNB
 ROUNDS = (((0, 1),), ((0, 2), (1, 0), (1, 2)), ((2, 0), (4, 0), (6, 0)), ((8, 0), (16, 0), (24, 0)))
 FOLDED = 2.0 * math.log2(math.e) / F
@@ -94,7 +94,7 @@
 
 def pack_kernel(half, sub, features, scales, lists, first, second):
     at = pl.multiple_of(sub[0] * ROWS, 128)
-    scale = jnp.concatenate([scales[:, pl.ds(at, ROWS)], jnp.ones((1, ROWS), jnp.float32)], axis=1)
+    scale = jnp.concatenate([scales[pl.ds(at, ROWS)].reshape(1, ROWS), jnp.ones((1, ROWS), jnp.float32)], axis=1)
     scale = jnp.broadcast_to(scale, (NNB, 2 * ROWS)).astype(jnp.bfloat16)
     for out, chosen in ((first, BAND[0::2]), (second, BAND[1::2])):
         out[:ROWS, :] = features[...]
@@ -126,7 +126,7 @@
         own_scale = moving[ROWS + NNB :, :ROWS].astype(jnp.float32)[0:1]
     else:
         pieces = [jnp.zeros((32, ROWS), jnp.float32)]
-        own_scale = scales[:, pl.ds(pl.multiple_of(me * ROWS, 128), ROWS)]
+        own_scale = scales[pl.ds(pl.multiple_of(me * ROWS, 128), ROWS)].reshape(1, ROWS)
     stacked = jnp.concatenate(
         pieces + [FOLDED / own_scale, jnp.zeros((95, ROWS), jnp.float32)], axis=0
     )
@@ -156,7 +156,7 @@
             low = low | jnp.where(same, first[m : m + 1, :], 0)
             high = high | jnp.where(same, second[m : m + 1, :], 0)
         norm = 0.5 * norms[slot : slot + 1, :]
-        scale = 1.0 / scales[:, pl.ds(start, ROWS)]
+        scale = 1.0 / scales[pl.ds(start, ROWS)].reshape(1, ROWS)
         row_sum = jnp.zeros((8, ROWS), jnp.float32)
         step = 32
         for at in range(0, ROWS, step):
@@ -260,7 +260,7 @@
     total_rows = ROWS * lax.axis_size("blk") * lax.axis_size("sub")
     sub_arg = sub.reshape(1)
 
-    block_scales = scales.astype(jnp.float32)[None, :]
+    block_scales = scales.astype(jnp.float32)
     own_lists = lax.dynamic_slice_in_dim(neighbor_lists, sub * ROWS, ROWS, axis=2)
     first, second = call(
         functools.partial(pack_kernel, half),

time: 114 us -> 113 us (level)
  waiting for transfers between devices: 48.2 us -> 40.7 us
  starting transfers between devices: 44.2 us -> 51 us
    ppermute x19, waiting for transfers between devices: 30.2 us -> 18.8 us  [moved(): return lax.ppermute(value, ('blk', 'sub'), pairs)]
    ppermute x19, starting transfers between devices: 27.3 us -> 31.8 us  [moved(): return lax.ppermute(value, ('blk', 'sub'), pairs)]
    ppermute x4, waiting for transfers between devices: 9.6 us -> 11.7 us  [routed(): outs.append(lax.ppermute(part, ('blk', 'sub'), pairs))]
    ppermute x10, waiting for transfers between devices: 8.41 us -> 10.2 us  [local(): parts.append(lax.ppermute(gram, ('blk', 'sub'), pairs))]
    ppermute x4, starting transfers between devices: 4.49 us -> 6.05 us  [routed(): outs.append(lax.ppermute(part, ('blk', 'sub'), pairs))]
  transfers between devices with their start and end apart: 33 -> 33, of which waited for: 26 -> 22; matrix products, arithmetic and copies ran while one was open for 0% -> 0% of each run, Pallas kernels for 12% -> 12%
where the time goes in v6:
time: 113 us
  starting transfers between devices  51 us (45%)
  waiting for transfers between devices  40.7 us (36%)
  Pallas kernels  18.4 us (16%)
  local copies, waits for them, and re-layouts  2.06 us (2%)
    ppermute x19, starting transfers between devices, moved(): return lax.ppermute(value, ('blk', 'sub'), pairs)  31.8 us
    ppermute x19, waiting for transfers between devices, moved(): return lax.ppermute(value, ('blk', 'sub'), pairs)  18.8 us
    pallas_call x10, Pallas kernels, run(): pl.pallas_call(body, grid=(1,), out_shape=outs, in_specs=list(specs) if s...  18.4 us
    ppermute x10, starting transfers between devices, local(): parts.append(lax.ppermute(gram, ('blk', 'sub'), pairs))  13.1 us
    ppermute x4, waiting for transfers between devices, routed(): outs.append(lax.ppermute(part, ('blk', 'sub'), pairs))  11.7 us
    ppermute x10, waiting for transfers between devices, local(): parts.append(lax.ppermute(gram, ('blk', 'sub'), pairs))  10.2 us
    ppermute x4, starting transfers between devices, routed(): outs.append(lax.ppermute(part, ('blk', 'sub'), pairs))  6.05 us
  transfers between devices with their start and end apart: 33, of which 22 were waited for; matrix products, arithmetic and copies ran while one was open for 0% of the time, Pallas kernels for 12%

profile of v6, /device:TPU:0, one launch (start us, length us, event | category | flops | bytes accessed | tf_op | source)
XLA Modules:
  0.0 113.3 jit_solution(7767302688190794242)
XLA Ops:
  0.0 0.8 convert_element_type.15.scales.refs_6_
  0.8 0.9 constant_dynamic-slice_fusion.lists
  1.7 0.0 copy-start.1
  1.7 1.1 copy-done.1
  2.8 0.1 shard_map.46
  2.9 1.7 %collective-permute-start.1 = (bf16[384,768]{1,0:T(8,128)(2,1)S(1)}, bf16[384,768]{1,0:T(8,128)(2,1)S(1)}, u32[]{:S(2)}, u32[]{:S(2)}) collective-permute-start(bf16[384,768]{1,0:T(8,128)(2,1)S(1)} %copy-done.1), channel_id=1, source_target_pairs={{0,2},{1,3},{2,0},{3,1},{4,6},{5,7},{6,4},{7,5},{8,10},{9,11},{10,... | collective-permute-start | bytes 1769480 | tf_op jit(solution)/shard_map/ppermute | solution.py:33
  4.6 1.5 %collective-permute-start.3 = (bf16[416,768]{1,0:T(8,128)(2,1)S(1)}, bf16[416,768]{1,0:T(8,128)(2,1)S(1)}, u32[]{:S(2)}, u32[]{:S(2)}) collective-permute-start(bf16[416,768]{1,0:T(8,128)(2,1)S(1)} %get-tuple-element.41), channel_id=1, source_target_pairs={{0,8},{1,9},{2,10},{3,11},{4,12},{5,13},{6,14},{7,15},{8,16},{9,17... | collective-permute-start | bytes 1916936 | tf_op jit(solution)/shard_map/ppermute | solution.py:33
  6.1 6.4 %collective-permute-start.4 = (bf16[416,768]{1,0:T(8,128)(2,1)S(1)}, bf16[416,768]{1,0:T(8,128)(2,1)S(1)}, u32[]{:S(2)}, u32[]{:S(2)}) collective-permute-start(bf16[416,768]{1,0:T(8,128)(2,1)S(1)} %get-tuple-element.42), channel_id=1, source_target_pairs={{0,126},{1,127},{2,124},{3,125},{4,2},{5,3},{6,0},{7,1},{8,6},{9,7... | collective-permute-start | bytes 1916936 | tf_op jit(solution)/shard_map/ppermute | solution.py:33
  12.5 5.5 %collective-permute-done.1.f2.refs_2_ = bf16[384,768]{1,0:T(8,128)(2,1)S(1)} collective-permute-done((bf16[384,768]{1,0:T(8,128)(2,1)S(1)}, bf16[384,768]{1,0:T(8,128)(2,1)S(1)}, u32[]{:S(2)}, u32[]{:S(2)}) %collective-permute-start.1) | collective-permute-done | bytes 589856 | tf_op jit(solution)/shard_map/ppermute | solution.py:33
  18.0 2.0 %collective-permute-done.2.f3.refs_3_ = bf16[384,768]{1,0:T(8,128)(2,1)S(1)} collective-permute-done((bf16[384,768]{1,0:T(8,128)(2,1)S(1)}, bf16[384,768]{1,0:T(8,128)(2,1)S(1)}, u32[]{:S(2)}, u32[]{:S(2)}) %collective-permute-start.2) | collective-permute-done | bytes 589856 | tf_op jit(solution)/shard_map/ppermute | solution.py:33
  20.0 3.2 %shard_map.47 = (bf16[384,1536]{1,0:T(8,128)(2,1)S(1)}, f32[4,384]{1,0:T(4,128)S(1)}, f32[1,384]{1,0:T(1,128)S(1)}, f32[4,384]{1,0:T(4,128)S(1)}) custom-call(s32[1]{0:T(128)} %bitcast.sub, bf16[384,768]{1,0:T(8,128)(2,1)S(1)} %copy-done.1, bf16[384,768]{1,0:T(8,128)(2,1)S(1)} %collective-permute-done.f1.refs_1_, ...), custom_call_target="tpu_custom_call" | custom-call | flops 1000 | bytes 1000 | tf_op jit(solution)/shard_map/pallas_call | solution.py:56
  23.2 1.8 %collective-permute-done.3.refs_4_ = bf16[416,768]{1,0:T(8,128)(2,1)S(1)} collective-permute-done((bf16[416,768]{1,0:T(8,128)(2,1)S(1)}, bf16[416,768]{1,0:T(8,128)(2,1)S(1)}, u32[]{:S(2)}, u32[]{:S(2)}) %collective-permute-start.3) | collective-permute-done | bytes 639008 | tf_op jit(solution)/shard_map/ppermute | solution.py:33
  25.0 0.9 collective-permute-done.4.refs_4_
  25.9 5.3 %collective-permute-start.5 = (bf16[416,768]{1,0:T(8,128)(2,1)S(1)}, bf16[416,768]{1,0:T(8,128)(2,1)S(1)}, u32[]{:S(2)}, u32[]{:S(2)}) collective-permute-start(bf16[416,768]{1,0:T(8,128)(2,1)S(1)} %collective-permute-done.4.refs_4_), channel_id=1, source_target_pairs={{0,120},{1,121},{2,122},{3,123},{4,124},{5,125},{6,126},{7,127},{8... | collective-permute-start | bytes 1916936 | tf_op jit(solution)/shard_map/ppermute | solution.py:33
  31.2 2.4 %shard_map.48 = (bf16[384,1536]{1,0:T(8,128)(2,1)S(1)}, f32[4,384]{1,0:T(4,128)S(1)}, f32[1,384]{1,0:T(1,128)S(1)}) custom-call(s32[1]{0:T(128)} %bitcast.sub, bf16[384,768]{1,0:T(8,128)(2,1)S(1)} %copy-done.1, bf16[384,768]{1,0:T(8,128)(2,1)S(1)} %collective-permute-done.f1.refs_1_, bf16[384,768]{1,0:T(8,128)(2,1)S(1)} %collective-permute-done.1.f2.refs_2_, ...), custom_call_target="tpu_custom_call" | custom-call | flops 1000 | bytes 1000 | tf_op jit(solution)/shard_map/pallas_call | solution.py:56
  33.6 0.6 collective-permute-start.7
  34.2 2.4 %shard_map.49 = (bf16[384,1536]{1,0:T(8,128)(2,1)S(1)}, f32[4,384]{1,0:T(4,128)S(1)}, f32[1,384]{1,0:T(1,128)S(1)}) custom-call(s32[1]{0:T(128)} %bitcast.sub, bf16[384,768]{1,0:T(8,128)(2,1)S(1)} %copy-done.1, bf16[384,768]{1,0:T(8,128)(2,1)S(1)} %collective-permute-done.f1.refs_1_, bf16[384,768]{1,0:T(8,128)(2,1)S(1)} %collective-permute-done.1.f2.refs_2_, ...), custom_call_target="tpu_custom_call" | custom-call | flops 1000 | bytes 1000 | tf_op jit(solution)/shard_map/pallas_call | solution.py:56
  36.6 4.9 %collective-permute-start.8 = (f32[1,384]{1,0:T(1,128)S(1)}, f32[1,384]{1,0:T(1,128)S(1)}, u32[]{:S(2)}, u32[]{:S(2)}) collective-permute-start(f32[1,384]{1,0:T(1,128)S(1)} %get-tuple-element.53), channel_id=1, source_target_pairs={{0,6},{1,7},{2,4},{3,5},{4,10},{5,11},{6,8},{7,9},{8,14},{9,15},{1... | collective-permute-start | bytes 4616 | tf_op jit(solution)/shard_map/ppermute | solution.py:33
  41.5 2.9 %collective-permute-done.6.refs_4_ = bf16[416,768]{1,0:T(8,128)(2,1)S(1)} collective-permute-done((bf16[416,768]{1,0:T(8,128)(2,1)S(1)}, bf16[416,768]{1,0:T(8,128)(2,1)S(1)}, u32[]{:S(2)}, u32[]{:S(2)}) %collective-permute-start.6) | collective-permute-done | bytes 639008 | tf_op jit(solution)/shard_map/ppermute | solution.py:33
  44.4 2.3 %shard_map.50 = (bf16[384,1536]{1,0:T(8,128)(2,1)S(1)}, f32[4,384]{1,0:T(4,128)S(1)}, f32[1,384]{1,0:T(1,128)S(1)}) custom-call(s32[1]{0:T(128)} %bitcast.sub, bf16[384,768]{1,0:T(8,128)(2,1)S(1)} %copy-done.1, bf16[384,768]{1,0:T(8,128)(2,1)S(1)} %collective-permute-done.f1.refs_1_, bf16[384,768]{1,0:T(8,128)(2,1)S(1)} %collective-permute-done.1.f2.refs_2_, ...), custom_call_target="tpu_custom_call" | custom-call | flops 1000 | bytes 1000 | tf_op jit(solution)/shard_map/pallas_call | solution.py:56
  46.7 0.3 collective-permute-done.8.refs_9_
  47.0 2.4 %shard_map.51 = (bf16[384,1536]{1,0:T(8,128)(2,1)S(1)}, f32[4,384]{1,0:T(4,128)S(1)}, f32[1,384]{1,0:T(1,128)S(1)}) custom-call(s32[1]{0:T(128)} %bitcast.sub, bf16[384,768]{1,0:T(8,128)(2,1)S(1)} %copy-done.1, bf16[384,768]{1,0:T(8,128)(2,1)S(1)} %collective-permute-done.f1.refs_1_, bf16[384,768]{1,0:T(8,128)(2,1)S(1)} %collective-permute-done.1.f2.refs_2_, ...), custom_call_target="tpu_custom_call" | custom-call | flops 4000000000 | bytes 1000 | tf_op jit(solution)/shard_map/pallas_call | solution.py:56
  49.4 1.5 %collective-permute-start.9 = (f32[2,384]{1,0:T(2,128)S(1)}, f32[2,384]{1,0:T(2,128)S(1)}, u32[]{:S(2)}, u32[]{:S(2)}) collective-permute-start(f32[2,384]{1,0:T(2,128)S(1)} %slice.43), channel_id=1, source_target_pairs={{0,2},{1,3},{2,0},{3,1},{4,6},{5,7},{6,4},{7,5},{8,10},{9,11},{10,... | collective-permute-start | bytes 9224 | tf_op jit(solution)/shard_map/ppermute | solution.py:33
  50.8 5.9 %collective-permute-start.11 = (f32[1,384]{1,0:T(1,128)S(1)}, f32[1,384]{1,0:T(1,128)S(1)}, u32[]{:S(2)}, u32[]{:S(2)}) collective-permute-start(f32[1,384]{1,0:T(1,128)S(1)} %get-tuple-element.56), channel_id=1, source_target_pairs={{0,112},{1,113},{2,114},{3,115},{4,116},{5,117},{6,118},{7,119},{8... | collective-permute-start | bytes 4616 | tf_op jit(solution)/shard_map/ppermute | solution.py:33
  56.7 0.1 collective-permute-start.10
  56.8 3.3 %collective-permute-done.12 = f32[1,384]{1,0:T(1,128)S(1)} collective-permute-done((f32[1,384]{1,0:T(1,128)S(1)}, f32[1,384]{1,0:T(1,128)S(1)}, u32[]{:S(2)}, u32[]{:S(2)}) %collective-permute-start.12) | collective-permute-done | bytes 1568 | tf_op jit(solution)/shard_map/ppermute | solution.py:33
  60.2 0.1 collective-permute-start.13
  60.3 1.2 %collective-permute-done.13.x1 = bf16[64,384]{1,0:T(8,128)(2,1)S(1)} collective-permute-done((bf16[64,384]{1,0:T(8,128)(2,1)S(1)}, bf16[64,384]{1,0:T(8,128)(2,1)S(1)}, u32[]{:S(2)}, u32[]{:S(2)}) %collective-permute-start.13) | collective-permute-done | bytes 49184 | tf_op jit(solution)/shard_map/ppermute | solution.py:33
  61.5 0.1 collective-permute-start.15
  61.6 2.0 %collective-permute-start.14 = (bf16[128,384]{1,0:T(8,128)(2,1)S(1)}, bf16[128,384]{1,0:T(8,128)(2,1)S(1)}, u32[]{:S(2)}, u32[]{:S(2)}) collective-permute-start(bf16[128,384]{1,0:T(8,128)(2,1)S(1)} %pad_maximum_fusion), channel_id=1, source_target_pairs={{0,16},{1,119},{2,18},{3,117},{4,20},{5,123},{6,22},{7,121},{8,24}... | collective-permute-start | bytes 294920 | tf_op jit(solution)/shard_map/ppermute | solution.py:45
  63.5 0.7 collective-permute-start.17
  64.2 6.0 %collective-permute-done.15.two = bf16[128,384]{1,0:T(8,128)(2,1)S(1)} collective-permute-done((bf16[128,384]{1,0:T(8,128)(2,1)S(1)}, bf16[128,384]{1,0:T(8,128)(2,1)S(1)}, u32[]{:S(2)}, u32[]{:S(2)}) %collective-permute-start.15) | collective-permute-done | bytes 98336 | tf_op jit(solution)/shard_map/ppermute | solution.py:45
  70.2 1.3 %collective-permute-done.14.one = bf16[128,384]{1,0:T(8,128)(2,1)S(1)} collective-permute-done((bf16[128,384]{1,0:T(8,128)(2,1)S(1)}, bf16[128,384]{1,0:T(8,128)(2,1)S(1)}, u32[]{:S(2)}, u32[]{:S(2)}) %collective-permute-start.14) | collective-permute-done | bytes 98336 | tf_op jit(solution)/shard_map/ppermute | solution.py:45
  71.5 0.1 collective-permute-start.16
  71.7 1.8 %shard_map.52 = (f32[64,384]{1,0:T(8,128)S(1)}, bf16[128,384]{1,0:T(8,128)(2,1)S(1)}, bf16[128,384]{1,0:T(8,128)(2,1)S(1)}) custom-call(s32[1]{0:T(128)} %bitcast.sub, bf16[64,384]{1,0:T(8,128)(2,1)S(1)} %multiply_convert_fusion.x0, bf16[64,384]{1,0:T(8,128)(2,1)S(1)} %collective-permute-done.13.x1, bf16[128,384]{1,0:T(8,128)(2,1)S(1)} %collective-permute-done.17.far, ...), custom_call_target="tpu_custom_call" | custom-call | flops 1000 | bytes 1000 | tf_op jit(solution)/shard_map/pallas_call | solution.py:56
  73.5 0.6 collective-permute-start.19
  74.1 1.0 shard_map.53
  75.1 0.9 collective-permute-start.18
  76.0 2.6 %collective-permute-start.20 = (bf16[128,384]{1,0:T(8,128)(2,1)S(1)}, bf16[128,384]{1,0:T(8,128)(2,1)S(1)}, u32[]{:S(2)}, u32[]{:S(2)}) collective-permute-start(bf16[128,384]{1,0:T(8,128)(2,1)S(1)} %pad_maximum_fusion.2), channel_id=1, source_target_pairs={{0,112},{1,15},{2,114},{3,13},{4,116},{5,19},{6,118},{7,17},{8,120... | collective-permute-start | bytes 294920 | tf_op jit(solution)/shard_map/ppermute | solution.py:45
  78.6 1.5 %collective-permute-start.21 = (bf16[128,384]{1,0:T(8,128)(2,1)S(1)}, bf16[128,384]{1,0:T(8,128)(2,1)S(1)}, u32[]{:S(2)}, u32[]{:S(2)}) collective-permute-start(bf16[128,384]{1,0:T(8,128)(2,1)S(1)} %pad_maximum_fusion.3), channel_id=1, source_target_pairs={{0,120},{1,7},{2,122},{3,5},{4,124},{5,11},{6,126},{7,9},{8,0},{9,... | collective-permute-start | bytes 294920 | tf_op jit(solution)/shard_map/ppermute | solution.py:45
  80.1 2.2 %collective-permute-done.20.one = bf16[128,384]{1,0:T(8,128)(2,1)S(1)} collective-permute-done((bf16[128,384]{1,0:T(8,128)(2,1)S(1)}, bf16[128,384]{1,0:T(8,128)(2,1)S(1)}, u32[]{:S(2)}, u32[]{:S(2)}) %collective-permute-start.20) | collective-permute-done | bytes 98336 | tf_op jit(solution)/shard_map/ppermute | solution.py:45
  82.2 2.3 %collective-permute-done.21.two = bf16[128,384]{1,0:T(8,128)(2,1)S(1)} collective-permute-done((bf16[128,384]{1,0:T(8,128)(2,1)S(1)}, bf16[128,384]{1,0:T(8,128)(2,1)S(1)}, u32[]{:S(2)}, u32[]{:S(2)}) %collective-permute-start.21) | collective-permute-done | bytes 98336 | tf_op jit(solution)/shard_map/ppermute | solution.py:45
  84.6 1.7 %collective-permute-start.22 = (f32[64,384]{1,0:T(8,128)S(1)}, f32[64,384]{1,0:T(8,128)S(1)}, u32[]{:S(2)}, u32[]{:S(2)}) collective-permute-start(f32[64,384]{1,0:T(8,128)S(1)} %convert_add_fusion), channel_id=1, source_target_pairs={{0,1},{1,0},{2,3},{3,2},{4,5},{5,4},{6,7},{7,6},{8,9},{9,8},{10,11... | collective-permute-start | bytes 294920 | tf_op jit(solution)/shard_map/ppermute | solution.py:33
  86.2 0.9 collective-permute-done.22.swapped
  87.2 0.3 shard_map.54
  87.5 0.4 collective-permute-start.23
  87.9 0.8 collective-permute-done.23
  88.7 0.9 collective-permute-start.26
  89.7 1.8 %collective-permute-start.25 = (f32[32,128]{1,0:T(8,128)S(1)}, f32[32,128]{1,0:T(8,128)S(1)}, u32[]{:S(2)}, u32[]{:S(2)}) collective-permute-start(f32[32,128]{1,0:T(8,128)S(1)} %add.82), channel_id=1, source_target_pairs={{0,4},{1,5},{2,6},{3,7},{4,0},{5,1},{6,2},{7,3},{8,12},{9,13},{10,... | collective-permute-start | bytes 49160 | tf_op jit(solution)/shard_map/ppermute | solution.py:356
  91.5 1.4 %collective-permute-start.24 = (f32[32,128]{1,0:T(8,128)S(1)}, f32[32,128]{1,0:T(8,128)S(1)}, u32[]{:S(2)}, u32[]{:S(2)}) collective-permute-start(f32[32,128]{1,0:T(8,128)S(1)} %add.82), channel_id=1, source_target_pairs={{0,2},{1,3},{2,0},{3,1},{4,6},{5,7},{6,4},{7,5},{8,10},{9,11},{10,... | collective-permute-start | bytes 49160 | tf_op jit(solution)/shard_map/ppermute | solution.py:356
  92.8 0.9 collective-permute-done.26
  93.7 1.2 %collective-permute-done.25 = f32[32,128]{1,0:T(8,128)S(1)} collective-permute-done((f32[32,128]{1,0:T(8,128)S(1)}, f32[32,128]{1,0:T(8,128)S(1)}, u32[]{:S(2)}, u32[]{:S(2)}) %collective-permute-start.25) | collective-permute-done | bytes 16416 | tf_op jit(solution)/shard_map/ppermute | solution.py:356
  94.9 0.3 collective-permute-done.24
  95.2 1.3 %collective-permute-start.29 = (f32[32,128]{1,0:T(8,128)S(1)}, f32[32,128]{1,0:T(8,128)S(1)}, u32[]{:S(2)}, u32[]{:S(2)}) collective-permute-start(f32[32,128]{1,0:T(8,128)S(1)} %add_add_fusion.2), channel_id=1, source_target_pairs={{0,24},{1,25},{2,26},{3,27},{4,28},{5,29},{6,30},{7,31},{8,16},{9,... | collective-permute-start | bytes 49160 | tf_op jit(solution)/shard_map/ppermute | solution.py:356
  96.5 1.8 %collective-permute-start.28 = (f32[32,128]{1,0:T(8,128)S(1)}, f32[32,128]{1,0:T(8,128)S(1)}, u32[]{:S(2)}, u32[]{:S(2)}) collective-permute-start(f32[32,128]{1,0:T(8,128)S(1)} %add_add_fusion.2), channel_id=1, source_target_pairs={{0,16},{1,17},{2,18},{3,19},{4,20},{5,21},{6,22},{7,23},{8,24},{9,... | collective-permute-start | bytes 49160 | tf_op jit(solution)/shard_map/ppermute | solution.py:356
  98.3 1.0 collective-permute-start.27
  99.3 0.9 collective-permute-done.29
  100.2 1.6 %collective-permute-done.28 = f32[32,128]{1,0:T(8,128)S(1)} collective-permute-done((f32[32,128]{1,0:T(8,128)S(1)}, f32[32,128]{1,0:T(8,128)S(1)}, u32[]{:S(2)}, u32[]{:S(2)}) %collective-permute-start.28) | collective-permute-done | bytes 16416 | tf_op jit(solution)/shard_map/ppermute | solution.py:356
  101.7 0.3 collective-permute-done.27
  102.0 3.6 %collective-permute-start.32 = (f32[32,128]{1,0:T(8,128)S(1)}, f32[32,128]{1,0:T(8,128)S(1)}, u32[]{:S(2)}, u32[]{:S(2)}) collective-permute-start(f32[32,128]{1,0:T(8,128)S(1)} %add_add_fusion.1), channel_id=1, source_target_pairs={{0,96},{1,97},{2,98},{3,99},{4,100},{5,101},{6,102},{7,103},{8,104... | collective-permute-start | bytes 49160 | tf_op jit(solution)/shard_map/ppermute | solution.py:356
  105.7 0.9 collective-permute-start.30
  106.6 0.8 collective-permute-done.32
  107.4 3.5 %collective-permute-done.31 = f32[32,128]{1,0:T(8,128)S(1)} collective-permute-done((f32[32,128]{1,0:T(8,128)S(1)}, f32[32,128]{1,0:T(8,128)S(1)}, u32[]{:S(2)}, u32[]{:S(2)}) %collective-permute-start.31) | collective-permute-done | bytes 16416 | tf_op jit(solution)/shard_map/ppermute | solution.py:356
  110.9 2.4 %shard_map.55 = f32[64,384]{1,0:T(8,128)} custom-call(f32[32,128]{1,0:T(8,128)S(1)} %add_add_fusion.gram, f32[64,384]{1,0:T(8,128)S(1)} %get-tuple-element.70.mixed), custom_call_target="tpu_custom_call" | custom-call | flops 1000 | bytes 1000 | tf_op jit(solution)/shard_map/pallas_call | solution.py:56
  (38 shorter events, 0.2 us)
Async XLA Ops:
  0.0 20.0 %copy-start = (s32[9,16,1536]{2,1,0:T(8,128)S(1)}, s32[9,16,1536]{2,1,0:T(8,128)}, u32[]{:S(2)}) copy-start(s32[9,16,1536]{2,1,0:T(8,128)} %refs_10_) | copy-start | bytes 2654212
  1.7 1.1 copy-start.1
  2.9 15.1 %collective-permute-start.1 = (bf16[384,768]{1,0:T(8,128)(2,1)S(1)}, bf16[384,768]{1,0:T(8,128)(2,1)S(1)}, u32[]{:S(2)}, u32[]{:S(2)}) collective-permute-start(bf16[384,768]{1,0:T(8,128)(2,1)S(1)} %copy-done.1), channel_id=1, source_target_pairs={{0,2},{1,3},{2,0},{3,1},{4,6},{5,7},{6,4},{7,5},{8,10},{9,11},{10,... | collective-permute-start | bytes 1769480 | tf_op jit(solution)/shard_map/ppermute | solution.py:33
  4.6 20.3 %collective-permute-start.3 = (bf16[416,768]{1,0:T(8,128)(2,1)S(1)}, bf16[416,768]{1,0:T(8,128)(2,1)S(1)}, u32[]{:S(2)}, u32[]{:S(2)}) collective-permute-start(bf16[416,768]{1,0:T(8,128)(2,1)S(1)} %get-tuple-element.41), channel_id=1, source_target_pairs={{0,8},{1,9},{2,10},{3,11},{4,12},{5,13},{6,14},{7,15},{8,16},{9,17... | collective-permute-start | bytes 1916936 | tf_op jit(solution)/shard_map/ppermute | solution.py:33
  6.1 19.7 %collective-permute-start.4 = (bf16[416,768]{1,0:T(8,128)(2,1)S(1)}, bf16[416,768]{1,0:T(8,128)(2,1)S(1)}, u32[]{:S(2)}, u32[]{:S(2)}) collective-permute-start(bf16[416,768]{1,0:T(8,128)(2,1)S(1)} %get-tuple-element.42), channel_id=1, source_target_pairs={{0,126},{1,127},{2,124},{3,125},{4,2},{5,3},{6,0},{7,1},{8,6},{9,7... | collective-permute-start | bytes 1916936 | tf_op jit(solution)/shard_map/ppermute | solution.py:33
  12.5 5.5 %collective-permute-start = (bf16[384,768]{1,0:T(8,128)(2,1)S(1)}, bf16[384,768]{1,0:T(8,128)(2,1)S(1)}, u32[]{:S(2)}, u32[]{:S(2)}) collective-permute-start(bf16[384,768]{1,0:T(8,128)(2,1)S(1)} %copy-done.1), channel_id=1, source_target_pairs={{0,1},{1,0},{2,3},{3,2},{4,5},{5,4},{6,7},{7,6},{8,9},{9,8},{10,11... | collective-permute-start | bytes 1769480 | tf_op jit(solution)/shard_map/ppermute | solution.py:33
  18.0 2.0 %collective-permute-start.2 = (bf16[384,768]{1,0:T(8,128)(2,1)S(1)}, bf16[384,768]{1,0:T(8,128)(2,1)S(1)}, u32[]{:S(2)}, u32[]{:S(2)}) collective-permute-start(bf16[384,768]{1,0:T(8,128)(2,1)S(1)} %collective-permute-done.1.f2.refs_2_), channel_id=1, source_target_pairs={{0,1},{1,0},{2,3},{3,2},{4,5},{5,4},{6,7},{7,6},{8,9},{9,8},{10,11... | collective-permute-start | bytes 1769480 | tf_op jit(solution)/shard_map/ppermute | solution.py:33
  25.8 18.5 %collective-permute-start.6 = (bf16[416,768]{1,0:T(8,128)(2,1)S(1)}, bf16[416,768]{1,0:T(8,128)(2,1)S(1)}, u32[]{:S(2)}, u32[]{:S(2)}) collective-permute-start(bf16[416,768]{1,0:T(8,128)(2,1)S(1)} %collective-permute-done.3.refs_4_), channel_id=1, source_target_pairs={{0,8},{1,9},{2,10},{3,11},{4,12},{5,13},{6,14},{7,15},{8,16},{9,17... | collective-permute-start | bytes 1916936 | tf_op jit(solution)/shard_map/ppermute | solution.py:33
  25.9 21.1 %collective-permute-start.5 = (bf16[416,768]{1,0:T(8,128)(2,1)S(1)}, bf16[416,768]{1,0:T(8,128)(2,1)S(1)}, u32[]{:S(2)}, u32[]{:S(2)}) collective-permute-start(bf16[416,768]{1,0:T(8,128)(2,1)S(1)} %collective-permute-done.4.refs_4_), channel_id=1, source_target_pairs={{0,120},{1,121},{2,122},{3,123},{4,124},{5,125},{6,126},{7,127},{8... | collective-permute-start | bytes 1916936 | tf_op jit(solution)/shard_map/ppermute | solution.py:33
  33.6 13.1 %collective-permute-start.7 = (f32[1,384]{1,0:T(1,128)S(1)}, f32[1,384]{1,0:T(1,128)S(1)}, u32[]{:S(2)}, u32[]{:S(2)}) collective-permute-start(f32[1,384]{1,0:T(1,128)S(1)} %get-tuple-element.52), channel_id=1, source_target_pairs={{0,120},{1,121},{2,122},{3,123},{4,124},{5,125},{6,126},{7,127},{8... | collective-permute-start | bytes 4616 | tf_op jit(solution)/shard_map/ppermute | solution.py:33
  36.6 10.4 %collective-permute-start.8 = (f32[1,384]{1,0:T(1,128)S(1)}, f32[1,384]{1,0:T(1,128)S(1)}, u32[]{:S(2)}, u32[]{:S(2)}) collective-permute-start(f32[1,384]{1,0:T(1,128)S(1)} %get-tuple-element.53), channel_id=1, source_target_pairs={{0,6},{1,7},{2,4},{3,5},{4,10},{5,11},{6,8},{7,9},{8,14},{9,15},{1... | collective-permute-start | bytes 4616 | tf_op jit(solution)/shard_map/ppermute | solution.py:33
  47.0 13.2 %copy-start.2 = (f32[64,384]{1,0:T(8,128)S(1)}, f32[64,384]{1,0:T(8,128)}, u32[]{:S(2)}) copy-start(f32[64,384]{1,0:T(8,128)} %own.1) | copy-start | bytes 294916
  49.4 7.3 %collective-permute-start.9 = (f32[2,384]{1,0:T(2,128)S(1)}, f32[2,384]{1,0:T(2,128)S(1)}, u32[]{:S(2)}, u32[]{:S(2)}) collective-permute-start(f32[2,384]{1,0:T(2,128)S(1)} %slice.43), channel_id=1, source_target_pairs={{0,2},{1,3},{2,0},{3,1},{4,6},{5,7},{6,4},{7,5},{8,10},{9,11},{10,... | collective-permute-start | bytes 9224 | tf_op jit(solution)/shard_map/ppermute | solution.py:33
  50.8 9.3 %collective-permute-start.12 = (f32[1,384]{1,0:T(1,128)S(1)}, f32[1,384]{1,0:T(1,128)S(1)}, u32[]{:S(2)}, u32[]{:S(2)}) collective-permute-start(f32[1,384]{1,0:T(1,128)S(1)} %get-tuple-element.57), channel_id=1, source_target_pairs={{0,14},{1,15},{2,12},{3,13},{4,18},{5,19},{6,16},{7,17},{8,22},{9,... | collective-permute-start | bytes 4616 | tf_op jit(solution)/shard_map/ppermute | solution.py:33
  50.8 9.3 %collective-permute-start.11 = (f32[1,384]{1,0:T(1,128)S(1)}, f32[1,384]{1,0:T(1,128)S(1)}, u32[]{:S(2)}, u32[]{:S(2)}) collective-permute-start(f32[1,384]{1,0:T(1,128)S(1)} %get-tuple-element.56), channel_id=1, source_target_pairs={{0,112},{1,113},{2,114},{3,115},{4,116},{5,117},{6,118},{7,119},{8... | collective-permute-start | bytes 4616 | tf_op jit(solution)/shard_map/ppermute | solution.py:33
  56.7 3.4 %collective-permute-start.10 = (f32[1,384]{1,0:T(1,128)S(1)}, f32[1,384]{1,0:T(1,128)S(1)}, u32[]{:S(2)}, u32[]{:S(2)}) collective-permute-start(f32[1,384]{1,0:T(1,128)S(1)} %slice.57), channel_id=1, source_target_pairs={{0,1},{1,0},{2,3},{3,2},{4,5},{5,4},{6,7},{7,6},{8,9},{9,8},{10,11... | collective-permute-start | bytes 4616 | tf_op jit(solution)/shard_map/ppermute | solution.py:33
  60.2 1.3 %collective-permute-start.13 = (bf16[64,384]{1,0:T(8,128)(2,1)S(1)}, bf16[64,384]{1,0:T(8,128)(2,1)S(1)}, u32[]{:S(2)}, u32[]{:S(2)}) collective-permute-start(bf16[64,384]{1,0:T(8,128)(2,1)S(1)} %multiply_convert_fusion.x0), channel_id=1, source_target_pairs={{0,1},{1,0},{2,3},{3,2},{4,5},{5,4},{6,7},{7,6},{8,9},{9,8},{10,11... | collective-permute-start | bytes 147464 | tf_op jit(solution)/shard_map/ppermute | solution.py:33
  61.5 8.7 %collective-permute-start.15 = (bf16[128,384]{1,0:T(8,128)(2,1)S(1)}, bf16[128,384]{1,0:T(8,128)(2,1)S(1)}, u32[]{:S(2)}, u32[]{:S(2)}) collective-permute-start(bf16[128,384]{1,0:T(8,128)(2,1)S(1)} %pad_maximum_fusion), channel_id=1, source_target_pairs={{0,8},{1,127},{2,10},{3,125},{4,12},{5,3},{6,14},{7,1},{8,16},{9,7... | collective-permute-start | bytes 294920 | tf_op jit(solution)/shard_map/ppermute | solution.py:45
  61.6 9.9 %collective-permute-start.14 = (bf16[128,384]{1,0:T(8,128)(2,1)S(1)}, bf16[128,384]{1,0:T(8,128)(2,1)S(1)}, u32[]{:S(2)}, u32[]{:S(2)}) collective-permute-start(bf16[128,384]{1,0:T(8,128)(2,1)S(1)} %pad_maximum_fusion), channel_id=1, source_target_pairs={{0,16},{1,119},{2,18},{3,117},{4,20},{5,123},{6,22},{7,121},{8,24}... | collective-permute-start | bytes 294920 | tf_op jit(solution)/shard_map/ppermute | solution.py:45
  63.5 8.1 %collective-permute-start.17 = (bf16[128,384]{1,0:T(8,128)(2,1)S(1)}, bf16[128,384]{1,0:T(8,128)(2,1)S(1)}, u32[]{:S(2)}, u32[]{:S(2)}) collective-permute-start(bf16[128,384]{1,0:T(8,128)(2,1)S(1)} %pad_maximum_fusion), channel_id=1, source_target_pairs={{0,2},{1,3},{2,0},{3,1},{4,6},{5,7},{6,4},{7,5},{8,10},{9,11},{10,... | collective-permute-start | bytes 294920 | tf_op jit(solution)/shard_map/ppermute | solution.py:33
  71.5 2.5 %collective-permute-start.16 = (bf16[128,384]{1,0:T(8,128)(2,1)S(1)}, bf16[128,384]{1,0:T(8,128)(2,1)S(1)}, u32[]{:S(2)}, u32[]{:S(2)}) collective-permute-start(bf16[128,384]{1,0:T(8,128)(2,1)S(1)} %pad_maximum_fusion.1), channel_id=1, source_target_pairs={{0,1},{1,0},{2,3},{3,2},{4,5},{5,4},{6,7},{7,6},{8,9},{9,8},{10,11... | collective-permute-start | bytes 294920 | tf_op jit(solution)/shard_map/ppermute | solution.py:33
  73.5 2.5 %collective-permute-start.19 = (bf16[128,384]{1,0:T(8,128)(2,1)S(1)}, bf16[128,384]{1,0:T(8,128)(2,1)S(1)}, u32[]{:S(2)}, u32[]{:S(2)}) collective-permute-start(bf16[128,384]{1,0:T(8,128)(2,1)S(1)} %get-tuple-element.68), channel_id=1, source_target_pairs={{0,1},{1,0},{2,3},{3,2},{4,5},{5,4},{6,7},{7,6},{8,9},{9,8},{10,11... | collective-permute-start | bytes 294920 | tf_op jit(solution)/shard_map/ppermute | solution.py:33
  75.1 5.0 %collective-permute-start.18 = (bf16[64,768]{1,0:T(8,128)(2,1)S(1)}, bf16[64,768]{1,0:T(8,128)(2,1)S(1)}, u32[]{:S(2)}, u32[]{:S(2)}) collective-permute-start(bf16[64,768]{1,0:T(8,128)(2,1)S(1)} %get-tuple-element.66), channel_id=1, source_target_pairs={{0,2},{1,3},{2,0},{3,1},{4,6},{5,7},{6,4},{7,5},{8,10},{9,11},{10,... | collective-permute-start | bytes 294920 | tf_op jit(solution)/shard_map/ppermute | solution.py:33
  76.0 6.2 %collective-permute-start.20 = (bf16[128,384]{1,0:T(8,128)(2,1)S(1)}, bf16[128,384]{1,0:T(8,128)(2,1)S(1)}, u32[]{:S(2)}, u32[]{:S(2)}) collective-permute-start(bf16[128,384]{1,0:T(8,128)(2,1)S(1)} %pad_maximum_fusion.2), channel_id=1, source_target_pairs={{0,112},{1,15},{2,114},{3,13},{4,116},{5,19},{6,118},{7,17},{8,120... | collective-permute-start | bytes 294920 | tf_op jit(solution)/shard_map/ppermute | solution.py:45
  78.6 5.9 %collective-permute-start.21 = (bf16[128,384]{1,0:T(8,128)(2,1)S(1)}, bf16[128,384]{1,0:T(8,128)(2,1)S(1)}, u32[]{:S(2)}, u32[]{:S(2)}) collective-permute-start(bf16[128,384]{1,0:T(8,128)(2,1)S(1)} %pad_maximum_fusion.3), channel_id=1, source_target_pairs={{0,120},{1,7},{2,122},{3,5},{4,124},{5,11},{6,126},{7,9},{8,0},{9,... | collective-permute-start | bytes 294920 | tf_op jit(solution)/shard_map/ppermute | solution.py:45
  84.6 2.6 %collective-permute-start.22 = (f32[64,384]{1,0:T(8,128)S(1)}, f32[64,384]{1,0:T(8,128)S(1)}, u32[]{:S(2)}, u32[]{:S(2)}) collective-permute-start(f32[64,384]{1,0:T(8,128)S(1)} %convert_add_fusion), channel_id=1, source_target_pairs={{0,1},{1,0},{2,3},{3,2},{4,5},{5,4},{6,7},{7,6},{8,9},{9,8},{10,11... | collective-permute-start | bytes 294920 | tf_op jit(solution)/shard_map/ppermute | solution.py:33
  87.5 1.2 %collective-permute-start.23 = (f32[32,128]{1,0:T(8,128)S(1)}, f32[32,128]{1,0:T(8,128)S(1)}, u32[]{:S(2)}, u32[]{:S(2)}) collective-permute-start(f32[32,128]{1,0:T(8,128)S(1)} %get-tuple-element.69), channel_id=1, source_target_pairs={{0,1},{1,0},{2,3},{3,2},{4,5},{5,4},{6,7},{7,6},{8,9},{9,8},{10,11... | collective-permute-start | bytes 49160 | tf_op jit(solution)/shard_map/ppermute | solution.py:356
  88.7 5.0 %collective-permute-start.26 = (f32[32,128]{1,0:T(8,128)S(1)}, f32[32,128]{1,0:T(8,128)S(1)}, u32[]{:S(2)}, u32[]{:S(2)}) collective-permute-start(f32[32,128]{1,0:T(8,128)S(1)} %add.82), channel_id=1, source_target_pairs={{0,6},{1,7},{2,4},{3,5},{4,2},{5,3},{6,0},{7,1},{8,14},{9,15},{10,... | collective-permute-start | bytes 49160 | tf_op jit(solution)/shard_map/ppermute | solution.py:356
  89.7 5.2 %collective-permute-start.25 = (f32[32,128]{1,0:T(8,128)S(1)}, f32[32,128]{1,0:T(8,128)S(1)}, u32[]{:S(2)}, u32[]{:S(2)}) collective-permute-start(f32[32,128]{1,0:T(8,128)S(1)} %add.82), channel_id=1, source_target_pairs={{0,4},{1,5},{2,6},{3,7},{4,0},{5,1},{6,2},{7,3},{8,12},{9,13},{10,... | collective-permute-start | bytes 49160 | tf_op jit(solution)/shard_map/ppermute | solution.py:356
  91.5 3.7 %collective-permute-start.24 = (f32[32,128]{1,0:T(8,128)S(1)}, f32[32,128]{1,0:T(8,128)S(1)}, u32[]{:S(2)}, u32[]{:S(2)}) collective-permute-start(f32[32,128]{1,0:T(8,128)S(1)} %add.82), channel_id=1, source_target_pairs={{0,2},{1,3},{2,0},{3,1},{4,6},{5,7},{6,4},{7,5},{8,10},{9,11},{10,... | collective-permute-start | bytes 49160 | tf_op jit(solution)/shard_map/ppermute | solution.py:356
  95.2 5.0 %collective-permute-start.29 = (f32[32,128]{1,0:T(8,128)S(1)}, f32[32,128]{1,0:T(8,128)S(1)}, u32[]{:S(2)}, u32[]{:S(2)}) collective-permute-start(f32[32,128]{1,0:T(8,128)S(1)} %add_add_fusion.2), channel_id=1, source_target_pairs={{0,24},{1,25},{2,26},{3,27},{4,28},{5,29},{6,30},{7,31},{8,16},{9,... | collective-permute-start | bytes 49160 | tf_op jit(solution)/shard_map/ppermute | solution.py:356
  96.5 5.2 %collective-permute-start.28 = (f32[32,128]{1,0:T(8,128)S(1)}, f32[32,128]{1,0:T(8,128)S(1)}, u32[]{:S(2)}, u32[]{:S(2)}) collective-permute-start(f32[32,128]{1,0:T(8,128)S(1)} %add_add_fusion.2), channel_id=1, source_target_pairs={{0,16},{1,17},{2,18},{3,19},{4,20},{5,21},{6,22},{7,23},{8,24},{9,... | collective-permute-start | bytes 49160 | tf_op jit(solution)/shard_map/ppermute | solution.py:356
  98.3 3.7 %collective-permute-start.27 = (f32[32,128]{1,0:T(8,128)S(1)}, f32[32,128]{1,0:T(8,128)S(1)}, u32[]{:S(2)}, u32[]{:S(2)}) collective-permute-start(f32[32,128]{1,0:T(8,128)S(1)} %add_add_fusion.2), channel_id=1, source_target_pairs={{0,8},{1,9},{2,10},{3,11},{4,12},{5,13},{6,14},{7,15},{8,0},{9,1},... | collective-permute-start | bytes 49160 | tf_op jit(solution)/shard_map/ppermute | solution.py:356
  102.0 5.3 %collective-permute-start.32 = (f32[32,128]{1,0:T(8,128)S(1)}, f32[32,128]{1,0:T(8,128)S(1)}, u32[]{:S(2)}, u32[]{:S(2)}) collective-permute-start(f32[32,128]{1,0:T(8,128)S(1)} %add_add_fusion.1), channel_id=1, source_target_pairs={{0,96},{1,97},{2,98},{3,99},{4,100},{5,101},{6,102},{7,103},{8,104... | collective-permute-start | bytes 49160 | tf_op jit(solution)/shard_map/ppermute | solution.py:356
  105.7 5.2 %collective-permute-start.31 = (f32[32,128]{1,0:T(8,128)S(1)}, f32[32,128]{1,0:T(8,128)S(1)}, u32[]{:S(2)}, u32[]{:S(2)}) collective-permute-start(f32[32,128]{1,0:T(8,128)S(1)} %add_add_fusion.1), channel_id=1, source_target_pairs={{0,64},{1,65},{2,66},{3,67},{4,68},{5,69},{6,70},{7,71},{8,72},{9,... | collective-permute-start | bytes 49160 | tf_op jit(solution)/shard_map/ppermute | solution.py:356
  105.7 5.2 %collective-permute-start.30 = (f32[32,128]{1,0:T(8,128)S(1)}, f32[32,128]{1,0:T(8,128)S(1)}, u32[]{:S(2)}, u32[]{:S(2)}) collective-permute-start(f32[32,128]{1,0:T(8,128)S(1)} %add_add_fusion.1), channel_id=1, source_target_pairs={{0,32},{1,33},{2,34},{3,35},{4,36},{5,37},{6,38},{7,39},{8,40},{9,... | collective-permute-start | bytes 49160 | tf_op jit(solution)/shard_map/ppermute | solution.py:356

commit v7 on v6

--- a/solution.py
+++ b/solution.py
@@ -318,7 +318,6 @@
     pair = jnp.concatenate([scaled_low, moved(scaled_low, 0, 1)], axis=0)
     one, two = routed((pair, pair))
     far = moved(pair, 0, 2)
-    swapped = moved(jnp.concatenate([one[EIG:], two[EIG:]], axis=0), 0, 1)
 
     with_sub = (SMEM,) + (VMEM,) * 8
     z_outs = (f32(EIG, ROWS), bf16(2 * EIG, ROWS), bf16(2 * EIG, ROWS))
@@ -333,7 +332,8 @@
         ),
         back=True,
     )
-    swapped, _ = lax.optimization_barrier((swapped, z0))
+    one, two, _ = lax.optimization_barrier((one, two, z0))
+    swapped = moved(jnp.concatenate([one[EIG:], two[EIG:]], axis=0), 0, 1)
     y_outs = (f32(EIG, 2 * ROWS), bf16(EIG, 2 * ROWS))
     kept, sent = call(row_kernel, y_outs, specs=with_sub + (VMEM,))(
         sub_arg, scaled_low, one, two, swapped, *tiles

time: 113 us -> 113 us (level)
  waiting for transfers between devices: 40.7 us -> 38.8 us
  starting transfers between devices: 51 us -> 52.3 us
    ppermute x4, waiting for transfers between devices: 11.7 us -> 7.73 us  [routed(): outs.append(lax.ppermute(part, ('blk', 'sub'), pairs))]
    ppermute x19, waiting for transfers between devices: 18.8 us -> 21.8 us  [moved(): return lax.ppermute(value, ('blk', 'sub'), pairs)]
  transfers between devices with their start and end apart: 33 -> 33, of which waited for: 22 -> 24; matrix products, arithmetic and copies ran while one was open for 0% -> 0% of each run, Pallas kernels for 12% -> 12%
where the time goes in v7:
time: 113 us
  starting transfers between devices  52.3 us (46%)
  waiting for transfers between devices  38.8 us (34%)
  Pallas kernels  18.4 us (16%)
  local copies, waits for them, and re-layouts  2.06 us (2%)
    ppermute x19, starting transfers between devices, moved(): return lax.ppermute(value, ('blk', 'sub'), pairs)  32.7 us
    ppermute x19, waiting for transfers between devices, moved(): return lax.ppermute(value, ('blk', 'sub'), pairs)  21.8 us
    pallas_call x10, Pallas kernels, run(): pl.pallas_call(body, grid=(1,), out_shape=outs, in_specs=list(specs) if s...  18.4 us
    ppermute x10, starting transfers between devices, local(): parts.append(lax.ppermute(gram, ('blk', 'sub'), pairs))  13.3 us
    ppermute x10, waiting for transfers between devices, local(): parts.append(lax.ppermute(gram, ('blk', 'sub'), pairs))  9.36 us
    ppermute x4, waiting for transfers between devices, routed(): outs.append(lax.ppermute(part, ('blk', 'sub'), pairs))  7.73 us
    ppermute x4, starting transfers between devices, routed(): outs.append(lax.ppermute(part, ('blk', 'sub'), pairs))  6.24 us
  transfers between devices with their start and end apart: 33, of which 24 were waited for; matrix products, arithmetic and copies ran while one was open for 0% of the time, Pallas kernels for 12%

profile of v7, /device:TPU:0, one launch (start us, length us, event | category | flops | bytes accessed | tf_op | source)
XLA Modules:
  0.0 112.7 jit_solution(1487152760419943546)
XLA Ops:
  0.0 0.8 convert_element_type.15.scales.refs_6_
  0.8 0.9 constant_dynamic-slice_fusion.lists
  1.7 1.1 copy-done.1
  2.8 0.1 shard_map.46
  2.9 1.7 %collective-permute-start.1 = (bf16[384,768]{1,0:T(8,128)(2,1)S(1)}, bf16[384,768]{1,0:T(8,128)(2,1)S(1)}, u32[]{:S(2)}, u32[]{:S(2)}) collective-permute-start(bf16[384,768]{1,0:T(8,128)(2,1)S(1)} %copy-done.1), channel_id=1, source_target_pairs={{0,2},{1,3},{2,0},{3,1},{4,6},{5,7},{6,4},{7,5},{8,10},{9,11},{10,... | collective-permute-start | bytes 1769480 | tf_op jit(solution)/shard_map/ppermute | solution.py:33
  4.6 1.5 %collective-permute-start.3 = (bf16[416,768]{1,0:T(8,128)(2,1)S(1)}, bf16[416,768]{1,0:T(8,128)(2,1)S(1)}, u32[]{:S(2)}, u32[]{:S(2)}) collective-permute-start(bf16[416,768]{1,0:T(8,128)(2,1)S(1)} %get-tuple-element.42), channel_id=1, source_target_pairs={{0,8},{1,9},{2,10},{3,11},{4,12},{5,13},{6,14},{7,15},{8,16},{9,17... | collective-permute-start | bytes 1916936 | tf_op jit(solution)/shard_map/ppermute | solution.py:33
  6.1 6.4 %collective-permute-start.4 = (bf16[416,768]{1,0:T(8,128)(2,1)S(1)}, bf16[416,768]{1,0:T(8,128)(2,1)S(1)}, u32[]{:S(2)}, u32[]{:S(2)}) collective-permute-start(bf16[416,768]{1,0:T(8,128)(2,1)S(1)} %get-tuple-element.43), channel_id=1, source_target_pairs={{0,126},{1,127},{2,124},{3,125},{4,2},{5,3},{6,0},{7,1},{8,6},{9,7... | collective-permute-start | bytes 1916936 | tf_op jit(solution)/shard_map/ppermute | solution.py:33
  12.5 5.5 %collective-permute-done.1.f2.refs_2_ = bf16[384,768]{1,0:T(8,128)(2,1)S(1)} collective-permute-done((bf16[384,768]{1,0:T(8,128)(2,1)S(1)}, bf16[384,768]{1,0:T(8,128)(2,1)S(1)}, u32[]{:S(2)}, u32[]{:S(2)}) %collective-permute-start.1) | collective-permute-done | bytes 589856 | tf_op jit(solution)/shard_map/ppermute | solution.py:33
  18.0 2.0 %collective-permute-done.2.f3.refs_3_ = bf16[384,768]{1,0:T(8,128)(2,1)S(1)} collective-permute-done((bf16[384,768]{1,0:T(8,128)(2,1)S(1)}, bf16[384,768]{1,0:T(8,128)(2,1)S(1)}, u32[]{:S(2)}, u32[]{:S(2)}) %collective-permute-start.2) | collective-permute-done | bytes 589856 | tf_op jit(solution)/shard_map/ppermute | solution.py:33
  20.0 3.2 %shard_map.47 = (bf16[384,1536]{1,0:T(8,128)(2,1)S(1)}, f32[4,384]{1,0:T(4,128)S(1)}, f32[1,384]{1,0:T(1,128)S(1)}, f32[4,384]{1,0:T(4,128)S(1)}) custom-call(s32[1]{0:T(128)} %bitcast.sub, bf16[384,768]{1,0:T(8,128)(2,1)S(1)} %copy-done.1, bf16[384,768]{1,0:T(8,128)(2,1)S(1)} %collective-permute-done.f1.refs_1_, ...), custom_call_target="tpu_custom_call" | custom-call | flops 1000 | bytes 1000 | tf_op jit(solution)/shard_map/pallas_call | solution.py:56
  23.2 1.8 %collective-permute-done.3.refs_4_ = bf16[416,768]{1,0:T(8,128)(2,1)S(1)} collective-permute-done((bf16[416,768]{1,0:T(8,128)(2,1)S(1)}, bf16[416,768]{1,0:T(8,128)(2,1)S(1)}, u32[]{:S(2)}, u32[]{:S(2)}) %collective-permute-start.3) | collective-permute-done | bytes 639008 | tf_op jit(solution)/shard_map/ppermute | solution.py:33
  25.0 0.9 collective-permute-done.4.refs_4_
  25.9 5.3 %collective-permute-start.5 = (bf16[416,768]{1,0:T(8,128)(2,1)S(1)}, bf16[416,768]{1,0:T(8,128)(2,1)S(1)}, u32[]{:S(2)}, u32[]{:S(2)}) collective-permute-start(bf16[416,768]{1,0:T(8,128)(2,1)S(1)} %collective-permute-done.4.refs_4_), channel_id=1, source_target_pairs={{0,120},{1,121},{2,122},{3,123},{4,124},{5,125},{6,126},{7,127},{8... | collective-permute-start | bytes 1916936 | tf_op jit(solution)/shard_map/ppermute | solution.py:33
  31.2 2.4 %shard_map.48 = (bf16[384,1536]{1,0:T(8,128)(2,1)S(1)}, f32[4,384]{1,0:T(4,128)S(1)}, f32[1,384]{1,0:T(1,128)S(1)}) custom-call(s32[1]{0:T(128)} %bitcast.sub, bf16[384,768]{1,0:T(8,128)(2,1)S(1)} %copy-done.1, bf16[384,768]{1,0:T(8,128)(2,1)S(1)} %collective-permute-done.f1.refs_1_, bf16[384,768]{1,0:T(8,128)(2,1)S(1)} %collective-permute-done.1.f2.refs_2_, ...), custom_call_target="tpu_custom_call" | custom-call | flops 1000 | bytes 1000 | tf_op jit(solution)/shard_map/pallas_call | solution.py:56
  33.6 0.6 collective-permute-start.7
  34.2 2.4 %shard_map.49 = (bf16[384,1536]{1,0:T(8,128)(2,1)S(1)}, f32[4,384]{1,0:T(4,128)S(1)}, f32[1,384]{1,0:T(1,128)S(1)}) custom-call(s32[1]{0:T(128)} %bitcast.sub, bf16[384,768]{1,0:T(8,128)(2,1)S(1)} %copy-done.1, bf16[384,768]{1,0:T(8,128)(2,1)S(1)} %collective-permute-done.f1.refs_1_, bf16[384,768]{1,0:T(8,128)(2,1)S(1)} %collective-permute-done.1.f2.refs_2_, ...), custom_call_target="tpu_custom_call" | custom-call | flops 1000 | bytes 1000 | tf_op jit(solution)/shard_map/pallas_call | solution.py:56
  36.6 4.9 %collective-permute-start.8 = (f32[1,384]{1,0:T(1,128)S(1)}, f32[1,384]{1,0:T(1,128)S(1)}, u32[]{:S(2)}, u32[]{:S(2)}) collective-permute-start(f32[1,384]{1,0:T(1,128)S(1)} %get-tuple-element.54), channel_id=1, source_target_pairs={{0,6},{1,7},{2,4},{3,5},{4,10},{5,11},{6,8},{7,9},{8,14},{9,15},{1... | collective-permute-start | bytes 4616 | tf_op jit(solution)/shard_map/ppermute | solution.py:33
  41.5 2.9 %collective-permute-done.6.refs_4_ = bf16[416,768]{1,0:T(8,128)(2,1)S(1)} collective-permute-done((bf16[416,768]{1,0:T(8,128)(2,1)S(1)}, bf16[416,768]{1,0:T(8,128)(2,1)S(1)}, u32[]{:S(2)}, u32[]{:S(2)}) %collective-permute-start.6) | collective-permute-done | bytes 639008 | tf_op jit(solution)/shard_map/ppermute | solution.py:33
  44.4 2.3 %shard_map.50 = (bf16[384,1536]{1,0:T(8,128)(2,1)S(1)}, f32[4,384]{1,0:T(4,128)S(1)}, f32[1,384]{1,0:T(1,128)S(1)}) custom-call(s32[1]{0:T(128)} %bitcast.sub, bf16[384,768]{1,0:T(8,128)(2,1)S(1)} %copy-done.1, bf16[384,768]{1,0:T(8,128)(2,1)S(1)} %collective-permute-done.f1.refs_1_, bf16[384,768]{1,0:T(8,128)(2,1)S(1)} %collective-permute-done.1.f2.refs_2_, ...), custom_call_target="tpu_custom_call" | custom-call | flops 1000 | bytes 1000 | tf_op jit(solution)/shard_map/pallas_call | solution.py:56
  46.7 0.3 collective-permute-done.8.refs_9_
  47.0 2.4 %shard_map.51 = (bf16[384,1536]{1,0:T(8,128)(2,1)S(1)}, f32[4,384]{1,0:T(4,128)S(1)}, f32[1,384]{1,0:T(1,128)S(1)}) custom-call(s32[1]{0:T(128)} %bitcast.sub, bf16[384,768]{1,0:T(8,128)(2,1)S(1)} %copy-done.1, bf16[384,768]{1,0:T(8,128)(2,1)S(1)} %collective-permute-done.f1.refs_1_, bf16[384,768]{1,0:T(8,128)(2,1)S(1)} %collective-permute-done.1.f2.refs_2_, ...), custom_call_target="tpu_custom_call" | custom-call | flops 4000000000 | bytes 1000 | tf_op jit(solution)/shard_map/pallas_call | solution.py:56
  49.4 1.5 %collective-permute-start.9 = (f32[2,384]{1,0:T(2,128)S(1)}, f32[2,384]{1,0:T(2,128)S(1)}, u32[]{:S(2)}, u32[]{:S(2)}) collective-permute-start(f32[2,384]{1,0:T(2,128)S(1)} %slice.43), channel_id=1, source_target_pairs={{0,2},{1,3},{2,0},{3,1},{4,6},{5,7},{6,4},{7,5},{8,10},{9,11},{10,... | collective-permute-start | bytes 9224 | tf_op jit(solution)/shard_map/ppermute | solution.py:33
  50.8 5.9 %collective-permute-start.11 = (f32[1,384]{1,0:T(1,128)S(1)}, f32[1,384]{1,0:T(1,128)S(1)}, u32[]{:S(2)}, u32[]{:S(2)}) collective-permute-start(f32[1,384]{1,0:T(1,128)S(1)} %get-tuple-element.57), channel_id=1, source_target_pairs={{0,112},{1,113},{2,114},{3,115},{4,116},{5,117},{6,118},{7,119},{8... | collective-permute-start | bytes 4616 | tf_op jit(solution)/shard_map/ppermute | solution.py:33
  56.8 3.3 %collective-permute-done.12 = f32[1,384]{1,0:T(1,128)S(1)} collective-permute-done((f32[1,384]{1,0:T(1,128)S(1)}, f32[1,384]{1,0:T(1,128)S(1)}, u32[]{:S(2)}, u32[]{:S(2)}) %collective-permute-start.12) | collective-permute-done | bytes 1568 | tf_op jit(solution)/shard_map/ppermute | solution.py:33
  60.2 0.1 collective-permute-start.13
  60.3 1.2 %collective-permute-done.13.x1 = bf16[64,384]{1,0:T(8,128)(2,1)S(1)} collective-permute-done((bf16[64,384]{1,0:T(8,128)(2,1)S(1)}, bf16[64,384]{1,0:T(8,128)(2,1)S(1)}, u32[]{:S(2)}, u32[]{:S(2)}) %collective-permute-start.13) | collective-permute-done | bytes 49184 | tf_op jit(solution)/shard_map/ppermute | solution.py:33
  61.5 0.1 collective-permute-start.16
  61.6 0.6 collective-permute-start.15
  62.2 2.0 %collective-permute-start.14 = (bf16[128,384]{1,0:T(8,128)(2,1)S(1)}, bf16[128,384]{1,0:T(8,128)(2,1)S(1)}, u32[]{:S(2)}, u32[]{:S(2)}) collective-permute-start(bf16[128,384]{1,0:T(8,128)(2,1)S(1)} %pad_maximum_fusion), channel_id=1, source_target_pairs={{0,16},{1,119},{2,18},{3,117},{4,20},{5,123},{6,22},{7,121},{8,24}... | collective-permute-start | bytes 294920 | tf_op jit(solution)/shard_map/ppermute | solution.py:45
  64.2 2.2 %collective-permute-done.16.far = bf16[128,384]{1,0:T(8,128)(2,1)S(1)} collective-permute-done((bf16[128,384]{1,0:T(8,128)(2,1)S(1)}, bf16[128,384]{1,0:T(8,128)(2,1)S(1)}, u32[]{:S(2)}, u32[]{:S(2)}) %collective-permute-start.16) | collective-permute-done | bytes 98336 | tf_op jit(solution)/shard_map/ppermute | solution.py:33
  66.4 1.8 %shard_map.52 = (f32[64,384]{1,0:T(8,128)S(1)}, bf16[128,384]{1,0:T(8,128)(2,1)S(1)}, bf16[128,384]{1,0:T(8,128)(2,1)S(1)}) custom-call(s32[1]{0:T(128)} %bitcast.sub, bf16[64,384]{1,0:T(8,128)(2,1)S(1)} %multiply_convert_fusion.x0, bf16[64,384]{1,0:T(8,128)(2,1)S(1)} %collective-permute-done.13.x1, bf16[128,384]{1,0:T(8,128)(2,1)S(1)} %collective-permute-done.16.far, ...), custom_call_target="tpu_custom_call" | custom-call | flops 1000 | bytes 1000 | tf_op jit(solution)/shard_map/pallas_call | solution.py:56
  68.3 2.0 %collective-permute-done.15.two = bf16[128,384]{1,0:T(8,128)(2,1)S(1)} collective-permute-done((bf16[128,384]{1,0:T(8,128)(2,1)S(1)}, bf16[128,384]{1,0:T(8,128)(2,1)S(1)}, u32[]{:S(2)}, u32[]{:S(2)}) %collective-permute-start.15) | collective-permute-done | bytes 98336 | tf_op jit(solution)/shard_map/ppermute | solution.py:45
  70.3 2.1 %collective-permute-done.14.one = bf16[128,384]{1,0:T(8,128)(2,1)S(1)} collective-permute-done((bf16[128,384]{1,0:T(8,128)(2,1)S(1)}, bf16[128,384]{1,0:T(8,128)(2,1)S(1)}, u32[]{:S(2)}, u32[]{:S(2)}) %collective-permute-start.14) | collective-permute-done | bytes 98336 | tf_op jit(solution)/shard_map/ppermute | solution.py:45
  72.4 0.1 collective-permute-start.17
  72.5 0.5 collective-permute-start.19
  73.0 0.8 collective-permute-done.17.got
  73.8 1.0 shard_map.53
  74.8 1.3 %collective-permute-start.18 = (bf16[64,768]{1,0:T(8,128)(2,1)S(1)}, bf16[64,768]{1,0:T(8,128)(2,1)S(1)}, u32[]{:S(2)}, u32[]{:S(2)}) collective-permute-start(bf16[64,768]{1,0:T(8,128)(2,1)S(1)} %get-tuple-element.68), channel_id=1, source_target_pairs={{0,2},{1,3},{2,0},{3,1},{4,6},{5,7},{6,4},{7,5},{8,10},{9,11},{10,... | collective-permute-start | bytes 294920 | tf_op jit(solution)/shard_map/ppermute | solution.py:33
  76.1 2.5 %collective-permute-start.20 = (bf16[128,384]{1,0:T(8,128)(2,1)S(1)}, bf16[128,384]{1,0:T(8,128)(2,1)S(1)}, u32[]{:S(2)}, u32[]{:S(2)}) collective-permute-start(bf16[128,384]{1,0:T(8,128)(2,1)S(1)} %pad_maximum_fusion.2), channel_id=1, source_target_pairs={{0,112},{1,15},{2,114},{3,13},{4,116},{5,19},{6,118},{7,17},{8,120... | collective-permute-start | bytes 294920 | tf_op jit(solution)/shard_map/ppermute | solution.py:45
  78.7 1.1 collective-permute-start.21
  79.8 2.6 %collective-permute-done.20.one = bf16[128,384]{1,0:T(8,128)(2,1)S(1)} collective-permute-done((bf16[128,384]{1,0:T(8,128)(2,1)S(1)}, bf16[128,384]{1,0:T(8,128)(2,1)S(1)}, u32[]{:S(2)}, u32[]{:S(2)}) %collective-permute-start.20) | collective-permute-done | bytes 98336 | tf_op jit(solution)/shard_map/ppermute | solution.py:45
  82.3 1.1 collective-permute-done.21.two
  83.5 2.8 %collective-permute-start.22 = (f32[64,384]{1,0:T(8,128)S(1)}, f32[64,384]{1,0:T(8,128)S(1)}, u32[]{:S(2)}, u32[]{:S(2)}) collective-permute-start(f32[64,384]{1,0:T(8,128)S(1)} %convert_add_fusion), channel_id=1, source_target_pairs={{0,1},{1,0},{2,3},{3,2},{4,5},{5,4},{6,7},{7,6},{8,9},{9,8},{10,11... | collective-permute-start | bytes 294920 | tf_op jit(solution)/shard_map/ppermute | solution.py:33
  86.3 0.9 collective-permute-done.22.swapped
  87.3 0.3 shard_map.54
  87.6 0.4 collective-permute-start.23
  88.0 0.8 collective-permute-done.23
  88.8 0.2 collective-permute-start.26
  89.0 1.6 %collective-permute-start.25 = (f32[32,128]{1,0:T(8,128)S(1)}, f32[32,128]{1,0:T(8,128)S(1)}, u32[]{:S(2)}, u32[]{:S(2)}) collective-permute-start(f32[32,128]{1,0:T(8,128)S(1)} %add.82), channel_id=1, source_target_pairs={{0,4},{1,5},{2,6},{3,7},{4,0},{5,1},{6,2},{7,3},{8,12},{9,13},{10,... | collective-permute-start | bytes 49160 | tf_op jit(solution)/shard_map/ppermute | solution.py:356
  90.6 2.3 %collective-permute-start.24 = (f32[32,128]{1,0:T(8,128)S(1)}, f32[32,128]{1,0:T(8,128)S(1)}, u32[]{:S(2)}, u32[]{:S(2)}) collective-permute-start(f32[32,128]{1,0:T(8,128)S(1)} %add.82), channel_id=1, source_target_pairs={{0,2},{1,3},{2,0},{3,1},{4,6},{5,7},{6,4},{7,5},{8,10},{9,11},{10,... | collective-permute-start | bytes 49160 | tf_op jit(solution)/shard_map/ppermute | solution.py:356
  92.9 0.9 collective-permute-done.26
  93.8 0.5 collective-permute-done.25
  94.3 0.5 collective-permute-done.24
  94.8 0.1 collective-permute-start.29
  94.9 2.6 %collective-permute-start.28 = (f32[32,128]{1,0:T(8,128)S(1)}, f32[32,128]{1,0:T(8,128)S(1)}, u32[]{:S(2)}, u32[]{:S(2)}) collective-permute-start(f32[32,128]{1,0:T(8,128)S(1)} %add_add_fusion.2), channel_id=1, source_target_pairs={{0,16},{1,17},{2,18},{3,19},{4,20},{5,21},{6,22},{7,23},{8,24},{9,... | collective-permute-start | bytes 49160 | tf_op jit(solution)/shard_map/ppermute | solution.py:356
  97.5 1.4 %collective-permute-start.27 = (f32[32,128]{1,0:T(8,128)S(1)}, f32[32,128]{1,0:T(8,128)S(1)}, u32[]{:S(2)}, u32[]{:S(2)}) collective-permute-start(f32[32,128]{1,0:T(8,128)S(1)} %add_add_fusion.2), channel_id=1, source_target_pairs={{0,8},{1,9},{2,10},{3,11},{4,12},{5,13},{6,14},{7,15},{8,0},{9,1},... | collective-permute-start | bytes 49160 | tf_op jit(solution)/shard_map/ppermute | solution.py:356
  98.9 0.9 collective-permute-done.29
  99.8 0.4 collective-permute-done.28
  100.2 1.1 collective-permute-done.27
  101.3 3.8 %collective-permute-start.32 = (f32[32,128]{1,0:T(8,128)S(1)}, f32[32,128]{1,0:T(8,128)S(1)}, u32[]{:S(2)}, u32[]{:S(2)}) collective-permute-start(f32[32,128]{1,0:T(8,128)S(1)} %add_add_fusion.1), channel_id=1, source_target_pairs={{0,96},{1,97},{2,98},{3,99},{4,100},{5,101},{6,102},{7,103},{8,104... | collective-permute-start | bytes 49160 | tf_op jit(solution)/shard_map/ppermute | solution.py:356
  105.1 0.9 collective-permute-start.30
  106.0 0.8 collective-permute-done.32
  106.8 3.5 %collective-permute-done.31 = f32[32,128]{1,0:T(8,128)S(1)} collective-permute-done((f32[32,128]{1,0:T(8,128)S(1)}, f32[32,128]{1,0:T(8,128)S(1)}, u32[]{:S(2)}, u32[]{:S(2)}) %collective-permute-start.31) | collective-permute-done | bytes 16416 | tf_op jit(solution)/shard_map/ppermute | solution.py:356
  110.3 2.4 %shard_map.55 = f32[64,384]{1,0:T(8,128)} custom-call(f32[32,128]{1,0:T(8,128)S(1)} %add_add_fusion.gram, f32[64,384]{1,0:T(8,128)S(1)} %get-tuple-element.72.mixed), custom_call_target="tpu_custom_call" | custom-call | flops 1000 | bytes 1000 | tf_op jit(solution)/shard_map/pallas_call | solution.py:56
  (38 shorter events, 0.3 us)
Async XLA Ops:
  0.0 20.0 %copy-start = (s32[9,16,1536]{2,1,0:T(8,128)S(1)}, s32[9,16,1536]{2,1,0:T(8,128)}, u32[]{:S(2)}) copy-start(s32[9,16,1536]{2,1,0:T(8,128)} %refs_10_) | copy-start | bytes 2654212
  1.7 1.1 copy-start.1
  2.9 15.1 %collective-permute-start.1 = (bf16[384,768]{1,0:T(8,128)(2,1)S(1)}, bf16[384,768]{1,0:T(8,128)(2,1)S(1)}, u32[]{:S(2)}, u32[]{:S(2)}) collective-permute-start(bf16[384,768]{1,0:T(8,128)(2,1)S(1)} %copy-done.1), channel_id=1, source_target_pairs={{0,2},{1,3},{2,0},{3,1},{4,6},{5,7},{6,4},{7,5},{8,10},{9,11},{10,... | collective-permute-start | bytes 1769480 | tf_op jit(solution)/shard_map/ppermute | solution.py:33
  4.6 20.3 %collective-permute-start.3 = (bf16[416,768]{1,0:T(8,128)(2,1)S(1)}, bf16[416,768]{1,0:T(8,128)(2,1)S(1)}, u32[]{:S(2)}, u32[]{:S(2)}) collective-permute-start(bf16[416,768]{1,0:T(8,128)(2,1)S(1)} %get-tuple-element.42), channel_id=1, source_target_pairs={{0,8},{1,9},{2,10},{3,11},{4,12},{5,13},{6,14},{7,15},{8,16},{9,17... | collective-permute-start | bytes 1916936 | tf_op jit(solution)/shard_map/ppermute | solution.py:33
  6.1 19.7 %collective-permute-start.4 = (bf16[416,768]{1,0:T(8,128)(2,1)S(1)}, bf16[416,768]{1,0:T(8,128)(2,1)S(1)}, u32[]{:S(2)}, u32[]{:S(2)}) collective-permute-start(bf16[416,768]{1,0:T(8,128)(2,1)S(1)} %get-tuple-element.43), channel_id=1, source_target_pairs={{0,126},{1,127},{2,124},{3,125},{4,2},{5,3},{6,0},{7,1},{8,6},{9,7... | collective-permute-start | bytes 1916936 | tf_op jit(solution)/shard_map/ppermute | solution.py:33
  12.5 5.5 %collective-permute-start = (bf16[384,768]{1,0:T(8,128)(2,1)S(1)}, bf16[384,768]{1,0:T(8,128)(2,1)S(1)}, u32[]{:S(2)}, u32[]{:S(2)}) collective-permute-start(bf16[384,768]{1,0:T(8,128)(2,1)S(1)} %copy-done.1), channel_id=1, source_target_pairs={{0,1},{1,0},{2,3},{3,2},{4,5},{5,4},{6,7},{7,6},{8,9},{9,8},{10,11... | collective-permute-start | bytes 1769480 | tf_op jit(solution)/shard_map/ppermute | solution.py:33
  18.0 2.0 %collective-permute-start.2 = (bf16[384,768]{1,0:T(8,128)(2,1)S(1)}, bf16[384,768]{1,0:T(8,128)(2,1)S(1)}, u32[]{:S(2)}, u32[]{:S(2)}) collective-permute-start(bf16[384,768]{1,0:T(8,128)(2,1)S(1)} %collective-permute-done.1.f2.refs_2_), channel_id=1, source_target_pairs={{0,1},{1,0},{2,3},{3,2},{4,5},{5,4},{6,7},{7,6},{8,9},{9,8},{10,11... | collective-permute-start | bytes 1769480 | tf_op jit(solution)/shard_map/ppermute | solution.py:33
  25.8 18.5 %collective-permute-start.6 = (bf16[416,768]{1,0:T(8,128)(2,1)S(1)}, bf16[416,768]{1,0:T(8,128)(2,1)S(1)}, u32[]{:S(2)}, u32[]{:S(2)}) collective-permute-start(bf16[416,768]{1,0:T(8,128)(2,1)S(1)} %collective-permute-done.3.refs_4_), channel_id=1, source_target_pairs={{0,8},{1,9},{2,10},{3,11},{4,12},{5,13},{6,14},{7,15},{8,16},{9,17... | collective-permute-start | bytes 1916936 | tf_op jit(solution)/shard_map/ppermute | solution.py:33
  25.9 21.1 %collective-permute-start.5 = (bf16[416,768]{1,0:T(8,128)(2,1)S(1)}, bf16[416,768]{1,0:T(8,128)(2,1)S(1)}, u32[]{:S(2)}, u32[]{:S(2)}) collective-permute-start(bf16[416,768]{1,0:T(8,128)(2,1)S(1)} %collective-permute-done.4.refs_4_), channel_id=1, source_target_pairs={{0,120},{1,121},{2,122},{3,123},{4,124},{5,125},{6,126},{7,127},{8... | collective-permute-start | bytes 1916936 | tf_op jit(solution)/shard_map/ppermute | solution.py:33
  33.6 13.1 %collective-permute-start.7 = (f32[1,384]{1,0:T(1,128)S(1)}, f32[1,384]{1,0:T(1,128)S(1)}, u32[]{:S(2)}, u32[]{:S(2)}) collective-permute-start(f32[1,384]{1,0:T(1,128)S(1)} %get-tuple-element.53), channel_id=1, source_target_pairs={{0,120},{1,121},{2,122},{3,123},{4,124},{5,125},{6,126},{7,127},{8... | collective-permute-start | bytes 4616 | tf_op jit(solution)/shard_map/ppermute | solution.py:33
  36.6 10.4 %collective-permute-start.8 = (f32[1,384]{1,0:T(1,128)S(1)}, f32[1,384]{1,0:T(1,128)S(1)}, u32[]{:S(2)}, u32[]{:S(2)}) collective-permute-start(f32[1,384]{1,0:T(1,128)S(1)} %get-tuple-element.54), channel_id=1, source_target_pairs={{0,6},{1,7},{2,4},{3,5},{4,10},{5,11},{6,8},{7,9},{8,14},{9,15},{1... | collective-permute-start | bytes 4616 | tf_op jit(solution)/shard_map/ppermute | solution.py:33
  47.0 13.2 %copy-start.2 = (f32[64,384]{1,0:T(8,128)S(1)}, f32[64,384]{1,0:T(8,128)}, u32[]{:S(2)}) copy-start(f32[64,384]{1,0:T(8,128)} %own.1) | copy-start | bytes 294916
  49.4 7.3 %collective-permute-start.9 = (f32[2,384]{1,0:T(2,128)S(1)}, f32[2,384]{1,0:T(2,128)S(1)}, u32[]{:S(2)}, u32[]{:S(2)}) collective-permute-start(f32[2,384]{1,0:T(2,128)S(1)} %slice.43), channel_id=1, source_target_pairs={{0,2},{1,3},{2,0},{3,1},{4,6},{5,7},{6,4},{7,5},{8,10},{9,11},{10,... | collective-permute-start | bytes 9224 | tf_op jit(solution)/shard_map/ppermute | solution.py:33
  50.8 9.3 %collective-permute-start.12 = (f32[1,384]{1,0:T(1,128)S(1)}, f32[1,384]{1,0:T(1,128)S(1)}, u32[]{:S(2)}, u32[]{:S(2)}) collective-permute-start(f32[1,384]{1,0:T(1,128)S(1)} %get-tuple-element.58), channel_id=1, source_target_pairs={{0,14},{1,15},{2,12},{3,13},{4,18},{5,19},{6,16},{7,17},{8,22},{9,... | collective-permute-start | bytes 4616 | tf_op jit(solution)/shard_map/ppermute | solution.py:33
  50.8 9.3 %collective-permute-start.11 = (f32[1,384]{1,0:T(1,128)S(1)}, f32[1,384]{1,0:T(1,128)S(1)}, u32[]{:S(2)}, u32[]{:S(2)}) collective-permute-start(f32[1,384]{1,0:T(1,128)S(1)} %get-tuple-element.57), channel_id=1, source_target_pairs={{0,112},{1,113},{2,114},{3,115},{4,116},{5,117},{6,118},{7,119},{8... | collective-permute-start | bytes 4616 | tf_op jit(solution)/shard_map/ppermute | solution.py:33
  56.7 3.4 %collective-permute-start.10 = (f32[1,384]{1,0:T(1,128)S(1)}, f32[1,384]{1,0:T(1,128)S(1)}, u32[]{:S(2)}, u32[]{:S(2)}) collective-permute-start(f32[1,384]{1,0:T(1,128)S(1)} %slice.57), channel_id=1, source_target_pairs={{0,1},{1,0},{2,3},{3,2},{4,5},{5,4},{6,7},{7,6},{8,9},{9,8},{10,11... | collective-permute-start | bytes 4616 | tf_op jit(solution)/shard_map/ppermute | solution.py:33
  60.2 1.3 %collective-permute-start.13 = (bf16[64,384]{1,0:T(8,128)(2,1)S(1)}, bf16[64,384]{1,0:T(8,128)(2,1)S(1)}, u32[]{:S(2)}, u32[]{:S(2)}) collective-permute-start(bf16[64,384]{1,0:T(8,128)(2,1)S(1)} %multiply_convert_fusion.x0), channel_id=1, source_target_pairs={{0,1},{1,0},{2,3},{3,2},{4,5},{5,4},{6,7},{7,6},{8,9},{9,8},{10,11... | collective-permute-start | bytes 147464 | tf_op jit(solution)/shard_map/ppermute | solution.py:33
  61.5 4.9 %collective-permute-start.16 = (bf16[128,384]{1,0:T(8,128)(2,1)S(1)}, bf16[128,384]{1,0:T(8,128)(2,1)S(1)}, u32[]{:S(2)}, u32[]{:S(2)}) collective-permute-start(bf16[128,384]{1,0:T(8,128)(2,1)S(1)} %pad_maximum_fusion), channel_id=1, source_target_pairs={{0,2},{1,3},{2,0},{3,1},{4,6},{5,7},{6,4},{7,5},{8,10},{9,11},{10,... | collective-permute-start | bytes 294920 | tf_op jit(solution)/shard_map/ppermute | solution.py:33
  61.6 8.7 %collective-permute-start.15 = (bf16[128,384]{1,0:T(8,128)(2,1)S(1)}, bf16[128,384]{1,0:T(8,128)(2,1)S(1)}, u32[]{:S(2)}, u32[]{:S(2)}) collective-permute-start(bf16[128,384]{1,0:T(8,128)(2,1)S(1)} %pad_maximum_fusion), channel_id=1, source_target_pairs={{0,8},{1,127},{2,10},{3,125},{4,12},{5,3},{6,14},{7,1},{8,16},{9,7... | collective-permute-start | bytes 294920 | tf_op jit(solution)/shard_map/ppermute | solution.py:45
  62.2 10.1 %collective-permute-start.14 = (bf16[128,384]{1,0:T(8,128)(2,1)S(1)}, bf16[128,384]{1,0:T(8,128)(2,1)S(1)}, u32[]{:S(2)}, u32[]{:S(2)}) collective-permute-start(bf16[128,384]{1,0:T(8,128)(2,1)S(1)} %pad_maximum_fusion), channel_id=1, source_target_pairs={{0,16},{1,119},{2,18},{3,117},{4,20},{5,123},{6,22},{7,121},{8,24}... | collective-permute-start | bytes 294920 | tf_op jit(solution)/shard_map/ppermute | solution.py:45
  72.4 1.4 %collective-permute-start.17 = (bf16[128,384]{1,0:T(8,128)(2,1)S(1)}, bf16[128,384]{1,0:T(8,128)(2,1)S(1)}, u32[]{:S(2)}, u32[]{:S(2)}) collective-permute-start(bf16[128,384]{1,0:T(8,128)(2,1)S(1)} %pad_maximum_fusion.1), channel_id=1, source_target_pairs={{0,1},{1,0},{2,3},{3,2},{4,5},{5,4},{6,7},{7,6},{8,9},{9,8},{10,11... | collective-permute-start | bytes 294920 | tf_op jit(solution)/shard_map/ppermute | solution.py:33
  72.5 3.6 %collective-permute-start.19 = (bf16[128,384]{1,0:T(8,128)(2,1)S(1)}, bf16[128,384]{1,0:T(8,128)(2,1)S(1)}, u32[]{:S(2)}, u32[]{:S(2)}) collective-permute-start(bf16[128,384]{1,0:T(8,128)(2,1)S(1)} %get-tuple-element.70), channel_id=1, source_target_pairs={{0,1},{1,0},{2,3},{3,2},{4,5},{5,4},{6,7},{7,6},{8,9},{9,8},{10,11... | collective-permute-start | bytes 294920 | tf_op jit(solution)/shard_map/ppermute | solution.py:33
  74.8 5.0 %collective-permute-start.18 = (bf16[64,768]{1,0:T(8,128)(2,1)S(1)}, bf16[64,768]{1,0:T(8,128)(2,1)S(1)}, u32[]{:S(2)}, u32[]{:S(2)}) collective-permute-start(bf16[64,768]{1,0:T(8,128)(2,1)S(1)} %get-tuple-element.68), channel_id=1, source_target_pairs={{0,2},{1,3},{2,0},{3,1},{4,6},{5,7},{6,4},{7,5},{8,10},{9,11},{10,... | collective-permute-start | bytes 294920 | tf_op jit(solution)/shard_map/ppermute | solution.py:33
  76.1 6.2 %collective-permute-start.20 = (bf16[128,384]{1,0:T(8,128)(2,1)S(1)}, bf16[128,384]{1,0:T(8,128)(2,1)S(1)}, u32[]{:S(2)}, u32[]{:S(2)}) collective-permute-start(bf16[128,384]{1,0:T(8,128)(2,1)S(1)} %pad_maximum_fusion.2), channel_id=1, source_target_pairs={{0,112},{1,15},{2,114},{3,13},{4,116},{5,19},{6,118},{7,17},{8,120... | collective-permute-start | bytes 294920 | tf_op jit(solution)/shard_map/ppermute | solution.py:45
  78.7 4.8 %collective-permute-start.21 = (bf16[128,384]{1,0:T(8,128)(2,1)S(1)}, bf16[128,384]{1,0:T(8,128)(2,1)S(1)}, u32[]{:S(2)}, u32[]{:S(2)}) collective-permute-start(bf16[128,384]{1,0:T(8,128)(2,1)S(1)} %pad_maximum_fusion.3), channel_id=1, source_target_pairs={{0,120},{1,7},{2,122},{3,5},{4,124},{5,11},{6,126},{7,9},{8,0},{9,... | collective-permute-start | bytes 294920 | tf_op jit(solution)/shard_map/ppermute | solution.py:45
  83.5 3.8 %collective-permute-start.22 = (f32[64,384]{1,0:T(8,128)S(1)}, f32[64,384]{1,0:T(8,128)S(1)}, u32[]{:S(2)}, u32[]{:S(2)}) collective-permute-start(f32[64,384]{1,0:T(8,128)S(1)} %convert_add_fusion), channel_id=1, source_target_pairs={{0,1},{1,0},{2,3},{3,2},{4,5},{5,4},{6,7},{7,6},{8,9},{9,8},{10,11... | collective-permute-start | bytes 294920 | tf_op jit(solution)/shard_map/ppermute | solution.py:33
  87.6 1.2 %collective-permute-start.23 = (f32[32,128]{1,0:T(8,128)S(1)}, f32[32,128]{1,0:T(8,128)S(1)}, u32[]{:S(2)}, u32[]{:S(2)}) collective-permute-start(f32[32,128]{1,0:T(8,128)S(1)} %get-tuple-element.71), channel_id=1, source_target_pairs={{0,1},{1,0},{2,3},{3,2},{4,5},{5,4},{6,7},{7,6},{8,9},{9,8},{10,11... | collective-permute-start | bytes 49160 | tf_op jit(solution)/shard_map/ppermute | solution.py:356
  88.8 4.9 %collective-permute-start.26 = (f32[32,128]{1,0:T(8,128)S(1)}, f32[32,128]{1,0:T(8,128)S(1)}, u32[]{:S(2)}, u32[]{:S(2)}) collective-permute-start(f32[32,128]{1,0:T(8,128)S(1)} %add.82), channel_id=1, source_target_pairs={{0,6},{1,7},{2,4},{3,5},{4,2},{5,3},{6,0},{7,1},{8,14},{9,15},{10,... | collective-permute-start | bytes 49160 | tf_op jit(solution)/shard_map/ppermute | solution.py:356
  89.0 5.2 %collective-permute-start.25 = (f32[32,128]{1,0:T(8,128)S(1)}, f32[32,128]{1,0:T(8,128)S(1)}, u32[]{:S(2)}, u32[]{:S(2)}) collective-permute-start(f32[32,128]{1,0:T(8,128)S(1)} %add.82), channel_id=1, source_target_pairs={{0,4},{1,5},{2,6},{3,7},{4,0},{5,1},{6,2},{7,3},{8,12},{9,13},{10,... | collective-permute-start | bytes 49160 | tf_op jit(solution)/shard_map/ppermute | solution.py:356
  90.6 4.2 %collective-permute-start.24 = (f32[32,128]{1,0:T(8,128)S(1)}, f32[32,128]{1,0:T(8,128)S(1)}, u32[]{:S(2)}, u32[]{:S(2)}) collective-permute-start(f32[32,128]{1,0:T(8,128)S(1)} %add.82), channel_id=1, source_target_pairs={{0,2},{1,3},{2,0},{3,1},{4,6},{5,7},{6,4},{7,5},{8,10},{9,11},{10,... | collective-permute-start | bytes 49160 | tf_op jit(solution)/shard_map/ppermute | solution.py:356
  94.8 4.9 %collective-permute-start.29 = (f32[32,128]{1,0:T(8,128)S(1)}, f32[32,128]{1,0:T(8,128)S(1)}, u32[]{:S(2)}, u32[]{:S(2)}) collective-permute-start(f32[32,128]{1,0:T(8,128)S(1)} %add_add_fusion.2), channel_id=1, source_target_pairs={{0,24},{1,25},{2,26},{3,27},{4,28},{5,29},{6,30},{7,31},{8,16},{9,... | collective-permute-start | bytes 49160 | tf_op jit(solution)/shard_map/ppermute | solution.py:356
  94.9 5.2 %collective-permute-start.28 = (f32[32,128]{1,0:T(8,128)S(1)}, f32[32,128]{1,0:T(8,128)S(1)}, u32[]{:S(2)}, u32[]{:S(2)}) collective-permute-start(f32[32,128]{1,0:T(8,128)S(1)} %add_add_fusion.2), channel_id=1, source_target_pairs={{0,16},{1,17},{2,18},{3,19},{4,20},{5,21},{6,22},{7,23},{8,24},{9,... | collective-permute-start | bytes 49160 | tf_op jit(solution)/shard_map/ppermute | solution.py:356
  97.5 3.7 %collective-permute-start.27 = (f32[32,128]{1,0:T(8,128)S(1)}, f32[32,128]{1,0:T(8,128)S(1)}, u32[]{:S(2)}, u32[]{:S(2)}) collective-permute-start(f32[32,128]{1,0:T(8,128)S(1)} %add_add_fusion.2), channel_id=1, source_target_pairs={{0,8},{1,9},{2,10},{3,11},{4,12},{5,13},{6,14},{7,15},{8,0},{9,1},... | collective-permute-start | bytes 49160 | tf_op jit(solution)/shard_map/ppermute | solution.py:356
  101.3 5.5 %collective-permute-start.32 = (f32[32,128]{1,0:T(8,128)S(1)}, f32[32,128]{1,0:T(8,128)S(1)}, u32[]{:S(2)}, u32[]{:S(2)}) collective-permute-start(f32[32,128]{1,0:T(8,128)S(1)} %add_add_fusion.1), channel_id=1, source_target_pairs={{0,96},{1,97},{2,98},{3,99},{4,100},{5,101},{6,102},{7,103},{8,104... | collective-permute-start | bytes 49160 | tf_op jit(solution)/shard_map/ppermute | solution.py:356
  105.1 5.2 %collective-permute-start.31 = (f32[32,128]{1,0:T(8,128)S(1)}, f32[32,128]{1,0:T(8,128)S(1)}, u32[]{:S(2)}, u32[]{:S(2)}) collective-permute-start(f32[32,128]{1,0:T(8,128)S(1)} %add_add_fusion.1), channel_id=1, source_target_pairs={{0,64},{1,65},{2,66},{3,67},{4,68},{5,69},{6,70},{7,71},{8,72},{9,... | collective-permute-start | bytes 49160 | tf_op jit(solution)/shard_map/ppermute | solution.py:356
  105.1 5.2 %collective-permute-start.30 = (f32[32,128]{1,0:T(8,128)S(1)}, f32[32,128]{1,0:T(8,128)S(1)}, u32[]{:S(2)}, u32[]{:S(2)}) collective-permute-start(f32[32,128]{1,0:T(8,128)S(1)} %add_add_fusion.1), channel_id=1, source_target_pairs={{0,32},{1,33},{2,34},{3,35},{4,36},{5,37},{6,38},{7,39},{8,40},{9,... | collective-permute-start | bytes 49160 | tf_op jit(solution)/shard_map/ppermute | solution.py:356

commit v8 on v7

--- a/solution.py
+++ b/solution.py
@@ -325,6 +325,9 @@
         sub_arg, scaled_low, pair[EIG:], far, *tiles
     )
     taken = moved(give, 0, 1)
+    one, two, _ = lax.optimization_barrier((one, two, z0))
+    swapped = moved(jnp.concatenate([one[EIG:], two[EIG:]], axis=0), 0, 1)
+    swapped, taken = lax.optimization_barrier((swapped, taken))
     one_back, two_back = routed(
         (
             jnp.concatenate([keep[:EIG], taken[:EIG]], axis=0),
@@ -332,8 +335,6 @@
         ),
         back=True,
     )
-    one, two, _ = lax.optimization_barrier((one, two, z0))
-    swapped = moved(jnp.concatenate([one[EIG:], two[EIG:]], axis=0), 0, 1)
     y_outs = (f32(EIG, 2 * ROWS), bf16(EIG, 2 * ROWS))
     kept, sent = call(row_kernel, y_outs, specs=with_sub + (VMEM,))(
         sub_arg, scaled_low, one, two, swapped, *tiles

time: 113 us -> 112 us (level)
  starting transfers between devices: 52.3 us -> 49.4 us
  waiting for transfers between devices: 38.8 us -> 40.7 us
    ppermute x19, starting transfers between devices: 32.7 us -> 29.7 us  [moved(): return lax.ppermute(value, ('blk', 'sub'), pairs)]
    ppermute x19, waiting for transfers between devices: 21.8 us -> 23.2 us  [moved(): return lax.ppermute(value, ('blk', 'sub'), pairs)]
    ppermute x10, waiting for transfers between devices: 9.36 us -> 10.7 us  [local(): parts.append(lax.ppermute(gram, ('blk', 'sub'), pairs))]
  transfers between devices with their start and end apart: 33 -> 33, of which waited for: 24 -> 25; matrix products, arithmetic and copies ran while one was open for 0% -> 0% of each run, Pallas kernels for 12% -> 12%
where the time goes in v8:
time: 112 us
  starting transfers between devices  49.4 us (44%)
  waiting for transfers between devices  40.7 us (36%)
  Pallas kernels  18.4 us (16%)
  local copies, waits for them, and re-layouts  2.06 us (2%)
    ppermute x19, starting transfers between devices, moved(): return lax.ppermute(value, ('blk', 'sub'), pairs)  29.7 us
    ppermute x19, waiting for transfers between devices, moved(): return lax.ppermute(value, ('blk', 'sub'), pairs)  23.2 us
    pallas_call x10, Pallas kernels, run(): pl.pallas_call(body, grid=(1,), out_shape=outs, in_specs=list(specs) if s...  18.4 us
    ppermute x10, starting transfers between devices, local(): parts.append(lax.ppermute(gram, ('blk', 'sub'), pairs))  12.7 us
    ppermute x10, waiting for transfers between devices, local(): parts.append(lax.ppermute(gram, ('blk', 'sub'), pairs))  10.7 us
    ppermute x4, starting transfers between devices, routed(): outs.append(lax.ppermute(part, ('blk', 'sub'), pairs))  6.93 us
    ppermute x4, waiting for transfers between devices, routed(): outs.append(lax.ppermute(part, ('blk', 'sub'), pairs))  6.83 us
  transfers between devices with their start and end apart: 33, of which 25 were waited for; matrix products, arithmetic and copies ran while one was open for 0% of the time, Pallas kernels for 12%

profile of v8, /device:TPU:0, one launch (start us, length us, event | category | flops | bytes accessed | tf_op | source)
XLA Modules:
  0.0 111.7 jit_solution(2383181594213461285)
XLA Ops:
  0.0 0.8 convert_element_type.15.scales.refs_6_
  0.8 0.9 constant_dynamic-slice_fusion.lists
  1.7 1.1 copy-done.1
  2.8 0.1 shard_map.46
  2.9 1.7 %collective-permute-start.1 = (bf16[384,768]{1,0:T(8,128)(2,1)S(1)}, bf16[384,768]{1,0:T(8,128)(2,1)S(1)}, u32[]{:S(2)}, u32[]{:S(2)}) collective-permute-start(bf16[384,768]{1,0:T(8,128)(2,1)S(1)} %copy-done.1), channel_id=1, source_target_pairs={{0,2},{1,3},{2,0},{3,1},{4,6},{5,7},{6,4},{7,5},{8,10},{9,11},{10,... | collective-permute-start | bytes 1769480 | tf_op jit(solution)/shard_map/ppermute | solution.py:33
  4.6 1.5 %collective-permute-start.3 = (bf16[416,768]{1,0:T(8,128)(2,1)S(1)}, bf16[416,768]{1,0:T(8,128)(2,1)S(1)}, u32[]{:S(2)}, u32[]{:S(2)}) collective-permute-start(bf16[416,768]{1,0:T(8,128)(2,1)S(1)} %get-tuple-element.44), channel_id=1, source_target_pairs={{0,8},{1,9},{2,10},{3,11},{4,12},{5,13},{6,14},{7,15},{8,16},{9,17... | collective-permute-start | bytes 1916936 | tf_op jit(solution)/shard_map/ppermute | solution.py:33
  6.1 6.4 %collective-permute-start.4 = (bf16[416,768]{1,0:T(8,128)(2,1)S(1)}, bf16[416,768]{1,0:T(8,128)(2,1)S(1)}, u32[]{:S(2)}, u32[]{:S(2)}) collective-permute-start(bf16[416,768]{1,0:T(8,128)(2,1)S(1)} %get-tuple-element.45), channel_id=1, source_target_pairs={{0,126},{1,127},{2,124},{3,125},{4,2},{5,3},{6,0},{7,1},{8,6},{9,7... | collective-permute-start | bytes 1916936 | tf_op jit(solution)/shard_map/ppermute | solution.py:33
  12.5 5.5 %collective-permute-done.1.f2.refs_2_ = bf16[384,768]{1,0:T(8,128)(2,1)S(1)} collective-permute-done((bf16[384,768]{1,0:T(8,128)(2,1)S(1)}, bf16[384,768]{1,0:T(8,128)(2,1)S(1)}, u32[]{:S(2)}, u32[]{:S(2)}) %collective-permute-start.1) | collective-permute-done | bytes 589856 | tf_op jit(solution)/shard_map/ppermute | solution.py:33
  18.0 2.0 %collective-permute-done.2.f3.refs_3_ = bf16[384,768]{1,0:T(8,128)(2,1)S(1)} collective-permute-done((bf16[384,768]{1,0:T(8,128)(2,1)S(1)}, bf16[384,768]{1,0:T(8,128)(2,1)S(1)}, u32[]{:S(2)}, u32[]{:S(2)}) %collective-permute-start.2) | collective-permute-done | bytes 589856 | tf_op jit(solution)/shard_map/ppermute | solution.py:33
  20.0 3.2 %shard_map.47 = (bf16[384,1536]{1,0:T(8,128)(2,1)S(1)}, f32[4,384]{1,0:T(4,128)S(1)}, f32[1,384]{1,0:T(1,128)S(1)}, f32[4,384]{1,0:T(4,128)S(1)}) custom-call(s32[1]{0:T(128)} %bitcast.sub, bf16[384,768]{1,0:T(8,128)(2,1)S(1)} %copy-done.1, bf16[384,768]{1,0:T(8,128)(2,1)S(1)} %collective-permute-done.f1.refs_1_, ...), custom_call_target="tpu_custom_call" | custom-call | flops 1000 | bytes 1000 | tf_op jit(solution)/shard_map/pallas_call | solution.py:56
  23.2 1.8 %collective-permute-done.3.refs_4_ = bf16[416,768]{1,0:T(8,128)(2,1)S(1)} collective-permute-done((bf16[416,768]{1,0:T(8,128)(2,1)S(1)}, bf16[416,768]{1,0:T(8,128)(2,1)S(1)}, u32[]{:S(2)}, u32[]{:S(2)}) %collective-permute-start.3) | collective-permute-done | bytes 639008 | tf_op jit(solution)/shard_map/ppermute | solution.py:33
  25.0 0.9 collective-permute-done.4.refs_4_
  25.9 5.3 %collective-permute-start.5 = (bf16[416,768]{1,0:T(8,128)(2,1)S(1)}, bf16[416,768]{1,0:T(8,128)(2,1)S(1)}, u32[]{:S(2)}, u32[]{:S(2)}) collective-permute-start(bf16[416,768]{1,0:T(8,128)(2,1)S(1)} %collective-permute-done.4.refs_4_), channel_id=1, source_target_pairs={{0,120},{1,121},{2,122},{3,123},{4,124},{5,125},{6,126},{7,127},{8... | collective-permute-start | bytes 1916936 | tf_op jit(solution)/shard_map/ppermute | solution.py:33
  31.2 2.4 %shard_map.48 = (bf16[384,1536]{1,0:T(8,128)(2,1)S(1)}, f32[4,384]{1,0:T(4,128)S(1)}, f32[1,384]{1,0:T(1,128)S(1)}) custom-call(s32[1]{0:T(128)} %bitcast.sub, bf16[384,768]{1,0:T(8,128)(2,1)S(1)} %copy-done.1, bf16[384,768]{1,0:T(8,128)(2,1)S(1)} %collective-permute-done.f1.refs_1_, bf16[384,768]{1,0:T(8,128)(2,1)S(1)} %collective-permute-done.1.f2.refs_2_, ...), custom_call_target="tpu_custom_call" | custom-call | flops 1000 | bytes 1000 | tf_op jit(solution)/shard_map/pallas_call | solution.py:56
  33.6 0.6 collective-permute-start.7
  34.2 2.4 %shard_map.49 = (bf16[384,1536]{1,0:T(8,128)(2,1)S(1)}, f32[4,384]{1,0:T(4,128)S(1)}, f32[1,384]{1,0:T(1,128)S(1)}) custom-call(s32[1]{0:T(128)} %bitcast.sub, bf16[384,768]{1,0:T(8,128)(2,1)S(1)} %copy-done.1, bf16[384,768]{1,0:T(8,128)(2,1)S(1)} %collective-permute-done.f1.refs_1_, bf16[384,768]{1,0:T(8,128)(2,1)S(1)} %collective-permute-done.1.f2.refs_2_, ...), custom_call_target="tpu_custom_call" | custom-call | flops 1000 | bytes 1000 | tf_op jit(solution)/shard_map/pallas_call | solution.py:56
  36.6 4.9 %collective-permute-start.8 = (f32[1,384]{1,0:T(1,128)S(1)}, f32[1,384]{1,0:T(1,128)S(1)}, u32[]{:S(2)}, u32[]{:S(2)}) collective-permute-start(f32[1,384]{1,0:T(1,128)S(1)} %get-tuple-element.56), channel_id=1, source_target_pairs={{0,6},{1,7},{2,4},{3,5},{4,10},{5,11},{6,8},{7,9},{8,14},{9,15},{1... | collective-permute-start | bytes 4616 | tf_op jit(solution)/shard_map/ppermute | solution.py:33
  41.5 2.9 %collective-permute-done.6.refs_4_ = bf16[416,768]{1,0:T(8,128)(2,1)S(1)} collective-permute-done((bf16[416,768]{1,0:T(8,128)(2,1)S(1)}, bf16[416,768]{1,0:T(8,128)(2,1)S(1)}, u32[]{:S(2)}, u32[]{:S(2)}) %collective-permute-start.6) | collective-permute-done | bytes 639008 | tf_op jit(solution)/shard_map/ppermute | solution.py:33
  44.4 2.3 %shard_map.50 = (bf16[384,1536]{1,0:T(8,128)(2,1)S(1)}, f32[4,384]{1,0:T(4,128)S(1)}, f32[1,384]{1,0:T(1,128)S(1)}) custom-call(s32[1]{0:T(128)} %bitcast.sub, bf16[384,768]{1,0:T(8,128)(2,1)S(1)} %copy-done.1, bf16[384,768]{1,0:T(8,128)(2,1)S(1)} %collective-permute-done.f1.refs_1_, bf16[384,768]{1,0:T(8,128)(2,1)S(1)} %collective-permute-done.1.f2.refs_2_, ...), custom_call_target="tpu_custom_call" | custom-call | flops 1000 | bytes 1000 | tf_op jit(solution)/shard_map/pallas_call | solution.py:56
  46.7 0.3 collective-permute-done.8.refs_9_
  47.0 2.4 %shard_map.51 = (bf16[384,1536]{1,0:T(8,128)(2,1)S(1)}, f32[4,384]{1,0:T(4,128)S(1)}, f32[1,384]{1,0:T(1,128)S(1)}) custom-call(s32[1]{0:T(128)} %bitcast.sub, bf16[384,768]{1,0:T(8,128)(2,1)S(1)} %copy-done.1, bf16[384,768]{1,0:T(8,128)(2,1)S(1)} %collective-permute-done.f1.refs_1_, bf16[384,768]{1,0:T(8,128)(2,1)S(1)} %collective-permute-done.1.f2.refs_2_, ...), custom_call_target="tpu_custom_call" | custom-call | flops 4000000000 | bytes 1000 | tf_op jit(solution)/shard_map/pallas_call | solution.py:56
  49.4 1.5 %collective-permute-start.9 = (f32[2,384]{1,0:T(2,128)S(1)}, f32[2,384]{1,0:T(2,128)S(1)}, u32[]{:S(2)}, u32[]{:S(2)}) collective-permute-start(f32[2,384]{1,0:T(2,128)S(1)} %slice.43), channel_id=1, source_target_pairs={{0,2},{1,3},{2,0},{3,1},{4,6},{5,7},{6,4},{7,5},{8,10},{9,11},{10,... | collective-permute-start | bytes 9224 | tf_op jit(solution)/shard_map/ppermute | solution.py:33
  50.8 5.9 %collective-permute-start.11 = (f32[1,384]{1,0:T(1,128)S(1)}, f32[1,384]{1,0:T(1,128)S(1)}, u32[]{:S(2)}, u32[]{:S(2)}) collective-permute-start(f32[1,384]{1,0:T(1,128)S(1)} %get-tuple-element.59), channel_id=1, source_target_pairs={{0,112},{1,113},{2,114},{3,115},{4,116},{5,117},{6,118},{7,119},{8... | collective-permute-start | bytes 4616 | tf_op jit(solution)/shard_map/ppermute | solution.py:33
  56.8 3.3 %collective-permute-done.12 = f32[1,384]{1,0:T(1,128)S(1)} collective-permute-done((f32[1,384]{1,0:T(1,128)S(1)}, f32[1,384]{1,0:T(1,128)S(1)}, u32[]{:S(2)}, u32[]{:S(2)}) %collective-permute-start.12) | collective-permute-done | bytes 1568 | tf_op jit(solution)/shard_map/ppermute | solution.py:33
  60.2 0.1 collective-permute-start.13
  60.3 1.2 %collective-permute-done.13.x1 = bf16[64,384]{1,0:T(8,128)(2,1)S(1)} collective-permute-done((bf16[64,384]{1,0:T(8,128)(2,1)S(1)}, bf16[64,384]{1,0:T(8,128)(2,1)S(1)}, u32[]{:S(2)}, u32[]{:S(2)}) %collective-permute-start.13) | collective-permute-done | bytes 49184 | tf_op jit(solution)/shard_map/ppermute | solution.py:33
  61.5 0.1 collective-permute-start.16
  61.6 0.6 collective-permute-start.15
  62.2 2.0 %collective-permute-start.14 = (bf16[128,384]{1,0:T(8,128)(2,1)S(1)}, bf16[128,384]{1,0:T(8,128)(2,1)S(1)}, u32[]{:S(2)}, u32[]{:S(2)}) collective-permute-start(bf16[128,384]{1,0:T(8,128)(2,1)S(1)} %pad_maximum_fusion), channel_id=1, source_target_pairs={{0,16},{1,119},{2,18},{3,117},{4,20},{5,123},{6,22},{7,121},{8,24}... | collective-permute-start | bytes 294920 | tf_op jit(solution)/shard_map/ppermute | solution.py:45
  64.2 2.2 %collective-permute-done.16.far = bf16[128,384]{1,0:T(8,128)(2,1)S(1)} collective-permute-done((bf16[128,384]{1,0:T(8,128)(2,1)S(1)}, bf16[128,384]{1,0:T(8,128)(2,1)S(1)}, u32[]{:S(2)}, u32[]{:S(2)}) %collective-permute-start.16) | collective-permute-done | bytes 98336 | tf_op jit(solution)/shard_map/ppermute | solution.py:33
  66.4 1.8 %shard_map.52 = (f32[64,384]{1,0:T(8,128)S(1)}, bf16[128,384]{1,0:T(8,128)(2,1)S(1)}, bf16[128,384]{1,0:T(8,128)(2,1)S(1)}) custom-call(s32[1]{0:T(128)} %bitcast.sub, bf16[64,384]{1,0:T(8,128)(2,1)S(1)} %multiply_convert_fusion.x0, bf16[64,384]{1,0:T(8,128)(2,1)S(1)} %collective-permute-done.13.x1, bf16[128,384]{1,0:T(8,128)(2,1)S(1)} %collective-permute-done.16.far, ...), custom_call_target="tpu_custom_call" | custom-call | flops 1000 | bytes 1000 | tf_op jit(solution)/shard_map/pallas_call | solution.py:56
  68.3 2.0 %collective-permute-done.15.two = bf16[128,384]{1,0:T(8,128)(2,1)S(1)} collective-permute-done((bf16[128,384]{1,0:T(8,128)(2,1)S(1)}, bf16[128,384]{1,0:T(8,128)(2,1)S(1)}, u32[]{:S(2)}, u32[]{:S(2)}) %collective-permute-start.15) | collective-permute-done | bytes 98336 | tf_op jit(solution)/shard_map/ppermute | solution.py:45
  70.3 2.1 %collective-permute-done.14.one = bf16[128,384]{1,0:T(8,128)(2,1)S(1)} collective-permute-done((bf16[128,384]{1,0:T(8,128)(2,1)S(1)}, bf16[128,384]{1,0:T(8,128)(2,1)S(1)}, u32[]{:S(2)}, u32[]{:S(2)}) %collective-permute-start.14) | collective-permute-done | bytes 98336 | tf_op jit(solution)/shard_map/ppermute | solution.py:45
  72.4 0.1 collective-permute-start.17
  72.5 0.5 collective-permute-start.18
  73.0 0.8 collective-permute-done.17.got
  73.8 0.2 collective-permute-done.18
  73.9 2.5 %collective-permute-start.20 = (bf16[128,384]{1,0:T(8,128)(2,1)S(1)}, bf16[128,384]{1,0:T(8,128)(2,1)S(1)}, u32[]{:S(2)}, u32[]{:S(2)}) collective-permute-start(bf16[128,384]{1,0:T(8,128)(2,1)S(1)} %pad_maximum_fusion.2), channel_id=1, source_target_pairs={{0,112},{1,15},{2,114},{3,13},{4,116},{5,19},{6,118},{7,17},{8,120... | collective-permute-start | bytes 294920 | tf_op jit(solution)/shard_map/ppermute | solution.py:45
  76.5 1.8 %collective-permute-start.21 = (bf16[128,384]{1,0:T(8,128)(2,1)S(1)}, bf16[128,384]{1,0:T(8,128)(2,1)S(1)}, u32[]{:S(2)}, u32[]{:S(2)}) collective-permute-start(bf16[128,384]{1,0:T(8,128)(2,1)S(1)} %pad_maximum_fusion.3), channel_id=1, source_target_pairs={{0,120},{1,7},{2,122},{3,5},{4,124},{5,11},{6,126},{7,9},{8,0},{9,... | collective-permute-start | bytes 294920 | tf_op jit(solution)/shard_map/ppermute | solution.py:45
  78.3 1.0 shard_map.53
  79.3 0.6 collective-permute-start.19
  79.9 0.2 collective-permute-done.20.one
  80.1 2.6 %collective-permute-done.21.two = bf16[128,384]{1,0:T(8,128)(2,1)S(1)} collective-permute-done((bf16[128,384]{1,0:T(8,128)(2,1)S(1)}, bf16[128,384]{1,0:T(8,128)(2,1)S(1)}, u32[]{:S(2)}, u32[]{:S(2)}) %collective-permute-start.21) | collective-permute-done | bytes 98336 | tf_op jit(solution)/shard_map/ppermute | solution.py:45
  82.7 1.3 %collective-permute-done.19.got = bf16[64,768]{1,0:T(8,128)(2,1)S(1)} collective-permute-done((bf16[64,768]{1,0:T(8,128)(2,1)S(1)}, bf16[64,768]{1,0:T(8,128)(2,1)S(1)}, u32[]{:S(2)}, u32[]{:S(2)}) %collective-permute-start.19) | collective-permute-done | bytes 98336 | tf_op jit(solution)/shard_map/ppermute | solution.py:33
  84.0 0.5 collective-permute-start.22
  84.6 0.9 collective-permute-done.22.swapped
  85.5 0.3 shard_map.54
  85.9 0.4 collective-permute-start.23
  86.2 0.8 collective-permute-done.23
  87.1 2.5 %collective-permute-start.26 = (f32[32,128]{1,0:T(8,128)S(1)}, f32[32,128]{1,0:T(8,128)S(1)}, u32[]{:S(2)}, u32[]{:S(2)}) collective-permute-start(f32[32,128]{1,0:T(8,128)S(1)} %add.82), channel_id=1, source_target_pairs={{0,6},{1,7},{2,4},{3,5},{4,2},{5,3},{6,0},{7,1},{8,14},{9,15},{10,... | collective-permute-start | bytes 49160 | tf_op jit(solution)/shard_map/ppermute | solution.py:357
  89.6 1.6 %collective-permute-start.24 = (f32[32,128]{1,0:T(8,128)S(1)}, f32[32,128]{1,0:T(8,128)S(1)}, u32[]{:S(2)}, u32[]{:S(2)}) collective-permute-start(f32[32,128]{1,0:T(8,128)S(1)} %add.82), channel_id=1, source_target_pairs={{0,2},{1,3},{2,0},{3,1},{4,6},{5,7},{6,4},{7,5},{8,10},{9,11},{10,... | collective-permute-start | bytes 49160 | tf_op jit(solution)/shard_map/ppermute | solution.py:357
  91.2 0.9 collective-permute-done.26
  92.0 2.8 %collective-permute-done.25 = f32[32,128]{1,0:T(8,128)S(1)} collective-permute-done((f32[32,128]{1,0:T(8,128)S(1)}, f32[32,128]{1,0:T(8,128)S(1)}, u32[]{:S(2)}, u32[]{:S(2)}) %collective-permute-start.25) | collective-permute-done | bytes 16416 | tf_op jit(solution)/shard_map/ppermute | solution.py:357
  94.8 0.1 collective-permute-start.29
  94.9 3.0 %collective-permute-start.28 = (f32[32,128]{1,0:T(8,128)S(1)}, f32[32,128]{1,0:T(8,128)S(1)}, u32[]{:S(2)}, u32[]{:S(2)}) collective-permute-start(f32[32,128]{1,0:T(8,128)S(1)} %add_add_fusion.2), channel_id=1, source_target_pairs={{0,16},{1,17},{2,18},{3,19},{4,20},{5,21},{6,22},{7,23},{8,24},{9,... | collective-permute-start | bytes 49160 | tf_op jit(solution)/shard_map/ppermute | solution.py:357
  97.9 1.1 collective-permute-start.27
  99.0 0.9 collective-permute-done.29
  99.9 0.4 collective-permute-done.28
  100.3 1.4 %collective-permute-done.27 = f32[32,128]{1,0:T(8,128)S(1)} collective-permute-done((f32[32,128]{1,0:T(8,128)S(1)}, f32[32,128]{1,0:T(8,128)S(1)}, u32[]{:S(2)}, u32[]{:S(2)}) %collective-permute-start.27) | collective-permute-done | bytes 16416 | tf_op jit(solution)/shard_map/ppermute | solution.py:357
  101.7 2.4 %collective-permute-start.32 = (f32[32,128]{1,0:T(8,128)S(1)}, f32[32,128]{1,0:T(8,128)S(1)}, u32[]{:S(2)}, u32[]{:S(2)}) collective-permute-start(f32[32,128]{1,0:T(8,128)S(1)} %add_add_fusion.1), channel_id=1, source_target_pairs={{0,96},{1,97},{2,98},{3,99},{4,100},{5,101},{6,102},{7,103},{8,104... | collective-permute-start | bytes 49160 | tf_op jit(solution)/shard_map/ppermute | solution.py:357
  104.1 1.7 %collective-permute-start.30 = (f32[32,128]{1,0:T(8,128)S(1)}, f32[32,128]{1,0:T(8,128)S(1)}, u32[]{:S(2)}, u32[]{:S(2)}) collective-permute-start(f32[32,128]{1,0:T(8,128)S(1)} %add_add_fusion.1), channel_id=1, source_target_pairs={{0,32},{1,33},{2,34},{3,35},{4,36},{5,37},{6,38},{7,39},{8,40},{9,... | collective-permute-start | bytes 49160 | tf_op jit(solution)/shard_map/ppermute | solution.py:357
  105.8 0.9 collective-permute-done.32
  106.6 2.7 %collective-permute-done.31 = f32[32,128]{1,0:T(8,128)S(1)} collective-permute-done((f32[32,128]{1,0:T(8,128)S(1)}, f32[32,128]{1,0:T(8,128)S(1)}, u32[]{:S(2)}, u32[]{:S(2)}) %collective-permute-start.31) | collective-permute-done | bytes 16416 | tf_op jit(solution)/shard_map/ppermute | solution.py:357
  109.3 2.4 %shard_map.55 = f32[64,384]{1,0:T(8,128)} custom-call(f32[32,128]{1,0:T(8,128)S(1)} %add_add_fusion.gram, f32[64,384]{1,0:T(8,128)S(1)} %get-tuple-element.76.mixed), custom_call_target="tpu_custom_call" | custom-call | flops 1000 | bytes 1000 | tf_op jit(solution)/shard_map/pallas_call | solution.py:56
  (38 shorter events, 0.3 us)
Async XLA Ops:
  0.0 20.0 %copy-start = (s32[9,16,1536]{2,1,0:T(8,128)S(1)}, s32[9,16,1536]{2,1,0:T(8,128)}, u32[]{:S(2)}) copy-start(s32[9,16,1536]{2,1,0:T(8,128)} %refs_10_) | copy-start | bytes 2654212
  1.7 1.1 copy-start.1
  2.9 15.1 %collective-permute-start.1 = (bf16[384,768]{1,0:T(8,128)(2,1)S(1)}, bf16[384,768]{1,0:T(8,128)(2,1)S(1)}, u32[]{:S(2)}, u32[]{:S(2)}) collective-permute-start(bf16[384,768]{1,0:T(8,128)(2,1)S(1)} %copy-done.1), channel_id=1, source_target_pairs={{0,2},{1,3},{2,0},{3,1},{4,6},{5,7},{6,4},{7,5},{8,10},{9,11},{10,... | collective-permute-start | bytes 1769480 | tf_op jit(solution)/shard_map/ppermute | solution.py:33
  4.6 20.3 %collective-permute-start.3 = (bf16[416,768]{1,0:T(8,128)(2,1)S(1)}, bf16[416,768]{1,0:T(8,128)(2,1)S(1)}, u32[]{:S(2)}, u32[]{:S(2)}) collective-permute-start(bf16[416,768]{1,0:T(8,128)(2,1)S(1)} %get-tuple-element.44), channel_id=1, source_target_pairs={{0,8},{1,9},{2,10},{3,11},{4,12},{5,13},{6,14},{7,15},{8,16},{9,17... | collective-permute-start | bytes 1916936 | tf_op jit(solution)/shard_map/ppermute | solution.py:33
  6.1 19.7 %collective-permute-start.4 = (bf16[416,768]{1,0:T(8,128)(2,1)S(1)}, bf16[416,768]{1,0:T(8,128)(2,1)S(1)}, u32[]{:S(2)}, u32[]{:S(2)}) collective-permute-start(bf16[416,768]{1,0:T(8,128)(2,1)S(1)} %get-tuple-element.45), channel_id=1, source_target_pairs={{0,126},{1,127},{2,124},{3,125},{4,2},{5,3},{6,0},{7,1},{8,6},{9,7... | collective-permute-start | bytes 1916936 | tf_op jit(solution)/shard_map/ppermute | solution.py:33
  12.5 5.5 %collective-permute-start = (bf16[384,768]{1,0:T(8,128)(2,1)S(1)}, bf16[384,768]{1,0:T(8,128)(2,1)S(1)}, u32[]{:S(2)}, u32[]{:S(2)}) collective-permute-start(bf16[384,768]{1,0:T(8,128)(2,1)S(1)} %copy-done.1), channel_id=1, source_target_pairs={{0,1},{1,0},{2,3},{3,2},{4,5},{5,4},{6,7},{7,6},{8,9},{9,8},{10,11... | collective-permute-start | bytes 1769480 | tf_op jit(solution)/shard_map/ppermute | solution.py:33
  18.0 2.0 %collective-permute-start.2 = (bf16[384,768]{1,0:T(8,128)(2,1)S(1)}, bf16[384,768]{1,0:T(8,128)(2,1)S(1)}, u32[]{:S(2)}, u32[]{:S(2)}) collective-permute-start(bf16[384,768]{1,0:T(8,128)(2,1)S(1)} %collective-permute-done.1.f2.refs_2_), channel_id=1, source_target_pairs={{0,1},{1,0},{2,3},{3,2},{4,5},{5,4},{6,7},{7,6},{8,9},{9,8},{10,11... | collective-permute-start | bytes 1769480 | tf_op jit(solution)/shard_map/ppermute | solution.py:33
  25.8 18.5 %collective-permute-start.6 = (bf16[416,768]{1,0:T(8,128)(2,1)S(1)}, bf16[416,768]{1,0:T(8,128)(2,1)S(1)}, u32[]{:S(2)}, u32[]{:S(2)}) collective-permute-start(bf16[416,768]{1,0:T(8,128)(2,1)S(1)} %collective-permute-done.3.refs_4_), channel_id=1, source_target_pairs={{0,8},{1,9},{2,10},{3,11},{4,12},{5,13},{6,14},{7,15},{8,16},{9,17... | collective-permute-start | bytes 1916936 | tf_op jit(solution)/shard_map/ppermute | solution.py:33
  25.9 21.1 %collective-permute-start.5 = (bf16[416,768]{1,0:T(8,128)(2,1)S(1)}, bf16[416,768]{1,0:T(8,128)(2,1)S(1)}, u32[]{:S(2)}, u32[]{:S(2)}) collective-permute-start(bf16[416,768]{1,0:T(8,128)(2,1)S(1)} %collective-permute-done.4.refs_4_), channel_id=1, source_target_pairs={{0,120},{1,121},{2,122},{3,123},{4,124},{5,125},{6,126},{7,127},{8... | collective-permute-start | bytes 1916936 | tf_op jit(solution)/shard_map/ppermute | solution.py:33
  33.6 13.1 %collective-permute-start.7 = (f32[1,384]{1,0:T(1,128)S(1)}, f32[1,384]{1,0:T(1,128)S(1)}, u32[]{:S(2)}, u32[]{:S(2)}) collective-permute-start(f32[1,384]{1,0:T(1,128)S(1)} %get-tuple-element.55), channel_id=1, source_target_pairs={{0,120},{1,121},{2,122},{3,123},{4,124},{5,125},{6,126},{7,127},{8... | collective-permute-start | bytes 4616 | tf_op jit(solution)/shard_map/ppermute | solution.py:33
  36.6 10.4 %collective-permute-start.8 = (f32[1,384]{1,0:T(1,128)S(1)}, f32[1,384]{1,0:T(1,128)S(1)}, u32[]{:S(2)}, u32[]{:S(2)}) collective-permute-start(f32[1,384]{1,0:T(1,128)S(1)} %get-tuple-element.56), channel_id=1, source_target_pairs={{0,6},{1,7},{2,4},{3,5},{4,10},{5,11},{6,8},{7,9},{8,14},{9,15},{1... | collective-permute-start | bytes 4616 | tf_op jit(solution)/shard_map/ppermute | solution.py:33
  47.0 13.2 %copy-start.2 = (f32[64,384]{1,0:T(8,128)S(1)}, f32[64,384]{1,0:T(8,128)}, u32[]{:S(2)}) copy-start(f32[64,384]{1,0:T(8,128)} %own.1) | copy-start | bytes 294916
  49.4 7.3 %collective-permute-start.9 = (f32[2,384]{1,0:T(2,128)S(1)}, f32[2,384]{1,0:T(2,128)S(1)}, u32[]{:S(2)}, u32[]{:S(2)}) collective-permute-start(f32[2,384]{1,0:T(2,128)S(1)} %slice.43), channel_id=1, source_target_pairs={{0,2},{1,3},{2,0},{3,1},{4,6},{5,7},{6,4},{7,5},{8,10},{9,11},{10,... | collective-permute-start | bytes 9224 | tf_op jit(solution)/shard_map/ppermute | solution.py:33
  50.8 9.3 %collective-permute-start.12 = (f32[1,384]{1,0:T(1,128)S(1)}, f32[1,384]{1,0:T(1,128)S(1)}, u32[]{:S(2)}, u32[]{:S(2)}) collective-permute-start(f32[1,384]{1,0:T(1,128)S(1)} %get-tuple-element.60), channel_id=1, source_target_pairs={{0,14},{1,15},{2,12},{3,13},{4,18},{5,19},{6,16},{7,17},{8,22},{9,... | collective-permute-start | bytes 4616 | tf_op jit(solution)/shard_map/ppermute | solution.py:33
  50.8 9.3 %collective-permute-start.11 = (f32[1,384]{1,0:T(1,128)S(1)}, f32[1,384]{1,0:T(1,128)S(1)}, u32[]{:S(2)}, u32[]{:S(2)}) collective-permute-start(f32[1,384]{1,0:T(1,128)S(1)} %get-tuple-element.59), channel_id=1, source_target_pairs={{0,112},{1,113},{2,114},{3,115},{4,116},{5,117},{6,118},{7,119},{8... | collective-permute-start | bytes 4616 | tf_op jit(solution)/shard_map/ppermute | solution.py:33
  56.7 3.4 %collective-permute-start.10 = (f32[1,384]{1,0:T(1,128)S(1)}, f32[1,384]{1,0:T(1,128)S(1)}, u32[]{:S(2)}, u32[]{:S(2)}) collective-permute-start(f32[1,384]{1,0:T(1,128)S(1)} %slice.57), channel_id=1, source_target_pairs={{0,1},{1,0},{2,3},{3,2},{4,5},{5,4},{6,7},{7,6},{8,9},{9,8},{10,11... | collective-permute-start | bytes 4616 | tf_op jit(solution)/shard_map/ppermute | solution.py:33
  60.2 1.3 %collective-permute-start.13 = (bf16[64,384]{1,0:T(8,128)(2,1)S(1)}, bf16[64,384]{1,0:T(8,128)(2,1)S(1)}, u32[]{:S(2)}, u32[]{:S(2)}) collective-permute-start(bf16[64,384]{1,0:T(8,128)(2,1)S(1)} %multiply_convert_fusion.x0), channel_id=1, source_target_pairs={{0,1},{1,0},{2,3},{3,2},{4,5},{5,4},{6,7},{7,6},{8,9},{9,8},{10,11... | collective-permute-start | bytes 147464 | tf_op jit(solution)/shard_map/ppermute | solution.py:33
  61.5 4.9 %collective-permute-start.16 = (bf16[128,384]{1,0:T(8,128)(2,1)S(1)}, bf16[128,384]{1,0:T(8,128)(2,1)S(1)}, u32[]{:S(2)}, u32[]{:S(2)}) collective-permute-start(bf16[128,384]{1,0:T(8,128)(2,1)S(1)} %pad_maximum_fusion), channel_id=1, source_target_pairs={{0,2},{1,3},{2,0},{3,1},{4,6},{5,7},{6,4},{7,5},{8,10},{9,11},{10,... | collective-permute-start | bytes 294920 | tf_op jit(solution)/shard_map/ppermute | solution.py:33
  61.6 8.7 %collective-permute-start.15 = (bf16[128,384]{1,0:T(8,128)(2,1)S(1)}, bf16[128,384]{1,0:T(8,128)(2,1)S(1)}, u32[]{:S(2)}, u32[]{:S(2)}) collective-permute-start(bf16[128,384]{1,0:T(8,128)(2,1)S(1)} %pad_maximum_fusion), channel_id=1, source_target_pairs={{0,8},{1,127},{2,10},{3,125},{4,12},{5,3},{6,14},{7,1},{8,16},{9,7... | collective-permute-start | bytes 294920 | tf_op jit(solution)/shard_map/ppermute | solution.py:45
  62.2 10.1 %collective-permute-start.14 = (bf16[128,384]{1,0:T(8,128)(2,1)S(1)}, bf16[128,384]{1,0:T(8,128)(2,1)S(1)}, u32[]{:S(2)}, u32[]{:S(2)}) collective-permute-start(bf16[128,384]{1,0:T(8,128)(2,1)S(1)} %pad_maximum_fusion), channel_id=1, source_target_pairs={{0,16},{1,119},{2,18},{3,117},{4,20},{5,123},{6,22},{7,121},{8,24}... | collective-permute-start | bytes 294920 | tf_op jit(solution)/shard_map/ppermute | solution.py:45
  72.4 1.4 %collective-permute-start.17 = (bf16[128,384]{1,0:T(8,128)(2,1)S(1)}, bf16[128,384]{1,0:T(8,128)(2,1)S(1)}, u32[]{:S(2)}, u32[]{:S(2)}) collective-permute-start(bf16[128,384]{1,0:T(8,128)(2,1)S(1)} %pad_maximum_fusion.1), channel_id=1, source_target_pairs={{0,1},{1,0},{2,3},{3,2},{4,5},{5,4},{6,7},{7,6},{8,9},{9,8},{10,11... | collective-permute-start | bytes 294920 | tf_op jit(solution)/shard_map/ppermute | solution.py:33
  72.5 1.4 %collective-permute-start.18 = (bf16[128,384]{1,0:T(8,128)(2,1)S(1)}, bf16[128,384]{1,0:T(8,128)(2,1)S(1)}, u32[]{:S(2)}, u32[]{:S(2)}) collective-permute-start(bf16[128,384]{1,0:T(8,128)(2,1)S(1)} %get-tuple-element.69), channel_id=1, source_target_pairs={{0,1},{1,0},{2,3},{3,2},{4,5},{5,4},{6,7},{7,6},{8,9},{9,8},{10,11... | collective-permute-start | bytes 294920 | tf_op jit(solution)/shard_map/ppermute | solution.py:33
  73.9 6.2 %collective-permute-start.20 = (bf16[128,384]{1,0:T(8,128)(2,1)S(1)}, bf16[128,384]{1,0:T(8,128)(2,1)S(1)}, u32[]{:S(2)}, u32[]{:S(2)}) collective-permute-start(bf16[128,384]{1,0:T(8,128)(2,1)S(1)} %pad_maximum_fusion.2), channel_id=1, source_target_pairs={{0,112},{1,15},{2,114},{3,13},{4,116},{5,19},{6,118},{7,17},{8,120... | collective-permute-start | bytes 294920 | tf_op jit(solution)/shard_map/ppermute | solution.py:45
  76.5 6.2 %collective-permute-start.21 = (bf16[128,384]{1,0:T(8,128)(2,1)S(1)}, bf16[128,384]{1,0:T(8,128)(2,1)S(1)}, u32[]{:S(2)}, u32[]{:S(2)}) collective-permute-start(bf16[128,384]{1,0:T(8,128)(2,1)S(1)} %pad_maximum_fusion.3), channel_id=1, source_target_pairs={{0,120},{1,7},{2,122},{3,5},{4,124},{5,11},{6,126},{7,9},{8,0},{9,... | collective-permute-start | bytes 294920 | tf_op jit(solution)/shard_map/ppermute | solution.py:45
  79.3 4.7 %collective-permute-start.19 = (bf16[64,768]{1,0:T(8,128)(2,1)S(1)}, bf16[64,768]{1,0:T(8,128)(2,1)S(1)}, u32[]{:S(2)}, u32[]{:S(2)}) collective-permute-start(bf16[64,768]{1,0:T(8,128)(2,1)S(1)} %get-tuple-element.72), channel_id=1, source_target_pairs={{0,2},{1,3},{2,0},{3,1},{4,6},{5,7},{6,4},{7,5},{8,10},{9,11},{10,... | collective-permute-start | bytes 294920 | tf_op jit(solution)/shard_map/ppermute | solution.py:33
  84.0 1.5 %collective-permute-start.22 = (f32[64,384]{1,0:T(8,128)S(1)}, f32[64,384]{1,0:T(8,128)S(1)}, u32[]{:S(2)}, u32[]{:S(2)}) collective-permute-start(f32[64,384]{1,0:T(8,128)S(1)} %convert_add_fusion), channel_id=1, source_target_pairs={{0,1},{1,0},{2,3},{3,2},{4,5},{5,4},{6,7},{7,6},{8,9},{9,8},{10,11... | collective-permute-start | bytes 294920 | tf_op jit(solution)/shard_map/ppermute | solution.py:33
  85.9 1.2 %collective-permute-start.23 = (f32[32,128]{1,0:T(8,128)S(1)}, f32[32,128]{1,0:T(8,128)S(1)}, u32[]{:S(2)}, u32[]{:S(2)}) collective-permute-start(f32[32,128]{1,0:T(8,128)S(1)} %get-tuple-element.75), channel_id=1, source_target_pairs={{0,1},{1,0},{2,3},{3,2},{4,5},{5,4},{6,7},{7,6},{8,9},{9,8},{10,11... | collective-permute-start | bytes 49160 | tf_op jit(solution)/shard_map/ppermute | solution.py:357
  87.1 4.9 %collective-permute-start.26 = (f32[32,128]{1,0:T(8,128)S(1)}, f32[32,128]{1,0:T(8,128)S(1)}, u32[]{:S(2)}, u32[]{:S(2)}) collective-permute-start(f32[32,128]{1,0:T(8,128)S(1)} %add.82), channel_id=1, source_target_pairs={{0,6},{1,7},{2,4},{3,5},{4,2},{5,3},{6,0},{7,1},{8,14},{9,15},{10,... | collective-permute-start | bytes 49160 | tf_op jit(solution)/shard_map/ppermute | solution.py:357
  89.6 5.2 %collective-permute-start.25 = (f32[32,128]{1,0:T(8,128)S(1)}, f32[32,128]{1,0:T(8,128)S(1)}, u32[]{:S(2)}, u32[]{:S(2)}) collective-permute-start(f32[32,128]{1,0:T(8,128)S(1)} %add.82), channel_id=1, source_target_pairs={{0,4},{1,5},{2,6},{3,7},{4,0},{5,1},{6,2},{7,3},{8,12},{9,13},{10,... | collective-permute-start | bytes 49160 | tf_op jit(solution)/shard_map/ppermute | solution.py:357
  89.6 5.2 %collective-permute-start.24 = (f32[32,128]{1,0:T(8,128)S(1)}, f32[32,128]{1,0:T(8,128)S(1)}, u32[]{:S(2)}, u32[]{:S(2)}) collective-permute-start(f32[32,128]{1,0:T(8,128)S(1)} %add.82), channel_id=1, source_target_pairs={{0,2},{1,3},{2,0},{3,1},{4,6},{5,7},{6,4},{7,5},{8,10},{9,11},{10,... | collective-permute-start | bytes 49160 | tf_op jit(solution)/shard_map/ppermute | solution.py:357
  94.8 5.0 %collective-permute-start.29 = (f32[32,128]{1,0:T(8,128)S(1)}, f32[32,128]{1,0:T(8,128)S(1)}, u32[]{:S(2)}, u32[]{:S(2)}) collective-permute-start(f32[32,128]{1,0:T(8,128)S(1)} %add_add_fusion.2), channel_id=1, source_target_pairs={{0,24},{1,25},{2,26},{3,27},{4,28},{5,29},{6,30},{7,31},{8,16},{9,... | collective-permute-start | bytes 49160 | tf_op jit(solution)/shard_map/ppermute | solution.py:357
  94.9 5.3 %collective-permute-start.28 = (f32[32,128]{1,0:T(8,128)S(1)}, f32[32,128]{1,0:T(8,128)S(1)}, u32[]{:S(2)}, u32[]{:S(2)}) collective-permute-start(f32[32,128]{1,0:T(8,128)S(1)} %add_add_fusion.2), channel_id=1, source_target_pairs={{0,16},{1,17},{2,18},{3,19},{4,20},{5,21},{6,22},{7,23},{8,24},{9,... | collective-permute-start | bytes 49160 | tf_op jit(solution)/shard_map/ppermute | solution.py:357
  97.9 3.7 %collective-permute-start.27 = (f32[32,128]{1,0:T(8,128)S(1)}, f32[32,128]{1,0:T(8,128)S(1)}, u32[]{:S(2)}, u32[]{:S(2)}) collective-permute-start(f32[32,128]{1,0:T(8,128)S(1)} %add_add_fusion.2), channel_id=1, source_target_pairs={{0,8},{1,9},{2,10},{3,11},{4,12},{5,13},{6,14},{7,15},{8,0},{9,1},... | collective-permute-start | bytes 49160 | tf_op jit(solution)/shard_map/ppermute | solution.py:357
  101.7 4.9 %collective-permute-start.32 = (f32[32,128]{1,0:T(8,128)S(1)}, f32[32,128]{1,0:T(8,128)S(1)}, u32[]{:S(2)}, u32[]{:S(2)}) collective-permute-start(f32[32,128]{1,0:T(8,128)S(1)} %add_add_fusion.1), channel_id=1, source_target_pairs={{0,96},{1,97},{2,98},{3,99},{4,100},{5,101},{6,102},{7,103},{8,104... | collective-permute-start | bytes 49160 | tf_op jit(solution)/shard_map/ppermute | solution.py:357
  104.1 5.2 %collective-permute-start.31 = (f32[32,128]{1,0:T(8,128)S(1)}, f32[32,128]{1,0:T(8,128)S(1)}, u32[]{:S(2)}, u32[]{:S(2)}) collective-permute-start(f32[32,128]{1,0:T(8,128)S(1)} %add_add_fusion.1), channel_id=1, source_target_pairs={{0,64},{1,65},{2,66},{3,67},{4,68},{5,69},{6,70},{7,71},{8,72},{9,... | collective-permute-start | bytes 49160 | tf_op jit(solution)/shard_map/ppermute | solution.py:357
  104.1 5.2 %collective-permute-start.30 = (f32[32,128]{1,0:T(8,128)S(1)}, f32[32,128]{1,0:T(8,128)S(1)}, u32[]{:S(2)}, u32[]{:S(2)}) collective-permute-start(f32[32,128]{1,0:T(8,128)S(1)} %add_add_fusion.1), channel_id=1, source_target_pairs={{0,32},{1,33},{2,34},{3,35},{4,36},{5,37},{6,38},{7,39},{8,40},{9,... | collective-permute-start | bytes 49160 | tf_op jit(solution)/shard_map/ppermute | solution.py:357
